TPU v7x, 32 devices: a whole 2x2x4 slice. The times are simulated.
32 devices in a mesh: group: 2 (over y), ctx: 4 (over x, core), exp: 4 (over z).
Axes of the slice: x: 2, y: 2, z: 4, core: 2. Of those that a mesh axis runs over, the one named last changes fastest.
Arguments:
- queries: bfloat16 [8, 512, 4608], P(('group', 'exp'), 'ctx'), parts along dimension 0, may hold values from -10 to 10
- latent_kv: bfloat16 [8, 512, 576], P(('group', 'exp'), 'ctx'), parts along dimension 0, may hold values from -8 to 8
- doc_lengths: int32 [8, 8], P(('group', 'exp')), parts along dimension 0, may hold values from 1 to 256, 512 in all within a row
- hidden_in: bfloat16 [8, 512, 1024], P(('group', 'exp'), 'ctx'), parts along dimension 0, may hold values from -6 to 6
- router_weight: bfloat16 [1024, 64], replicated, may hold values from -0.1875 to 0.1875
- expert_ids: int32 [8, 512, 6], P(('group', 'exp'), 'ctx'), parts along dimension 0, may hold values from 0 to 63, all different within a row; in each aligned block of 128 rows (0 to 127, 128 to 255, ..., all dimensions but the last counted through in order) at most 16 rows name the same one
- gate_up: bfloat16 [64, 704, 2, 1024], P('exp', 'ctx'), may hold values from -0.1875 to 0.1875
- w_down: bfloat16 [64, 704, 1024], P('exp', 'ctx'), may hold values from -0.21875 to 0.21875
Outputs:
- attn_context: bfloat16 [8, 512, 4096], P(('group', 'exp'), 'ctx'), parts along dimension 0
- expert_mix: bfloat16 [8, 512, 1024], P(('group', 'exp'), 'ctx'), parts along dimension 0
- balance: float32 [8, 8], P(('group', 'exp')), parts along dimension 0
There are 2 independent parts, one for each index of `group`. A program takes and returns all parts, laid end to end along the dimension named above; an argument that names none is the same for every part. Nothing has to cross between parts.
Inputs may be any that keep to these rules, and one draw needn't show every extreme that they name: `doc_lengths`: the 8 lengths of a row add up to 512; in every row the longest is exactly 256. `expert_ids`: each position names 6 different experts; among the positions of one device no expert is named more than 16 times, a bound that some block reaches.
All inputs are finite; a program needn't handle non-finite values.
Results may differ from a plain program's by a relative error of at most 0.008.
Values may be sent and summed in bfloat16 or wider, within the bound.
No kernel may reach another device: no remote copies, remote signals or barrier semaphores. Data moves between devices by JAX's collectives and lax.ppermute only.
A program may use at most 256 MiB of HBM per device.

v0:
```python
import jax
import jax.numpy as jnp
from jax import lax
from jax.sharding import PartitionSpec as P

D = 1024
EXPERTS = 64
TOPK = 6
HEADS = 8
LATENT = 512
CAP = 16
NDOC = 8
KDIM = 576


qk_scale = 192.0 ** (-0.5)


def segment_of(positions, lengths):
    ends = jnp.cumsum(lengths)
    return jnp.sum((positions[:, None] >= ends[None, :]).astype(jnp.int32), axis=1)


def shards(queries, latent_kv, doc_lengths, hidden_in, router_weight, expert_ids, gate_up, w_down):
    tok_rows = hidden_in.shape[1]
    ctx_index = lax.axis_index("ctx")
    lengths = doc_lengths[0]
    local_pos = jnp.arange(tok_rows, dtype=jnp.int32)
    query_pos = ctx_index * tok_rows + local_pos
    query_seg = segment_of(query_pos, lengths)
    own_keys = latent_kv[0]
    keys = lax.all_gather(own_keys, "ctx", axis=0, tiled=True)
    key_pos = jnp.arange(keys.shape[0], dtype=jnp.int32)
    key_seg = segment_of(key_pos, lengths)
    allowed = (
        (key_seg[None, :] == query_seg[:, None])
        & (key_pos[None, :] <= query_pos[:, None])
        & (key_pos[None, :] >= 0)
    )
    heads_q = queries[0].reshape(tok_rows, HEADS, KDIM)
    scores = jnp.einsum("thd,kd->htk", heads_q, keys, preferred_element_type=jnp.float32) * qk_scale
    scores = jnp.where(allowed[None], scores, -1e30)
    top = jnp.max(scores, axis=-1, keepdims=True)
    expo = jnp.exp(scores - top)
    weights = (expo / jnp.sum(expo, axis=-1, keepdims=True)).astype(jnp.bfloat16)
    context = jnp.einsum(
        "htk,kl->thl", weights, keys[:, :LATENT], preferred_element_type=jnp.float32
    )
    attn_context = context.astype(jnp.bfloat16).reshape(1, tok_rows, HEADS * LATENT)
    tokens = hidden_in[0]
    logits = jnp.dot(tokens, router_weight, preferred_element_type=jnp.float32)
    router = jax.nn.softmax(logits, axis=-1)
    ids = expert_ids[0]
    onehot = (ids[:, :, None] == jnp.arange(EXPERTS, dtype=jnp.int32)[None, None, :]).astype(
        jnp.float32
    )
    chosen = jnp.sum(onehot * router[:, None, :], axis=-1)
    gates = chosen / jnp.sum(chosen, axis=-1, keepdims=True)
    flat_hot = onehot.reshape(-1, EXPERTS).astype(jnp.int32)
    before = jnp.cumsum(flat_hot, axis=0) - flat_hot
    slot_of = jnp.sum(before * flat_hot, axis=1)
    target = ids.reshape(-1) * CAP + slot_of
    pair_rows = jnp.repeat(tokens, TOPK, axis=0)
    outgoing = jnp.zeros((EXPERTS * CAP, D), jnp.bfloat16).at[target].set(pair_rows)
    senders = lax.axis_size("exp")
    local_count = EXPERTS // senders
    outgoing = outgoing.reshape(senders, local_count, CAP, D)
    arrived = lax.all_to_all(outgoing, "exp", split_axis=0, concat_axis=0, tiled=True)
    both = jnp.einsum(
        "secd,efzd->zsecf",
        arrived,
        lax.all_gather(gate_up, "ctx", axis=1, tiled=True),
        preferred_element_type=jnp.float32,
    )
    inner = (jax.nn.silu(both[0]) * both[1]).astype(jnp.bfloat16)
    produced = jnp.einsum(
        "secf,efd->secd",
        inner,
        lax.all_gather(w_down, "ctx", axis=1, tiled=True),
        preferred_element_type=jnp.float32,
    )
    returned = lax.all_to_all(
        produced.astype(jnp.bfloat16), "exp", split_axis=0, concat_axis=0, tiled=True
    )
    pair_out = returned.reshape(EXPERTS * CAP, D)[target].reshape(tok_rows, TOPK, D)
    mix = jnp.zeros((tok_rows, D), jnp.float32)
    for slot in range(TOPK):
        mix = mix + gates[:, slot, None] * pair_out[:, slot].astype(jnp.float32)
    expert_mix = mix.astype(jnp.bfloat16).reshape(1, tok_rows, D)
    tok_exp = jnp.sum(onehot, axis=1)
    doc_index = jnp.arange(NDOC, dtype=jnp.int32)
    router_all, picks_all = (
        lax.all_gather(router.astype(jnp.bfloat16), "ctx", axis=0, tiled=True).astype(router.dtype),
        lax.all_gather(tok_exp.astype(jnp.bfloat16), "ctx", axis=0, tiled=True).astype(
            tok_exp.dtype
        ),
    )
    all_pos = jnp.arange(router_all.shape[0], dtype=jnp.int32)
    seg_all = segment_of(all_pos, lengths)
    seg_hot = (seg_all[:, None] == doc_index[None, :]).astype(jnp.float32)
    counts = jnp.dot(seg_hot.T, picks_all, precision=lax.Precision.HIGHEST)
    mass = jnp.dot(seg_hot.T, router_all, precision=lax.Precision.HIGHEST)
    sizes_f = lengths.astype(jnp.float32)[:, None]
    balance = jnp.sum(EXPERTS * counts / (TOPK * sizes_f) * (mass / sizes_f), axis=-1)
    return (attn_context, expert_mix, balance.reshape(1, NDOC))


def solution(mesh):
    placed = (
        P(("group", "exp"), "ctx", None),
        P(("group", "exp"), "ctx", None),
        P(("group", "exp"), None),
        P(("group", "exp"), "ctx", None),
        P(),
        P(("group", "exp"), "ctx", None),
        P("exp", "ctx", None, None),
        P("exp", "ctx", None),
    )
    return jax.shard_map(
        shards,
        mesh=mesh,
        in_specs=placed,
        out_specs=(
            P(("group", "exp"), "ctx", None),
            P(("group", "exp"), "ctx", None),
            P(("group", "exp"), None),
        ),
        check_vma=False,
    )
```

profile of v0, /device:TPU:0, one launch (start us, length us, event | category | flops | bytes accessed | tf_op | source)
XLA Modules:
  0.0 525.3 jit_solution(5322464797739320049)
XLA Ops:
  7.2 11.4 %copy.64 = bf16[16,176,2,1024]{3,1,2,0:T(8,128)(2,1)} copy(bf16[16,176,2,1024]{3,2,1,0:T(2,128)(2,1)} %param.14) | data formatting | bytes 23068672 | tf_op args[6]
  19.9 1.8 reduce-window.19
  22.6 1.5 reshape.470
  24.3 8.2 %scatter_custom_fusion = bf16[1024,1024]{1,0:T(8,128)(2,1)} fusion(s32[768]{0:T(1024)S(1)} %fusion.58, bf16[768,1024]{1,0:T(8,128)(2,1)} %reshape.470, bf16[]{:T(256)} %constant.37.clone.1), kind=kCustom, calls=%fused_computation.26 | custom fusion | bytes 2097664 | tf_op jit(solution)/shard_map/scatter | solution.py:64
  32.5 6.4 %all-to-all-start = ((bf16[4,16,16,1024]{3,2,1,0:T(8,128)(2,1)}), bf16[4,16,16,1024]{3,2,1,0:T(8,128)(2,1)S(1)}, u32[]{:S(2)}, u32[]{:S(2)}) async-start(bf16[4,16,16,1024]{3,2,1,0:T(8,128)(2,1)} %bitcast.12), calls=%async_computation | async-start | bytes 4194304 | tf_op jit(solution)/shard_map/all_to_all | solution.py:68
  39.7 1.4 copy.56
  42.6 44.6 %all-to-all-done = bf16[4,16,16,1024]{3,2,1,0:T(8,128)(2,1)S(1)} async-done(((bf16[4,16,16,1024]{3,2,1,0:T(8,128)(2,1)}), bf16[4,16,16,1024]{3,2,1,0:T(8,128)(2,1)S(1)}, u32[]{:S(2)}, u32[]{:S(2)}) %all-to-all-start) | async-done | bytes 2097184 | tf_op jit(solution)/shard_map/all_to_all | solution.py:68
  87.2 207.6 %all-gather.4.cloned.1.call-done = bf16[16,704,2,1024]{3,1,2,0:T(8,128)(2,1)} async-done(((bf16[16,176,2,1024]{3,1,2,0:T(8,128)(2,1)}), bf16[16,704,2,1024]{3,1,2,0:T(8,128)(2,1)}) %all-gather.4.cloned.1.call-update) | async-done | bytes 46137360 | tf_op jit(solution)/shard_map/all_gather | solution.py:72
  294.8 26.7 %fusion.7 = f32[2,4,16,16,704]{4,3,0,1,2:T(8,128)} fusion(bf16[16,704,2,1024]{3,1,2,0:T(8,128)(2,1)} %all-gather.4.cloned.1.call-done, bf16[4,16,16,1024]{3,2,1,0:T(8,128)(2,1)S(1)} %all-to-all-done), kind=kOutput, calls=%fused_computation.11 | convolution fusion | flops 2952790016 | bytes 54001664 | tf_op jit(solution)/shard_map/secd,efzd->zsecf/dot_general | solution.py:69
  321.6 117.8 %all-gather.6.cloned.1.call-done = bf16[16,704,1024]{2,1,0:T(8,128)(2,1)} async-done(((bf16[16,176,1024]{2,1,0:T(8,128)(2,1)}), bf16[16,704,1024]{2,1,0:T(8,128)(2,1)}) %all-gather.6.cloned.1.call-update) | async-done | bytes 23068688 | tf_op jit(solution)/shard_map/all_gather | solution.py:79
  439.4 13.6 %convert_bitcast_fusion = bf16[4,16,16,1024]{3,2,0,1:T(8,128)(2,1)S(1)} fusion(bf16[16,704,1024]{2,1,0:T(8,128)(2,1)} %all-gather.6.cloned.1.call-done, f32[2,4,16,16,704]{4,3,0,1,2:T(8,128)} %fusion.7), kind=kOutput, calls=%fused_computation.14 | convolution fusion | flops 1481768960 | bytes 30932992 | tf_op jit(solution)/shard_map/secf,efd->secd/dot_general | solution.py:76
  453.0 1.5 copy.67
  454.5 4.7 all-to-all-start.1
  459.3 7.7 %all-gather = bf16[1,512,576]{1,2,0:T(8,128)(2,1)} all-gather(bf16[1,128,576]{1,2,0:T(8,128)(2,1)S(1)} %copy-done.5), channel_id=2, replica_groups=mesh['group'=2,'ctx'=4,'exp'=4] {'ctx'}, dimensions={1}, use_global_device_ids=true | all-gather | bytes 737280 | tf_op jit(solution)/shard_map/all_gather | solution.py:32
  467.0 2.4 fusion.71
  469.4 3.4 fusion.25
  472.8 3.8 fusion.16
  476.7 1.7 copy.59
  480.0 5.3 %all_gather.18 = bf16[512,64]{0,1:T(8,128)(2,1)S(1)} all-gather(bf16[128,64]{0,1:T(8,128)(2,1)S(1)} %get-tuple-element.14), channel_id=1, replica_groups=mesh['group'=2,'ctx'=4,'exp'=4] {'ctx'}, dimensions={0}, use_global_device_ids=true | all-gather | bytes 81920 | tf_op jit(solution)/shard_map/all_gather | solution.py:94
  485.3 5.5 %all_gather.19 = bf16[512,64]{0,1:T(8,128)(2,1)S(1)} all-gather(bf16[128,64]{0,1:T(8,128)(2,1)S(1)} %get-tuple-element.15), channel_id=1, replica_groups=mesh['group'=2,'ctx'=4,'exp'=4] {'ctx'}, dimensions={0}, use_global_device_ids=true | all-gather | bytes 81920 | tf_op jit(solution)/shard_map/all_gather | solution.py:93
  492.0 15.9 %all-to-all-done.1 = bf16[4,16,16,1024]{3,2,1,0:T(8,128)(2,1)S(1)} async-done(((bf16[4,16,16,1024]{3,2,1,0:T(8,128)(2,1)}), bf16[4,16,16,1024]{3,2,1,0:T(8,128)(2,1)S(1)}, u32[]{:S(2)}, u32[]{:S(2)}) %all-to-all-start.1) | async-done | bytes 2097184 | tf_op jit(solution)/shard_map/all_to_all | solution.py:82
  507.9 3.6 gather_fusion
  511.4 2.5 reshape.450
  513.9 3.8 fusion.44
  (63 shorter events, 8.2 us)
Async XLA Ops:
  7.2 472.5 %copy-start = (bf16[1024,64]{0,1:T(8,128)(2,1)S(1)}, bf16[1024,64]{0,1:T(8,128)(2,1)}, u32[]{:S(2)}) copy-start(bf16[1024,64]{0,1:T(8,128)(2,1)} %param.12) | copy-start | bytes 393220
  7.2 287.6 %all-gather.4.cloned.1.call-start = ((), (), s32[]{:S(2)}) async-start(), calls=%async_computation.2 | async-start | bytes 57671680 | tf_op jit(solution)/shard_map/all_gather | solution.py:72
  18.7 0.8 copy-start.6
  18.7 3.6 copy-start.3
  18.7 420.7 %all-gather.6.cloned.1.call-start = ((), (), s32[]{:S(2)}) async-start(), calls=%async_computation.3 | async-start | bytes 28835840 | tf_op jit(solution)/shard_map/all_gather | solution.py:79
  24.2 8.3 %copy-start.8 = (s32[768]{0:T(1024)}, s32[768]{0:T(1024)S(1)}, u32[]{:S(2)}) copy-start(s32[768]{0:T(1024)S(1)} %fusion.58) | copy-start | bytes 9220
  32.5 7.0 %copy-start.12 = (s32[1,8]{1,0:T(1,128)S(1)}, s32[1,8]{1,0:T(1,128)}, u32[]{:S(2)}) copy-start(s32[1,8]{1,0:T(1,128)} %param.10) | copy-start | bytes 100
  32.5 7.2 %copy-start.1 = (bf16[1,128,4608]{2,1,0:T(8,128)(2,1)S(1)}, bf16[1,128,4608]{2,1,0:T(8,128)(2,1)}, u32[]{:S(2)}) copy-start(bf16[1,128,4608]{2,1,0:T(8,128)(2,1)} %param.8) | copy-start | bytes 3538948
  32.5 54.7 %all-to-all-start = ((bf16[4,16,16,1024]{3,2,1,0:T(8,128)(2,1)}), bf16[4,16,16,1024]{3,2,1,0:T(8,128)(2,1)S(1)}, u32[]{:S(2)}, u32[]{:S(2)}) async-start(bf16[4,16,16,1024]{3,2,1,0:T(8,128)(2,1)} %bitcast.12), calls=%async_computation | async-start | bytes 4194304 | tf_op jit(solution)/shard_map/all_to_all | solution.py:68
  41.2 0.6 copy-start.10
  454.5 4.7 copy-start.5
  454.5 12.5 %copy-start.2 = (bf16[1,128,4608]{1,2,0:T(8,128)(2,1)S(1)}, bf16[1,128,4608]{1,2,0:T(8,128)(2,1)}, u32[]{:S(2)}) copy-start(bf16[1,128,4608]{1,2,0:T(8,128)(2,1)} %copy.56) | copy-start | bytes 3538948
  454.5 53.3 %all-to-all-start.1 = ((bf16[4,16,16,1024]{3,2,1,0:T(8,128)(2,1)}), bf16[4,16,16,1024]{3,2,1,0:T(8,128)(2,1)S(1)}, u32[]{:S(2)}, u32[]{:S(2)}) async-start(bf16[4,16,16,1024]{3,2,1,0:T(8,128)(2,1)} %copy.67), calls=%async_computation.1 | async-start | bytes 4194304 | tf_op jit(solution)/shard_map/all_to_all | solution.py:82
  476.6 3.0 copy-start.4
  476.6 3.3 copy-start.7
  476.6 14.1 %copy-start.9 = (s32[768]{0:T(1024)S(1)}, s32[768]{0:T(1024)}, u32[]{:S(2)}) copy-start(s32[768]{0:T(1024)} %copy-done.8) | copy-start | bytes 9220
  476.6 14.1 %copy-start.13 = (s32[1,8]{1,0:T(1,128)S(1)}, s32[1,8]{1,0:T(1,128)}, u32[]{:S(2)}) copy-start(s32[1,8]{1,0:T(1,128)} %param.10) | copy-start | bytes 100
  476.7 14.1 %copy-start.11 = (s32[512]{0:T(512)S(1)}, s32[512]{0:T(512)}, u32[]{:S(2)}) copy-start(s32[512]{0:T(512)} %copy-done.10) | copy-start | bytes 6148
Sparse Core Ops, SparseCore 0:
  18.8 275.9 all-gather.3
  296.4 142.9 all-gather.5
where the time goes:
time: 526 us; the launch traced here: 525 us
  waiting for transfers between devices  387 us (74%)
  matrix products  51.4 us (10%)
  local copies, waits for them, and re-layouts  36.3 us (7%)
  blocking collectives  18.5 us (4%)
  between operations  14.2 us (3%)
  starting transfers between devices  11.3 us (2%)
  other arithmetic  7.02 us (1%)
    all_gather x1, waiting for transfers between devices, shards(): lax.all_gather(gate_up, 'ctx', axis=1, tiled=True)  208 us
    all_gather x1, waiting for transfers between devices, shards(): lax.all_gather(w_down, 'ctx', axis=1, tiled=True)  118 us
    all_to_all x1, waiting for transfers between devices, shards(): lax.all_to_all(outgoing, 'exp', split_axis=0, concat_axis=0, tiled=True)  44.6 us
    dot_general x1, matrix products, shards(): jnp.einsum('secd,efzd->zsecf', arrived, lax.all_gather(gate_up, 'ctx', ax...  26.7 us
    unnamed x34, local copies, waits for them, and re-layouts  16.2 us
    all_to_all x1, waiting for transfers between devices, shards(): lax.all_to_all(produced.astype(jnp.bfloat16), 'exp', split_axis=0, concat...  15.9 us
    dot_general x1, matrix products, shards(): jnp.einsum('secf,efd->secd', inner, lax.all_gather(w_down, 'ctx', axis=1,...  13.6 us
  transfers between devices with their start and end apart: 4, of which 4 were waited for; matrix products, arithmetic and copies ran while one was open for 11% of the time, Pallas kernels for 0%

commit v1 on v0

v1 whole, which is shorter than its diff:
```python
import functools

import jax
import jax.numpy as jnp
from jax import lax
from jax.experimental import pallas as pl
from jax.experimental.pallas import tpu as pltpu
from jax.sharding import PartitionSpec as P

EXPERTS = 64
HEADS = 8
LATENT = 512
CAP = 16
NDOC = 8
BLOCK = 128
LANES = 128
CHUNK_BLOCKS = 16
VMEM = 56 * 2**20

qk_scale = 192.0 ** (-0.5)


def moe_kernel(n_parts, with_balance, *refs):
    parts, refs = refs[:n_parts], refs[n_parts:]
    ids_ref, rw_ref, seg_ref, scale_ref, gate_ref, up_ref, down_ref = refs[:7]
    outs, refs = refs[7 : 7 + n_parts], refs[7 + n_parts :]
    bal_ref = refs[0]
    x, y, keys, gates, picks, rows, weight, made, in_sem, out_sem = refs[1:]
    chunk, e = pl.program_id(0), pl.program_id(1)
    n_exp = pl.num_programs(1)
    tokens = x.shape[0]
    blocks = tokens // BLOCK
    share = tokens // n_parts
    local = rows.shape[0]
    slots = local * CAP

    def part_of(ref):
        return ref.at[pl.ds(pl.multiple_of(chunk * share, share), share), :]

    @pl.when(e == 0)
    def _():
        copies = [
            pltpu.make_async_copy(
                part_of(parts[i]), x.at[pl.ds(i * share, share), :], in_sem.at[i]
            )
            for i in range(n_parts)
        ]
        for copy in copies:
            copy.start()
        for copy in copies:
            copy.wait()
        logits = lax.dot_general(
            rw_ref[...], x[...], (((1,), (1,)), ((), ())), preferred_element_type=jnp.float32
        )
        expo = jnp.exp(logits - jnp.max(logits, axis=0, keepdims=True))
        router = expo / jnp.sum(expo, axis=0, keepdims=True)
        names = lax.broadcasted_iota(jnp.int32, (EXPERTS, BLOCK), 0)
        before = (
            lax.broadcasted_iota(jnp.int32, (BLOCK, BLOCK), 0)
            < lax.broadcasted_iota(jnp.int32, (BLOCK, BLOCK), 1)
        ).astype(jnp.bfloat16)
        hots, probs = [], []
        for b in range(blocks):
            ids = ids_ref[b]
            hot = names == ids[0:1]
            for k in range(1, ids.shape[0]):
                hot = hot | (names == ids[k : k + 1])
            hot = hot.astype(jnp.float32)
            prob = router[:, b * BLOCK : (b + 1) * BLOCK]
            chosen = prob * hot
            total = jnp.sum(chosen, axis=0, keepdims=True)
            own = hot[:local]
            rank = jnp.dot(own.astype(jnp.bfloat16), before, preferred_element_type=jnp.float32)
            keys[b] = jnp.where(own > 0.0, rank, -1.0)
            gates[b] = chosen[:local] / total
            hots.append(hot)
            probs.append(prob)
        if with_balance:
            n_row = seg_ref.shape[0]
            for d in range(NDOC):
                counts = jnp.zeros((EXPERTS, BLOCK), jnp.float32)
                mass = jnp.zeros((EXPERTS, BLOCK), jnp.float32)
                for b in range(n_row):
                    inside = seg_ref[b] == d
                    counts = counts + jnp.where(inside, hots[b], 0.0)
                    mass = mass + jnp.where(inside, probs[b], 0.0)
                both = jnp.sum(counts, axis=1, keepdims=True) * jnp.sum(
                    mass, axis=1, keepdims=True
                )
                bal_ref[d : d + 1, :] = (
                    jnp.broadcast_to(jnp.sum(both, axis=0, keepdims=True), (1, LANES))
                    * scale_ref[d : d + 1, :]
                )
        else:
            bal_ref[...] = jnp.zeros_like(bal_ref)

        slot = lax.broadcasted_iota(jnp.int32, (local, CAP, BLOCK), 1).astype(jnp.float32)

        @pl.loop(0, blocks)
        def _(b):
            pick = (keys[b][:, None, :] == slot).astype(jnp.float32)
            gate = jnp.sum(pick * gates[b][:, None, :], axis=-1, keepdims=True)
            at = pl.ds(pl.multiple_of(b * CAP, CAP), CAP)
            weight[:, at, :] = jnp.broadcast_to(gate, (local, CAP, LANES))
            pick = pick.reshape(slots, BLOCK).astype(jnp.bfloat16)
            picks[b] = pick
            taken = jnp.dot(
                pick,
                x[pl.ds(pl.multiple_of(b * BLOCK, BLOCK), BLOCK), :],
                preferred_element_type=jnp.float32,
            )
            rows[:, at, :] = taken.astype(jnp.bfloat16).reshape(local, CAP, x.shape[1])

    held = rows[e]
    nt = (((1,), (1,)), ((), ()))
    g = lax.dot_general(held, gate_ref[0], nt, preferred_element_type=jnp.float32)
    u = lax.dot_general(held, up_ref[0], nt, preferred_element_type=jnp.float32)
    width = g.shape[1]
    w = jnp.concatenate([weight[e]] * pl.cdiv(width, LANES), axis=1)[:, :width]
    inner = (g * lax.logistic(g) * u * w).astype(jnp.bfloat16)
    made[e] = jnp.dot(inner, down_ref[0], preferred_element_type=jnp.float32).astype(jnp.bfloat16)

    @pl.when(e == n_exp - 1)
    def _():
        @pl.loop(0, blocks)
        def _(b):
            at = pl.ds(pl.multiple_of(b * CAP, CAP), CAP)
            mix = lax.dot_general(
                picks[b],
                made[:, at, :].reshape(slots, x.shape[1]),
                (((0,), (0,)), ((), ())),
                preferred_element_type=jnp.float32,
            )
            y[pl.ds(pl.multiple_of(b * BLOCK, BLOCK), BLOCK), :] = mix.astype(jnp.bfloat16)

        copies = [
            pltpu.make_async_copy(
                y.at[pl.ds(i * share, share), :], part_of(outs[i]), out_sem.at[i]
            )
            for i in range(n_parts)
        ]
        for copy in copies:
            copy.start()
        for copy in copies:
            copy.wait()


def moe(parts, ids, rw, seg, scale, gate, up, down, with_balance):
    n_parts = len(parts)
    part_rows, width = parts[0].shape
    local, hidden, _ = gate.shape
    share = min(part_rows, max(CHUNK_BLOCKS // n_parts, 1) * BLOCK)
    chunks = part_rows // share
    tokens = n_parts * share
    blocks = tokens // BLOCK
    anywhere = pl.BlockSpec(memory_space=pl.ANY)

    def whole(a):
        return pl.BlockSpec(a.shape, lambda c, e: (0,) * a.ndim)

    def expert(a):
        return pl.BlockSpec((1,) + a.shape[1:], lambda c, e: (e, 0, 0))

    rounds = chunks * local
    flops = 2 * rounds * blocks * CAP * width * (3 * hidden + 2 * BLOCK)
    moved = 6 * local * hidden * width + 4 * chunks * tokens * width
    result = pl.pallas_call(
        functools.partial(moe_kernel, n_parts, with_balance),
        grid=(chunks, local),
        in_specs=[anywhere] * n_parts
        + [
            pl.BlockSpec((blocks,) + ids.shape[1:], lambda c, e: (c, 0, 0)),
            whole(rw),
            whole(seg),
            whole(scale),
            expert(gate),
            expert(up),
            expert(down),
        ],
        out_specs=[anywhere] * n_parts + [pl.BlockSpec((NDOC, LANES), lambda c, e: (0, 0))],
        out_shape=[jax.ShapeDtypeStruct(p.shape, jnp.bfloat16) for p in parts]
        + [jax.ShapeDtypeStruct((NDOC, LANES), jnp.float32)],
        scratch_shapes=[
            pltpu.VMEM((tokens, width), jnp.bfloat16),
            pltpu.VMEM((tokens, width), jnp.bfloat16),
            pltpu.VMEM((blocks, local, BLOCK), jnp.float32),
            pltpu.VMEM((blocks, local, BLOCK), jnp.float32),
            pltpu.VMEM((blocks, local * CAP, BLOCK), jnp.bfloat16),
            pltpu.VMEM((local, blocks * CAP, width), jnp.bfloat16),
            pltpu.VMEM((local, blocks * CAP, LANES), jnp.float32),
            pltpu.VMEM((local, blocks * CAP, width), jnp.bfloat16),
            pltpu.SemaphoreType.DMA((n_parts,)),
            pltpu.SemaphoreType.DMA((n_parts,)),
        ],
        compiler_params=pltpu.CompilerParams(
            dimension_semantics=("arbitrary", "arbitrary"), vmem_limit_bytes=VMEM
        ),
        cost_estimate=pl.CostEstimate(flops=flops, bytes_accessed=moved, transcendentals=0),
        name="experts",
    )(*parts, ids, rw, seg, scale, gate, up, down)
    return list(result[:n_parts]), result[n_parts]


def attend_kernel(first_ref, last_ref, q_ref, kv_ref, out_ref, even, odd):
    length, kdim = kv_ref.shape
    wide = even.shape[1]
    half = wide - kdim

    @pl.when(pl.program_id(0) == 0)
    def _():
        pad = jnp.zeros((length, half), jnp.bfloat16)
        even[...] = jnp.concatenate([kv_ref[...], pad], axis=1)
        odd[...] = jnp.concatenate([pad, kv_ref[...]], axis=1)

    rows = q_ref.shape[0]
    kpos = lax.broadcasted_iota(jnp.int32, (rows, length), 1)
    allowed = (kpos >= first_ref[...]) & (kpos <= last_ref[...])
    for i, keys in enumerate((even, odd)):
        at = i * (kdim - half)
        scores = lax.dot_general(
            q_ref[:, at : at + wide],
            keys[...],
            (((1,), (1,)), ((), ())),
            preferred_element_type=jnp.float32,
        )
        scores = jnp.where(allowed, scores * qk_scale, -1e30)
        expo = jnp.exp(scores - jnp.max(scores, axis=-1, keepdims=True))
        probs = (expo / jnp.sum(expo, axis=-1, keepdims=True)).astype(jnp.bfloat16)
        out_ref[:, i * LATENT : (i + 1) * LATENT] = jnp.dot(
            probs, kv_ref[:, :LATENT], preferred_element_type=jnp.float32
        ).astype(jnp.bfloat16)


def attend(queries, kv, first, last):
    rows = queries.shape[0]
    length, kdim = kv.shape
    wide = -(-kdim // LANES) * LANES
    return pl.pallas_call(
        attend_kernel,
        grid=(HEADS // 2,),
        in_specs=[
            pl.BlockSpec((rows, 1), lambda h: (0, 0)),
            pl.BlockSpec((rows, 1), lambda h: (0, 0)),
            pl.BlockSpec((rows, 2 * kdim), lambda h: (0, h)),
            pl.BlockSpec((length, kdim), lambda h: (0, 0)),
        ],
        out_specs=pl.BlockSpec((rows, 2 * LATENT), lambda h: (0, h)),
        out_shape=jax.ShapeDtypeStruct((rows, HEADS * LATENT), jnp.bfloat16),
        scratch_shapes=[pltpu.VMEM((length, wide), jnp.bfloat16)] * 2,
        compiler_params=pltpu.CompilerParams(
            dimension_semantics=("arbitrary",), vmem_limit_bytes=VMEM // 2
        ),
        cost_estimate=pl.CostEstimate(
            flops=2 * HEADS * rows * length * (wide + LATENT),
            bytes_accessed=2 * rows * HEADS * (kdim + LATENT),
            transcendentals=HEADS * rows * length,
        ),
        name="attention",
    )(first, last, queries, kv)


def add(a, b):
    return (a.astype(jnp.float32) + b.astype(jnp.float32)).astype(jnp.bfloat16)


def shards(queries, latent_kv, doc_lengths, hidden_in, router_weight, expert_ids, gate_up, w_down):
    tok_rows = hidden_in.shape[1]
    n_ctx, n_exp = lax.axis_size("ctx"), lax.axis_size("exp")
    ctx, exp = lax.axis_index("ctx"), lax.axis_index("exp")
    local = gate_up.shape[0]
    flips = [1 << i for i in range(n_ctx.bit_length() - 1)]
    shifts = range(n_exp) if n_exp <= 4 else (0,)
    tokens = hidden_in[0]

    def flip(a, bit):
        return lax.ppermute(a, "ctx", [(i, i ^ bit) for i in range(n_ctx)])

    def shift(a, d):
        return lax.ppermute(a, "exp", [(i, (i + d) % n_exp) for i in range(n_exp)])

    if n_exp <= 4:
        spread = [[tokens if d == 0 else shift(tokens, d)] for d in shifts]
    else:
        spread = [[lax.all_gather(tokens, "exp", axis=0, tiled=True)]]
    for bit in reversed(flips):
        spread = [held + [flip(a, bit) for a in held] for held in spread]
    masks = [0]
    for bit in reversed(flips):
        masks = masks + [m ^ bit for m in masks]

    picks = jnp.swapaxes(expert_ids[0].reshape(tok_rows // BLOCK, BLOCK, -1), 1, 2)
    all_picks = lax.all_gather(picks, ("exp", "ctx"), axis=0, tiled=False)
    all_picks = jnp.mod(all_picks - exp * local, EXPERTS)
    all_picks = all_picks.reshape((n_exp, n_ctx) + picks.shape)
    order = jnp.stack([ctx ^ m for m in masks])
    all_picks = jnp.take(all_picks, order, axis=1)

    lengths = doc_lengths[0]
    ends = jnp.cumsum(lengths)
    row_pos = (order[:, None] * tok_rows + jnp.arange(tok_rows, dtype=jnp.int32)[None, :]).reshape(
        -1, 1, BLOCK
    )
    seg = jnp.sum((row_pos[..., None] >= ends).astype(jnp.int32), axis=-1)
    sizes = lengths.astype(jnp.float32)
    scale = jnp.broadcast_to((EXPERTS / (expert_ids.shape[2] * sizes * sizes))[:, None], (NDOC, LANES))

    rw = jnp.roll(router_weight.T, -exp * local, axis=0)
    gate, up = gate_up[:, :, 0, :], gate_up[:, :, 1, :]
    if n_exp <= 4:
        back = jnp.stack([jnp.mod(exp - d, n_exp) for d in shifts])
        ids = jnp.take(all_picks, back, axis=0).reshape(-1, picks.shape[1], BLOCK)
        flat = [a for held in spread for a in held]
        made, balance = moe(flat, ids, rw, seg, scale, gate, up, w_down, True)
        made = [made[i * n_ctx : (i + 1) * n_ctx] for i in range(n_exp)]
    else:
        made = []
        for i, a in enumerate(spread[0]):
            ids = all_picks[:, i].reshape(-1, picks.shape[1], BLOCK)
            made.append(moe([a], ids, rw, seg, scale, gate, up, w_down, False)[0][0])
        made = [made]
        balance = None

    for bit in flips:
        half = len(made[0]) // 2
        made = [[add(h[i], flip(h[half + i], bit)) for i in range(half)] for h in made]
    if n_exp <= 4:
        total = made[0][0].astype(jnp.float32)
        for d in shifts[1:]:
            total = total + shift(made[d][0], -d).astype(jnp.float32)
        expert_mix = total.astype(jnp.bfloat16)
    else:
        expert_mix = lax.psum_scatter(made[0][0], "exp", scatter_dimension=0, tiled=True)

    kv = lax.all_gather(latent_kv[0], "ctx", axis=0, tiled=True)
    pos = ctx * tok_rows + jnp.arange(tok_rows, dtype=jnp.int32)
    passed = pos[:, None] >= ends[None, :]
    first = jnp.max(jnp.where(passed, ends[None, :], 0), axis=1)
    context = attend(queries[0], kv, first[:, None], pos[:, None])

    if balance is None:
        row = lax.all_gather(tokens, "ctx", axis=0, tiled=True)
        router = jax.nn.softmax(
            jnp.dot(row, router_weight, preferred_element_type=jnp.float32), axis=-1
        )
        row_ids = lax.all_gather(expert_ids[0], "ctx", axis=0, tiled=True)
        hot = (row_ids[:, :, None] == jnp.arange(EXPERTS, dtype=jnp.int32)).astype(jnp.float32)
        at = jnp.arange(row.shape[0], dtype=jnp.int32)
        seg_at = jnp.sum((at[:, None] >= ends[None, :]).astype(jnp.int32), axis=1)
        seg_hot = (seg_at[:, None] == jnp.arange(NDOC, dtype=jnp.int32)).astype(jnp.float32)
        exact = lax.Precision.HIGHEST
        counts = jnp.dot(seg_hot.T, hot.sum(axis=1), precision=exact)
        mass = jnp.dot(seg_hot.T, router, precision=exact)
        per_doc = jnp.sum(counts * mass, axis=1) * scale[:, 0]
    else:
        per_doc = balance[:, 0]
    return context[None], expert_mix[None], per_doc.reshape(1, NDOC)


def solution(mesh):
    rows = P(("group", "exp"), "ctx", None)
    docs = P(("group", "exp"), None)
    return jax.shard_map(
        shards,
        mesh=mesh,
        in_specs=(rows, rows, docs, rows, P(), rows, P("exp", "ctx", None, None), P("exp", "ctx", None)),
        out_specs=(rows, rows, docs),
        check_vma=False,
    )
```

time: 526 us -> 183 us (0.35)
  waiting for transfers between devices: 387 us -> 35.5 us
  matrix products: 51.4 us -> 0 us
  Pallas kernels: 0 us -> 38.3 us
  between operations: 14.2 us -> 0.99 us
  local copies, waits for them, and re-layouts: 36.3 us -> 46 us
  blocking collectives: 18.5 us -> 28.1 us
  other arithmetic: 7.02 us -> 14.9 us
  starting transfers between devices: 11.3 us -> 18.1 us
    all_gather x2 -> x0, waiting for transfers between devices: 325 us -> none  [the longest x1 208 us: shards(): lax.all_gather(gate_up, 'ctx', axis=1, tiled=True)]
    all_to_all x2 -> x0, waiting for transfers between devices: 60.5 us -> none  [the longest x1 44.6 us: shards(): lax.all_to_all(outgoing, 'exp', split_axis=0, concat_axis=0, tiled=True)]
    dot_general x7 -> x0, matrix products: 49 us -> none  [the longest x1 26.7 us: shards(): jnp.einsum('secd,efzd->zsecf', arrived, lax.all_gather(gate_up, 'ctx', ax...]
    pallas_call x0 -> x2, Pallas kernels: none -> 38.3 us  [the longest x1 32.1 us: moe(): pl.pallas_call(functools.partial(moe_kernel, n_parts, with_balance), grid...]
    ppermute x0 -> x30, waiting for transfers between devices: none -> 35.5 us  [the longest x24 27.6 us: flip(): return lax.ppermute(a, 'ctx', [(i, i ^ bit) for i in range(n_ctx)])]
    slice x1 -> x2, local copies, waits for them, and re-layouts: 0.28 us -> 27.5 us  [the longest x1 26.9 us: shards(): gate, up = (gate_up[:, :, 0, :], gate_up[:, :, 1, :])]
    ppermute x0 -> x30, starting transfers between devices: none -> 18.1 us  [the longest x24 11.7 us: flip(): return lax.ppermute(a, 'ctx', [(i, i ^ bit) for i in range(n_ctx)])]
    squeeze x0 -> x1, local copies, waits for them, and re-layouts: none -> 15.7 us  [shards(): gate, up = (gate_up[:, :, 0, :], gate_up[:, :, 1, :])]
  transfers between devices with their start and end apart: 4 -> 30, of which waited for: 4 -> 6; matrix products, arithmetic and copies ran while one was open for 11% -> 32% of each run, Pallas kernels for 0% -> 3%
where the time goes in v1:
time: 183 us; the launch traced here: 182 us
  local copies, waits for them, and re-layouts  46 us (25%)
  Pallas kernels  38.3 us (21%)
  waiting for transfers between devices  35.5 us (19%)
  blocking collectives  28.1 us (15%)
  starting transfers between devices  18.1 us (10%)
  other arithmetic  14.9 us (8%)
    pallas_call x1, Pallas kernels, moe(): pl.pallas_call(functools.partial(moe_kernel, n_parts, with_balance), grid...  32.1 us
    ppermute x24, waiting for transfers between devices, flip(): return lax.ppermute(a, 'ctx', [(i, i ^ bit) for i in range(n_ctx)])  27.6 us
    slice x1, local copies, waits for them, and re-layouts, shards(): gate, up = (gate_up[:, :, 0, :], gate_up[:, :, 1, :])  26.9 us
    all_gather x1, blocking collectives, shards(): all_picks = lax.all_gather(picks, ('exp', 'ctx'), axis=0, tiled=False)  20.4 us
    squeeze x1, local copies, waits for them, and re-layouts, shards(): gate, up = (gate_up[:, :, 0, :], gate_up[:, :, 1, :])  15.7 us
    ppermute x24, starting transfers between devices, flip(): return lax.ppermute(a, 'ctx', [(i, i ^ bit) for i in range(n_ctx)])  11.7 us
    convert_element_type x7, other arithmetic, add(): return (a.astype(jnp.float32) + b.astype(jnp.float32)).astype(jnp.bfloat16)  8.7 us
    ppermute x6, waiting for transfers between devices, shift(): return lax.ppermute(a, 'exp', [(i, (i + d) % n_exp) for i in range(n_exp)])  7.84 us
  transfers between devices with their start and end apart: 30, of which 6 were waited for; matrix products, arithmetic and copies ran while one was open for 32% of the time, Pallas kernels for 3%

profile of v1, /device:TPU:0, one launch (start us, length us, event | category | flops | bytes accessed | tf_op | source)
XLA Modules:
  0.0 181.9 jit_solution(7549560911415976098)
XLA Ops:
  0.6 4.1 %collective-permute-start.7 = (bf16[128,1024]{1,0:T(8,128)(2,1)}, bf16[128,1024]{1,0:T(8,128)(2,1)S(1)}, u32[]{:S(2)}, u32[]{:S(2)}) collective-permute-start(bf16[128,1024]{1,0:T(8,128)(2,1)} %bitcast.66), channel_id=1, source_target_pairs={{0,2},{1,3},{2,0},{3,1},{4,6},{5,7},{6,4},{7,5},{8,10},{9,11},{10,... | collective-permute-start | bytes 786440 | tf_op jit(solution)/shard_map/ppermute | solution.py:279
  4.7 1.3 collective-permute-start.11
  6.8 1.5 collective-permute-start
  9.9 26.9 %fusion.7 = (bf16[16,176,1,1024]{3,2,1,0:T(2,128)(2,1)}, bf16[16,176,1,1024]{3,2,1,0:T(2,128)(2,1)}) fusion(bf16[16,176,2,1024]{3,2,1,0:T(2,128)(2,1)} %param.14), kind=kLoop, calls=%fused_computation.49 | loop fusion | bytes 23068672 | tf_op jit(solution)/shard_map/slice | solution.py:308
  38.3 15.7 %copy_bitcast_fusion = (bf16[16,176,1024]{2,1,0:T(8,128)(2,1)}, bf16[16,176,1024]{2,1,0:T(8,128)(2,1)}) fusion(bf16[16,176,1,1024]{3,2,1,0:T(2,128)(2,1)} %get-tuple-element.39, bf16[16,176,1,1024]{3,2,1,0:T(2,128)(2,1)} %get-tuple-element.40), kind=kLoop, calls=%fused_computation.2 | loop fusion | bytes 23068672 | tf_op jit(solution)/shard_map/squeeze | solution.py:308
  54.1 20.4 %all-gather.1 = s32[16,6,128]{2,1,0:T(8,128)S(1)} all-gather(s32[1,6,128]{2,1,0:T(8,128)S(1)} %bitcast.60), channel_id=3, replica_groups=mesh['group'=2,'ctx'=4,'exp'=4] {'exp','ctx'}, dimensions={0}, use_global_device_ids=true | all-gather | bytes 52224 | tf_op jit(solution)/shard_map/all_gather | solution.py:292
  75.1 1.7 collective-permute-start.4
  78.1 16.4 %collective-permute-done.8.refs_9_ = bf16[128,1024]{1,0:T(8,128)(2,1)S(1)} collective-permute-done((bf16[128,1024]{1,0:T(8,128)(2,1)S(1)}, bf16[128,1024]{1,0:T(8,128)(2,1)S(1)}, u32[]{:S(2)}, u32[]{:S(2)}) %collective-permute-start.8) | collective-permute-done | bytes 262176 | tf_op jit(solution)/shard_map/ppermute | solution.py:276
  98.7 32.1 %experts.1 = (bf16[128,1024]{1,0:T(8,128)(2,1)}, bf16[128,1024]{1,0:T(8,128)(2,1)}, bf16[128,1024]{1,0:T(8,128)(2,1)}, bf16[128,1024]{1,0:T(8,128)(2,1)}, bf16[1...) custom-call(bf16[128,1024]{1,0:T(8,128)(2,1)} %bitcast.71, ...), custom_call_target="tpu_custom_call" | custom-call | flops 6576668672 | bytes 25690112 | tf_op jit(solution)/shard_map/experts/pallas_call | solution.py:167
  131.2 7.7 %all-gather = bf16[1,512,576]{2,1,0:T(8,128)(2,1)S(1)} all-gather(bf16[1,128,576]{2,1,0:T(8,128)(2,1)S(1)} %copy.37), channel_id=2, replica_groups=mesh['group'=2,'ctx'=4,'exp'=4] {'ctx'}, dimensions={1}, use_global_device_ids=true | all-gather | bytes 737280 | tf_op jit(solution)/shard_map/all_gather | solution.py:334
  141.7 1.0 add_convert_fusion.8
  143.5 1.0 add_convert_fusion.5
  144.5 1.4 collective-permute-start.24
  145.9 1.0 add_convert_fusion.2
  147.0 4.9 %collective-permute-done.20 = bf16[128,1024]{1,0:T(8,128)(2,1)S(1)} collective-permute-done((bf16[128,1024]{1,0:T(8,128)(2,1)S(1)}, bf16[128,1024]{1,0:T(8,128)(2,1)S(1)}, u32[]{:S(2)}, u32[]{:S(2)}) %collective-permute-start.20) | collective-permute-done | bytes 262176 | tf_op jit(solution)/shard_map/ppermute | solution.py:276
  152.6 1.1 add_convert_fusion.7
  153.7 1.4 collective-permute-start.17
  155.1 2.4 %collective-permute-done.24 = bf16[128,1024]{1,0:T(8,128)(2,1)S(1)} collective-permute-done((bf16[128,1024]{1,0:T(8,128)(2,1)S(1)}, bf16[128,1024]{1,0:T(8,128)(2,1)S(1)}, u32[]{:S(2)}, u32[]{:S(2)}) %collective-permute-start.24) | collective-permute-done | bytes 262176 | tf_op jit(solution)/shard_map/ppermute | solution.py:276
  157.5 1.8 add_convert_fusion.4
  159.5 3.6 %collective-permute-done.28 = bf16[128,1024]{1,0:T(8,128)(2,1)S(1)} collective-permute-done((bf16[128,1024]{1,0:T(8,128)(2,1)S(1)}, bf16[128,1024]{1,0:T(8,128)(2,1)S(1)}, u32[]{:S(2)}, u32[]{:S(2)}) %collective-permute-start.28) | collective-permute-done | bytes 262176 | tf_op jit(solution)/shard_map/ppermute | solution.py:276
  163.1 1.8 add_convert_fusion.1
  165.1 6.3 %attention.1 = bf16[128,4096]{1,0:T(8,128)(2,1)} custom-call(s32[128,1]{1,0:T(8,128)S(1)} %copy.38.first_ref, s32[128,1]{1,0:T(8,128)S(1)} %iota_add_fusion.last_ref, bf16[128,4608]{1,0:T(8,128)(2,1)S(1)} %bitcast.57, bf16[512,576]{1,0:T(8,128)(2,1)S(1)} %bitcast.56), custom_call_target="tpu_custom_call" | custom-call | flops 1207959552 | bytes 2228224 | tf_op jit(solution)/shard_map/attention/pallas_call | solution.py:238
  172.0 7.8 %collective-permute-done.25 = bf16[128,1024]{1,0:T(8,128)(2,1)} collective-permute-done((bf16[128,1024]{1,0:T(8,128)(2,1)}, bf16[128,1024]{1,0:T(8,128)(2,1)}, u32[]{:S(2)}, u32[]{:S(2)}) %collective-permute-start.25) | collective-permute-done | bytes 262176 | tf_op jit(solution)/shard_map/ppermute | solution.py:279
  179.9 2.0 %fusion = bf16[1,128,1024]{2,1,0:T(8,128)(2,1)} fusion(bf16[128,1024]{1,0:T(8,128)(2,1)} %collective-permute-done.29, bf16[128,1024]{1,0:T(8,128)(2,1)} %collective-permute-done.25, bf16[128,1024]{1,0:T(8,128)(2,1)S(1)} %collective-permute-done.21, bf16[128,1024]{1,0:T(8,128)(2,1)S(1)} %collective-permute-done.17, ...), kind=kLoop, calls=%fused_computation.17 | loop fusion | flops 2097152 | bytes 1835008 | tf_op jit(solution)/shard_map/broadcast_in_dim | solution.py:356
  (113 shorter events, 15.6 us)
Async XLA Ops:
  0.6 74.0 %collective-permute-start.7 = (bf16[128,1024]{1,0:T(8,128)(2,1)}, bf16[128,1024]{1,0:T(8,128)(2,1)S(1)}, u32[]{:S(2)}, u32[]{:S(2)}) collective-permute-start(bf16[128,1024]{1,0:T(8,128)(2,1)} %bitcast.66), channel_id=1, source_target_pairs={{0,2},{1,3},{2,0},{3,1},{4,6},{5,7},{6,4},{7,5},{8,10},{9,11},{10,... | collective-permute-start | bytes 786440 | tf_op jit(solution)/shard_map/ppermute | solution.py:279
  4.7 69.8 %collective-permute-start.11 = (bf16[128,1024]{1,0:T(8,128)(2,1)}, bf16[128,1024]{1,0:T(8,128)(2,1)S(1)}, u32[]{:S(2)}, u32[]{:S(2)}) collective-permute-start(bf16[128,1024]{1,0:T(8,128)(2,1)} %bitcast.67), channel_id=1, source_target_pairs={{0,3},{1,0},{2,1},{3,2},{4,7},{5,4},{6,5},{7,6},{8,11},{9,8},{10,9... | collective-permute-start | bytes 786440 | tf_op jit(solution)/shard_map/ppermute | solution.py:279
  6.1 69.0 %collective-permute-start.3 = (bf16[128,1024]{1,0:T(8,128)(2,1)}, bf16[128,1024]{1,0:T(8,128)(2,1)S(1)}, u32[]{:S(2)}, u32[]{:S(2)}) collective-permute-start(bf16[128,1024]{1,0:T(8,128)(2,1)} %bitcast.68), channel_id=1, source_target_pairs={{0,1},{1,2},{2,3},{3,0},{4,5},{5,6},{6,7},{7,4},{8,9},{9,10},{10,1... | collective-permute-start | bytes 786440 | tf_op jit(solution)/shard_map/ppermute | solution.py:279
  6.8 70.0 %collective-permute-start = (bf16[128,1024]{1,0:T(8,128)(2,1)}, bf16[128,1024]{1,0:T(8,128)(2,1)S(1)}, u32[]{:S(2)}, u32[]{:S(2)}) collective-permute-start(bf16[128,1024]{1,0:T(8,128)(2,1)} %bitcast.69), channel_id=1, source_target_pairs={{0,8},{4,12},{8,0},{12,4},{1,9},{5,13},{9,1},{13,5},{2,10},{6,14},... | collective-permute-start | bytes 786440 | tf_op jit(solution)/shard_map/ppermute | solution.py:276
  8.2 68.7 %collective-permute-start.1 = (bf16[128,1024]{1,0:T(8,128)(2,1)}, bf16[128,1024]{1,0:T(8,128)(2,1)S(1)}, u32[]{:S(2)}, u32[]{:S(2)}) collective-permute-start(bf16[128,1024]{1,0:T(8,128)(2,1)} %bitcast.70), channel_id=1, source_target_pairs={{0,4},{4,0},{8,12},{12,8},{1,5},{5,1},{9,13},{13,9},{2,6},{6,2},{1... | collective-permute-start | bytes 786440 | tf_op jit(solution)/shard_map/ppermute | solution.py:276
  74.6 19.9 %collective-permute-start.12 = (bf16[128,1024]{1,0:T(8,128)(2,1)S(1)}, bf16[128,1024]{1,0:T(8,128)(2,1)S(1)}, u32[]{:S(2)}, u32[]{:S(2)}) collective-permute-start(bf16[128,1024]{1,0:T(8,128)(2,1)S(1)} %collective-permute-done.11.refs_12_), channel_id=1, source_target_pairs={{0,8},{4,12},{8,0},{12,4},{1,9},{5,13},{9,1},{13,5},{2,10},{6,14},... | collective-permute-start | bytes 786440 | tf_op jit(solution)/shard_map/ppermute | solution.py:276
  74.7 20.4 %collective-permute-start.13 = (bf16[128,1024]{1,0:T(8,128)(2,1)S(1)}, bf16[128,1024]{1,0:T(8,128)(2,1)S(1)}, u32[]{:S(2)}, u32[]{:S(2)}) collective-permute-start(bf16[128,1024]{1,0:T(8,128)(2,1)S(1)} %collective-permute-done.11.refs_12_), channel_id=1, source_target_pairs={{0,4},{4,0},{8,12},{12,8},{1,5},{5,1},{9,13},{13,9},{2,6},{6,2},{1... | collective-permute-start | bytes 786440 | tf_op jit(solution)/shard_map/ppermute | solution.py:276
  75.1 19.9 %collective-permute-start.4 = (bf16[128,1024]{1,0:T(8,128)(2,1)S(1)}, bf16[128,1024]{1,0:T(8,128)(2,1)S(1)}, u32[]{:S(2)}, u32[]{:S(2)}) collective-permute-start(bf16[128,1024]{1,0:T(8,128)(2,1)S(1)} %collective-permute-done.3.refs_4_), channel_id=1, source_target_pairs={{0,8},{4,12},{8,0},{12,4},{1,9},{5,13},{9,1},{13,5},{2,10},{6,14},... | collective-permute-start | bytes 786440 | tf_op jit(solution)/shard_map/ppermute | solution.py:276
  76.8 18.7 %collective-permute-start.5 = (bf16[128,1024]{1,0:T(8,128)(2,1)S(1)}, bf16[128,1024]{1,0:T(8,128)(2,1)S(1)}, u32[]{:S(2)}, u32[]{:S(2)}) collective-permute-start(bf16[128,1024]{1,0:T(8,128)(2,1)S(1)} %collective-permute-done.3.refs_4_), channel_id=1, source_target_pairs={{0,4},{4,0},{8,12},{12,8},{1,5},{5,1},{9,13},{13,9},{2,6},{6,2},{1... | collective-permute-start | bytes 786440 | tf_op jit(solution)/shard_map/ppermute | solution.py:276
  76.9 17.5 %collective-permute-start.8 = (bf16[128,1024]{1,0:T(8,128)(2,1)S(1)}, bf16[128,1024]{1,0:T(8,128)(2,1)S(1)}, u32[]{:S(2)}, u32[]{:S(2)}) collective-permute-start(bf16[128,1024]{1,0:T(8,128)(2,1)S(1)} %collective-permute-done.7.refs_8_), channel_id=1, source_target_pairs={{0,8},{4,12},{8,0},{12,4},{1,9},{5,13},{9,1},{13,5},{2,10},{6,14},... | collective-permute-start | bytes 786440 | tf_op jit(solution)/shard_map/ppermute | solution.py:276
  130.8 9.3 %collective-permute-start.16 = (bf16[128,1024]{1,0:T(8,128)(2,1)}, bf16[128,1024]{1,0:T(8,128)(2,1)S(1)}, u32[]{:S(2)}, u32[]{:S(2)}) collective-permute-start(bf16[128,1024]{1,0:T(8,128)(2,1)} %get-tuple-element.23), channel_id=1, source_target_pairs={{0,4},{4,0},{8,12},{12,8},{1,5},{5,1},{9,13},{13,9},{2,6},{6,2},{1... | collective-permute-start | bytes 786440 | tf_op jit(solution)/shard_map/ppermute | solution.py:276
  139.4 7.5 %collective-permute-start.18 = (bf16[128,1024]{1,0:T(8,128)(2,1)}, bf16[128,1024]{1,0:T(8,128)(2,1)S(1)}, u32[]{:S(2)}, u32[]{:S(2)}) collective-permute-start(bf16[128,1024]{1,0:T(8,128)(2,1)} %get-tuple-element.25), channel_id=1, source_target_pairs={{0,4},{4,0},{8,12},{12,8},{1,5},{5,1},{9,13},{13,9},{2,6},{6,2},{1... | collective-permute-start | bytes 786440 | tf_op jit(solution)/shard_map/ppermute | solution.py:276
  139.6 3.1 %collective-permute-start.23 = (bf16[128,1024]{1,0:T(8,128)(2,1)}, bf16[128,1024]{1,0:T(8,128)(2,1)S(1)}, u32[]{:S(2)}, u32[]{:S(2)}) collective-permute-start(bf16[128,1024]{1,0:T(8,128)(2,1)} %get-tuple-element.31), channel_id=1, source_target_pairs={{0,4},{4,0},{8,12},{12,8},{1,5},{5,1},{9,13},{13,9},{2,6},{6,2},{1... | collective-permute-start | bytes 786440 | tf_op jit(solution)/shard_map/ppermute | solution.py:276
  139.9 13.8 %collective-permute-start.22 = (bf16[128,1024]{1,0:T(8,128)(2,1)}, bf16[128,1024]{1,0:T(8,128)(2,1)S(1)}, u32[]{:S(2)}, u32[]{:S(2)}) collective-permute-start(bf16[128,1024]{1,0:T(8,128)(2,1)} %get-tuple-element.29), channel_id=1, source_target_pairs={{0,4},{4,0},{8,12},{12,8},{1,5},{5,1},{9,13},{13,9},{2,6},{6,2},{1... | collective-permute-start | bytes 786440 | tf_op jit(solution)/shard_map/ppermute | solution.py:276
  140.1 4.4 %collective-permute-start.27 = (bf16[128,1024]{1,0:T(8,128)(2,1)}, bf16[128,1024]{1,0:T(8,128)(2,1)S(1)}, u32[]{:S(2)}, u32[]{:S(2)}) collective-permute-start(bf16[128,1024]{1,0:T(8,128)(2,1)} %get-tuple-element.35), channel_id=1, source_target_pairs={{0,4},{4,0},{8,12},{12,8},{1,5},{5,1},{9,13},{13,9},{2,6},{6,2},{1... | collective-permute-start | bytes 786440 | tf_op jit(solution)/shard_map/ppermute | solution.py:276
  141.5 17.9 %collective-permute-start.26 = (bf16[128,1024]{1,0:T(8,128)(2,1)}, bf16[128,1024]{1,0:T(8,128)(2,1)S(1)}, u32[]{:S(2)}, u32[]{:S(2)}) collective-permute-start(bf16[128,1024]{1,0:T(8,128)(2,1)} %get-tuple-element.33), channel_id=1, source_target_pairs={{0,4},{4,0},{8,12},{12,8},{1,5},{5,1},{9,13},{13,9},{2,6},{6,2},{1... | collective-permute-start | bytes 786440 | tf_op jit(solution)/shard_map/ppermute | solution.py:276
  142.7 9.2 %collective-permute-start.20 = (bf16[128,1024]{1,0:T(8,128)(2,1)S(1)}, bf16[128,1024]{1,0:T(8,128)(2,1)S(1)}, u32[]{:S(2)}, u32[]{:S(2)}) collective-permute-start(bf16[128,1024]{1,0:T(8,128)(2,1)S(1)} %add_convert_fusion.8), channel_id=1, source_target_pairs={{0,8},{4,12},{8,0},{12,4},{1,9},{5,13},{9,1},{13,5},{2,10},{6,14},... | collective-permute-start | bytes 786440 | tf_op jit(solution)/shard_map/ppermute | solution.py:276
  144.5 13.0 %collective-permute-start.24 = (bf16[128,1024]{1,0:T(8,128)(2,1)S(1)}, bf16[128,1024]{1,0:T(8,128)(2,1)S(1)}, u32[]{:S(2)}, u32[]{:S(2)}) collective-permute-start(bf16[128,1024]{1,0:T(8,128)(2,1)S(1)} %add_convert_fusion.5), channel_id=1, source_target_pairs={{0,8},{4,12},{8,0},{12,4},{1,9},{5,13},{9,1},{13,5},{2,10},{6,14},... | collective-permute-start | bytes 786440 | tf_op jit(solution)/shard_map/ppermute | solution.py:276
  146.9 25.1 %collective-permute-start.15 = (bf16[128,1024]{1,0:T(8,128)(2,1)}, bf16[128,1024]{1,0:T(8,128)(2,1)S(1)}, u32[]{:S(2)}, u32[]{:S(2)}) collective-permute-start(bf16[128,1024]{1,0:T(8,128)(2,1)} %get-tuple-element.21), channel_id=1, source_target_pairs={{0,4},{4,0},{8,12},{12,8},{1,5},{5,1},{9,13},{13,9},{2,6},{6,2},{1... | collective-permute-start | bytes 786440 | tf_op jit(solution)/shard_map/ppermute | solution.py:276
  151.9 11.2 %collective-permute-start.28 = (bf16[128,1024]{1,0:T(8,128)(2,1)S(1)}, bf16[128,1024]{1,0:T(8,128)(2,1)S(1)}, u32[]{:S(2)}, u32[]{:S(2)}) collective-permute-start(bf16[128,1024]{1,0:T(8,128)(2,1)S(1)} %add_convert_fusion.2), channel_id=1, source_target_pairs={{0,8},{4,12},{8,0},{12,4},{1,9},{5,13},{9,1},{13,5},{2,10},{6,14},... | collective-permute-start | bytes 786440 | tf_op jit(solution)/shard_map/ppermute | solution.py:276
  153.7 18.4 %collective-permute-start.17 = (bf16[128,1024]{1,0:T(8,128)(2,1)S(1)}, bf16[128,1024]{1,0:T(8,128)(2,1)S(1)}, u32[]{:S(2)}, u32[]{:S(2)}) collective-permute-start(bf16[128,1024]{1,0:T(8,128)(2,1)S(1)} %add_convert_fusion.11), channel_id=1, source_target_pairs={{0,8},{4,12},{8,0},{12,4},{1,9},{5,13},{9,1},{13,5},{2,10},{6,14},... | collective-permute-start | bytes 786440 | tf_op jit(solution)/shard_map/ppermute | solution.py:276
  157.5 14.5 %collective-permute-start.21 = (bf16[128,1024]{1,0:T(8,128)(2,1)S(1)}, bf16[128,1024]{1,0:T(8,128)(2,1)S(1)}, u32[]{:S(2)}, u32[]{:S(2)}) collective-permute-start(bf16[128,1024]{1,0:T(8,128)(2,1)S(1)} %add_convert_fusion.7), channel_id=1, source_target_pairs={{0,3},{1,0},{2,1},{3,2},{4,7},{5,4},{6,5},{7,6},{8,11},{9,8},{10,9... | collective-permute-start | bytes 786440 | tf_op jit(solution)/shard_map/ppermute | solution.py:279
  159.3 20.6 %collective-permute-start.25 = (bf16[128,1024]{1,0:T(8,128)(2,1)}, bf16[128,1024]{1,0:T(8,128)(2,1)}, u32[]{:S(2)}, u32[]{:S(2)}) collective-permute-start(bf16[128,1024]{1,0:T(8,128)(2,1)} %add_convert_fusion.4), channel_id=1, source_target_pairs={{0,2},{1,3},{2,0},{3,1},{4,6},{5,7},{6,4},{7,5},{8,10},{9,11},{10,... | collective-permute-start | bytes 786440 | tf_op jit(solution)/shard_map/ppermute | solution.py:279
  164.9 15.0 %collective-permute-start.29 = (bf16[128,1024]{1,0:T(8,128)(2,1)}, bf16[128,1024]{1,0:T(8,128)(2,1)}, u32[]{:S(2)}, u32[]{:S(2)}) collective-permute-start(bf16[128,1024]{1,0:T(8,128)(2,1)} %add_convert_fusion.1), channel_id=1, source_target_pairs={{0,1},{1,2},{2,3},{3,0},{4,5},{5,6},{6,7},{7,4},{8,9},{9,10},{10,1... | collective-permute-start | bytes 786440 | tf_op jit(solution)/shard_map/ppermute | solution.py:279
  (23 other events, 401.2 us)

commit v2 on v0

v2 whole, which is shorter than its diff:
```python
import functools

import jax
import jax.numpy as jnp
from jax import lax
from jax.experimental import pallas as pl
from jax.experimental.pallas import tpu as pltpu
from jax.sharding import PartitionSpec as P

EXPERTS = 64
HEADS = 8
LATENT = 512
CAP = 16
NDOC = 8
BLOCK = 128
LANES = 128
EXPERT_ROWS = 256
VMEM = 48 * 2**20
PEAK = 1.1e9

qk_scale = 192.0 ** (-0.5)
NT = (((1,), (1,)), ((), ()))
TN = (((0,), (0,)), ((), ()))


def call(kernel, micros, grid, in_specs, out_specs, out_shape, scratch, name):
    return pl.pallas_call(
        kernel,
        grid=grid,
        in_specs=in_specs,
        out_specs=out_specs,
        out_shape=out_shape,
        scratch_shapes=scratch,
        compiler_params=pltpu.CompilerParams(
            dimension_semantics=("arbitrary",) * len(grid), vmem_limit_bytes=VMEM
        ),
        cost_estimate=pl.CostEstimate(
            flops=int(micros * PEAK), bytes_accessed=0, transcendentals=0
        ),
        name=name,
    )


def dispatch_kernel(n_parts, n_row, base_ref, ids_ref, rw_ref, *refs):
    parts, refs = refs[:n_parts], refs[n_parts:]
    if n_row:
        seg_ref, scale_ref = refs[:2]
        refs = refs[2:]
    rows_ref, weight_ref, picks_ref = refs[:3]
    local = rows_ref.shape[0]
    width = rows_ref.shape[2]
    names = lax.broadcasted_iota(jnp.int32, (EXPERTS, BLOCK), 0)
    before = (
        lax.broadcasted_iota(jnp.int32, (BLOCK, BLOCK), 0)
        < lax.broadcasted_iota(jnp.int32, (BLOCK, BLOCK), 1)
    ).astype(jnp.bfloat16)
    slot = lax.broadcasted_iota(jnp.int32, (local, CAP, BLOCK), 1).astype(jnp.float32)
    hots, probs = [], []
    for p in range(n_parts):
        x = parts[p][...]
        logits = lax.dot_general(rw_ref[...], x, NT, preferred_element_type=jnp.float32)
        expo = jnp.exp(logits - jnp.max(logits, axis=0, keepdims=True))
        prob = expo / jnp.sum(expo, axis=0, keepdims=True)
        ids = ids_ref[p] - base_ref[0]
        ids = jnp.where(ids < 0, ids + EXPERTS, ids)
        hot = names == ids[0:1]
        for k in range(1, ids.shape[0]):
            hot = hot | (names == ids[k : k + 1])
        hot = hot.astype(jnp.float32)
        chosen = prob * hot
        gate = chosen[:local] / jnp.sum(chosen, axis=0, keepdims=True)
        own = hot[:local]
        rank = jnp.dot(own.astype(jnp.bfloat16), before, preferred_element_type=jnp.float32)
        key = jnp.where(own > 0.0, rank, -1.0)
        pick = (key[:, None, :] == slot).astype(jnp.float32)
        at = slice(p * CAP, (p + 1) * CAP)
        weight_ref[:, at, :] = jnp.broadcast_to(
            jnp.sum(pick * gate[:, None, :], axis=-1, keepdims=True), (local, CAP, LANES)
        )
        pick = pick.reshape(local * CAP, BLOCK).astype(jnp.bfloat16)
        picks_ref[p] = pick
        taken = jnp.dot(pick, x, preferred_element_type=jnp.float32)
        rows_ref[:, at, :] = taken.astype(jnp.bfloat16).reshape(local, CAP, width)
        hots.append(hot)
        probs.append(prob)
    if n_row:
        bal_ref = refs[3]
        for d in range(NDOC):
            counts = jnp.zeros((EXPERTS, BLOCK), jnp.float32)
            mass = jnp.zeros((EXPERTS, BLOCK), jnp.float32)
            for p in range(n_row):
                inside = seg_ref[p] == d
                counts = counts + jnp.where(inside, hots[p], 0.0)
                mass = mass + jnp.where(inside, probs[p], 0.0)
            both = jnp.sum(counts, axis=1, keepdims=True) * jnp.sum(mass, axis=1, keepdims=True)
            bal_ref[d : d + 1, :] = (
                jnp.broadcast_to(jnp.sum(both, axis=0, keepdims=True), (1, LANES))
                * scale_ref[d : d + 1, :]
            )


def whole(a):
    return pl.BlockSpec(a.shape, lambda *i: (0,) * a.ndim)


def dispatch(parts, ids, base, rw, local, row=None):
    n_parts = len(parts)
    n, width = parts[0].shape[0] // BLOCK, parts[0].shape[1]
    slots = n_parts * CAP
    in_specs = [
        pl.BlockSpec(memory_space=pltpu.SMEM),
        pl.BlockSpec((n_parts,) + ids.shape[1:], lambda i: (i, 0, 0)),
        whole(rw),
    ] + [pl.BlockSpec((BLOCK, width), lambda i: (i, 0))] * n_parts
    out_specs = [
        pl.BlockSpec((local, slots, width), lambda i: (0, i, 0)),
        pl.BlockSpec((local, slots, LANES), lambda i: (0, i, 0)),
        pl.BlockSpec((n_parts, local * CAP, BLOCK), lambda i: (i, 0, 0)),
    ]
    out_shape = [
        jax.ShapeDtypeStruct((local, n * slots, width), jnp.bfloat16),
        jax.ShapeDtypeStruct((local, n * slots, LANES), jnp.float32),
        jax.ShapeDtypeStruct((n * n_parts, local * CAP, BLOCK), jnp.bfloat16),
    ]
    extra = ()
    if row is not None:
        extra = row
        in_specs += [whole(a) for a in row]
        out_specs.append(pl.BlockSpec((NDOC, LANES), lambda i: (0, 0)))
        out_shape.append(jax.ShapeDtypeStruct((NDOC, LANES), jnp.float32))
    return call(
        functools.partial(dispatch_kernel, n_parts, n_parts if row is not None else 0),
        3 * n,
        (n,),
        in_specs,
        out_specs,
        out_shape,
        [],
        "dispatch",
    )(base, ids, rw, *parts, *extra)


def expert_kernel(n, *refs):
    rows, weights = refs[:n], refs[n : 2 * n]
    gu_ref, down_ref = refs[2 * n : 2 * n + 2]
    outs = refs[2 * n + 2 : 3 * n + 2]
    both = refs[3 * n + 2]
    held = jnp.concatenate([r[0] for r in rows], axis=0)
    hidden = lax.dot_general(gu_ref[0], held, NT, preferred_element_type=jnp.float32)
    half = both.shape[1] // 2
    inner = []
    for c in range(both.shape[0]):
        both[c] = hidden[:, c * LANES : (c + 1) * LANES]
        g = both[c, pl.ds(0, half, stride=2), :]
        u = both[c, pl.ds(1, half, stride=2), :]
        inner.append((g * lax.logistic(g) * u).astype(jnp.bfloat16))
    inner = jnp.concatenate(inner, axis=1)
    made = lax.dot_general(inner, down_ref[0], TN, preferred_element_type=jnp.float32)
    size = rows[0].shape[1]
    for i in range(n):
        w = weights[i][0]
        part = made[i * size : (i + 1) * size]
        for c in range(part.shape[1] // LANES):
            at = slice(c * LANES, (c + 1) * LANES)
            outs[i][0, :, at] = (part[:, at] * w).astype(jnp.bfloat16)


def experts(rows, weights, gate_up, down):
    n = len(rows)
    local, slots, width = rows[0].shape
    size = min(slots, EXPERT_ROWS)
    hidden = down.shape[1]
    rows_spec = pl.BlockSpec((1, size, width), lambda e, i: (e, i, 0))
    weight_spec = pl.BlockSpec((1, size, LANES), lambda e, i: (e, i, 0))
    return call(
        functools.partial(expert_kernel, n),
        10,
        (local, slots // size),
        [rows_spec] * n
        + [weight_spec] * n
        + [
            pl.BlockSpec((1, 2 * hidden, width), lambda e, i: (e, 0, 0)),
            pl.BlockSpec((1, hidden, width), lambda e, i: (e, 0, 0)),
        ],
        [rows_spec] * n,
        [jax.ShapeDtypeStruct(r.shape, jnp.bfloat16) for r in rows],
        [pltpu.VMEM((n * size // LANES, 2 * hidden, LANES), jnp.float32)],
        "experts",
    )(*rows, *weights, gate_up, down)


def combine_kernel(groups, picks_ref, made_ref, *outs):
    local, _, width = made_ref.shape
    per = outs[0].shape[1] // BLOCK
    for p in range(picks_ref.shape[0]):
        held = made_ref[:, p * CAP : (p + 1) * CAP, :].reshape(local * CAP, width)
        mix = lax.dot_general(picks_ref[p], held, TN, preferred_element_type=jnp.float32)
        out, at = outs[p // per], p % per
        out[0, at * BLOCK : (at + 1) * BLOCK, :] = mix.astype(jnp.bfloat16)


def combine(picks, made, n_parts):
    n = picks.shape[0] // n_parts
    local, _, width = made.shape
    slots = n_parts * CAP
    half = n_parts // 2 * BLOCK
    out = pl.BlockSpec((1, half, width), lambda i: (i, 0, 0))
    return call(
        functools.partial(combine_kernel, 2),
        2 * n,
        (n,),
        [
            pl.BlockSpec((n_parts,) + picks.shape[1:], lambda i: (i, 0, 0)),
            pl.BlockSpec((local, slots, width), lambda i: (0, i, 0)),
        ],
        [out, out],
        [jax.ShapeDtypeStruct((n, half, width), jnp.bfloat16)] * 2,
        [],
        "combine",
    )(picks, made)


def attend_kernel(n, first_ref, last_ref, kpos_ref, q_ref, *refs):
    parts, (out_ref, even, odd) = refs[:n], refs[n:]
    rows, kdim = parts[0].shape
    wide = even.shape[1]
    half = wide - kdim

    @pl.when(pl.program_id(0) == 0)
    def _():
        pad = jnp.zeros((rows, half), jnp.bfloat16)
        for i in range(n):
            at = slice(i * rows, (i + 1) * rows)
            even[at, :] = jnp.concatenate([parts[i][...], pad], axis=1)
            odd[at, :] = jnp.concatenate([pad, parts[i][...]], axis=1)

    allowed = (kpos_ref[...] >= first_ref[...]) & (kpos_ref[...] <= last_ref[...])
    for i, keys in enumerate((even, odd)):
        at = i * (kdim - half)
        scores = lax.dot_general(
            q_ref[:, at : at + wide], keys[...], NT, preferred_element_type=jnp.float32
        )
        scores = jnp.where(allowed, scores * qk_scale, -1e30)
        expo = jnp.exp(scores - jnp.max(scores, axis=-1, keepdims=True))
        probs = (expo / jnp.sum(expo, axis=-1, keepdims=True)).astype(jnp.bfloat16)
        out_ref[:, i * LATENT : (i + 1) * LATENT] = jnp.dot(
            probs, even[:, :LATENT], preferred_element_type=jnp.float32
        ).astype(jnp.bfloat16)


def attend(queries, parts, first, last, kpos):
    n = len(parts)
    rows, kdim = parts[0].shape
    wide = -(-kdim // LANES) * LANES
    return call(
        functools.partial(attend_kernel, n),
        6,
        (HEADS // 2,),
        [whole(first), whole(last), whole(kpos)]
        + [pl.BlockSpec((rows, 2 * kdim), lambda h: (0, h))]
        + [whole(p) for p in parts],
        pl.BlockSpec((rows, 2 * LATENT), lambda h: (0, h)),
        jax.ShapeDtypeStruct((rows, HEADS * LATENT), jnp.bfloat16),
        [pltpu.VMEM((n * rows, wide), jnp.bfloat16)] * 2,
        "attention",
    )(first, last, kpos, queries, *parts)


def added(*terms):
    total = terms[0].astype(jnp.float32)
    for term in terms[1:]:
        total = total + term.astype(jnp.float32)
    return total.astype(jnp.bfloat16)


def shards(queries, latent_kv, doc_lengths, hidden_in, router_weight, expert_ids, gate_up, w_down):
    tok_rows, width = hidden_in.shape[1:]
    n_ctx, n_exp = lax.axis_size("ctx"), lax.axis_size("exp")
    ctx, exp = lax.axis_index("ctx"), lax.axis_index("exp")
    local = gate_up.shape[0]
    near = n_exp <= 4
    shifts = [0, 1, 3, 2][:n_exp] if near else [0]
    flips = (2, 1)
    tokens = hidden_in[0]

    def flip(a, bit):
        return lax.ppermute(a, "ctx", [(i, i ^ bit) for i in range(n_ctx)])

    def shift(a, d):
        return lax.ppermute(a, "exp", [(i, (i + d) % n_exp) for i in range(n_exp)])

    def along_exp(a):
        if near:
            return [a if d == 0 else shift(a, d) for d in shifts]
        return [lax.all_gather(a, "exp", axis=0, tiled=True)]

    masks = [0, 2, 1, 3]
    order = jnp.stack([ctx ^ m for m in masks])

    picks = jnp.swapaxes(expert_ids[0].reshape(tok_rows // BLOCK, BLOCK, -1), 1, 2)
    ids = jnp.stack(along_exp(picks))
    ids = jnp.stack([ids, flip(ids, 2)], axis=2)
    ids = jnp.concatenate([ids, flip(ids, 1)], axis=2)
    ids = ids.reshape((len(shifts), -1) + picks.shape[1:])

    spread = [[a] for a in along_exp(tokens)]
    spread = [held + [flip(a, 2) for a in held] for held in spread]
    spread = [held + [flip(a, 1) for a in held] for held in spread]
    kv = [latent_kv[0]]
    for bit in flips:
        kv = kv + [flip(a, bit) for a in kv]

    lengths = doc_lengths[0]
    ends = jnp.cumsum(lengths)
    row_pos = order[:, None] * tok_rows + jnp.arange(tok_rows, dtype=jnp.int32)[None, :]
    pos = row_pos[0]
    passed = pos[:, None] >= ends[None, :]
    first = jnp.max(jnp.where(passed, ends[None, :], 0), axis=1)
    context = attend(queries[0], kv, first[:, None], pos[:, None], row_pos.reshape(1, -1))

    seg = jnp.sum((row_pos[..., None] >= ends).astype(jnp.int32), axis=-1)
    sizes = lengths.astype(jnp.float32)
    scale = jnp.broadcast_to((EXPERTS / (expert_ids.shape[2] * sizes * sizes))[:, None], (NDOC, LANES))

    base = (exp * local).reshape(1).astype(jnp.int32)
    rw = jnp.roll(router_weight.T, -exp * local, axis=0)
    gu = gate_up.reshape(local, -1, width)
    balance = None
    sent = []
    for i, held in enumerate(spread):
        row = (seg.reshape(-1, 1, BLOCK), scale) if near and i == 0 else None
        out = dispatch(held, ids[i], base, rw, local, row)
        sent.append(out[:3])
        if row is not None:
            balance = out[3]
    made = experts([s[0] for s in sent], [s[1] for s in sent], gu, w_down)

    back = []
    for i in reversed(range(len(shifts))):
        keep, give = combine(sent[i][2], made[i], n_ctx)
        got = flip(give, 1)
        far = added(keep[:, tok_rows:], got[:, tok_rows:])
        terms = [keep[:, :tok_rows], got[:, :tok_rows], flip(far, 2)]
        if i:
            back.append(shift(added(*terms), -shifts[i]))
        else:
            back = back + terms
    if near:
        expert_mix = added(*back)
    else:
        expert_mix = lax.psum_scatter(
            added(*back).reshape(-1, width), "exp", scatter_dimension=0, tiled=True
        ).reshape(1, tok_rows, width)

    if balance is None:
        row = lax.all_gather(tokens, "ctx", axis=0, tiled=True)
        router = jax.nn.softmax(
            jnp.dot(row, router_weight, preferred_element_type=jnp.float32), axis=-1
        )
        row_ids = lax.all_gather(expert_ids[0], "ctx", axis=0, tiled=True)
        hot = (row_ids[:, :, None] == jnp.arange(EXPERTS, dtype=jnp.int32)).astype(jnp.float32)
        at = jnp.arange(row.shape[0], dtype=jnp.int32)
        seg_at = jnp.sum((at[:, None] >= ends[None, :]).astype(jnp.int32), axis=1)
        seg_hot = (seg_at[:, None] == jnp.arange(NDOC, dtype=jnp.int32)).astype(jnp.float32)
        exact = lax.Precision.HIGHEST
        counts = jnp.dot(seg_hot.T, hot.sum(axis=1), precision=exact)
        mass = jnp.dot(seg_hot.T, router, precision=exact)
        per_doc = jnp.sum(counts * mass, axis=1) * scale[:, 0]
    else:
        per_doc = balance[:, 0]
    return context[None], expert_mix, per_doc.reshape(1, NDOC)


def solution(mesh):
    rows = P(("group", "exp"), "ctx", None)
    docs = P(("group", "exp"), None)
    return jax.shard_map(
        shards,
        mesh=mesh,
        in_specs=(rows, rows, docs, rows, P(), rows, P("exp", "ctx", None, None), P("exp", "ctx", None)),
        out_specs=(rows, rows, docs),
        check_vma=False,
    )
```

time: 526 us -> 141 us (0.27)
  waiting for transfers between devices: 387 us -> 38 us
  matrix products: 51.4 us -> 0 us
  Pallas kernels: 0 us -> 36.2 us
  starting transfers between devices: 11.3 us -> 32.9 us
  blocking collectives: 18.5 us -> 0 us
  between operations: 14.2 us -> 0.89 us
  local copies, waits for them, and re-layouts: 36.3 us -> 27.4 us
    all_gather x2 -> x0, waiting for transfers between devices: 325 us -> none  [the longest x1 208 us: shards(): lax.all_gather(gate_up, 'ctx', axis=1, tiled=True)]
    all_to_all x2 -> x0, waiting for transfers between devices: 60.5 us -> none  [the longest x1 44.6 us: shards(): lax.all_to_all(outgoing, 'exp', split_axis=0, concat_axis=0, tiled=True)]
    dot_general x7 -> x0, matrix products: 49 us -> none  [the longest x1 26.7 us: shards(): jnp.einsum('secd,efzd->zsecf', arrived, lax.all_gather(gate_up, 'ctx', ax...]
    ppermute x0 -> x34, waiting for transfers between devices: none -> 38 us  [the longest x25 29.2 us: flip(): return lax.ppermute(a, 'ctx', [(i, i ^ bit) for i in range(n_ctx)])]
    pallas_call x0 -> x10, Pallas kernels: none -> 36.2 us  [the longest x1 22 us: experts(): call(functools.partial(expert_kernel, n), 10, (local, slots // size), [ro...]
    ppermute x0 -> x34, starting transfers between devices: none -> 32.9 us  [the longest x25 16.5 us: flip(): return lax.ppermute(a, 'ctx', [(i, i ^ bit) for i in range(n_ctx)])]
    all_gather x3 -> x0, blocking collectives: 18.5 us -> none  [the longest x1 7.73 us: shards(): keys = lax.all_gather(own_keys, 'ctx', axis=0, tiled=True)]
    reshape x2 -> x1, local copies, waits for them, and re-layouts: 3.95 us -> 17.6 us  [shards(): gu = gate_up.reshape(local, -1, width)]
  transfers between devices with their start and end apart: 4 -> 34, of which waited for: 4 -> 9; matrix products, arithmetic and copies ran while one was open for 11% -> 16% of each run, Pallas kernels for 0% -> 26%
where the time goes in v2:
time: 141 us; the launch traced here: 140 us
  waiting for transfers between devices  38 us (27%)
  Pallas kernels  36.2 us (26%)
  starting transfers between devices  32.9 us (23%)
  local copies, waits for them, and re-layouts  27.4 us (19%)
  other arithmetic  4.38 us (3%)
    ppermute x25, waiting for transfers between devices, flip(): return lax.ppermute(a, 'ctx', [(i, i ^ bit) for i in range(n_ctx)])  29.2 us
    pallas_call x1, Pallas kernels, experts(): call(functools.partial(expert_kernel, n), 10, (local, slots // size), [ro...  22 us
    reshape x1, local copies, waits for them, and re-layouts, shards(): gu = gate_up.reshape(local, -1, width)  17.6 us
    ppermute x25, starting transfers between devices, flip(): return lax.ppermute(a, 'ctx', [(i, i ^ bit) for i in range(n_ctx)])  16.5 us
    ppermute x9, starting transfers between devices, shift(): return lax.ppermute(a, 'exp', [(i, (i + d) % n_exp) for i in range(n_exp)])  16.4 us
    unnamed x22, local copies, waits for them, and re-layouts  8.86 us
    ppermute x9, waiting for transfers between devices, shift(): return lax.ppermute(a, 'exp', [(i, (i + d) % n_exp) for i in range(n_exp)])  8.77 us
    pallas_call x1, Pallas kernels, attend(): call(functools.partial(attend_kernel, n), 6, (HEADS // 2,), [whole(first)...  6.17 us
  transfers between devices with their start and end apart: 34, of which 9 were waited for; matrix products, arithmetic and copies ran while one was open for 16% of the time, Pallas kernels for 26%

profile of v2, /device:TPU:0, one launch (start us, length us, event | category | flops | bytes accessed | tf_op | source)
XLA Modules:
  0.0 139.7 jit_solution(6628844028658447024)
XLA Ops:
  1.3 3.0 %collective-permute-start.3 = (s32[1,6,128]{2,1,0:T(8,128)S(1)}, s32[1,6,128]{2,1,0:T(8,128)S(1)}, u32[]{:S(2)}, u32[]{:S(2)}) collective-permute-start(s32[1,6,128]{2,1,0:T(8,128)S(1)} %bitcast.65), channel_id=1, source_target_pairs={{0,1},{1,2},{2,3},{3,0},{4,5},{5,6},{6,7},{7,4},{8,9},{9,10},{10,1... | collective-permute-start | bytes 9224 | tf_op jit(solution)/shard_map/ppermute | solution.py:290
  4.3 2.0 %collective-permute-start.4 = (s32[1,6,128]{2,1,0:T(8,128)S(1)}, s32[1,6,128]{2,1,0:T(8,128)S(1)}, u32[]{:S(2)}, u32[]{:S(2)}) collective-permute-start(s32[1,6,128]{2,1,0:T(8,128)S(1)} %bitcast.66), channel_id=1, source_target_pairs={{0,3},{1,0},{2,1},{3,2},{4,7},{5,4},{6,5},{7,6},{8,11},{9,8},{10,9... | collective-permute-start | bytes 9224 | tf_op jit(solution)/shard_map/ppermute | solution.py:290
  7.4 1.6 %collective-permute-start.15 = (bf16[128,1024]{1,0:T(8,128)(2,1)}, bf16[128,1024]{1,0:T(8,128)(2,1)S(1)}, u32[]{:S(2)}, u32[]{:S(2)}) collective-permute-start(bf16[128,1024]{1,0:T(8,128)(2,1)} %bitcast.56), channel_id=1, source_target_pairs={{0,1},{1,2},{2,3},{3,0},{4,5},{5,6},{6,7},{7,4},{8,9},{9,10},{10,1... | collective-permute-start | bytes 786440 | tf_op jit(solution)/shard_map/ppermute | solution.py:290
  9.0 2.2 %collective-permute-start.19 = (bf16[128,1024]{1,0:T(8,128)(2,1)}, bf16[128,1024]{1,0:T(8,128)(2,1)S(1)}, u32[]{:S(2)}, u32[]{:S(2)}) collective-permute-start(bf16[128,1024]{1,0:T(8,128)(2,1)} %bitcast.57), channel_id=1, source_target_pairs={{0,3},{1,0},{2,1},{3,2},{4,7},{5,4},{6,5},{7,6},{8,11},{9,8},{10,9... | collective-permute-start | bytes 786440 | tf_op jit(solution)/shard_map/ppermute | solution.py:290
  13.9 1.7 %collective-permute-start.12 = (bf16[128,1024]{1,0:T(8,128)(2,1)}, bf16[128,1024]{1,0:T(8,128)(2,1)S(1)}, u32[]{:S(2)}, u32[]{:S(2)}) collective-permute-start(bf16[128,1024]{1,0:T(8,128)(2,1)} %bitcast.59), channel_id=1, source_target_pairs={{0,8},{4,12},{8,0},{12,4},{1,9},{5,13},{9,1},{13,5},{2,10},{6,14},... | collective-permute-start | bytes 786440 | tf_op jit(solution)/shard_map/ppermute | solution.py:287
  16.0 5.1 %collective-permute-done.6 = s32[4,1,6,128]{3,2,0,1:T(8,128)S(1)} collective-permute-done((s32[4,1,6,128]{3,2,0,1:T(8,128)S(1)}, s32[4,1,6,128]{3,2,0,1:T(8,128)S(1)}, u32[]{:S(2)}, u32[]{:S(2)}) %collective-permute-start.6) | collective-permute-done | bytes 12320 | tf_op jit(solution)/shard_map/ppermute | solution.py:287
  21.2 17.6 %reshape.141.refs_8_ = bf16[16,352,1024]{2,1,0:T(8,128)(2,1)} reshape(bf16[16,176,2,1024]{3,2,1,0:T(2,128)(2,1)} %param.14) | data formatting | bytes 23068672 | tf_op jit(solution)/shard_map/reshape | solution.py:327
  39.8 1.5 %collective-permute-start.16 = (bf16[128,1024]{1,0:T(8,128)(2,1)S(1)}, bf16[128,1024]{1,0:T(8,128)(2,1)S(1)}, u32[]{:S(2)}, u32[]{:S(2)}) collective-permute-start(bf16[128,1024]{1,0:T(8,128)(2,1)S(1)} %collective-permute-done.15.refs_0_), channel_id=1, source_target_pairs={{0,8},{4,12},{8,0},{12,4},{1,9},{5,13},{9,1},{13,5},{2,10},{6,14},... | collective-permute-start | bytes 786440 | tf_op jit(solution)/shard_map/ppermute | solution.py:287
  42.2 6.8 %collective-permute-done.16.refs_1_ = bf16[128,1024]{1,0:T(8,128)(2,1)S(1)} collective-permute-done((bf16[128,1024]{1,0:T(8,128)(2,1)S(1)}, bf16[128,1024]{1,0:T(8,128)(2,1)S(1)}, u32[]{:S(2)}, u32[]{:S(2)}) %collective-permute-start.16) | collective-permute-done | bytes 262176 | tf_op jit(solution)/shard_map/ppermute | solution.py:287
  50.6 1.6 %dispatch.5 = (bf16[16,64,1024]{2,1,0:T(8,128)(2,1)S(1)}, f32[16,64,128]{2,1,0:T(8,128)S(1)}, bf16[4,256,128]{2,1,0:T(8,128)(2,1)S(1)}, f32[8,128]{1,0:T(8,128)S(1)}) custom-call(s32[1]{0:T(128)} %bitcast.13.base_ref, s32[4,6,128]{2,1,0:T(8,128)S(1)} %get-tuple-element.56.ids_ref, bf16[64,1024]{1,0:T(8,128)(2,1)S(1)} %fusion.rw_ref, ...), custom_call_target="tpu_custom_call" | custom-call | flops 3300000000 | tf_op jit(solution)/shard_map/dispatch/pallas_call | solution.py:131
  54.6 2.7 %collective-permute-done.20.refs_1_ = bf16[128,1024]{1,0:T(8,128)(2,1)S(1)} collective-permute-done((bf16[128,1024]{1,0:T(8,128)(2,1)S(1)}, bf16[128,1024]{1,0:T(8,128)(2,1)S(1)}, u32[]{:S(2)}, u32[]{:S(2)}) %collective-permute-start.20) | collective-permute-done | bytes 262176 | tf_op jit(solution)/shard_map/ppermute | solution.py:287
  62.1 2.5 %collective-permute-done.9.refs_1_ = bf16[128,1024]{1,0:T(8,128)(2,1)S(1)} collective-permute-done((bf16[128,1024]{1,0:T(8,128)(2,1)S(1)}, bf16[128,1024]{1,0:T(8,128)(2,1)S(1)}, u32[]{:S(2)}, u32[]{:S(2)}) %collective-permute-start.9) | collective-permute-done | bytes 262176 | tf_op jit(solution)/shard_map/ppermute | solution.py:287
  70.3 22.0 %experts.1 = (bf16[16,64,1024]{2,1,0:T(8,128)(2,1)S(1)}, bf16[16,64,1024]{2,1,0:T(8,128)(2,1)}, bf16[16,64,1024]{2,1,0:T(8,128)(2,1)}, bf16[16,64,1024]{2,1,0:T(8,128)(2,1)}) custom-call(bf16[16,64,1024]{2,1,0:T(8,128)(2,1)} %copy-done.5, bf16[16,64,1024]{2,1,0:T(8,128)(2,1)} %copy-done.6, bf16[16,64,1024]{2,1,0:T(8,128)(2,1)} %copy-done.7, ...), custom_call_target="tpu_custom_call" | custom-call | flops 11000000512 | tf_op jit(solution)/shard_map/experts/pallas_call | solution.py:175
  92.3 1.6 %copy-done.4 = bf16[16,64,1024]{2,1,0:T(8,128)(2,1)S(1)} copy-done((bf16[16,64,1024]{2,1,0:T(8,128)(2,1)S(1)}, bf16[16,64,1024]{2,1,0:T(8,128)(2,1)}, u32[]{:S(2)}) %copy-start.4) | copy-done | bytes 2097176
  98.8 1.6 %collective-permute-start.24 = (bf16[1,128,1024]{2,1,0:T(8,128)(2,1)S(1)}, bf16[1,128,1024]{2,1,0:T(8,128)(2,1)S(1)}, u32[]{:S(2)}, u32[]{:S(2)}) collective-permute-start(bf16[1,128,1024]{2,1,0:T(8,128)(2,1)S(1)} %add_convert_fusion.7), channel_id=1, source_target_pairs={{0,8},{4,12},{8,0},{12,4},{1,9},{5,13},{9,1},{13,5},{2,10},{6,14},... | collective-permute-start | bytes 786440 | tf_op jit(solution)/shard_map/ppermute | solution.py:287
  102.7 5.2 %collective-permute-done.24 = bf16[1,128,1024]{2,1,0:T(8,128)(2,1)S(1)} collective-permute-done((bf16[1,128,1024]{2,1,0:T(8,128)(2,1)S(1)}, bf16[1,128,1024]{2,1,0:T(8,128)(2,1)S(1)}, u32[]{:S(2)}, u32[]{:S(2)}) %collective-permute-start.24) | collective-permute-done | bytes 262176 | tf_op jit(solution)/shard_map/ppermute | solution.py:287
  107.9 1.5 %collective-permute-start.33 = (bf16[1,128,1024]{2,1,0:T(8,128)(2,1)S(1)}, bf16[1,128,1024]{2,1,0:T(8,128)(2,1)S(1)}, u32[]{:S(2)}, u32[]{:S(2)}) collective-permute-start(bf16[1,128,1024]{2,1,0:T(8,128)(2,1)S(1)} %add_convert_fusion.1), channel_id=1, source_target_pairs={{0,8},{4,12},{8,0},{12,4},{1,9},{5,13},{9,1},{13,5},{2,10},{6,14},... | collective-permute-start | bytes 786440 | tf_op jit(solution)/shard_map/ppermute | solution.py:287
  109.6 4.0 %collective-permute-done.27 = bf16[1,128,1024]{2,1,0:T(8,128)(2,1)S(1)} collective-permute-done((bf16[1,128,1024]{2,1,0:T(8,128)(2,1)S(1)}, bf16[1,128,1024]{2,1,0:T(8,128)(2,1)S(1)}, u32[]{:S(2)}, u32[]{:S(2)}) %collective-permute-start.27) | collective-permute-done | bytes 262176 | tf_op jit(solution)/shard_map/ppermute | solution.py:287
  113.5 2.6 %collective-permute-start.25 = (bf16[1,128,1024]{2,1,0:T(8,128)(2,1)S(1)}, bf16[1,128,1024]{2,1,0:T(8,128)(2,1)S(1)}, u32[]{:S(2)}, u32[]{:S(2)}) collective-permute-start(bf16[1,128,1024]{2,1,0:T(8,128)(2,1)S(1)} %add_convert_fusion.6), channel_id=1, source_target_pairs={{0,2},{1,3},{2,0},{3,1},{4,6},{5,7},{6,4},{7,5},{8,10},{9,11},{10,... | collective-permute-start | bytes 786440 | tf_op jit(solution)/shard_map/ppermute | solution.py:290
  116.2 2.9 %collective-permute-done.30 = bf16[1,128,1024]{2,1,0:T(8,128)(2,1)S(1)} collective-permute-done((bf16[1,128,1024]{2,1,0:T(8,128)(2,1)S(1)}, bf16[1,128,1024]{2,1,0:T(8,128)(2,1)S(1)}, u32[]{:S(2)}, u32[]{:S(2)}) %collective-permute-start.30) | collective-permute-done | bytes 262176 | tf_op jit(solution)/shard_map/ppermute | solution.py:287
  119.8 3.4 %collective-permute-start.31 = (bf16[1,128,1024]{2,1,0:T(8,128)(2,1)S(1)}, bf16[1,128,1024]{2,1,0:T(8,128)(2,1)S(1)}, u32[]{:S(2)}, u32[]{:S(2)}) collective-permute-start(bf16[1,128,1024]{2,1,0:T(8,128)(2,1)S(1)} %add_convert_fusion.2), channel_id=1, source_target_pairs={{0,3},{1,0},{2,1},{3,2},{4,7},{5,4},{6,5},{7,6},{8,11},{9,8},{10,9... | collective-permute-start | bytes 786440 | tf_op jit(solution)/shard_map/ppermute | solution.py:290
  123.2 6.2 %attention.1 = bf16[128,4096]{1,0:T(8,128)(2,1)} custom-call(s32[128,1]{1,0:T(8,128)S(1)} %copy.30.first_ref, s32[128,1]{1,0:T(8,128)S(1)} %copy.31.last_ref, s32[1,512]{1,0:T(1,128)S(1)} %bitcast.53, bf16[128,4608]{1,0:T(8,128)(2,1)S(1)} %bitcast.55, bf16[128,576]{1,0:T(8,128)(2,1)S(1)} %bitcast.52, bf16[128,576]{1,0:T(8,128)(2,1)S(1)} %collective-permute-done.refs_1_, ...), custom_call_target="tpu_custom_call" | custom-call | flops 6600000000 | tf_op jit(solution)/shard_map/attention/pallas_call | solution.py:255
  130.0 3.3 %collective-permute-done.25 = bf16[1,128,1024]{2,1,0:T(8,128)(2,1)S(1)} collective-permute-done((bf16[1,128,1024]{2,1,0:T(8,128)(2,1)S(1)}, bf16[1,128,1024]{2,1,0:T(8,128)(2,1)S(1)}, u32[]{:S(2)}, u32[]{:S(2)}) %collective-permute-start.25) | collective-permute-done | bytes 262176 | tf_op jit(solution)/shard_map/ppermute | solution.py:290
  133.3 5.5 %collective-permute-done.31 = bf16[1,128,1024]{2,1,0:T(8,128)(2,1)S(1)} collective-permute-done((bf16[1,128,1024]{2,1,0:T(8,128)(2,1)S(1)}, bf16[1,128,1024]{2,1,0:T(8,128)(2,1)S(1)}, u32[]{:S(2)}, u32[]{:S(2)}) %collective-permute-start.31) | collective-permute-done | bytes 262176 | tf_op jit(solution)/shard_map/ppermute | solution.py:290
  (101 shorter events, 30.8 us)
Async XLA Ops:
  1.3 12.5 %collective-permute-start.3 = (s32[1,6,128]{2,1,0:T(8,128)S(1)}, s32[1,6,128]{2,1,0:T(8,128)S(1)}, u32[]{:S(2)}, u32[]{:S(2)}) collective-permute-start(s32[1,6,128]{2,1,0:T(8,128)S(1)} %bitcast.65), channel_id=1, source_target_pairs={{0,1},{1,2},{2,3},{3,0},{4,5},{5,6},{6,7},{7,4},{8,9},{9,10},{10,1... | collective-permute-start | bytes 9224 | tf_op jit(solution)/shard_map/ppermute | solution.py:290
  4.3 9.6 %collective-permute-start.4 = (s32[1,6,128]{2,1,0:T(8,128)S(1)}, s32[1,6,128]{2,1,0:T(8,128)S(1)}, u32[]{:S(2)}, u32[]{:S(2)}) collective-permute-start(s32[1,6,128]{2,1,0:T(8,128)S(1)} %bitcast.66), channel_id=1, source_target_pairs={{0,3},{1,0},{2,1},{3,2},{4,7},{5,4},{6,5},{7,6},{8,11},{9,8},{10,9... | collective-permute-start | bytes 9224 | tf_op jit(solution)/shard_map/ppermute | solution.py:290
  6.4 9.3 %collective-permute-start.5 = (s32[1,6,128]{2,1,0:T(8,128)S(1)}, s32[1,6,128]{2,1,0:T(8,128)S(1)}, u32[]{:S(2)}, u32[]{:S(2)}) collective-permute-start(s32[1,6,128]{2,1,0:T(8,128)S(1)} %bitcast.67), channel_id=1, source_target_pairs={{0,2},{1,3},{2,0},{3,1},{4,6},{5,7},{6,4},{7,5},{8,10},{9,11},{10,... | collective-permute-start | bytes 9224 | tf_op jit(solution)/shard_map/ppermute | solution.py:290
  7.4 32.4 %collective-permute-start.15 = (bf16[128,1024]{1,0:T(8,128)(2,1)}, bf16[128,1024]{1,0:T(8,128)(2,1)S(1)}, u32[]{:S(2)}, u32[]{:S(2)}) collective-permute-start(bf16[128,1024]{1,0:T(8,128)(2,1)} %bitcast.56), channel_id=1, source_target_pairs={{0,1},{1,2},{2,3},{3,0},{4,5},{5,6},{6,7},{7,4},{8,9},{9,10},{10,1... | collective-permute-start | bytes 786440 | tf_op jit(solution)/shard_map/ppermute | solution.py:290
  9.0 32.4 %collective-permute-start.19 = (bf16[128,1024]{1,0:T(8,128)(2,1)}, bf16[128,1024]{1,0:T(8,128)(2,1)S(1)}, u32[]{:S(2)}, u32[]{:S(2)}) collective-permute-start(bf16[128,1024]{1,0:T(8,128)(2,1)} %bitcast.57), channel_id=1, source_target_pairs={{0,3},{1,0},{2,1},{3,2},{4,7},{5,4},{6,5},{7,6},{8,11},{9,8},{10,9... | collective-permute-start | bytes 786440 | tf_op jit(solution)/shard_map/ppermute | solution.py:290
  13.8 40.2 %collective-permute-start.8 = (bf16[128,1024]{1,0:T(8,128)(2,1)}, bf16[128,1024]{1,0:T(8,128)(2,1)S(1)}, u32[]{:S(2)}, u32[]{:S(2)}) collective-permute-start(bf16[128,1024]{1,0:T(8,128)(2,1)} %bitcast.58), channel_id=1, source_target_pairs={{0,2},{1,3},{2,0},{3,1},{4,6},{5,7},{6,4},{7,5},{8,10},{9,11},{10,... | collective-permute-start | bytes 786440 | tf_op jit(solution)/shard_map/ppermute | solution.py:290
  13.9 27.4 %collective-permute-start.12 = (bf16[128,1024]{1,0:T(8,128)(2,1)}, bf16[128,1024]{1,0:T(8,128)(2,1)S(1)}, u32[]{:S(2)}, u32[]{:S(2)}) collective-permute-start(bf16[128,1024]{1,0:T(8,128)(2,1)} %bitcast.59), channel_id=1, source_target_pairs={{0,8},{4,12},{8,0},{12,4},{1,9},{5,13},{9,1},{13,5},{2,10},{6,14},... | collective-permute-start | bytes 786440 | tf_op jit(solution)/shard_map/ppermute | solution.py:287
  21.1 18.1 %collective-permute-start.7 = (s32[4,1,2,6,128]{4,3,2,1,0:T(8,128)S(1)}, s32[4,1,2,6,128]{4,3,2,1,0:T(8,128)S(1)}, u32[]{:S(2)}, u32[]{:S(2)}) collective-permute-start(s32[4,1,2,6,128]{4,3,2,1,0:T(8,128)S(1)} %pad_add_fusion.1), channel_id=1, source_target_pairs={{0,4},{4,0},{8,12},{12,8},{1,5},{5,1},{9,13},{13,9},{2,6},{6,2},{1... | collective-permute-start | bytes 73736 | tf_op jit(solution)/shard_map/ppermute | solution.py:287
  39.8 9.2 %collective-permute-start.16 = (bf16[128,1024]{1,0:T(8,128)(2,1)S(1)}, bf16[128,1024]{1,0:T(8,128)(2,1)S(1)}, u32[]{:S(2)}, u32[]{:S(2)}) collective-permute-start(bf16[128,1024]{1,0:T(8,128)(2,1)S(1)} %collective-permute-done.15.refs_0_), channel_id=1, source_target_pairs={{0,8},{4,12},{8,0},{12,4},{1,9},{5,13},{9,1},{13,5},{2,10},{6,14},... | collective-permute-start | bytes 786440 | tf_op jit(solution)/shard_map/ppermute | solution.py:287
  41.3 9.2 %collective-permute-start.14 = (bf16[128,1024]{1,0:T(8,128)(2,1)S(1)}, bf16[128,1024]{1,0:T(8,128)(2,1)S(1)}, u32[]{:S(2)}, u32[]{:S(2)}) collective-permute-start(bf16[128,1024]{1,0:T(8,128)(2,1)S(1)} %collective-permute-done.12.refs_1_), channel_id=1, source_target_pairs={{0,4},{4,0},{8,12},{12,8},{1,5},{5,1},{9,13},{13,9},{2,6},{6,2},{1... | collective-permute-start | bytes 786440 | tf_op jit(solution)/shard_map/ppermute | solution.py:287
  41.4 12.2 %collective-permute-start = (bf16[128,576]{1,0:T(8,128)(2,1)S(1)}, bf16[128,576]{1,0:T(8,128)(2,1)S(1)}, u32[]{:S(2)}, u32[]{:S(2)}) collective-permute-start(bf16[128,576]{1,0:T(8,128)(2,1)S(1)} %bitcast.50), channel_id=1, source_target_pairs={{0,8},{4,12},{8,0},{12,4},{1,9},{5,13},{9,1},{13,5},{2,10},{6,14},... | collective-permute-start | bytes 442376 | tf_op jit(solution)/shard_map/ppermute | solution.py:287
  42.0 12.2 %collective-permute-start.17 = (bf16[128,1024]{1,0:T(8,128)(2,1)S(1)}, bf16[128,1024]{1,0:T(8,128)(2,1)S(1)}, u32[]{:S(2)}, u32[]{:S(2)}) collective-permute-start(bf16[128,1024]{1,0:T(8,128)(2,1)S(1)} %collective-permute-done.15.refs_0_), channel_id=1, source_target_pairs={{0,4},{4,0},{8,12},{12,8},{1,5},{5,1},{9,13},{13,9},{2,6},{6,2},{1... | collective-permute-start | bytes 786440 | tf_op jit(solution)/shard_map/ppermute | solution.py:287
  49.0 8.3 %collective-permute-start.20 = (bf16[128,1024]{1,0:T(8,128)(2,1)S(1)}, bf16[128,1024]{1,0:T(8,128)(2,1)S(1)}, u32[]{:S(2)}, u32[]{:S(2)}) collective-permute-start(bf16[128,1024]{1,0:T(8,128)(2,1)S(1)} %collective-permute-done.19.refs_0_), channel_id=1, source_target_pairs={{0,8},{4,12},{8,0},{12,4},{1,9},{5,13},{9,1},{13,5},{2,10},{6,14},... | collective-permute-start | bytes 786440 | tf_op jit(solution)/shard_map/ppermute | solution.py:287
  50.5 8.3 %collective-permute-start.18 = (bf16[128,1024]{1,0:T(8,128)(2,1)S(1)}, bf16[128,1024]{1,0:T(8,128)(2,1)S(1)}, u32[]{:S(2)}, u32[]{:S(2)}) collective-permute-start(bf16[128,1024]{1,0:T(8,128)(2,1)S(1)} %collective-permute-done.16.refs_1_), channel_id=1, source_target_pairs={{0,4},{4,0},{8,12},{12,8},{1,5},{5,1},{9,13},{13,9},{2,6},{6,2},{1... | collective-permute-start | bytes 786440 | tf_op jit(solution)/shard_map/ppermute | solution.py:287
  53.5 66.3 %collective-permute-start.1 = (bf16[128,576]{1,0:T(8,128)(2,1)S(1)}, bf16[128,576]{1,0:T(8,128)(2,1)S(1)}, u32[]{:S(2)}, u32[]{:S(2)}) collective-permute-start(bf16[128,576]{1,0:T(8,128)(2,1)S(1)} %bitcast.51), channel_id=1, source_target_pairs={{0,4},{4,0},{8,12},{12,8},{1,5},{5,1},{9,13},{13,9},{2,6},{6,2},{1... | collective-permute-start | bytes 442376 | tf_op jit(solution)/shard_map/ppermute | solution.py:287
  54.1 69.1 %collective-permute-start.2 = (bf16[128,576]{1,0:T(8,128)(2,1)S(1)}, bf16[128,576]{1,0:T(8,128)(2,1)S(1)}, u32[]{:S(2)}, u32[]{:S(2)}) collective-permute-start(bf16[128,576]{1,0:T(8,128)(2,1)S(1)} %collective-permute-done.refs_1_), channel_id=1, source_target_pairs={{0,4},{4,0},{8,12},{12,8},{1,5},{5,1},{9,13},{13,9},{2,6},{6,2},{1... | collective-permute-start | bytes 442376 | tf_op jit(solution)/shard_map/ppermute | solution.py:287
  54.1 7.5 %collective-permute-start.21 = (bf16[128,1024]{1,0:T(8,128)(2,1)S(1)}, bf16[128,1024]{1,0:T(8,128)(2,1)S(1)}, u32[]{:S(2)}, u32[]{:S(2)}) collective-permute-start(bf16[128,1024]{1,0:T(8,128)(2,1)S(1)} %collective-permute-done.19.refs_0_), channel_id=1, source_target_pairs={{0,4},{4,0},{8,12},{12,8},{1,5},{5,1},{9,13},{13,9},{2,6},{6,2},{1... | collective-permute-start | bytes 786440 | tf_op jit(solution)/shard_map/ppermute | solution.py:287
  98.8 9.2 %collective-permute-start.24 = (bf16[1,128,1024]{2,1,0:T(8,128)(2,1)S(1)}, bf16[1,128,1024]{2,1,0:T(8,128)(2,1)S(1)}, u32[]{:S(2)}, u32[]{:S(2)}) collective-permute-start(bf16[1,128,1024]{2,1,0:T(8,128)(2,1)S(1)} %add_convert_fusion.7), channel_id=1, source_target_pairs={{0,8},{4,12},{8,0},{12,4},{1,9},{5,13},{9,1},{13,5},{2,10},{6,14},... | collective-permute-start | bytes 786440 | tf_op jit(solution)/shard_map/ppermute | solution.py:287
  100.4 13.1 %collective-permute-start.27 = (bf16[1,128,1024]{2,1,0:T(8,128)(2,1)S(1)}, bf16[1,128,1024]{2,1,0:T(8,128)(2,1)S(1)}, u32[]{:S(2)}, u32[]{:S(2)}) collective-permute-start(bf16[1,128,1024]{2,1,0:T(8,128)(2,1)S(1)} %add_convert_fusion.5), channel_id=1, source_target_pairs={{0,8},{4,12},{8,0},{12,4},{1,9},{5,13},{9,1},{13,5},{2,10},{6,14},... | collective-permute-start | bytes 786440 | tf_op jit(solution)/shard_map/ppermute | solution.py:287
  101.2 17.9 %collective-permute-start.30 = (bf16[1,128,1024]{2,1,0:T(8,128)(2,1)S(1)}, bf16[1,128,1024]{2,1,0:T(8,128)(2,1)S(1)}, u32[]{:S(2)}, u32[]{:S(2)}) collective-permute-start(bf16[1,128,1024]{2,1,0:T(8,128)(2,1)S(1)} %add_convert_fusion.3), channel_id=1, source_target_pairs={{0,8},{4,12},{8,0},{12,4},{1,9},{5,13},{9,1},{13,5},{2,10},{6,14},... | collective-permute-start | bytes 786440 | tf_op jit(solution)/shard_map/ppermute | solution.py:287
  107.9 22.1 %collective-permute-start.33 = (bf16[1,128,1024]{2,1,0:T(8,128)(2,1)S(1)}, bf16[1,128,1024]{2,1,0:T(8,128)(2,1)S(1)}, u32[]{:S(2)}, u32[]{:S(2)}) collective-permute-start(bf16[1,128,1024]{2,1,0:T(8,128)(2,1)S(1)} %add_convert_fusion.1), channel_id=1, source_target_pairs={{0,8},{4,12},{8,0},{12,4},{1,9},{5,13},{9,1},{13,5},{2,10},{6,14},... | collective-permute-start | bytes 786440 | tf_op jit(solution)/shard_map/ppermute | solution.py:287
  113.5 19.7 %collective-permute-start.25 = (bf16[1,128,1024]{2,1,0:T(8,128)(2,1)S(1)}, bf16[1,128,1024]{2,1,0:T(8,128)(2,1)S(1)}, u32[]{:S(2)}, u32[]{:S(2)}) collective-permute-start(bf16[1,128,1024]{2,1,0:T(8,128)(2,1)S(1)} %add_convert_fusion.6), channel_id=1, source_target_pairs={{0,2},{1,3},{2,0},{3,1},{4,6},{5,7},{6,4},{7,5},{8,10},{9,11},{10,... | collective-permute-start | bytes 786440 | tf_op jit(solution)/shard_map/ppermute | solution.py:290
  119.2 14.1 %collective-permute-start.28 = (bf16[1,128,1024]{2,1,0:T(8,128)(2,1)S(1)}, bf16[1,128,1024]{2,1,0:T(8,128)(2,1)S(1)}, u32[]{:S(2)}, u32[]{:S(2)}) collective-permute-start(bf16[1,128,1024]{2,1,0:T(8,128)(2,1)S(1)} %add_convert_fusion.4), channel_id=1, source_target_pairs={{0,1},{1,2},{2,3},{3,0},{4,5},{5,6},{6,7},{7,4},{8,9},{9,10},{10,1... | collective-permute-start | bytes 786440 | tf_op jit(solution)/shard_map/ppermute | solution.py:290
  119.8 19.0 %collective-permute-start.31 = (bf16[1,128,1024]{2,1,0:T(8,128)(2,1)S(1)}, bf16[1,128,1024]{2,1,0:T(8,128)(2,1)S(1)}, u32[]{:S(2)}, u32[]{:S(2)}) collective-permute-start(bf16[1,128,1024]{2,1,0:T(8,128)(2,1)S(1)} %add_convert_fusion.2), channel_id=1, source_target_pairs={{0,3},{1,0},{2,1},{3,2},{4,7},{5,4},{6,5},{7,6},{8,11},{9,8},{10,9... | collective-permute-start | bytes 786440 | tf_op jit(solution)/shard_map/ppermute | solution.py:290
  (20 other events, 110.6 us)

commit v3 on v2

--- a/solution.py
+++ b/solution.py
@@ -15,7 +15,8 @@
 BLOCK = 128
 LANES = 128
 EXPERT_ROWS = 256
-VMEM = 48 * 2**20
+EXTRA = 16
+VMEM = 20 * 2**20
 PEAK = 1.1e9
 
 qk_scale = 192.0 ** (-0.5)
@@ -41,7 +42,7 @@
     )
 
 
-def dispatch_kernel(n_parts, n_row, base_ref, ids_ref, rw_ref, *refs):
+def dispatch_kernel(n_parts, n_row, top, base_ref, rw_ref, *refs):
     parts, refs = refs[:n_parts], refs[n_parts:]
     if n_row:
         seg_ref, scale_ref = refs[:2]
@@ -49,7 +50,8 @@
     rows_ref, weight_ref, picks_ref = refs[:3]
     local = rows_ref.shape[0]
     width = rows_ref.shape[2]
-    names = lax.broadcasted_iota(jnp.int32, (EXPERTS, BLOCK), 0)
+    names = lax.broadcasted_iota(jnp.int32, (EXPERTS, BLOCK), 0).astype(jnp.float32)
+    base = base_ref[0].astype(jnp.float32)
     before = (
         lax.broadcasted_iota(jnp.int32, (BLOCK, BLOCK), 0)
         < lax.broadcasted_iota(jnp.int32, (BLOCK, BLOCK), 1)
@@ -57,15 +59,15 @@
     slot = lax.broadcasted_iota(jnp.int32, (local, CAP, BLOCK), 1).astype(jnp.float32)
     hots, probs = [], []
     for p in range(n_parts):
-        x = parts[p][...]
+        x = parts[p][:BLOCK, :]
+        ids = parts[p][BLOCK : BLOCK + EXTRA, :].astype(jnp.float32)[0:1] - base
+        ids = jnp.where(ids < 0.0, ids + EXPERTS, ids)
         logits = lax.dot_general(rw_ref[...], x, NT, preferred_element_type=jnp.float32)
         expo = jnp.exp(logits - jnp.max(logits, axis=0, keepdims=True))
         prob = expo / jnp.sum(expo, axis=0, keepdims=True)
-        ids = ids_ref[p] - base_ref[0]
-        ids = jnp.where(ids < 0, ids + EXPERTS, ids)
-        hot = names == ids[0:1]
-        for k in range(1, ids.shape[0]):
-            hot = hot | (names == ids[k : k + 1])
+        hot = names == ids[:, :BLOCK]
+        for k in range(1, top):
+            hot = hot | (names == ids[:, k * BLOCK : (k + 1) * BLOCK])
         hot = hot.astype(jnp.float32)
         chosen = prob * hot
         gate = chosen[:local] / jnp.sum(chosen, axis=0, keepdims=True)
@@ -103,15 +105,14 @@
     return pl.BlockSpec(a.shape, lambda *i: (0,) * a.ndim)
 
 
-def dispatch(parts, ids, base, rw, local, row=None):
+def dispatch(parts, top, base, rw, local, row=None):
     n_parts = len(parts)
-    n, width = parts[0].shape[0] // BLOCK, parts[0].shape[1]
+    n, width = parts[0].shape[0] // (BLOCK + EXTRA), parts[0].shape[1]
     slots = n_parts * CAP
     in_specs = [
         pl.BlockSpec(memory_space=pltpu.SMEM),
-        pl.BlockSpec((n_parts,) + ids.shape[1:], lambda i: (i, 0, 0)),
         whole(rw),
-    ] + [pl.BlockSpec((BLOCK, width), lambda i: (i, 0))] * n_parts
+    ] + [pl.BlockSpec((BLOCK + EXTRA, width), lambda i: (i, 0))] * n_parts
     out_specs = [
         pl.BlockSpec((local, slots, width), lambda i: (0, i, 0)),
         pl.BlockSpec((local, slots, LANES), lambda i: (0, i, 0)),
@@ -129,7 +130,7 @@
         out_specs.append(pl.BlockSpec((NDOC, LANES), lambda i: (0, 0)))
         out_shape.append(jax.ShapeDtypeStruct((NDOC, LANES), jnp.float32))
     return call(
-        functools.partial(dispatch_kernel, n_parts, n_parts if row is not None else 0),
+        functools.partial(dispatch_kernel, n_parts, n_parts if row is not None else 0, top),
         3 * n,
         (n,),
         in_specs,
@@ -137,32 +138,42 @@
         out_shape,
         [],
         "dispatch",
-    )(base, ids, rw, *parts, *extra)
+    )(base, rw, *parts, *extra)
 
 
 def expert_kernel(n, *refs):
     rows, weights = refs[:n], refs[n : 2 * n]
     gu_ref, down_ref = refs[2 * n : 2 * n + 2]
-    outs = refs[2 * n + 2 : 3 * n + 2]
-    both = refs[3 * n + 2]
-    held = jnp.concatenate([r[0] for r in rows], axis=0)
-    hidden = lax.dot_general(gu_ref[0], held, NT, preferred_element_type=jnp.float32)
-    half = both.shape[1] // 2
-    inner = []
-    for c in range(both.shape[0]):
-        both[c] = hidden[:, c * LANES : (c + 1) * LANES]
-        g = both[c, pl.ds(0, half, stride=2), :]
-        u = both[c, pl.ds(1, half, stride=2), :]
-        inner.append((g * lax.logistic(g) * u).astype(jnp.bfloat16))
-    inner = jnp.concatenate(inner, axis=1)
-    made = lax.dot_general(inner, down_ref[0], TN, preferred_element_type=jnp.float32)
+    outs, wide = refs[2 * n + 2 : 3 * n + 2], refs[3 * n + 2]
+    group, hidden, width = down_ref.shape
     size = rows[0].shape[1]
-    for i in range(n):
-        w = weights[i][0]
-        part = made[i * size : (i + 1) * size]
-        for c in range(part.shape[1] // LANES):
-            at = slice(c * LANES, (c + 1) * LANES)
-            outs[i][0, :, at] = (part[:, at] * w).astype(jnp.bfloat16)
+    chunks = width // LANES
+    for e in range(group):
+        wide[e] = gu_ref[e].astype(jnp.float32)
+        gu = jnp.concatenate(
+            [
+                jnp.concatenate(
+                    [
+                        wide[e, pl.ds(2 * c + z, hidden, stride=2 * chunks), :].astype(jnp.bfloat16)
+                        for c in range(chunks)
+                    ],
+                    axis=1,
+                )
+                for z in range(2)
+            ],
+            axis=0,
+        )
+        held = jnp.concatenate([r[e] for r in rows], axis=0)
+        both = lax.dot_general(gu, held, NT, preferred_element_type=jnp.float32)
+        g, u = both[:hidden], both[hidden:]
+        inner = (g * lax.logistic(g) * u).astype(jnp.bfloat16)
+        made = lax.dot_general(inner, down_ref[e], TN, preferred_element_type=jnp.float32)
+        for i in range(n):
+            w = weights[i][e]
+            part = made[i * size : (i + 1) * size]
+            for c in range(chunks):
+                at = slice(c * LANES, (c + 1) * LANES)
+                outs[i][e, :, at] = (part[:, at] * w).astype(jnp.bfloat16)
 
 
 def experts(rows, weights, gate_up, down):
@@ -170,23 +181,27 @@
     local, slots, width = rows[0].shape
     size = min(slots, EXPERT_ROWS)
     hidden = down.shape[1]
-    rows_spec = pl.BlockSpec((1, size, width), lambda e, i: (e, i, 0))
-    weight_spec = pl.BlockSpec((1, size, LANES), lambda e, i: (e, i, 0))
+    group = 2 if local % 2 == 0 else 1
+    chunks = width // LANES
+    gu = gate_up.reshape(local, hidden, 2, chunks, LANES).swapaxes(2, 3)
+    gu = gu.reshape(local, hidden * 2 * chunks, LANES)
+    rows_spec = pl.BlockSpec((group, size, width), lambda e, i: (e, i, 0))
+    weight_spec = pl.BlockSpec((group, size, LANES), lambda e, i: (e, i, 0))
     return call(
         functools.partial(expert_kernel, n),
         10,
-        (local, slots // size),
+        (local // group, slots // size),
         [rows_spec] * n
         + [weight_spec] * n
         + [
-            pl.BlockSpec((1, 2 * hidden, width), lambda e, i: (e, 0, 0)),
-            pl.BlockSpec((1, hidden, width), lambda e, i: (e, 0, 0)),
+            pl.BlockSpec((group,) + gu.shape[1:], lambda e, i: (e, 0, 0)),
+            pl.BlockSpec((group, hidden, width), lambda e, i: (e, 0, 0)),
         ],
         [rows_spec] * n,
         [jax.ShapeDtypeStruct(r.shape, jnp.bfloat16) for r in rows],
-        [pltpu.VMEM((n * size // LANES, 2 * hidden, LANES), jnp.float32)],
+        [pltpu.VMEM((group,) + gu.shape[1:], jnp.float32)],
         "experts",
-    )(*rows, *weights, gate_up, down)
+    )(*rows, *weights, gu, down)
 
 
 def combine_kernel(groups, picks_ref, made_ref, *outs):
@@ -297,13 +312,13 @@
     masks = [0, 2, 1, 3]
     order = jnp.stack([ctx ^ m for m in masks])
 
-    picks = jnp.swapaxes(expert_ids[0].reshape(tok_rows // BLOCK, BLOCK, -1), 1, 2)
-    ids = jnp.stack(along_exp(picks))
-    ids = jnp.stack([ids, flip(ids, 2)], axis=2)
-    ids = jnp.concatenate([ids, flip(ids, 1)], axis=2)
-    ids = ids.reshape((len(shifts), -1) + picks.shape[1:])
-
-    spread = [[a] for a in along_exp(tokens)]
+    top = expert_ids.shape[2]
+    picks = expert_ids[0].T.astype(jnp.bfloat16).reshape(1, top * tok_rows)
+    picks = jnp.pad(picks, ((0, EXTRA - 1), (0, width - top * tok_rows)))
+    packed = jnp.concatenate([tokens, picks], axis=0)
+
+    near_parts = along_exp(packed)
+    spread = [[a] for a in near_parts]
     spread = [held + [flip(a, 2) for a in held] for held in spread]
     spread = [held + [flip(a, 1) for a in held] for held in spread]
     kv = [latent_kv[0]]
@@ -320,20 +335,19 @@
 
     seg = jnp.sum((row_pos[..., None] >= ends).astype(jnp.int32), axis=-1)
     sizes = lengths.astype(jnp.float32)
-    scale = jnp.broadcast_to((EXPERTS / (expert_ids.shape[2] * sizes * sizes))[:, None], (NDOC, LANES))
+    scale = jnp.broadcast_to((EXPERTS / (top * sizes * sizes))[:, None], (NDOC, LANES))
 
     base = (exp * local).reshape(1).astype(jnp.int32)
     rw = jnp.roll(router_weight.T, -exp * local, axis=0)
-    gu = gate_up.reshape(local, -1, width)
     balance = None
     sent = []
     for i, held in enumerate(spread):
         row = (seg.reshape(-1, 1, BLOCK), scale) if near and i == 0 else None
-        out = dispatch(held, ids[i], base, rw, local, row)
+        out = dispatch(held, top, base, rw, local, row)
         sent.append(out[:3])
         if row is not None:
             balance = out[3]
-    made = experts([s[0] for s in sent], [s[1] for s in sent], gu, w_down)
+    made = experts([s[0] for s in sent], [s[1] for s in sent], gate_up, w_down)
 
     back = []
     for i in reversed(range(len(shifts))):

time: 141 us -> 114 us (0.81)
  local copies, waits for them, and re-layouts: 27.4 us -> 2.02 us
  Pallas kernels: 36.2 us -> 31.6 us
  starting transfers between devices: 32.9 us -> 34.8 us
  other arithmetic: 4.38 us -> 6.04 us
    reshape x1 -> x0, local copies, waits for them, and re-layouts: 17.6 us -> none  [shards(): gu = gate_up.reshape(local, -1, width)]
    ppermute x9 -> x6, waiting for transfers between devices: 8.77 us -> 20.8 us  [shift(): return lax.ppermute(a, 'exp', [(i, (i + d) % n_exp) for i in range(n_exp)])]
    ppermute x25 -> x23, waiting for transfers between devices: 29.2 us -> 17.7 us  [flip(): return lax.ppermute(a, 'ctx', [(i, i ^ bit) for i in range(n_ctx)])]
    unnamed x22 -> x9, local copies, waits for them, and re-layouts: 8.86 us -> 1.09 us
    pallas_call x1, Pallas kernels: 22 us -> 17.5 us  [experts(): call(functools.partial(expert_kernel, n), 10, (local // group, slots // s...]
    ppermute x9 -> x6, starting transfers between devices: 16.4 us -> 19.7 us  [shift(): return lax.ppermute(a, 'exp', [(i, (i + d) % n_exp) for i in range(n_exp)])]
    ppermute x25 -> x23, starting transfers between devices: 16.5 us -> 15 us  [flip(): return lax.ppermute(a, 'ctx', [(i, i ^ bit) for i in range(n_ctx)])]
  transfers between devices with their start and end apart: 34 -> 29, of which waited for: 9 -> 12; matrix products, arithmetic and copies ran while one was open for 16% -> 5% of each run, Pallas kernels for 26% -> 28%
where the time goes in v3:
time: 114 us
  waiting for transfers between devices  38.5 us (34%)
  starting transfers between devices  34.8 us (31%)
  Pallas kernels  31.6 us (28%)
  other arithmetic  6.04 us (5%)
  local copies, waits for them, and re-layouts  2.02 us (2%)
    ppermute x6, waiting for transfers between devices, shift(): return lax.ppermute(a, 'exp', [(i, (i + d) % n_exp) for i in range(n_exp)])  20.8 us
    ppermute x6, starting transfers between devices, shift(): return lax.ppermute(a, 'exp', [(i, (i + d) % n_exp) for i in range(n_exp)])  19.7 us
    ppermute x23, waiting for transfers between devices, flip(): return lax.ppermute(a, 'ctx', [(i, i ^ bit) for i in range(n_ctx)])  17.7 us
    pallas_call x1, Pallas kernels, experts(): call(functools.partial(expert_kernel, n), 10, (local // group, slots // s...  17.5 us
    ppermute x23, starting transfers between devices, flip(): return lax.ppermute(a, 'ctx', [(i, i ^ bit) for i in range(n_ctx)])  15 us
    pallas_call x1, Pallas kernels, attend(): call(functools.partial(attend_kernel, n), 6, (HEADS // 2,), [whole(first)...  6.18 us
    pallas_call x4, Pallas kernels, dispatch(): call(functools.partial(dispatch_kernel, n_parts, n_parts if row is not No...  6.01 us
  transfers between devices with their start and end apart: 29, of which 12 were waited for; matrix products, arithmetic and copies ran while one was open for 5% of the time, Pallas kernels for 28%

profile of v3, /device:TPU:0, one launch (start us, length us, event | category | flops | bytes accessed | tf_op | source)
XLA Modules:
  0.0 113.8 jit_solution(15038338947916544495)
XLA Ops:
  2.3 3.1 %collective-permute-start.10 = (bf16[144,1024]{1,0:T(8,128)(2,1)S(1)}, bf16[144,1024]{1,0:T(8,128)(2,1)S(1)}, u32[]{:S(2)}, u32[]{:S(2)}) collective-permute-start(bf16[144,1024]{1,0:T(8,128)(2,1)S(1)} %fusion.1.refs_0_), channel_id=1, source_target_pairs={{0,1},{1,2},{2,3},{3,0},{4,5},{5,6},{6,7},{7,4},{8,9},{9,10},{10,1... | collective-permute-start | bytes 884744 | tf_op jit(solution)/shard_map/ppermute | solution.py:305
  5.4 2.1 %collective-permute-start.14 = (bf16[144,1024]{1,0:T(8,128)(2,1)S(1)}, bf16[144,1024]{1,0:T(8,128)(2,1)S(1)}, u32[]{:S(2)}, u32[]{:S(2)}) collective-permute-start(bf16[144,1024]{1,0:T(8,128)(2,1)S(1)} %fusion.1.refs_0_), channel_id=1, source_target_pairs={{0,3},{1,0},{2,1},{3,2},{4,7},{5,4},{6,5},{7,6},{8,11},{9,8},{10,9... | collective-permute-start | bytes 884744 | tf_op jit(solution)/shard_map/ppermute | solution.py:305
  8.4 1.5 %collective-permute-start.7 = (bf16[144,1024]{1,0:T(8,128)(2,1)S(1)}, bf16[144,1024]{1,0:T(8,128)(2,1)S(1)}, u32[]{:S(2)}, u32[]{:S(2)}) collective-permute-start(bf16[144,1024]{1,0:T(8,128)(2,1)S(1)} %fusion.1.refs_0_), channel_id=1, source_target_pairs={{0,8},{4,12},{8,0},{12,4},{1,9},{5,13},{9,1},{13,5},{2,10},{6,14},... | collective-permute-start | bytes 884744 | tf_op jit(solution)/shard_map/ppermute | solution.py:302
  13.3 2.0 %collective-permute-done.10.refs_0_ = bf16[144,1024]{1,0:T(8,128)(2,1)S(1)} collective-permute-done((bf16[144,1024]{1,0:T(8,128)(2,1)S(1)}, bf16[144,1024]{1,0:T(8,128)(2,1)S(1)}, u32[]{:S(2)}, u32[]{:S(2)}) %collective-permute-start.10) | collective-permute-done | bytes 294944 | tf_op jit(solution)/shard_map/ppermute | solution.py:305
  15.3 1.7 %collective-permute-start.11 = (bf16[144,1024]{1,0:T(8,128)(2,1)S(1)}, bf16[144,1024]{1,0:T(8,128)(2,1)S(1)}, u32[]{:S(2)}, u32[]{:S(2)}) collective-permute-start(bf16[144,1024]{1,0:T(8,128)(2,1)S(1)} %collective-permute-done.10.refs_0_), channel_id=1, source_target_pairs={{0,8},{4,12},{8,0},{12,4},{1,9},{5,13},{9,1},{13,5},{2,10},{6,14},... | collective-permute-start | bytes 884744 | tf_op jit(solution)/shard_map/ppermute | solution.py:302
  17.8 2.4 %collective-permute-done.14.refs_0_ = bf16[144,1024]{1,0:T(8,128)(2,1)S(1)} collective-permute-done((bf16[144,1024]{1,0:T(8,128)(2,1)S(1)}, bf16[144,1024]{1,0:T(8,128)(2,1)S(1)}, u32[]{:S(2)}, u32[]{:S(2)}) %collective-permute-start.14) | collective-permute-done | bytes 294944 | tf_op jit(solution)/shard_map/ppermute | solution.py:305
  20.2 1.5 %collective-permute-start = (bf16[128,576]{1,0:T(8,128)(2,1)S(1)}, bf16[128,576]{1,0:T(8,128)(2,1)S(1)}, u32[]{:S(2)}, u32[]{:S(2)}) collective-permute-start(bf16[128,576]{1,0:T(8,128)(2,1)S(1)} %bitcast.37), channel_id=1, source_target_pairs={{0,8},{4,12},{8,0},{12,4},{1,9},{5,13},{9,1},{13,5},{2,10},{6,14},... | collective-permute-start | bytes 442376 | tf_op jit(solution)/shard_map/ppermute | solution.py:302
  21.7 1.6 %collective-permute-done.11.refs_1_ = bf16[144,1024]{1,0:T(8,128)(2,1)S(1)} collective-permute-done((bf16[144,1024]{1,0:T(8,128)(2,1)S(1)}, bf16[144,1024]{1,0:T(8,128)(2,1)S(1)}, u32[]{:S(2)}, u32[]{:S(2)}) %collective-permute-start.11) | collective-permute-done | bytes 294944 | tf_op jit(solution)/shard_map/ppermute | solution.py:302
  24.6 1.6 %dispatch.5 = (bf16[16,64,1024]{2,1,0:T(8,128)(2,1)S(1)}, f32[16,64,128]{2,1,0:T(8,128)S(1)}, bf16[4,256,128]{2,1,0:T(8,128)(2,1)S(1)}, f32[8,128]{1,0:T(8,128)S(1)}) custom-call(s32[1]{0:T(128)} %bitcast.13.base_ref, bf16[64,1024]{1,0:T(8,128)(2,1)S(1)} %fusion.2.rw_ref, bf16[144,1024]{1,0:T(8,128)(2,1)S(1)} %fusion.1.refs_0_, ...), custom_call_target="tpu_custom_call" | custom-call | flops 3300000000 | tf_op jit(solution)/shard_map/dispatch/pallas_call | solution.py:132
  27.3 6.1 %collective-permute-done.3.refs_0_ = bf16[144,1024]{1,0:T(8,128)(2,1)S(1)} collective-permute-done((bf16[144,1024]{1,0:T(8,128)(2,1)S(1)}, bf16[144,1024]{1,0:T(8,128)(2,1)S(1)}, u32[]{:S(2)}, u32[]{:S(2)}) %collective-permute-start.3) | collective-permute-done | bytes 294944 | tf_op jit(solution)/shard_map/ppermute | solution.py:305
  33.9 1.5 %collective-permute-start.4 = (bf16[144,1024]{1,0:T(8,128)(2,1)S(1)}, bf16[144,1024]{1,0:T(8,128)(2,1)S(1)}, u32[]{:S(2)}, u32[]{:S(2)}) collective-permute-start(bf16[144,1024]{1,0:T(8,128)(2,1)S(1)} %collective-permute-done.3.refs_0_), channel_id=1, source_target_pairs={{0,8},{4,12},{8,0},{12,4},{1,9},{5,13},{9,1},{13,5},{2,10},{6,14},... | collective-permute-start | bytes 884744 | tf_op jit(solution)/shard_map/ppermute | solution.py:302
  37.5 5.4 %collective-permute-done.4.refs_1_ = bf16[144,1024]{1,0:T(8,128)(2,1)S(1)} collective-permute-done((bf16[144,1024]{1,0:T(8,128)(2,1)S(1)}, bf16[144,1024]{1,0:T(8,128)(2,1)S(1)}, u32[]{:S(2)}, u32[]{:S(2)}) %collective-permute-start.4) | collective-permute-done | bytes 294944 | tf_op jit(solution)/shard_map/ppermute | solution.py:302
  44.5 1.5 %dispatch.4 = (bf16[16,64,1024]{2,1,0:T(8,128)(2,1)S(1)}, f32[16,64,128]{2,1,0:T(8,128)S(1)}, bf16[4,256,128]{2,1,0:T(8,128)(2,1)S(1)}) custom-call(s32[1]{0:T(128)} %bitcast.13.base_ref, bf16[64,1024]{1,0:T(8,128)(2,1)S(1)} %fusion.2.rw_ref, bf16[144,1024]{1,0:T(8,128)(2,1)S(1)} %collective-permute-done.3.refs_0_, ...), custom_call_target="tpu_custom_call" | custom-call | flops 3300000000 | tf_op jit(solution)/shard_map/dispatch/pallas_call | solution.py:132
  46.0 17.5 %experts.1 = (bf16[16,64,1024]{2,1,0:T(8,128)(2,1)S(1)}, bf16[16,64,1024]{2,1,0:T(8,128)(2,1)S(1)}, bf16[16,64,1024]{2,1,0:T(8,128)(2,1)S(1)}, bf16[16,64,1024]{2,1,0:T(8,128)(2,1)S(1)}) custom-call(bf16[16,64,1024]{2,1,0:T(8,128)(2,1)S(1)} %get-tuple-element.29.refs_0_, bf16[16,64,1024]{2,1,0:T(8,128)(2,1)S(1)} %get-tuple-element.30.refs_1_, ...), custom_call_target="tpu_custom_call" | custom-call | flops 11000000512 | tf_op jit(solution)/shard_map/experts/pallas_call | solution.py:190
  66.9 1.5 %collective-permute-start.19 = (bf16[1,128,1024]{2,1,0:T(8,128)(2,1)S(1)}, bf16[1,128,1024]{2,1,0:T(8,128)(2,1)S(1)}, u32[]{:S(2)}, u32[]{:S(2)}) collective-permute-start(bf16[1,128,1024]{2,1,0:T(8,128)(2,1)S(1)} %add_convert_fusion.7), channel_id=1, source_target_pairs={{0,8},{4,12},{8,0},{12,4},{1,9},{5,13},{9,1},{13,5},{2,10},{6,14},... | collective-permute-start | bytes 786440 | tf_op jit(solution)/shard_map/ppermute | solution.py:302
  69.3 1.5 %collective-permute-start.25 = (bf16[1,128,1024]{2,1,0:T(8,128)(2,1)S(1)}, bf16[1,128,1024]{2,1,0:T(8,128)(2,1)S(1)}, u32[]{:S(2)}, u32[]{:S(2)}) collective-permute-start(bf16[1,128,1024]{2,1,0:T(8,128)(2,1)S(1)} %add_convert_fusion.3), channel_id=1, source_target_pairs={{0,8},{4,12},{8,0},{12,4},{1,9},{5,13},{9,1},{13,5},{2,10},{6,14},... | collective-permute-start | bytes 786440 | tf_op jit(solution)/shard_map/ppermute | solution.py:302
  70.9 5.2 %collective-permute-done.19 = bf16[1,128,1024]{2,1,0:T(8,128)(2,1)S(1)} collective-permute-done((bf16[1,128,1024]{2,1,0:T(8,128)(2,1)S(1)}, bf16[1,128,1024]{2,1,0:T(8,128)(2,1)S(1)}, u32[]{:S(2)}, u32[]{:S(2)}) %collective-permute-start.19) | collective-permute-done | bytes 262176 | tf_op jit(solution)/shard_map/ppermute | solution.py:302
  76.1 1.5 %collective-permute-start.28 = (bf16[1,128,1024]{2,1,0:T(8,128)(2,1)S(1)}, bf16[1,128,1024]{2,1,0:T(8,128)(2,1)S(1)}, u32[]{:S(2)}, u32[]{:S(2)}) collective-permute-start(bf16[1,128,1024]{2,1,0:T(8,128)(2,1)S(1)} %add_convert_fusion.1), channel_id=1, source_target_pairs={{0,8},{4,12},{8,0},{12,4},{1,9},{5,13},{9,1},{13,5},{2,10},{6,14},... | collective-permute-start | bytes 786440 | tf_op jit(solution)/shard_map/ppermute | solution.py:302
  77.7 4.0 %collective-permute-done.22 = bf16[1,128,1024]{2,1,0:T(8,128)(2,1)S(1)} collective-permute-done((bf16[1,128,1024]{2,1,0:T(8,128)(2,1)S(1)}, bf16[1,128,1024]{2,1,0:T(8,128)(2,1)S(1)}, u32[]{:S(2)}, u32[]{:S(2)}) %collective-permute-start.22) | collective-permute-done | bytes 262176 | tf_op jit(solution)/shard_map/ppermute | solution.py:302
  81.7 9.7 %collective-permute-start.20 = (bf16[1,128,1024]{2,1,0:T(8,128)(2,1)S(1)}, bf16[1,128,1024]{2,1,0:T(8,128)(2,1)S(1)}, u32[]{:S(2)}, u32[]{:S(2)}) collective-permute-start(bf16[1,128,1024]{2,1,0:T(8,128)(2,1)S(1)} %add_convert_fusion.6), channel_id=1, source_target_pairs={{0,2},{1,3},{2,0},{3,1},{4,6},{5,7},{6,4},{7,5},{8,10},{9,11},{10,... | collective-permute-start | bytes 786440 | tf_op jit(solution)/shard_map/ppermute | solution.py:305
  91.5 3.6 %collective-permute-start.23 = (bf16[1,128,1024]{2,1,0:T(8,128)(2,1)S(1)}, bf16[1,128,1024]{2,1,0:T(8,128)(2,1)S(1)}, u32[]{:S(2)}, u32[]{:S(2)}) collective-permute-start(bf16[1,128,1024]{2,1,0:T(8,128)(2,1)S(1)} %add_convert_fusion.4), channel_id=1, source_target_pairs={{0,1},{1,2},{2,3},{3,0},{4,5},{5,6},{6,7},{7,4},{8,9},{9,10},{10,1... | collective-permute-start | bytes 786440 | tf_op jit(solution)/shard_map/ppermute | solution.py:305
  95.6 6.2 %attention.1 = bf16[128,4096]{1,0:T(8,128)(2,1)} custom-call(s32[128,1]{1,0:T(8,128)S(1)} %copy.20.first_ref, s32[128,1]{1,0:T(8,128)S(1)} %copy.21.last_ref, s32[1,512]{1,0:T(1,128)S(1)} %bitcast.40, bf16[128,4608]{1,0:T(8,128)(2,1)S(1)} %bitcast.44, bf16[128,576]{1,0:T(8,128)(2,1)S(1)} %bitcast.39, bf16[128,576]{1,0:T(8,128)(2,1)S(1)} %collective-permute-done.refs_1_, ...), custom_call_target="tpu_custom_call" | custom-call | flops 6600000000 | tf_op jit(solution)/shard_map/attention/pallas_call | solution.py:270
  102.4 6.0 %collective-permute-done.20 = bf16[1,128,1024]{2,1,0:T(8,128)(2,1)S(1)} collective-permute-done((bf16[1,128,1024]{2,1,0:T(8,128)(2,1)S(1)}, bf16[1,128,1024]{2,1,0:T(8,128)(2,1)S(1)}, u32[]{:S(2)}, u32[]{:S(2)}) %collective-permute-start.20) | collective-permute-done | bytes 262176 | tf_op jit(solution)/shard_map/ppermute | solution.py:305
  108.4 4.4 %collective-permute-done.26 = bf16[1,128,1024]{2,1,0:T(8,128)(2,1)S(1)} collective-permute-done((bf16[1,128,1024]{2,1,0:T(8,128)(2,1)S(1)}, bf16[1,128,1024]{2,1,0:T(8,128)(2,1)S(1)}, u32[]{:S(2)}, u32[]{:S(2)}) %collective-permute-start.26) | collective-permute-done | bytes 262176 | tf_op jit(solution)/shard_map/ppermute | solution.py:305
  (76 shorter events, 20.0 us)
Async XLA Ops:
  2.3 13.0 %collective-permute-start.10 = (bf16[144,1024]{1,0:T(8,128)(2,1)S(1)}, bf16[144,1024]{1,0:T(8,128)(2,1)S(1)}, u32[]{:S(2)}, u32[]{:S(2)}) collective-permute-start(bf16[144,1024]{1,0:T(8,128)(2,1)S(1)} %fusion.1.refs_0_), channel_id=1, source_target_pairs={{0,1},{1,2},{2,3},{3,0},{4,5},{5,6},{6,7},{7,4},{8,9},{9,10},{10,1... | collective-permute-start | bytes 884744 | tf_op jit(solution)/shard_map/ppermute | solution.py:305
  5.4 14.8 %collective-permute-start.14 = (bf16[144,1024]{1,0:T(8,128)(2,1)S(1)}, bf16[144,1024]{1,0:T(8,128)(2,1)S(1)}, u32[]{:S(2)}, u32[]{:S(2)}) collective-permute-start(bf16[144,1024]{1,0:T(8,128)(2,1)S(1)} %fusion.1.refs_0_), channel_id=1, source_target_pairs={{0,3},{1,0},{2,1},{3,2},{4,7},{5,4},{6,5},{7,6},{8,11},{9,8},{10,9... | collective-permute-start | bytes 884744 | tf_op jit(solution)/shard_map/ppermute | solution.py:305
  7.5 25.9 %collective-permute-start.3 = (bf16[144,1024]{1,0:T(8,128)(2,1)S(1)}, bf16[144,1024]{1,0:T(8,128)(2,1)S(1)}, u32[]{:S(2)}, u32[]{:S(2)}) collective-permute-start(bf16[144,1024]{1,0:T(8,128)(2,1)S(1)} %fusion.1.refs_0_), channel_id=1, source_target_pairs={{0,2},{1,3},{2,0},{3,1},{4,6},{5,7},{6,4},{7,5},{8,10},{9,11},{10,... | collective-permute-start | bytes 884744 | tf_op jit(solution)/shard_map/ppermute | solution.py:305
  8.4 8.6 %collective-permute-start.7 = (bf16[144,1024]{1,0:T(8,128)(2,1)S(1)}, bf16[144,1024]{1,0:T(8,128)(2,1)S(1)}, u32[]{:S(2)}, u32[]{:S(2)}) collective-permute-start(bf16[144,1024]{1,0:T(8,128)(2,1)S(1)} %fusion.1.refs_0_), channel_id=1, source_target_pairs={{0,8},{4,12},{8,0},{12,4},{1,9},{5,13},{9,1},{13,5},{2,10},{6,14},... | collective-permute-start | bytes 884744 | tf_op jit(solution)/shard_map/ppermute | solution.py:302
  9.9 11.8 %collective-permute-start.8 = (bf16[144,1024]{1,0:T(8,128)(2,1)S(1)}, bf16[144,1024]{1,0:T(8,128)(2,1)S(1)}, u32[]{:S(2)}, u32[]{:S(2)}) collective-permute-start(bf16[144,1024]{1,0:T(8,128)(2,1)S(1)} %fusion.1.refs_0_), channel_id=1, source_target_pairs={{0,4},{4,0},{8,12},{12,8},{1,5},{5,1},{9,13},{13,9},{2,6},{6,2},{1... | collective-permute-start | bytes 884744 | tf_op jit(solution)/shard_map/ppermute | solution.py:302
  15.3 8.0 %collective-permute-start.11 = (bf16[144,1024]{1,0:T(8,128)(2,1)S(1)}, bf16[144,1024]{1,0:T(8,128)(2,1)S(1)}, u32[]{:S(2)}, u32[]{:S(2)}) collective-permute-start(bf16[144,1024]{1,0:T(8,128)(2,1)S(1)} %collective-permute-done.10.refs_0_), channel_id=1, source_target_pairs={{0,8},{4,12},{8,0},{12,4},{1,9},{5,13},{9,1},{13,5},{2,10},{6,14},... | collective-permute-start | bytes 884744 | tf_op jit(solution)/shard_map/ppermute | solution.py:302
  17.0 7.5 %collective-permute-start.9 = (bf16[144,1024]{1,0:T(8,128)(2,1)S(1)}, bf16[144,1024]{1,0:T(8,128)(2,1)S(1)}, u32[]{:S(2)}, u32[]{:S(2)}) collective-permute-start(bf16[144,1024]{1,0:T(8,128)(2,1)S(1)} %collective-permute-done.7.refs_1_), channel_id=1, source_target_pairs={{0,4},{4,0},{8,12},{12,8},{1,5},{5,1},{9,13},{13,9},{2,6},{6,2},{1... | collective-permute-start | bytes 884744 | tf_op jit(solution)/shard_map/ppermute | solution.py:302
  20.2 7.1 %collective-permute-start = (bf16[128,576]{1,0:T(8,128)(2,1)S(1)}, bf16[128,576]{1,0:T(8,128)(2,1)S(1)}, u32[]{:S(2)}, u32[]{:S(2)}) collective-permute-start(bf16[128,576]{1,0:T(8,128)(2,1)S(1)} %bitcast.37), channel_id=1, source_target_pairs={{0,8},{4,12},{8,0},{12,4},{1,9},{5,13},{9,1},{13,5},{2,10},{6,14},... | collective-permute-start | bytes 442376 | tf_op jit(solution)/shard_map/ppermute | solution.py:302
  21.7 11.7 %collective-permute-start.12 = (bf16[144,1024]{1,0:T(8,128)(2,1)S(1)}, bf16[144,1024]{1,0:T(8,128)(2,1)S(1)}, u32[]{:S(2)}, u32[]{:S(2)}) collective-permute-start(bf16[144,1024]{1,0:T(8,128)(2,1)S(1)} %collective-permute-done.10.refs_0_), channel_id=1, source_target_pairs={{0,4},{4,0},{8,12},{12,8},{1,5},{5,1},{9,13},{13,9},{2,6},{6,2},{1... | collective-permute-start | bytes 884744 | tf_op jit(solution)/shard_map/ppermute | solution.py:302
  23.3 10.6 %collective-permute-start.15 = (bf16[144,1024]{1,0:T(8,128)(2,1)S(1)}, bf16[144,1024]{1,0:T(8,128)(2,1)S(1)}, u32[]{:S(2)}, u32[]{:S(2)}) collective-permute-start(bf16[144,1024]{1,0:T(8,128)(2,1)S(1)} %collective-permute-done.14.refs_0_), channel_id=1, source_target_pairs={{0,8},{4,12},{8,0},{12,4},{1,9},{5,13},{9,1},{13,5},{2,10},{6,14},... | collective-permute-start | bytes 884744 | tf_op jit(solution)/shard_map/ppermute | solution.py:302
  24.6 10.8 %collective-permute-start.13 = (bf16[144,1024]{1,0:T(8,128)(2,1)S(1)}, bf16[144,1024]{1,0:T(8,128)(2,1)S(1)}, u32[]{:S(2)}, u32[]{:S(2)}) collective-permute-start(bf16[144,1024]{1,0:T(8,128)(2,1)S(1)} %collective-permute-done.11.refs_1_), channel_id=1, source_target_pairs={{0,4},{4,0},{8,12},{12,8},{1,5},{5,1},{9,13},{13,9},{2,6},{6,2},{1... | collective-permute-start | bytes 884744 | tf_op jit(solution)/shard_map/ppermute | solution.py:302
  27.3 67.9 %collective-permute-start.1 = (bf16[128,576]{1,0:T(8,128)(2,1)S(1)}, bf16[128,576]{1,0:T(8,128)(2,1)S(1)}, u32[]{:S(2)}, u32[]{:S(2)}) collective-permute-start(bf16[128,576]{1,0:T(8,128)(2,1)S(1)} %bitcast.38), channel_id=1, source_target_pairs={{0,4},{4,0},{8,12},{12,8},{1,5},{5,1},{9,13},{13,9},{2,6},{6,2},{1... | collective-permute-start | bytes 442376 | tf_op jit(solution)/shard_map/ppermute | solution.py:302
  33.4 62.2 %collective-permute-start.2 = (bf16[128,576]{1,0:T(8,128)(2,1)S(1)}, bf16[128,576]{1,0:T(8,128)(2,1)S(1)}, u32[]{:S(2)}, u32[]{:S(2)}) collective-permute-start(bf16[128,576]{1,0:T(8,128)(2,1)S(1)} %collective-permute-done.refs_1_), channel_id=1, source_target_pairs={{0,4},{4,0},{8,12},{12,8},{1,5},{5,1},{9,13},{13,9},{2,6},{6,2},{1... | collective-permute-start | bytes 442376 | tf_op jit(solution)/shard_map/ppermute | solution.py:302
  33.4 3.5 %collective-permute-start.16 = (bf16[144,1024]{1,0:T(8,128)(2,1)S(1)}, bf16[144,1024]{1,0:T(8,128)(2,1)S(1)}, u32[]{:S(2)}, u32[]{:S(2)}) collective-permute-start(bf16[144,1024]{1,0:T(8,128)(2,1)S(1)} %collective-permute-done.14.refs_0_), channel_id=1, source_target_pairs={{0,4},{4,0},{8,12},{12,8},{1,5},{5,1},{9,13},{13,9},{2,6},{6,2},{1... | collective-permute-start | bytes 884744 | tf_op jit(solution)/shard_map/ppermute | solution.py:302
  33.9 9.0 %collective-permute-start.4 = (bf16[144,1024]{1,0:T(8,128)(2,1)S(1)}, bf16[144,1024]{1,0:T(8,128)(2,1)S(1)}, u32[]{:S(2)}, u32[]{:S(2)}) collective-permute-start(bf16[144,1024]{1,0:T(8,128)(2,1)S(1)} %collective-permute-done.3.refs_0_), channel_id=1, source_target_pairs={{0,8},{4,12},{8,0},{12,4},{1,9},{5,13},{9,1},{13,5},{2,10},{6,14},... | collective-permute-start | bytes 884744 | tf_op jit(solution)/shard_map/ppermute | solution.py:302
  35.4 7.5 %collective-permute-start.17 = (bf16[144,1024]{1,0:T(8,128)(2,1)S(1)}, bf16[144,1024]{1,0:T(8,128)(2,1)S(1)}, u32[]{:S(2)}, u32[]{:S(2)}) collective-permute-start(bf16[144,1024]{1,0:T(8,128)(2,1)S(1)} %collective-permute-done.15.refs_1_), channel_id=1, source_target_pairs={{0,4},{4,0},{8,12},{12,8},{1,5},{5,1},{9,13},{13,9},{2,6},{6,2},{1... | collective-permute-start | bytes 884744 | tf_op jit(solution)/shard_map/ppermute | solution.py:302
  36.9 7.5 %collective-permute-start.5 = (bf16[144,1024]{1,0:T(8,128)(2,1)S(1)}, bf16[144,1024]{1,0:T(8,128)(2,1)S(1)}, u32[]{:S(2)}, u32[]{:S(2)}) collective-permute-start(bf16[144,1024]{1,0:T(8,128)(2,1)S(1)} %collective-permute-done.3.refs_0_), channel_id=1, source_target_pairs={{0,4},{4,0},{8,12},{12,8},{1,5},{5,1},{9,13},{13,9},{2,6},{6,2},{1... | collective-permute-start | bytes 884744 | tf_op jit(solution)/shard_map/ppermute | solution.py:302
  66.9 9.1 %collective-permute-start.19 = (bf16[1,128,1024]{2,1,0:T(8,128)(2,1)S(1)}, bf16[1,128,1024]{2,1,0:T(8,128)(2,1)S(1)}, u32[]{:S(2)}, u32[]{:S(2)}) collective-permute-start(bf16[1,128,1024]{2,1,0:T(8,128)(2,1)S(1)} %add_convert_fusion.7), channel_id=1, source_target_pairs={{0,8},{4,12},{8,0},{12,4},{1,9},{5,13},{9,1},{13,5},{2,10},{6,14},... | collective-permute-start | bytes 786440 | tf_op jit(solution)/shard_map/ppermute | solution.py:302
  68.5 13.2 %collective-permute-start.22 = (bf16[1,128,1024]{2,1,0:T(8,128)(2,1)S(1)}, bf16[1,128,1024]{2,1,0:T(8,128)(2,1)S(1)}, u32[]{:S(2)}, u32[]{:S(2)}) collective-permute-start(bf16[1,128,1024]{2,1,0:T(8,128)(2,1)S(1)} %add_convert_fusion.5), channel_id=1, source_target_pairs={{0,8},{4,12},{8,0},{12,4},{1,9},{5,13},{9,1},{13,5},{2,10},{6,14},... | collective-permute-start | bytes 786440 | tf_op jit(solution)/shard_map/ppermute | solution.py:302
  69.3 22.3 %collective-permute-start.25 = (bf16[1,128,1024]{2,1,0:T(8,128)(2,1)S(1)}, bf16[1,128,1024]{2,1,0:T(8,128)(2,1)S(1)}, u32[]{:S(2)}, u32[]{:S(2)}) collective-permute-start(bf16[1,128,1024]{2,1,0:T(8,128)(2,1)S(1)} %add_convert_fusion.3), channel_id=1, source_target_pairs={{0,8},{4,12},{8,0},{12,4},{1,9},{5,13},{9,1},{13,5},{2,10},{6,14},... | collective-permute-start | bytes 786440 | tf_op jit(solution)/shard_map/ppermute | solution.py:302
  76.1 26.3 %collective-permute-start.28 = (bf16[1,128,1024]{2,1,0:T(8,128)(2,1)S(1)}, bf16[1,128,1024]{2,1,0:T(8,128)(2,1)S(1)}, u32[]{:S(2)}, u32[]{:S(2)}) collective-permute-start(bf16[1,128,1024]{2,1,0:T(8,128)(2,1)S(1)} %add_convert_fusion.1), channel_id=1, source_target_pairs={{0,8},{4,12},{8,0},{12,4},{1,9},{5,13},{9,1},{13,5},{2,10},{6,14},... | collective-permute-start | bytes 786440 | tf_op jit(solution)/shard_map/ppermute | solution.py:302
  81.7 26.7 %collective-permute-start.20 = (bf16[1,128,1024]{2,1,0:T(8,128)(2,1)S(1)}, bf16[1,128,1024]{2,1,0:T(8,128)(2,1)S(1)}, u32[]{:S(2)}, u32[]{:S(2)}) collective-permute-start(bf16[1,128,1024]{2,1,0:T(8,128)(2,1)S(1)} %add_convert_fusion.6), channel_id=1, source_target_pairs={{0,2},{1,3},{2,0},{3,1},{4,6},{5,7},{6,4},{7,5},{8,10},{9,11},{10,... | collective-permute-start | bytes 786440 | tf_op jit(solution)/shard_map/ppermute | solution.py:305
  91.5 16.8 %collective-permute-start.23 = (bf16[1,128,1024]{2,1,0:T(8,128)(2,1)S(1)}, bf16[1,128,1024]{2,1,0:T(8,128)(2,1)S(1)}, u32[]{:S(2)}, u32[]{:S(2)}) collective-permute-start(bf16[1,128,1024]{2,1,0:T(8,128)(2,1)S(1)} %add_convert_fusion.4), channel_id=1, source_target_pairs={{0,1},{1,2},{2,3},{3,0},{4,5},{5,6},{6,7},{7,4},{8,9},{9,10},{10,1... | collective-permute-start | bytes 786440 | tf_op jit(solution)/shard_map/ppermute | solution.py:305
  95.2 17.5 %collective-permute-start.26 = (bf16[1,128,1024]{2,1,0:T(8,128)(2,1)S(1)}, bf16[1,128,1024]{2,1,0:T(8,128)(2,1)S(1)}, u32[]{:S(2)}, u32[]{:S(2)}) collective-permute-start(bf16[1,128,1024]{2,1,0:T(8,128)(2,1)S(1)} %add_convert_fusion.2), channel_id=1, source_target_pairs={{0,3},{1,0},{2,1},{3,2},{4,7},{5,4},{6,5},{7,6},{8,11},{9,8},{10,9... | collective-permute-start | bytes 786440 | tf_op jit(solution)/shard_map/ppermute | solution.py:305
  (8 other events, 42.9 us)

commit v4 on v3

--- a/solution.py
+++ b/solution.py
@@ -141,65 +141,76 @@
     )(base, rw, *parts, *extra)
 
 
+def sort_kernel(gu_ref, out_ref, wide):
+    group, _, hidden, width = out_ref.shape
+    chunks = width // LANES
+    for e in range(group):
+        wide[e] = gu_ref[e].astype(jnp.float32)
+        for z in range(2):
+            for c in range(chunks):
+                part = wide[e, pl.ds(2 * c + z, hidden, stride=2 * chunks), :]
+                out_ref[e, z, :, c * LANES : (c + 1) * LANES] = part.astype(jnp.bfloat16)
+
+
+def sort_rows(gate_up):
+    local, hidden, _, width = gate_up.shape
+    group = 2 if local % 2 == 0 else 1
+    chunks = width // LANES
+    gu = gate_up.reshape(local, hidden, 2, chunks, LANES).swapaxes(2, 3)
+    gu = gu.reshape(local, hidden * 2 * chunks, LANES)
+    return call(
+        sort_kernel,
+        8,
+        (local // group,),
+        [pl.BlockSpec((group,) + gu.shape[1:], lambda e: (e, 0, 0))],
+        pl.BlockSpec((group, 2, hidden, width), lambda e: (e, 0, 0, 0)),
+        jax.ShapeDtypeStruct((local, 2, hidden, width), jnp.bfloat16),
+        [pltpu.VMEM((group,) + gu.shape[1:], jnp.float32)],
+        "sort",
+    )(gu)
+
+
 def expert_kernel(n, *refs):
     rows, weights = refs[:n], refs[n : 2 * n]
     gu_ref, down_ref = refs[2 * n : 2 * n + 2]
-    outs, wide = refs[2 * n + 2 : 3 * n + 2], refs[3 * n + 2]
-    group, hidden, width = down_ref.shape
+    outs = refs[2 * n + 2 :]
+    group = down_ref.shape[0]
     size = rows[0].shape[1]
-    chunks = width // LANES
     for e in range(group):
-        wide[e] = gu_ref[e].astype(jnp.float32)
-        gu = jnp.concatenate(
-            [
-                jnp.concatenate(
-                    [
-                        wide[e, pl.ds(2 * c + z, hidden, stride=2 * chunks), :].astype(jnp.bfloat16)
-                        for c in range(chunks)
-                    ],
-                    axis=1,
-                )
-                for z in range(2)
-            ],
-            axis=0,
-        )
         held = jnp.concatenate([r[e] for r in rows], axis=0)
-        both = lax.dot_general(gu, held, NT, preferred_element_type=jnp.float32)
-        g, u = both[:hidden], both[hidden:]
+        g = lax.dot_general(held, gu_ref[e, 0], NT, preferred_element_type=jnp.float32)
+        u = lax.dot_general(held, gu_ref[e, 1], NT, preferred_element_type=jnp.float32)
         inner = (g * lax.logistic(g) * u).astype(jnp.bfloat16)
-        made = lax.dot_general(inner, down_ref[e], TN, preferred_element_type=jnp.float32)
+        made = jnp.dot(inner, down_ref[e], preferred_element_type=jnp.float32)
         for i in range(n):
             w = weights[i][e]
             part = made[i * size : (i + 1) * size]
-            for c in range(chunks):
+            for c in range(part.shape[1] // LANES):
                 at = slice(c * LANES, (c + 1) * LANES)
                 outs[i][e, :, at] = (part[:, at] * w).astype(jnp.bfloat16)
 
 
-def experts(rows, weights, gate_up, down):
+def experts(rows, weights, gu, down):
     n = len(rows)
     local, slots, width = rows[0].shape
     size = min(slots, EXPERT_ROWS)
     hidden = down.shape[1]
     group = 2 if local % 2 == 0 else 1
-    chunks = width // LANES
-    gu = gate_up.reshape(local, hidden, 2, chunks, LANES).swapaxes(2, 3)
-    gu = gu.reshape(local, hidden * 2 * chunks, LANES)
     rows_spec = pl.BlockSpec((group, size, width), lambda e, i: (e, i, 0))
     weight_spec = pl.BlockSpec((group, size, LANES), lambda e, i: (e, i, 0))
     return call(
         functools.partial(expert_kernel, n),
-        10,
+        6,
         (local // group, slots // size),
         [rows_spec] * n
         + [weight_spec] * n
         + [
-            pl.BlockSpec((group,) + gu.shape[1:], lambda e, i: (e, 0, 0)),
+            pl.BlockSpec((group, 2, hidden, width), lambda e, i: (e, 0, 0, 0)),
             pl.BlockSpec((group, hidden, width), lambda e, i: (e, 0, 0)),
         ],
         [rows_spec] * n,
         [jax.ShapeDtypeStruct(r.shape, jnp.bfloat16) for r in rows],
-        [pltpu.VMEM((group,) + gu.shape[1:], jnp.float32)],
+        [],
         "experts",
     )(*rows, *weights, gu, down)
 
@@ -347,18 +358,21 @@
         sent.append(out[:3])
         if row is not None:
             balance = out[3]
-    made = experts([s[0] for s in sent], [s[1] for s in sent], gate_up, w_down)
-
+
+    gu = sort_rows(gate_up)
+    groups = [[1, 0], [3, 2]] if len(shifts) == 4 else [range(len(shifts))]
     back = []
-    for i in reversed(range(len(shifts))):
-        keep, give = combine(sent[i][2], made[i], n_ctx)
-        got = flip(give, 1)
-        far = added(keep[:, tok_rows:], got[:, tok_rows:])
-        terms = [keep[:, :tok_rows], got[:, :tok_rows], flip(far, 2)]
-        if i:
-            back.append(shift(added(*terms), -shifts[i]))
-        else:
-            back = back + terms
+    for group in groups:
+        made = experts([sent[i][0] for i in group], [sent[i][1] for i in group], gu, w_down)
+        for i, part in zip(group, made):
+            keep, give = combine(sent[i][2], part, n_ctx)
+            got = flip(give, 1)
+            far = added(keep[:, tok_rows:], got[:, tok_rows:])
+            terms = [keep[:, :tok_rows], got[:, :tok_rows], flip(far, 2)]
+            if i:
+                back.append(shift(added(*terms), -shifts[i]))
+            else:
+                back = back + terms
     if near:
         expert_mix = added(*back)
     else:

time: 114 us -> 128 us (1.12); the launches traced: 114 us -> 126 us
  local copies, waits for them, and re-layouts: 2.02 us -> 13.9 us
  starting transfers between devices: 34.8 us -> 23.8 us
  Pallas kernels: 31.6 us -> 40.1 us
  waiting for transfers between devices: 38.5 us -> 43 us
  other arithmetic: 6.04 us -> 3.84 us
    ppermute x23, waiting for transfers between devices: 17.7 us -> 37 us  [flip(): return lax.ppermute(a, 'ctx', [(i, i ^ bit) for i in range(n_ctx)])]
    ppermute x6, waiting for transfers between devices: 20.8 us -> 6 us  [shift(): return lax.ppermute(a, 'exp', [(i, (i + d) % n_exp) for i in range(n_exp)])]
    unnamed x9 -> x27, local copies, waits for them, and re-layouts: 1.09 us -> 13 us
    pallas_call x1 -> x3, Pallas kernels: 17.5 us -> 26 us  [the longest x2 15.7 us: experts(): call(functools.partial(expert_kernel, n), 6, (local // group, slots // si...]
    ppermute x6, starting transfers between devices: 19.7 us -> 13.5 us  [shift(): return lax.ppermute(a, 'exp', [(i, (i + d) % n_exp) for i in range(n_exp)])]
    ppermute x23, starting transfers between devices: 15 us -> 10.3 us  [flip(): return lax.ppermute(a, 'ctx', [(i, i ^ bit) for i in range(n_ctx)])]
  transfers between devices with their start and end apart: 29 -> 29, of which waited for: 12 -> 10; matrix products, arithmetic and copies ran while one was open for 5% -> 2% of each run, Pallas kernels for 28% -> 32%
where the time goes in v4:
time: 128 us; the launch traced here: 126 us
  waiting for transfers between devices  43 us (34%)
  Pallas kernels  40.1 us (31%)
  starting transfers between devices  23.8 us (19%)
  local copies, waits for them, and re-layouts  13.9 us (11%)
  other arithmetic  3.84 us (3%)
    ppermute x23, waiting for transfers between devices, flip(): return lax.ppermute(a, 'ctx', [(i, i ^ bit) for i in range(n_ctx)])  37 us
    pallas_call x2, Pallas kernels, experts(): call(functools.partial(expert_kernel, n), 6, (local // group, slots // si...  15.7 us
    ppermute x6, starting transfers between devices, shift(): return lax.ppermute(a, 'exp', [(i, (i + d) % n_exp) for i in range(n_exp)])  13.5 us
    unnamed x27, local copies, waits for them, and re-layouts  13 us
    ppermute x23, starting transfers between devices, flip(): return lax.ppermute(a, 'ctx', [(i, i ^ bit) for i in range(n_ctx)])  10.3 us
    pallas_call x1, Pallas kernels, sort_rows(): call(sort_kernel, 8, (local // group,), [pl.BlockSpec((group,) + gu.shape...  10.3 us
    pallas_call x1, Pallas kernels, attend(): call(functools.partial(attend_kernel, n), 6, (HEADS // 2,), [whole(first)...  6.18 us
    pallas_call x4, Pallas kernels, dispatch(): call(functools.partial(dispatch_kernel, n_parts, n_parts if row is not No...  6.01 us
  transfers between devices with their start and end apart: 29, of which 10 were waited for; matrix products, arithmetic and copies ran while one was open for 2% of the time, Pallas kernels for 32%

profile of v4, /device:TPU:0, one launch (start us, length us, event | category | flops | bytes accessed | tf_op | source)
XLA Modules:
  0.0 125.6 jit_solution(12796650639583893012)
XLA Ops:
  2.3 5.1 %collective-permute-start.19 = (bf16[144,1024]{1,0:T(8,128)(2,1)S(1)}, bf16[144,1024]{1,0:T(8,128)(2,1)S(1)}, u32[]{:S(2)}, u32[]{:S(2)}) collective-permute-start(bf16[144,1024]{1,0:T(8,128)(2,1)S(1)} %fusion.1.refs_0_), channel_id=1, source_target_pairs={{0,3},{1,0},{2,1},{3,2},{4,7},{5,4},{6,5},{7,6},{8,11},{9,8},{10,9... | collective-permute-start | bytes 884744 | tf_op jit(solution)/shard_map/ppermute | solution.py:316
  7.4 1.5 %collective-permute-start.7 = (bf16[144,1024]{1,0:T(8,128)(2,1)S(1)}, bf16[144,1024]{1,0:T(8,128)(2,1)S(1)}, u32[]{:S(2)}, u32[]{:S(2)}) collective-permute-start(bf16[144,1024]{1,0:T(8,128)(2,1)S(1)} %fusion.1.refs_0_), channel_id=1, source_target_pairs={{0,8},{4,12},{8,0},{12,4},{1,9},{5,13},{9,1},{13,5},{2,10},{6,14},... | collective-permute-start | bytes 884744 | tf_op jit(solution)/shard_map/ppermute | solution.py:313
  10.1 4.3 %copy-done = bf16[16,176,2,1024]{3,2,1,0:T(2,128)(2,1)S(1)} copy-done((bf16[16,176,2,1024]{3,2,1,0:T(2,128)(2,1)S(1)}, bf16[16,176,2,1024]{3,2,1,0:T(2,128)(2,1)}, u32[]{:S(2)}) %copy-start) | copy-done | bytes 11534360
  14.4 10.3 %sort.1.refs_4_ = bf16[16,2,176,1024]{3,2,1,0:T(8,128)(2,1)S(1)} custom-call(bf16[16,2816,128]{2,1,0:T(8,128)(2,1)S(1)} %bitcast.42), custom_call_target="tpu_custom_call" | custom-call | flops 8800000000 | tf_op jit(solution)/shard_map/sort/pallas_call | solution.py:161
  24.7 4.2 %copy-done.2 = bf16[16,2,176,1024]{3,2,1,0:T(8,128)(2,1)} copy-done((bf16[16,2,176,1024]{3,2,1,0:T(8,128)(2,1)}, bf16[16,2,176,1024]{3,2,1,0:T(8,128)(2,1)S(1)}, u32[]{:S(2)}) %copy-start.2) | copy-done | bytes 11534360
  30.4 2.1 %collective-permute-done.15.refs_0_ = bf16[144,1024]{1,0:T(8,128)(2,1)S(1)} collective-permute-done((bf16[144,1024]{1,0:T(8,128)(2,1)S(1)}, bf16[144,1024]{1,0:T(8,128)(2,1)S(1)}, u32[]{:S(2)}, u32[]{:S(2)}) %collective-permute-start.15) | collective-permute-done | bytes 294944 | tf_op jit(solution)/shard_map/ppermute | solution.py:316
  32.5 1.5 %collective-permute-start = (bf16[128,576]{1,0:T(8,128)(2,1)S(1)}, bf16[128,576]{1,0:T(8,128)(2,1)S(1)}, u32[]{:S(2)}, u32[]{:S(2)}) collective-permute-start(bf16[128,576]{1,0:T(8,128)(2,1)S(1)} %bitcast.37), channel_id=1, source_target_pairs={{0,8},{4,12},{8,0},{12,4},{1,9},{5,13},{9,1},{13,5},{2,10},{6,14},... | collective-permute-start | bytes 442376 | tf_op jit(solution)/shard_map/ppermute | solution.py:313
  34.0 5.6 %collective-permute-done.20.refs_1_ = bf16[144,1024]{1,0:T(8,128)(2,1)S(1)} collective-permute-done((bf16[144,1024]{1,0:T(8,128)(2,1)S(1)}, bf16[144,1024]{1,0:T(8,128)(2,1)S(1)}, u32[]{:S(2)}, u32[]{:S(2)}) %collective-permute-start.20) | collective-permute-done | bytes 294944 | tf_op jit(solution)/shard_map/ppermute | solution.py:313
  40.2 1.6 %dispatch.5 = (bf16[16,64,1024]{2,1,0:T(8,128)(2,1)S(1)}, f32[16,64,128]{2,1,0:T(8,128)S(1)}, bf16[4,256,128]{2,1,0:T(8,128)(2,1)S(1)}, f32[8,128]{1,0:T(8,128)S(1)}) custom-call(s32[1]{0:T(128)} %bitcast.13.base_ref, bf16[64,1024]{1,0:T(8,128)(2,1)S(1)} %fusion.2.rw_ref, bf16[144,1024]{1,0:T(8,128)(2,1)S(1)} %fusion.1.refs_0_, ...), custom_call_target="tpu_custom_call" | custom-call | flops 3300000000 | tf_op jit(solution)/shard_map/dispatch/pallas_call | solution.py:132
  43.7 5.0 %collective-permute-done.16.refs_1_ = bf16[144,1024]{1,0:T(8,128)(2,1)S(1)} collective-permute-done((bf16[144,1024]{1,0:T(8,128)(2,1)S(1)}, bf16[144,1024]{1,0:T(8,128)(2,1)S(1)}, u32[]{:S(2)}, u32[]{:S(2)}) %collective-permute-start.16) | collective-permute-done | bytes 294944 | tf_op jit(solution)/shard_map/ppermute | solution.py:313
  49.3 1.5 %dispatch.7 = (bf16[16,64,1024]{2,1,0:T(8,128)(2,1)S(1)}, f32[16,64,128]{2,1,0:T(8,128)S(1)}, bf16[4,256,128]{2,1,0:T(8,128)(2,1)S(1)}) custom-call(s32[1]{0:T(128)} %bitcast.13.base_ref, bf16[64,1024]{1,0:T(8,128)(2,1)S(1)} %fusion.2.rw_ref, bf16[144,1024]{1,0:T(8,128)(2,1)S(1)} %collective-permute-done.19.refs_0_, ...), custom_call_target="tpu_custom_call" | custom-call | flops 3300000000 | tf_op jit(solution)/shard_map/dispatch/pallas_call | solution.py:132
  51.4 5.6 %collective-permute-done.4.refs_1_ = bf16[144,1024]{1,0:T(8,128)(2,1)S(1)} collective-permute-done((bf16[144,1024]{1,0:T(8,128)(2,1)S(1)}, bf16[144,1024]{1,0:T(8,128)(2,1)S(1)}, u32[]{:S(2)}, u32[]{:S(2)}) %collective-permute-start.4) | collective-permute-done | bytes 294944 | tf_op jit(solution)/shard_map/ppermute | solution.py:313
  57.0 1.5 %dispatch.6 = (bf16[16,64,1024]{2,1,0:T(8,128)(2,1)S(1)}, f32[16,64,128]{2,1,0:T(8,128)S(1)}, bf16[4,256,128]{2,1,0:T(8,128)(2,1)S(1)}) custom-call(s32[1]{0:T(128)} %bitcast.13.base_ref, bf16[64,1024]{1,0:T(8,128)(2,1)S(1)} %fusion.2.rw_ref, bf16[144,1024]{1,0:T(8,128)(2,1)S(1)} %collective-permute-done.15.refs_0_, ...), custom_call_target="tpu_custom_call" | custom-call | flops 3300000000 | tf_op jit(solution)/shard_map/dispatch/pallas_call | solution.py:132
  58.5 7.8 %experts.3 = (bf16[16,64,1024]{2,1,0:T(8,128)(2,1)S(1)}, bf16[16,64,1024]{2,1,0:T(8,128)(2,1)S(1)}) custom-call(bf16[16,64,1024]{2,1,0:T(8,128)(2,1)S(1)} %get-tuple-element.41.refs_0_, bf16[16,64,1024]{2,1,0:T(8,128)(2,1)S(1)} %get-tuple-element.42.refs_1_, f32[16,64,128]{2,1,0:T(8,128)S(1)} %get-tuple-element.43.refs_2_, ...), custom_call_target="tpu_custom_call" | custom-call | flops 6600000000 | tf_op jit(solution)/shard_map/experts/pallas_call | solution.py:201
  69.4 4.3 %copy-done.3 = bf16[16,2,176,1024]{3,2,1,0:T(8,128)(2,1)S(1)} copy-done((bf16[16,2,176,1024]{3,2,1,0:T(8,128)(2,1)S(1)}, bf16[16,2,176,1024]{3,2,1,0:T(8,128)(2,1)}, u32[]{:S(2)}) %copy-start.3) | copy-done | bytes 11534360
  73.7 7.9 %experts.2 = (bf16[16,64,1024]{2,1,0:T(8,128)(2,1)S(1)}, bf16[16,64,1024]{2,1,0:T(8,128)(2,1)S(1)}) custom-call(bf16[16,64,1024]{2,1,0:T(8,128)(2,1)S(1)} %get-tuple-element.29.refs_0_, bf16[16,64,1024]{2,1,0:T(8,128)(2,1)S(1)} %get-tuple-element.30.refs_1_, f32[16,64,128]{2,1,0:T(8,128)S(1)} %get-tuple-element.31.refs_2_, ...), custom_call_target="tpu_custom_call" | custom-call | flops 6600000000 | tf_op jit(solution)/shard_map/experts/pallas_call | solution.py:201
  86.5 6.0 %collective-permute-done.27 = bf16[1,128,1024]{2,1,0:T(8,128)(2,1)S(1)} collective-permute-done((bf16[1,128,1024]{2,1,0:T(8,128)(2,1)S(1)}, bf16[1,128,1024]{2,1,0:T(8,128)(2,1)S(1)}, u32[]{:S(2)}, u32[]{:S(2)}) %collective-permute-start.27) | collective-permute-done | bytes 262176 | tf_op jit(solution)/shard_map/ppermute | solution.py:313
  93.2 5.0 %collective-permute-done.24 = bf16[1,128,1024]{2,1,0:T(8,128)(2,1)S(1)} collective-permute-done((bf16[1,128,1024]{2,1,0:T(8,128)(2,1)S(1)}, bf16[1,128,1024]{2,1,0:T(8,128)(2,1)S(1)}, u32[]{:S(2)}, u32[]{:S(2)}) %collective-permute-start.24) | collective-permute-done | bytes 262176 | tf_op jit(solution)/shard_map/ppermute | solution.py:313
  98.1 2.5 %collective-permute-start.28 = (bf16[1,128,1024]{2,1,0:T(8,128)(2,1)S(1)}, bf16[1,128,1024]{2,1,0:T(8,128)(2,1)S(1)}, u32[]{:S(2)}, u32[]{:S(2)}) collective-permute-start(bf16[1,128,1024]{2,1,0:T(8,128)(2,1)S(1)} %add_convert_fusion.1), channel_id=1, source_target_pairs={{0,1},{1,2},{2,3},{3,0},{4,5},{5,6},{6,7},{7,4},{8,9},{9,10},{10,1... | collective-permute-start | bytes 786440 | tf_op jit(solution)/shard_map/ppermute | solution.py:316
  100.7 8.2 %collective-permute-done.11 = bf16[1,128,1024]{2,1,0:T(8,128)(2,1)S(1)} collective-permute-done((bf16[1,128,1024]{2,1,0:T(8,128)(2,1)S(1)}, bf16[1,128,1024]{2,1,0:T(8,128)(2,1)S(1)}, u32[]{:S(2)}, u32[]{:S(2)}) %collective-permute-start.11) | collective-permute-done | bytes 262176 | tf_op jit(solution)/shard_map/ppermute | solution.py:313
  108.9 2.5 %collective-permute-start.25 = (bf16[1,128,1024]{2,1,0:T(8,128)(2,1)S(1)}, bf16[1,128,1024]{2,1,0:T(8,128)(2,1)S(1)}, u32[]{:S(2)}, u32[]{:S(2)}) collective-permute-start(bf16[1,128,1024]{2,1,0:T(8,128)(2,1)S(1)} %add_convert_fusion.3), channel_id=1, source_target_pairs={{0,2},{1,3},{2,0},{3,1},{4,6},{5,7},{6,4},{7,5},{8,10},{9,11},{10,... | collective-permute-start | bytes 786440 | tf_op jit(solution)/shard_map/ppermute | solution.py:316
  111.6 2.4 %collective-permute-start.12 = (bf16[1,128,1024]{2,1,0:T(8,128)(2,1)S(1)}, bf16[1,128,1024]{2,1,0:T(8,128)(2,1)S(1)}, u32[]{:S(2)}, u32[]{:S(2)}) collective-permute-start(bf16[1,128,1024]{2,1,0:T(8,128)(2,1)S(1)} %add_convert_fusion.6), channel_id=1, source_target_pairs={{0,3},{1,0},{2,1},{3,2},{4,7},{5,4},{6,5},{7,6},{8,11},{9,8},{10,9... | collective-permute-start | bytes 786440 | tf_op jit(solution)/shard_map/ppermute | solution.py:316
  114.0 6.2 %attention.1 = bf16[128,4096]{1,0:T(8,128)(2,1)} custom-call(s32[128,1]{1,0:T(8,128)S(1)} %copy.20.first_ref, s32[128,1]{1,0:T(8,128)S(1)} %copy.21.last_ref, s32[1,512]{1,0:T(1,128)S(1)} %bitcast.40, bf16[128,4608]{1,0:T(8,128)(2,1)S(1)} %bitcast.45, bf16[128,576]{1,0:T(8,128)(2,1)S(1)} %bitcast.39, bf16[128,576]{1,0:T(8,128)(2,1)S(1)} %collective-permute-done.refs_1_, ...), custom_call_target="tpu_custom_call" | custom-call | flops 6600000000 | tf_op jit(solution)/shard_map/attention/pallas_call | solution.py:281
  120.8 3.9 %collective-permute-done.25 = bf16[1,128,1024]{2,1,0:T(8,128)(2,1)S(1)} collective-permute-done((bf16[1,128,1024]{2,1,0:T(8,128)(2,1)S(1)}, bf16[1,128,1024]{2,1,0:T(8,128)(2,1)S(1)}, u32[]{:S(2)}, u32[]{:S(2)}) %collective-permute-start.25) | collective-permute-done | bytes 262176 | tf_op jit(solution)/shard_map/ppermute | solution.py:316
  (97 shorter events, 18.3 us)
Async XLA Ops:
  2.3 27.4 %collective-permute-start.19 = (bf16[144,1024]{1,0:T(8,128)(2,1)S(1)}, bf16[144,1024]{1,0:T(8,128)(2,1)S(1)}, u32[]{:S(2)}, u32[]{:S(2)}) collective-permute-start(bf16[144,1024]{1,0:T(8,128)(2,1)S(1)} %fusion.1.refs_0_), channel_id=1, source_target_pairs={{0,3},{1,0},{2,1},{3,2},{4,7},{5,4},{6,5},{7,6},{8,11},{9,8},{10,9... | collective-permute-start | bytes 884744 | tf_op jit(solution)/shard_map/ppermute | solution.py:316
  7.4 25.1 %collective-permute-start.15 = (bf16[144,1024]{1,0:T(8,128)(2,1)S(1)}, bf16[144,1024]{1,0:T(8,128)(2,1)S(1)}, u32[]{:S(2)}, u32[]{:S(2)}) collective-permute-start(bf16[144,1024]{1,0:T(8,128)(2,1)S(1)} %fusion.1.refs_0_), channel_id=1, source_target_pairs={{0,2},{1,3},{2,0},{3,1},{4,6},{5,7},{6,4},{7,5},{8,10},{9,11},{10,... | collective-permute-start | bytes 884744 | tf_op jit(solution)/shard_map/ppermute | solution.py:316
  7.4 22.9 %collective-permute-start.7 = (bf16[144,1024]{1,0:T(8,128)(2,1)S(1)}, bf16[144,1024]{1,0:T(8,128)(2,1)S(1)}, u32[]{:S(2)}, u32[]{:S(2)}) collective-permute-start(bf16[144,1024]{1,0:T(8,128)(2,1)S(1)} %fusion.1.refs_0_), channel_id=1, source_target_pairs={{0,8},{4,12},{8,0},{12,4},{1,9},{5,13},{9,1},{13,5},{2,10},{6,14},... | collective-permute-start | bytes 884744 | tf_op jit(solution)/shard_map/ppermute | solution.py:313
  8.9 25.1 %collective-permute-start.8 = (bf16[144,1024]{1,0:T(8,128)(2,1)S(1)}, bf16[144,1024]{1,0:T(8,128)(2,1)S(1)}, u32[]{:S(2)}, u32[]{:S(2)}) collective-permute-start(bf16[144,1024]{1,0:T(8,128)(2,1)S(1)} %fusion.1.refs_0_), channel_id=1, source_target_pairs={{0,4},{4,0},{8,12},{12,8},{1,5},{5,1},{9,13},{13,9},{2,6},{6,2},{1... | collective-permute-start | bytes 884744 | tf_op jit(solution)/shard_map/ppermute | solution.py:313
  8.9 34.2 %collective-permute-start.3 = (bf16[144,1024]{1,0:T(8,128)(2,1)S(1)}, bf16[144,1024]{1,0:T(8,128)(2,1)S(1)}, u32[]{:S(2)}, u32[]{:S(2)}) collective-permute-start(bf16[144,1024]{1,0:T(8,128)(2,1)S(1)} %fusion.1.refs_0_), channel_id=1, source_target_pairs={{0,1},{1,2},{2,3},{3,0},{4,5},{5,6},{6,7},{7,4},{8,9},{9,10},{10,1... | collective-permute-start | bytes 884744 | tf_op jit(solution)/shard_map/ppermute | solution.py:316
  29.7 9.9 %collective-permute-start.20 = (bf16[144,1024]{1,0:T(8,128)(2,1)S(1)}, bf16[144,1024]{1,0:T(8,128)(2,1)S(1)}, u32[]{:S(2)}, u32[]{:S(2)}) collective-permute-start(bf16[144,1024]{1,0:T(8,128)(2,1)S(1)} %collective-permute-done.19.refs_0_), channel_id=1, source_target_pairs={{0,8},{4,12},{8,0},{12,4},{1,9},{5,13},{9,1},{13,5},{2,10},{6,14},... | collective-permute-start | bytes 884744 | tf_op jit(solution)/shard_map/ppermute | solution.py:313
  30.3 9.8 %collective-permute-start.9 = (bf16[144,1024]{1,0:T(8,128)(2,1)S(1)}, bf16[144,1024]{1,0:T(8,128)(2,1)S(1)}, u32[]{:S(2)}, u32[]{:S(2)}) collective-permute-start(bf16[144,1024]{1,0:T(8,128)(2,1)S(1)} %collective-permute-done.7.refs_1_), channel_id=1, source_target_pairs={{0,4},{4,0},{8,12},{12,8},{1,5},{5,1},{9,13},{13,9},{2,6},{6,2},{1... | collective-permute-start | bytes 884744 | tf_op jit(solution)/shard_map/ppermute | solution.py:313
  32.5 10.6 %collective-permute-start = (bf16[128,576]{1,0:T(8,128)(2,1)S(1)}, bf16[128,576]{1,0:T(8,128)(2,1)S(1)}, u32[]{:S(2)}, u32[]{:S(2)}) collective-permute-start(bf16[128,576]{1,0:T(8,128)(2,1)S(1)} %bitcast.37), channel_id=1, source_target_pairs={{0,8},{4,12},{8,0},{12,4},{1,9},{5,13},{9,1},{13,5},{2,10},{6,14},... | collective-permute-start | bytes 442376 | tf_op jit(solution)/shard_map/ppermute | solution.py:313
  34.0 9.6 %collective-permute-start.21 = (bf16[144,1024]{1,0:T(8,128)(2,1)S(1)}, bf16[144,1024]{1,0:T(8,128)(2,1)S(1)}, u32[]{:S(2)}, u32[]{:S(2)}) collective-permute-start(bf16[144,1024]{1,0:T(8,128)(2,1)S(1)} %collective-permute-done.19.refs_0_), channel_id=1, source_target_pairs={{0,4},{4,0},{8,12},{12,8},{1,5},{5,1},{9,13},{13,9},{2,6},{6,2},{1... | collective-permute-start | bytes 884744 | tf_op jit(solution)/shard_map/ppermute | solution.py:313
  39.6 9.1 %collective-permute-start.16 = (bf16[144,1024]{1,0:T(8,128)(2,1)S(1)}, bf16[144,1024]{1,0:T(8,128)(2,1)S(1)}, u32[]{:S(2)}, u32[]{:S(2)}) collective-permute-start(bf16[144,1024]{1,0:T(8,128)(2,1)S(1)} %collective-permute-done.15.refs_0_), channel_id=1, source_target_pairs={{0,8},{4,12},{8,0},{12,4},{1,9},{5,13},{9,1},{13,5},{2,10},{6,14},... | collective-permute-start | bytes 884744 | tf_op jit(solution)/shard_map/ppermute | solution.py:313
  40.2 9.1 %collective-permute-start.22 = (bf16[144,1024]{1,0:T(8,128)(2,1)S(1)}, bf16[144,1024]{1,0:T(8,128)(2,1)S(1)}, u32[]{:S(2)}, u32[]{:S(2)}) collective-permute-start(bf16[144,1024]{1,0:T(8,128)(2,1)S(1)} %collective-permute-done.20.refs_1_), channel_id=1, source_target_pairs={{0,4},{4,0},{8,12},{12,8},{1,5},{5,1},{9,13},{13,9},{2,6},{6,2},{1... | collective-permute-start | bytes 884744 | tf_op jit(solution)/shard_map/ppermute | solution.py:313
  43.1 68.4 %collective-permute-start.1 = (bf16[128,576]{1,0:T(8,128)(2,1)S(1)}, bf16[128,576]{1,0:T(8,128)(2,1)S(1)}, u32[]{:S(2)}, u32[]{:S(2)}) collective-permute-start(bf16[128,576]{1,0:T(8,128)(2,1)S(1)} %bitcast.38), channel_id=1, source_target_pairs={{0,4},{4,0},{8,12},{12,8},{1,5},{5,1},{9,13},{13,9},{2,6},{6,2},{1... | collective-permute-start | bytes 442376 | tf_op jit(solution)/shard_map/ppermute | solution.py:313
  43.1 70.8 %collective-permute-start.2 = (bf16[128,576]{1,0:T(8,128)(2,1)S(1)}, bf16[128,576]{1,0:T(8,128)(2,1)S(1)}, u32[]{:S(2)}, u32[]{:S(2)}) collective-permute-start(bf16[128,576]{1,0:T(8,128)(2,1)S(1)} %collective-permute-done.refs_1_), channel_id=1, source_target_pairs={{0,4},{4,0},{8,12},{12,8},{1,5},{5,1},{9,13},{13,9},{2,6},{6,2},{1... | collective-permute-start | bytes 442376 | tf_op jit(solution)/shard_map/ppermute | solution.py:313
  50.8 17.0 %collective-permute-start.5 = (bf16[144,1024]{1,0:T(8,128)(2,1)S(1)}, bf16[144,1024]{1,0:T(8,128)(2,1)S(1)}, u32[]{:S(2)}, u32[]{:S(2)}) collective-permute-start(bf16[144,1024]{1,0:T(8,128)(2,1)S(1)} %collective-permute-done.3.refs_0_), channel_id=1, source_target_pairs={{0,4},{4,0},{8,12},{12,8},{1,5},{5,1},{9,13},{13,9},{2,6},{6,2},{1... | collective-permute-start | bytes 884744 | tf_op jit(solution)/shard_map/ppermute | solution.py:313
  57.0 11.0 %collective-permute-start.6 = (bf16[144,1024]{1,0:T(8,128)(2,1)S(1)}, bf16[144,1024]{1,0:T(8,128)(2,1)S(1)}, u32[]{:S(2)}, u32[]{:S(2)}) collective-permute-start(bf16[144,1024]{1,0:T(8,128)(2,1)S(1)} %collective-permute-done.4.refs_1_), channel_id=1, source_target_pairs={{0,4},{4,0},{8,12},{12,8},{1,5},{5,1},{9,13},{13,9},{2,6},{6,2},{1... | collective-permute-start | bytes 884744 | tf_op jit(solution)/shard_map/ppermute | solution.py:313
  66.8 16.3 %collective-permute-start.26 = (bf16[1,256,1024]{2,1,0:T(8,128)(2,1)S(1)}, bf16[1,256,1024]{2,1,0:T(8,128)(2,1)S(1)}, u32[]{:S(2)}, u32[]{:S(2)}) collective-permute-start(bf16[1,256,1024]{2,1,0:T(8,128)(2,1)S(1)} %get-tuple-element.51), channel_id=1, source_target_pairs={{0,4},{4,0},{8,12},{12,8},{1,5},{5,1},{9,13},{13,9},{2,6},{6,2},{1... | collective-permute-start | bytes 1572872 | tf_op jit(solution)/shard_map/ppermute | solution.py:313
  67.9 15.4 %collective-permute-start.23 = (bf16[1,256,1024]{2,1,0:T(8,128)(2,1)S(1)}, bf16[1,256,1024]{2,1,0:T(8,128)(2,1)S(1)}, u32[]{:S(2)}, u32[]{:S(2)}) collective-permute-start(bf16[1,256,1024]{2,1,0:T(8,128)(2,1)S(1)} %get-tuple-element.47), channel_id=1, source_target_pairs={{0,4},{4,0},{8,12},{12,8},{1,5},{5,1},{9,13},{13,9},{2,6},{6,2},{1... | collective-permute-start | bytes 1572872 | tf_op jit(solution)/shard_map/ppermute | solution.py:313
  83.3 9.2 %collective-permute-start.27 = (bf16[1,128,1024]{2,1,0:T(8,128)(2,1)S(1)}, bf16[1,128,1024]{2,1,0:T(8,128)(2,1)S(1)}, u32[]{:S(2)}, u32[]{:S(2)}) collective-permute-start(bf16[1,128,1024]{2,1,0:T(8,128)(2,1)S(1)} %add_convert_fusion.2), channel_id=1, source_target_pairs={{0,8},{4,12},{8,0},{12,4},{1,9},{5,13},{9,1},{13,5},{2,10},{6,14},... | collective-permute-start | bytes 786440 | tf_op jit(solution)/shard_map/ppermute | solution.py:313
  84.2 13.9 %collective-permute-start.24 = (bf16[1,128,1024]{2,1,0:T(8,128)(2,1)S(1)}, bf16[1,128,1024]{2,1,0:T(8,128)(2,1)S(1)}, u32[]{:S(2)}, u32[]{:S(2)}) collective-permute-start(bf16[1,128,1024]{2,1,0:T(8,128)(2,1)S(1)} %add_convert_fusion.4), channel_id=1, source_target_pairs={{0,8},{4,12},{8,0},{12,4},{1,9},{5,13},{9,1},{13,5},{2,10},{6,14},... | collective-permute-start | bytes 786440 | tf_op jit(solution)/shard_map/ppermute | solution.py:313
  85.7 35.1 %collective-permute-start.14 = (bf16[1,128,1024]{2,1,0:T(8,128)(2,1)S(1)}, bf16[1,128,1024]{2,1,0:T(8,128)(2,1)S(1)}, u32[]{:S(2)}, u32[]{:S(2)}) collective-permute-start(bf16[1,128,1024]{2,1,0:T(8,128)(2,1)S(1)} %add_convert_fusion.5), channel_id=1, source_target_pairs={{0,8},{4,12},{8,0},{12,4},{1,9},{5,13},{9,1},{13,5},{2,10},{6,14},... | collective-permute-start | bytes 786440 | tf_op jit(solution)/shard_map/ppermute | solution.py:313
  92.5 16.4 %collective-permute-start.11 = (bf16[1,128,1024]{2,1,0:T(8,128)(2,1)S(1)}, bf16[1,128,1024]{2,1,0:T(8,128)(2,1)S(1)}, u32[]{:S(2)}, u32[]{:S(2)}) collective-permute-start(bf16[1,128,1024]{2,1,0:T(8,128)(2,1)S(1)} %add_convert_fusion.7), channel_id=1, source_target_pairs={{0,8},{4,12},{8,0},{12,4},{1,9},{5,13},{9,1},{13,5},{2,10},{6,14},... | collective-permute-start | bytes 786440 | tf_op jit(solution)/shard_map/ppermute | solution.py:313
  98.1 22.7 %collective-permute-start.28 = (bf16[1,128,1024]{2,1,0:T(8,128)(2,1)S(1)}, bf16[1,128,1024]{2,1,0:T(8,128)(2,1)S(1)}, u32[]{:S(2)}, u32[]{:S(2)}) collective-permute-start(bf16[1,128,1024]{2,1,0:T(8,128)(2,1)S(1)} %add_convert_fusion.1), channel_id=1, source_target_pairs={{0,1},{1,2},{2,3},{3,0},{4,5},{5,6},{6,7},{7,4},{8,9},{9,10},{10,1... | collective-permute-start | bytes 786440 | tf_op jit(solution)/shard_map/ppermute | solution.py:316
  108.9 15.7 %collective-permute-start.25 = (bf16[1,128,1024]{2,1,0:T(8,128)(2,1)S(1)}, bf16[1,128,1024]{2,1,0:T(8,128)(2,1)S(1)}, u32[]{:S(2)}, u32[]{:S(2)}) collective-permute-start(bf16[1,128,1024]{2,1,0:T(8,128)(2,1)S(1)} %add_convert_fusion.3), channel_id=1, source_target_pairs={{0,2},{1,3},{2,0},{3,1},{4,6},{5,7},{6,4},{7,5},{8,10},{9,11},{10,... | collective-permute-start | bytes 786440 | tf_op jit(solution)/shard_map/ppermute | solution.py:316
  111.6 13.1 %collective-permute-start.12 = (bf16[1,128,1024]{2,1,0:T(8,128)(2,1)S(1)}, bf16[1,128,1024]{2,1,0:T(8,128)(2,1)S(1)}, u32[]{:S(2)}, u32[]{:S(2)}) collective-permute-start(bf16[1,128,1024]{2,1,0:T(8,128)(2,1)S(1)} %add_convert_fusion.6), channel_id=1, source_target_pairs={{0,3},{1,0},{2,1},{3,2},{4,7},{5,4},{6,5},{7,6},{8,11},{9,8},{10,9... | collective-permute-start | bytes 786440 | tf_op jit(solution)/shard_map/ppermute | solution.py:316
  (17 other events, 173.2 us)

commit v5 on v4

--- a/solution.py
+++ b/solution.py
@@ -16,7 +16,9 @@
 LANES = 128
 EXPERT_ROWS = 256
 EXTRA = 16
-VMEM = 20 * 2**20
+VMEM = 14 * 2**20
+VMEM_EXPERTS = 40 * 2**20
+VMEM_SORT = 56 * 2**20
 PEAK = 1.1e9
 
 qk_scale = 192.0 ** (-0.5)
@@ -24,7 +26,7 @@
 TN = (((0,), (0,)), ((), ()))
 
 
-def call(kernel, micros, grid, in_specs, out_specs, out_shape, scratch, name):
+def call(kernel, micros, grid, in_specs, out_specs, out_shape, scratch, name, limit=VMEM):
     return pl.pallas_call(
         kernel,
         grid=grid,
@@ -33,7 +35,7 @@
         out_shape=out_shape,
         scratch_shapes=scratch,
         compiler_params=pltpu.CompilerParams(
-            dimension_semantics=("arbitrary",) * len(grid), vmem_limit_bytes=VMEM
+            dimension_semantics=("arbitrary",) * len(grid), vmem_limit_bytes=limit
         ),
         cost_estimate=pl.CostEstimate(
             flops=int(micros * PEAK), bytes_accessed=0, transcendentals=0
@@ -42,8 +44,8 @@
     )
 
 
-def dispatch_kernel(n_parts, n_row, top, base_ref, rw_ref, *refs):
-    parts, refs = refs[:n_parts], refs[n_parts:]
+def dispatch_kernel(n_parts, n_row, top, n_after, base_ref, rw_ref, *refs):
+    parts, refs = refs[:n_parts], refs[n_parts + n_after :]
     if n_row:
         seg_ref, scale_ref = refs[:2]
         refs = refs[2:]
@@ -101,11 +103,15 @@
             )
 
 
+IN_HBM = pl.BlockSpec(memory_space=pltpu.HBM)
+ANYWHERE = pl.BlockSpec(memory_space=pl.ANY)
+
+
 def whole(a):
     return pl.BlockSpec(a.shape, lambda *i: (0,) * a.ndim)
 
 
-def dispatch(parts, top, base, rw, local, row=None):
+def dispatch(parts, top, base, rw, local, row=None, after=()):
     n_parts = len(parts)
     n, width = parts[0].shape[0] // (BLOCK + EXTRA), parts[0].shape[1]
     slots = n_parts * CAP
@@ -113,6 +119,7 @@
         pl.BlockSpec(memory_space=pltpu.SMEM),
         whole(rw),
     ] + [pl.BlockSpec((BLOCK + EXTRA, width), lambda i: (i, 0))] * n_parts
+    in_specs += [ANYWHERE] * len(after)
     out_specs = [
         pl.BlockSpec((local, slots, width), lambda i: (0, i, 0)),
         pl.BlockSpec((local, slots, LANES), lambda i: (0, i, 0)),
@@ -130,7 +137,7 @@
         out_specs.append(pl.BlockSpec((NDOC, LANES), lambda i: (0, 0)))
         out_shape.append(jax.ShapeDtypeStruct((NDOC, LANES), jnp.float32))
     return call(
-        functools.partial(dispatch_kernel, n_parts, n_parts if row is not None else 0, top),
+        functools.partial(dispatch_kernel, n_parts, n_parts if row is not None else 0, top, len(after)),
         3 * n,
         (n,),
         in_specs,
@@ -138,18 +145,70 @@
         out_shape,
         [],
         "dispatch",
-    )(base, rw, *parts, *extra)
-
-
-def sort_kernel(gu_ref, out_ref, wide):
-    group, _, hidden, width = out_ref.shape
+    )(base, rw, *parts, *after, *extra)
+
+
+def fetch(sources, slots, sem, step, steps, first):
+    group = slots[0].shape[1]
+
+    def copies(at):
+        slot = lax.rem(at, 2)
+        return [
+            pltpu.make_async_copy(
+                source.at[pl.ds(at * group, group)], held.at[slot], sem.at[i, slot]
+            )
+            for i, (source, held) in enumerate(zip(sources, slots))
+        ]
+
+    @pl.when(first & (step == 0))
+    def _():
+        for copy in copies(step):
+            copy.start()
+
+    @pl.when(first & (step + 1 < steps))
+    def _():
+        for copy in copies(step + 1):
+            copy.start()
+
+    @pl.when(first)
+    def _():
+        for copy in copies(step):
+            copy.wait()
+
+    return lax.rem(step, 2)
+
+
+def sort_kernel(gu_ref, out_ref, held, made, wide, in_sem, out_sem):
+    step, steps = pl.program_id(0), pl.num_programs(0)
+    _, group, _, hidden, width = made.shape
     chunks = width // LANES
+    slot = fetch([gu_ref], [held], in_sem, step, steps, step >= 0)
+
+    def leave(at):
+        to = lax.rem(at, 2)
+        return pltpu.make_async_copy(
+            made.at[to], out_ref.at[pl.ds(at * group, group)], out_sem.at[to]
+        )
+
+    @pl.when(step >= 2)
+    def _():
+        leave(step - 2).wait()
+
     for e in range(group):
-        wide[e] = gu_ref[e].astype(jnp.float32)
+        wide[e] = held[slot, e].astype(jnp.float32)
         for z in range(2):
             for c in range(chunks):
                 part = wide[e, pl.ds(2 * c + z, hidden, stride=2 * chunks), :]
-                out_ref[e, z, :, c * LANES : (c + 1) * LANES] = part.astype(jnp.bfloat16)
+                made[slot, e, z, :, c * LANES : (c + 1) * LANES] = part.astype(jnp.bfloat16)
+    leave(step).start()
+
+    @pl.when(step == steps - 1)
+    def _():
+        @pl.when(step >= 1)
+        def _():
+            leave(step - 1).wait()
+
+        leave(step).wait()
 
 
 def sort_rows(gate_up):
@@ -162,26 +221,41 @@
         sort_kernel,
         8,
         (local // group,),
-        [pl.BlockSpec((group,) + gu.shape[1:], lambda e: (e, 0, 0))],
-        pl.BlockSpec((group, 2, hidden, width), lambda e: (e, 0, 0, 0)),
+        [IN_HBM],
+        IN_HBM,
         jax.ShapeDtypeStruct((local, 2, hidden, width), jnp.bfloat16),
-        [pltpu.VMEM((group,) + gu.shape[1:], jnp.float32)],
+        [
+            pltpu.VMEM((2, group) + gu.shape[1:], jnp.bfloat16),
+            pltpu.VMEM((2, group, 2, hidden, width), jnp.bfloat16),
+            pltpu.VMEM((group,) + gu.shape[1:], jnp.float32),
+            pltpu.SemaphoreType.DMA((1, 2)),
+            pltpu.SemaphoreType.DMA((2,)),
+        ],
         "sort",
+        VMEM_SORT,
     )(gu)
 
 
 def expert_kernel(n, *refs):
     rows, weights = refs[:n], refs[n : 2 * n]
     gu_ref, down_ref = refs[2 * n : 2 * n + 2]
-    outs = refs[2 * n + 2 :]
-    group = down_ref.shape[0]
+    outs, (gu, down, sem) = refs[-3 - n : -3], refs[-3:]
+    group = gu.shape[1]
     size = rows[0].shape[1]
+    slot = fetch(
+        [gu_ref, down_ref],
+        [gu, down],
+        sem,
+        pl.program_id(0),
+        pl.num_programs(0),
+        pl.program_id(1) == 0,
+    )
     for e in range(group):
         held = jnp.concatenate([r[e] for r in rows], axis=0)
-        g = lax.dot_general(held, gu_ref[e, 0], NT, preferred_element_type=jnp.float32)
-        u = lax.dot_general(held, gu_ref[e, 1], NT, preferred_element_type=jnp.float32)
+        g = lax.dot_general(held, gu[slot, e, 0], NT, preferred_element_type=jnp.float32)
+        u = lax.dot_general(held, gu[slot, e, 1], NT, preferred_element_type=jnp.float32)
         inner = (g * lax.logistic(g) * u).astype(jnp.bfloat16)
-        made = jnp.dot(inner, down_ref[e], preferred_element_type=jnp.float32)
+        made = jnp.dot(inner, down[slot, e], preferred_element_type=jnp.float32)
         for i in range(n):
             w = weights[i][e]
             part = made[i * size : (i + 1) * size]
@@ -190,7 +264,7 @@
                 outs[i][e, :, at] = (part[:, at] * w).astype(jnp.bfloat16)
 
 
-def experts(rows, weights, gu, down):
+def experts(rows, weights, gu, down, after=()):
     n = len(rows)
     local, slots, width = rows[0].shape
     size = min(slots, EXPERT_ROWS)
@@ -202,17 +276,17 @@
         functools.partial(expert_kernel, n),
         6,
         (local // group, slots // size),
-        [rows_spec] * n
-        + [weight_spec] * n
-        + [
-            pl.BlockSpec((group, 2, hidden, width), lambda e, i: (e, 0, 0, 0)),
-            pl.BlockSpec((group, hidden, width), lambda e, i: (e, 0, 0)),
-        ],
+        [rows_spec] * n + [weight_spec] * n + [IN_HBM, IN_HBM] + [ANYWHERE] * len(after),
         [rows_spec] * n,
         [jax.ShapeDtypeStruct(r.shape, jnp.bfloat16) for r in rows],
-        [],
+        [
+            pltpu.VMEM((2, group, 2, hidden, width), jnp.bfloat16),
+            pltpu.VMEM((2, group, hidden, width), jnp.bfloat16),
+            pltpu.SemaphoreType.DMA((2, 2)),
+        ],
         "experts",
-    )(*rows, *weights, gu, down)
+        VMEM_EXPERTS,
+    )(*rows, *weights, gu, down, *after)
 
 
 def combine_kernel(groups, picks_ref, made_ref, *outs):
@@ -351,23 +425,28 @@
     base = (exp * local).reshape(1).astype(jnp.int32)
     rw = jnp.roll(router_weight.T, -exp * local, axis=0)
     balance = None
-    sent = []
-    for i, held in enumerate(spread):
-        row = (seg.reshape(-1, 1, BLOCK), scale) if near and i == 0 else None
-        out = dispatch(held, top, base, rw, local, row)
-        sent.append(out[:3])
-        if row is not None:
-            balance = out[3]
-
     gu = sort_rows(gate_up)
-    groups = [[1, 0], [3, 2]] if len(shifts) == 4 else [range(len(shifts))]
-    back = []
-    for group in groups:
-        made = experts([sent[i][0] for i in group], [sent[i][1] for i in group], gu, w_down)
-        for i, part in zip(group, made):
-            keep, give = combine(sent[i][2], part, n_ctx)
+    groups = [[1, 2], [3, 0]] if len(shifts) == 4 else [range(len(shifts))]
+    back, before, begun = [], (), []
+    for n, group in enumerate(groups):
+        sent = []
+        for i in group:
+            row = (seg.reshape(-1, 1, BLOCK), scale) if near and i == 0 else None
+            out = dispatch(spread[i], top, base, rw, local, row, before if i else ())
+            sent.append(out[:3])
+            if row is not None:
+                balance = out[3]
+        if n + 1 < len(groups):
+            after = (near_parts[groups[n + 1][0]],)
+        else:
+            after = begun
+        made = experts([a[0] for a in sent], [a[1] for a in sent], gu, w_down, after)
+        before, begun = (made[0],), []
+        for i, dispatched, part in zip(group, sent, made):
+            keep, give = combine(dispatched[2], part, n_ctx)
             got = flip(give, 1)
             far = added(keep[:, tok_rows:], got[:, tok_rows:])
+            begun.append(far)
             terms = [keep[:, :tok_rows], got[:, :tok_rows], flip(far, 2)]
             if i:
                 back.append(shift(added(*terms), -shifts[i]))

time: 128 us -> 111 us (0.87); the launches traced: 126 us -> 110 us
  waiting for transfers between devices: 43 us -> 20.7 us
  Pallas kernels: 40.1 us -> 52.1 us
  local copies, waits for them, and re-layouts: 13.9 us -> 4.1 us
  other arithmetic: 3.84 us -> 6.68 us
  starting transfers between devices: 23.8 us -> 25.5 us
    ppermute x23, waiting for transfers between devices: 37 us -> 16.4 us  [flip(): return lax.ppermute(a, 'ctx', [(i, i ^ bit) for i in range(n_ctx)])]
    unnamed x27 -> x23, local copies, waits for them, and re-layouts: 13 us -> 3.17 us
    pallas_call x2, Pallas kernels: 15.7 us -> 23.1 us  [experts(): call(functools.partial(expert_kernel, n), 6, (local // group, slots // si...]
    pallas_call x1, Pallas kernels: 10.3 us -> 15 us  [sort_rows(): call(sort_kernel, 8, (local // group,), [IN_HBM], IN_HBM, jax.ShapeDtypeS...]
    ppermute x23, starting transfers between devices: 10.3 us -> 13.3 us  [flip(): return lax.ppermute(a, 'ctx', [(i, i ^ bit) for i in range(n_ctx)])]
    convert_element_type x8, other arithmetic: 1.59 us -> 4.44 us  [added(): return total.astype(jnp.bfloat16)]
    ppermute x6, waiting for transfers between devices: 6 us -> 4.23 us  [shift(): return lax.ppermute(a, 'exp', [(i, (i + d) % n_exp) for i in range(n_exp)])]
    ppermute x6, starting transfers between devices: 13.5 us -> 12.2 us  [shift(): return lax.ppermute(a, 'exp', [(i, (i + d) % n_exp) for i in range(n_exp)])]
  transfers between devices with their start and end apart: 29 -> 29, of which waited for: 10 -> 5; matrix products, arithmetic and copies ran while one was open for 2% -> 5% of each run, Pallas kernels for 32% -> 47%
where the time goes in v5:
time: 111 us; the launch traced here: 110 us
  Pallas kernels  52.1 us (47%)
  starting transfers between devices  25.5 us (23%)
  waiting for transfers between devices  20.7 us (19%)
  other arithmetic  6.68 us (6%)
  local copies, waits for them, and re-layouts  4.1 us (4%)
    pallas_call x2, Pallas kernels, experts(): call(functools.partial(expert_kernel, n), 6, (local // group, slots // si...  23.1 us
    ppermute x23, waiting for transfers between devices, flip(): return lax.ppermute(a, 'ctx', [(i, i ^ bit) for i in range(n_ctx)])  16.4 us
    pallas_call x1, Pallas kernels, sort_rows(): call(sort_kernel, 8, (local // group,), [IN_HBM], IN_HBM, jax.ShapeDtypeS...  15 us
    ppermute x23, starting transfers between devices, flip(): return lax.ppermute(a, 'ctx', [(i, i ^ bit) for i in range(n_ctx)])  13.3 us
    ppermute x6, starting transfers between devices, shift(): return lax.ppermute(a, 'exp', [(i, (i + d) % n_exp) for i in range(n_exp)])  12.2 us
    pallas_call x1, Pallas kernels, attend(): call(functools.partial(attend_kernel, n), 6, (HEADS // 2,), [whole(first)...  6.18 us
    pallas_call x4, Pallas kernels, dispatch(): call(functools.partial(dispatch_kernel, n_parts, n_parts if row is not No...  5.99 us
    convert_element_type x8, other arithmetic, added(): return total.astype(jnp.bfloat16)  4.44 us
  transfers between devices with their start and end apart: 29, of which 5 were waited for; matrix products, arithmetic and copies ran while one was open for 5% of the time, Pallas kernels for 47%

profile of v5, /device:TPU:0, one launch (start us, length us, event | category | flops | bytes accessed | tf_op | source)
XLA Modules:
  0.0 110.0 jit_solution(7496328344938549041)
XLA Ops:
  2.3 3.1 %collective-permute-start.3 = (bf16[144,1024]{1,0:T(8,128)(2,1)S(1)}, bf16[144,1024]{1,0:T(8,128)(2,1)S(1)}, u32[]{:S(2)}, u32[]{:S(2)}) collective-permute-start(bf16[144,1024]{1,0:T(8,128)(2,1)S(1)} %fusion.1.refs_0_), channel_id=1, source_target_pairs={{0,1},{1,2},{2,3},{3,0},{4,5},{5,6},{6,7},{7,4},{8,9},{9,10},{10,1... | collective-permute-start | bytes 884744 | tf_op jit(solution)/shard_map/ppermute | solution.py:390
  5.4 2.1 %collective-permute-start.7 = (bf16[144,1024]{1,0:T(8,128)(2,1)S(1)}, bf16[144,1024]{1,0:T(8,128)(2,1)S(1)}, u32[]{:S(2)}, u32[]{:S(2)}) collective-permute-start(bf16[144,1024]{1,0:T(8,128)(2,1)S(1)} %fusion.1.refs_0_), channel_id=1, source_target_pairs={{0,3},{1,0},{2,1},{3,2},{4,7},{5,4},{6,5},{7,6},{8,11},{9,8},{10,9... | collective-permute-start | bytes 884744 | tf_op jit(solution)/shard_map/ppermute | solution.py:390
  8.4 1.5 %collective-permute-start.21 = (bf16[144,1024]{1,0:T(8,128)(2,1)S(1)}, bf16[144,1024]{1,0:T(8,128)(2,1)S(1)}, u32[]{:S(2)}, u32[]{:S(2)}) collective-permute-start(bf16[144,1024]{1,0:T(8,128)(2,1)S(1)} %fusion.1.refs_0_), channel_id=1, source_target_pairs={{0,8},{4,12},{8,0},{12,4},{1,9},{5,13},{9,1},{13,5},{2,10},{6,14},... | collective-permute-start | bytes 884744 | tf_op jit(solution)/shard_map/ppermute | solution.py:387
  9.9 15.0 %sort.1.refs_4_ = bf16[16,2,176,1024]{3,2,1,0:T(8,128)(2,1)} custom-call(bf16[16,2816,128]{2,1,0:T(8,128)(2,1)} %bitcast.51), custom_call_target="tpu_custom_call" | custom-call | flops 8800000000 | tf_op jit(solution)/shard_map/sort/pallas_call | solution.py:220
  26.2 1.5 %collective-permute-start.8 = (bf16[144,1024]{1,0:T(8,128)(2,1)S(1)}, bf16[144,1024]{1,0:T(8,128)(2,1)S(1)}, u32[]{:S(2)}, u32[]{:S(2)}) collective-permute-start(bf16[144,1024]{1,0:T(8,128)(2,1)S(1)} %collective-permute-done.7.refs_0_), channel_id=1, source_target_pairs={{0,8},{4,12},{8,0},{12,4},{1,9},{5,13},{9,1},{13,5},{2,10},{6,14},... | collective-permute-start | bytes 884744 | tf_op jit(solution)/shard_map/ppermute | solution.py:387
  27.7 7.7 %collective-permute-done.4.refs_1_ = bf16[144,1024]{1,0:T(8,128)(2,1)S(1)} collective-permute-done((bf16[144,1024]{1,0:T(8,128)(2,1)S(1)}, bf16[144,1024]{1,0:T(8,128)(2,1)S(1)}, u32[]{:S(2)}, u32[]{:S(2)}) %collective-permute-start.4) | collective-permute-done | bytes 294944 | tf_op jit(solution)/shard_map/ppermute | solution.py:387
  36.1 3.3 %collective-permute-done.8.refs_1_ = bf16[144,1024]{1,0:T(8,128)(2,1)S(1)} collective-permute-done((bf16[144,1024]{1,0:T(8,128)(2,1)S(1)}, bf16[144,1024]{1,0:T(8,128)(2,1)S(1)}, u32[]{:S(2)}, u32[]{:S(2)}) %collective-permute-start.8) | collective-permute-done | bytes 294944 | tf_op jit(solution)/shard_map/ppermute | solution.py:387
  39.9 1.5 %dispatch.4 = (bf16[16,64,1024]{2,1,0:T(8,128)(2,1)S(1)}, f32[16,64,128]{2,1,0:T(8,128)S(1)}, bf16[4,256,128]{2,1,0:T(8,128)(2,1)S(1)}) custom-call(s32[1]{0:T(128)} %bitcast.13.base_ref, bf16[64,1024]{1,0:T(8,128)(2,1)S(1)} %fusion.2.rw_ref, bf16[144,1024]{1,0:T(8,128)(2,1)S(1)} %collective-permute-done.3.refs_0_, ...), custom_call_target="tpu_custom_call" | custom-call | flops 3300000000 | tf_op jit(solution)/shard_map/dispatch/pallas_call | solution.py:139
  42.0 1.6 %collective-permute-start.18 = (bf16[144,1024]{1,0:T(8,128)(2,1)S(1)}, bf16[144,1024]{1,0:T(8,128)(2,1)S(1)}, u32[]{:S(2)}, u32[]{:S(2)}) collective-permute-start(bf16[144,1024]{1,0:T(8,128)(2,1)S(1)} %collective-permute-done.11.refs_6_.refs_0_), channel_id=1, source_target_pairs={{0,8},{4,12},{8,0},{12,4},{1,9},{5,13},{9,1},{13,5},{2,10},{6,14},... | collective-permute-start | bytes 884744 | tf_op jit(solution)/shard_map/ppermute | solution.py:387
  43.7 1.5 %dispatch.5 = (bf16[16,64,1024]{2,1,0:T(8,128)(2,1)S(1)}, f32[16,64,128]{2,1,0:T(8,128)S(1)}, bf16[4,256,128]{2,1,0:T(8,128)(2,1)S(1)}) custom-call(s32[1]{0:T(128)} %bitcast.13.base_ref, bf16[64,1024]{1,0:T(8,128)(2,1)S(1)} %fusion.2.rw_ref, bf16[144,1024]{1,0:T(8,128)(2,1)S(1)} %collective-permute-done.7.refs_0_, ...), custom_call_target="tpu_custom_call" | custom-call | flops 3300000000 | tf_op jit(solution)/shard_map/dispatch/pallas_call | solution.py:139
  45.2 11.5 %experts.2 = (bf16[16,64,1024]{2,1,0:T(8,128)(2,1)S(1)}, bf16[16,64,1024]{2,1,0:T(8,128)(2,1)S(1)}) custom-call(bf16[16,64,1024]{2,1,0:T(8,128)(2,1)S(1)} %get-tuple-element.29.refs_0_, bf16[16,64,1024]{2,1,0:T(8,128)(2,1)S(1)} %get-tuple-element.30.refs_1_, f32[16,64,128]{2,1,0:T(8,128)S(1)} %get-tuple-element.31.refs_2_, ...), custom_call_target="tpu_custom_call" | custom-call | flops 6600000000 | tf_op jit(solution)/shard_map/experts/pallas_call | solution.py:275
  58.2 1.6 %dispatch.7 = (bf16[16,64,1024]{2,1,0:T(8,128)(2,1)S(1)}, f32[16,64,128]{2,1,0:T(8,128)S(1)}, bf16[4,256,128]{2,1,0:T(8,128)(2,1)S(1)}, f32[8,128]{1,0:T(8,128)S(1)}) custom-call(s32[1]{0:T(128)} %bitcast.13.base_ref, bf16[64,1024]{1,0:T(8,128)(2,1)S(1)} %fusion.2.rw_ref, bf16[144,1024]{1,0:T(8,128)(2,1)S(1)} %fusion.1.refs_0_, ...), custom_call_target="tpu_custom_call" | custom-call | flops 3300000000 | tf_op jit(solution)/shard_map/dispatch/pallas_call | solution.py:139
  60.5 1.5 %dispatch.6 = (bf16[16,64,1024]{2,1,0:T(8,128)(2,1)S(1)}, f32[16,64,128]{2,1,0:T(8,128)S(1)}, bf16[4,256,128]{2,1,0:T(8,128)(2,1)S(1)}) custom-call(s32[1]{0:T(128)} %bitcast.13.base_ref, bf16[64,1024]{1,0:T(8,128)(2,1)S(1)} %fusion.2.rw_ref, bf16[144,1024]{1,0:T(8,128)(2,1)S(1)} %collective-permute-done.11.refs_6_.refs_0_, ...), custom_call_target="tpu_custom_call" | custom-call | flops 3300000000 | tf_op jit(solution)/shard_map/dispatch/pallas_call | solution.py:139
  62.8 11.6 %experts.3 = (bf16[16,64,1024]{2,1,0:T(8,128)(2,1)S(1)}, bf16[16,64,1024]{2,1,0:T(8,128)(2,1)S(1)}) custom-call(bf16[16,64,1024]{2,1,0:T(8,128)(2,1)S(1)} %get-tuple-element.41.refs_0_, bf16[16,64,1024]{2,1,0:T(8,128)(2,1)S(1)} %get-tuple-element.42.refs_1_, f32[16,64,128]{2,1,0:T(8,128)S(1)} %get-tuple-element.43.refs_2_, ...), custom_call_target="tpu_custom_call" | custom-call | flops 6600000000 | tf_op jit(solution)/shard_map/experts/pallas_call | solution.py:275
  76.6 1.5 %collective-permute-start.16 = (bf16[1,128,1024]{2,1,0:T(8,128)(2,1)S(1)}, bf16[1,128,1024]{2,1,0:T(8,128)(2,1)S(1)}, u32[]{:S(2)}, u32[]{:S(2)}) collective-permute-start(bf16[1,128,1024]{2,1,0:T(8,128)(2,1)S(1)} %add_convert_fusion.5.refs_7_), channel_id=1, source_target_pairs={{0,8},{4,12},{8,0},{12,4},{1,9},{5,13},{9,1},{13,5},{2,10},{6,14},... | collective-permute-start | bytes 786440 | tf_op jit(solution)/shard_map/ppermute | solution.py:387
  78.1 1.6 %copy-done.2 = bf16[16,64,1024]{2,1,0:T(8,128)(2,1)S(1)} copy-done((bf16[16,64,1024]{2,1,0:T(8,128)(2,1)S(1)}, bf16[16,64,1024]{2,1,0:T(8,128)(2,1)}, u32[]{:S(2)}) %copy-start.2) | copy-done | bytes 2097176
  81.9 1.4 %collective-permute-start.14 = (bf16[1,128,1024]{2,1,0:T(8,128)(2,1)S(1)}, bf16[1,128,1024]{2,1,0:T(8,128)(2,1)S(1)}, u32[]{:S(2)}, u32[]{:S(2)}) collective-permute-start(bf16[1,128,1024]{2,1,0:T(8,128)(2,1)S(1)} %add_convert_fusion.6), channel_id=1, source_target_pairs={{0,3},{1,0},{2,1},{3,2},{4,7},{5,4},{6,5},{7,6},{8,11},{9,8},{10,9... | collective-permute-start | bytes 786440 | tf_op jit(solution)/shard_map/ppermute | solution.py:390
  85.1 1.3 %collective-permute-start.25 = (bf16[1,128,1024]{2,1,0:T(8,128)(2,1)S(1)}, bf16[1,128,1024]{2,1,0:T(8,128)(2,1)S(1)}, u32[]{:S(2)}, u32[]{:S(2)}) collective-permute-start(bf16[1,128,1024]{2,1,0:T(8,128)(2,1)S(1)} %add_convert_fusion.3), channel_id=1, source_target_pairs={{0,8},{4,12},{8,0},{12,4},{1,9},{5,13},{9,1},{13,5},{2,10},{6,14},... | collective-permute-start | bytes 786440 | tf_op jit(solution)/shard_map/ppermute | solution.py:387
  86.6 1.6 %collective-permute-start.17 = (bf16[1,128,1024]{2,1,0:T(8,128)(2,1)S(1)}, bf16[1,128,1024]{2,1,0:T(8,128)(2,1)S(1)}, u32[]{:S(2)}, u32[]{:S(2)}) collective-permute-start(bf16[1,128,1024]{2,1,0:T(8,128)(2,1)S(1)} %add_convert_fusion.4), channel_id=1, source_target_pairs={{0,1},{1,2},{2,3},{3,0},{4,5},{5,6},{6,7},{7,4},{8,9},{9,10},{10,1... | collective-permute-start | bytes 786440 | tf_op jit(solution)/shard_map/ppermute | solution.py:390
  88.3 4.5 %collective-permute-done.25 = bf16[1,128,1024]{2,1,0:T(8,128)(2,1)S(1)} collective-permute-done((bf16[1,128,1024]{2,1,0:T(8,128)(2,1)S(1)}, bf16[1,128,1024]{2,1,0:T(8,128)(2,1)S(1)}, u32[]{:S(2)}, u32[]{:S(2)}) %collective-permute-start.25) | collective-permute-done | bytes 262176 | tf_op jit(solution)/shard_map/ppermute | solution.py:387
  92.8 1.1 collective-permute-start.28
  95.0 3.0 %collective-permute-start.26 = (bf16[1,128,1024]{2,1,0:T(8,128)(2,1)S(1)}, bf16[1,128,1024]{2,1,0:T(8,128)(2,1)S(1)}, u32[]{:S(2)}, u32[]{:S(2)}) collective-permute-start(bf16[1,128,1024]{2,1,0:T(8,128)(2,1)S(1)} %add_convert_fusion.2), channel_id=1, source_target_pairs={{0,2},{1,3},{2,0},{3,1},{4,6},{5,7},{6,4},{7,5},{8,10},{9,11},{10,... | collective-permute-start | bytes 786440 | tf_op jit(solution)/shard_map/ppermute | solution.py:390
  98.0 6.2 %attention.1 = bf16[128,4096]{1,0:T(8,128)(2,1)} custom-call(s32[128,1]{1,0:T(8,128)S(1)} %copy.20.first_ref, s32[128,1]{1,0:T(8,128)S(1)} %copy.21.last_ref, s32[1,512]{1,0:T(1,128)S(1)} %bitcast.40, bf16[128,4608]{1,0:T(8,128)(2,1)S(1)} %bitcast.42, bf16[128,576]{1,0:T(8,128)(2,1)S(1)} %bitcast.39, bf16[128,576]{1,0:T(8,128)(2,1)S(1)} %collective-permute-done.refs_1_, ...), custom_call_target="tpu_custom_call" | custom-call | flops 6600000000 | tf_op jit(solution)/shard_map/attention/pallas_call | solution.py:355
  104.8 4.2 %collective-permute-done.26 = bf16[1,128,1024]{2,1,0:T(8,128)(2,1)S(1)} collective-permute-done((bf16[1,128,1024]{2,1,0:T(8,128)(2,1)S(1)}, bf16[1,128,1024]{2,1,0:T(8,128)(2,1)S(1)}, u32[]{:S(2)}, u32[]{:S(2)}) %collective-permute-start.26) | collective-permute-done | bytes 262176 | tf_op jit(solution)/shard_map/ppermute | solution.py:390
  (91 shorter events, 17.8 us)
Async XLA Ops:
  2.3 23.1 %collective-permute-start.3 = (bf16[144,1024]{1,0:T(8,128)(2,1)S(1)}, bf16[144,1024]{1,0:T(8,128)(2,1)S(1)}, u32[]{:S(2)}, u32[]{:S(2)}) collective-permute-start(bf16[144,1024]{1,0:T(8,128)(2,1)S(1)} %fusion.1.refs_0_), channel_id=1, source_target_pairs={{0,1},{1,2},{2,3},{3,0},{4,5},{5,6},{6,7},{7,4},{8,9},{9,10},{10,1... | collective-permute-start | bytes 884744 | tf_op jit(solution)/shard_map/ppermute | solution.py:390
  5.4 20.8 %collective-permute-start.7 = (bf16[144,1024]{1,0:T(8,128)(2,1)S(1)}, bf16[144,1024]{1,0:T(8,128)(2,1)S(1)}, u32[]{:S(2)}, u32[]{:S(2)}) collective-permute-start(bf16[144,1024]{1,0:T(8,128)(2,1)S(1)} %fusion.1.refs_0_), channel_id=1, source_target_pairs={{0,3},{1,0},{2,1},{3,2},{4,7},{5,4},{6,5},{7,6},{8,11},{9,8},{10,9... | collective-permute-start | bytes 884744 | tf_op jit(solution)/shard_map/ppermute | solution.py:390
  7.5 33.9 %collective-permute-start.11 = (bf16[144,1024]{1,0:T(8,128)(2,1)S(1)}, bf16[144,1024]{1,0:T(8,128)(2,1)S(1)}, u32[]{:S(2)}, u32[]{:S(2)}) collective-permute-start(bf16[144,1024]{1,0:T(8,128)(2,1)S(1)} %fusion.1.refs_0_), channel_id=1, source_target_pairs={{0,2},{1,3},{2,0},{3,1},{4,6},{5,7},{6,4},{7,5},{8,10},{9,11},{10,... | collective-permute-start | bytes 884744 | tf_op jit(solution)/shard_map/ppermute | solution.py:390
  8.4 33.6 %collective-permute-start.21 = (bf16[144,1024]{1,0:T(8,128)(2,1)S(1)}, bf16[144,1024]{1,0:T(8,128)(2,1)S(1)}, u32[]{:S(2)}, u32[]{:S(2)}) collective-permute-start(bf16[144,1024]{1,0:T(8,128)(2,1)S(1)} %fusion.1.refs_0_), channel_id=1, source_target_pairs={{0,8},{4,12},{8,0},{12,4},{1,9},{5,13},{9,1},{13,5},{2,10},{6,14},... | collective-permute-start | bytes 884744 | tf_op jit(solution)/shard_map/ppermute | solution.py:387
  25.4 10.0 %collective-permute-start.4 = (bf16[144,1024]{1,0:T(8,128)(2,1)S(1)}, bf16[144,1024]{1,0:T(8,128)(2,1)S(1)}, u32[]{:S(2)}, u32[]{:S(2)}) collective-permute-start(bf16[144,1024]{1,0:T(8,128)(2,1)S(1)} %collective-permute-done.3.refs_0_), channel_id=1, source_target_pairs={{0,8},{4,12},{8,0},{12,4},{1,9},{5,13},{9,1},{13,5},{2,10},{6,14},... | collective-permute-start | bytes 884744 | tf_op jit(solution)/shard_map/ppermute | solution.py:387
  26.1 9.3 %collective-permute-start.5 = (bf16[144,1024]{1,0:T(8,128)(2,1)S(1)}, bf16[144,1024]{1,0:T(8,128)(2,1)S(1)}, u32[]{:S(2)}, u32[]{:S(2)}) collective-permute-start(bf16[144,1024]{1,0:T(8,128)(2,1)S(1)} %collective-permute-done.3.refs_0_), channel_id=1, source_target_pairs={{0,4},{4,0},{8,12},{12,8},{1,5},{5,1},{9,13},{13,9},{2,6},{6,2},{1... | collective-permute-start | bytes 884744 | tf_op jit(solution)/shard_map/ppermute | solution.py:387
  26.2 13.2 %collective-permute-start.8 = (bf16[144,1024]{1,0:T(8,128)(2,1)S(1)}, bf16[144,1024]{1,0:T(8,128)(2,1)S(1)}, u32[]{:S(2)}, u32[]{:S(2)}) collective-permute-start(bf16[144,1024]{1,0:T(8,128)(2,1)S(1)} %collective-permute-done.7.refs_0_), channel_id=1, source_target_pairs={{0,8},{4,12},{8,0},{12,4},{1,9},{5,13},{9,1},{13,5},{2,10},{6,14},... | collective-permute-start | bytes 884744 | tf_op jit(solution)/shard_map/ppermute | solution.py:387
  35.5 21.7 %collective-permute-start.22 = (bf16[144,1024]{1,0:T(8,128)(2,1)S(1)}, bf16[144,1024]{1,0:T(8,128)(2,1)S(1)}, u32[]{:S(2)}, u32[]{:S(2)}) collective-permute-start(bf16[144,1024]{1,0:T(8,128)(2,1)S(1)} %fusion.1.refs_0_), channel_id=1, source_target_pairs={{0,4},{4,0},{8,12},{12,8},{1,5},{5,1},{9,13},{13,9},{2,6},{6,2},{1... | collective-permute-start | bytes 884744 | tf_op jit(solution)/shard_map/ppermute | solution.py:387
  39.4 4.2 %collective-permute-start.10 = (bf16[144,1024]{1,0:T(8,128)(2,1)S(1)}, bf16[144,1024]{1,0:T(8,128)(2,1)S(1)}, u32[]{:S(2)}, u32[]{:S(2)}) collective-permute-start(bf16[144,1024]{1,0:T(8,128)(2,1)S(1)} %collective-permute-done.8.refs_1_), channel_id=1, source_target_pairs={{0,4},{4,0},{8,12},{12,8},{1,5},{5,1},{9,13},{13,9},{2,6},{6,2},{1... | collective-permute-start | bytes 884744 | tf_op jit(solution)/shard_map/ppermute | solution.py:387
  41.4 34.9 %collective-permute-start = (bf16[128,576]{1,0:T(8,128)(2,1)S(1)}, bf16[128,576]{1,0:T(8,128)(2,1)S(1)}, u32[]{:S(2)}, u32[]{:S(2)}) collective-permute-start(bf16[128,576]{1,0:T(8,128)(2,1)S(1)} %bitcast.37), channel_id=1, source_target_pairs={{0,8},{4,12},{8,0},{12,4},{1,9},{5,13},{9,1},{13,5},{2,10},{6,14},... | collective-permute-start | bytes 442376 | tf_op jit(solution)/shard_map/ppermute | solution.py:387
  42.0 52.9 %collective-permute-start.1 = (bf16[128,576]{1,0:T(8,128)(2,1)S(1)}, bf16[128,576]{1,0:T(8,128)(2,1)S(1)}, u32[]{:S(2)}, u32[]{:S(2)}) collective-permute-start(bf16[128,576]{1,0:T(8,128)(2,1)S(1)} %bitcast.38), channel_id=1, source_target_pairs={{0,4},{4,0},{8,12},{12,8},{1,5},{5,1},{9,13},{13,9},{2,6},{6,2},{1... | collective-permute-start | bytes 442376 | tf_op jit(solution)/shard_map/ppermute | solution.py:387
  42.0 15.6 %collective-permute-start.18 = (bf16[144,1024]{1,0:T(8,128)(2,1)S(1)}, bf16[144,1024]{1,0:T(8,128)(2,1)S(1)}, u32[]{:S(2)}, u32[]{:S(2)}) collective-permute-start(bf16[144,1024]{1,0:T(8,128)(2,1)S(1)} %collective-permute-done.11.refs_6_.refs_0_), channel_id=1, source_target_pairs={{0,8},{4,12},{8,0},{12,4},{1,9},{5,13},{9,1},{13,5},{2,10},{6,14},... | collective-permute-start | bytes 884744 | tf_op jit(solution)/shard_map/ppermute | solution.py:387
  43.6 14.2 %collective-permute-start.23 = (bf16[144,1024]{1,0:T(8,128)(2,1)S(1)}, bf16[144,1024]{1,0:T(8,128)(2,1)S(1)}, u32[]{:S(2)}, u32[]{:S(2)}) collective-permute-start(bf16[144,1024]{1,0:T(8,128)(2,1)S(1)} %collective-permute-done.21.refs_1_), channel_id=1, source_target_pairs={{0,4},{4,0},{8,12},{12,8},{1,5},{5,1},{9,13},{13,9},{2,6},{6,2},{1... | collective-permute-start | bytes 884744 | tf_op jit(solution)/shard_map/ppermute | solution.py:387
  57.8 4.2 %collective-permute-start.12 = (bf16[1,256,1024]{2,1,0:T(8,128)(2,1)S(1)}, bf16[1,256,1024]{2,1,0:T(8,128)(2,1)S(1)}, u32[]{:S(2)}, u32[]{:S(2)}) collective-permute-start(bf16[1,256,1024]{2,1,0:T(8,128)(2,1)S(1)} %get-tuple-element.35), channel_id=1, source_target_pairs={{0,4},{4,0},{8,12},{12,8},{1,5},{5,1},{9,13},{13,9},{2,6},{6,2},{1... | collective-permute-start | bytes 1572872 | tf_op jit(solution)/shard_map/ppermute | solution.py:387
  62.1 18.1 %collective-permute-start.13 = (bf16[1,128,1024]{2,1,0:T(8,128)(2,1)S(1)}, bf16[1,128,1024]{2,1,0:T(8,128)(2,1)}, u32[]{:S(2)}, u32[]{:S(2)}) collective-permute-start(bf16[1,128,1024]{2,1,0:T(8,128)(2,1)S(1)} %add_convert_fusion.7.refs_6_), channel_id=1, source_target_pairs={{0,8},{4,12},{8,0},{12,4},{1,9},{5,13},{9,1},{13,5},{2,10},{6,14},... | collective-permute-start | bytes 786440 | tf_op jit(solution)/shard_map/ppermute | solution.py:387
  75.7 6.1 %collective-permute-start.24 = (bf16[1,256,1024]{2,1,0:T(8,128)(2,1)S(1)}, bf16[1,256,1024]{2,1,0:T(8,128)(2,1)}, u32[]{:S(2)}, u32[]{:S(2)}) collective-permute-start(bf16[1,256,1024]{2,1,0:T(8,128)(2,1)S(1)} %get-tuple-element.47), channel_id=1, source_target_pairs={{0,4},{4,0},{8,12},{12,8},{1,5},{5,1},{9,13},{13,9},{2,6},{6,2},{1... | collective-permute-start | bytes 1572872 | tf_op jit(solution)/shard_map/ppermute | solution.py:387
  76.3 21.7 %collective-permute-start.2 = (bf16[128,576]{1,0:T(8,128)(2,1)S(1)}, bf16[128,576]{1,0:T(8,128)(2,1)S(1)}, u32[]{:S(2)}, u32[]{:S(2)}) collective-permute-start(bf16[128,576]{1,0:T(8,128)(2,1)S(1)} %collective-permute-done.refs_1_), channel_id=1, source_target_pairs={{0,4},{4,0},{8,12},{12,8},{1,5},{5,1},{9,13},{13,9},{2,6},{6,2},{1... | collective-permute-start | bytes 442376 | tf_op jit(solution)/shard_map/ppermute | solution.py:387
  76.6 8.5 %collective-permute-start.16 = (bf16[1,128,1024]{2,1,0:T(8,128)(2,1)S(1)}, bf16[1,128,1024]{2,1,0:T(8,128)(2,1)S(1)}, u32[]{:S(2)}, u32[]{:S(2)}) collective-permute-start(bf16[1,128,1024]{2,1,0:T(8,128)(2,1)S(1)} %add_convert_fusion.5.refs_7_), channel_id=1, source_target_pairs={{0,8},{4,12},{8,0},{12,4},{1,9},{5,13},{9,1},{13,5},{2,10},{6,14},... | collective-permute-start | bytes 786440 | tf_op jit(solution)/shard_map/ppermute | solution.py:387
  80.2 6.3 %collective-permute-start.27 = (bf16[1,256,1024]{2,1,0:T(8,128)(2,1)S(1)}, bf16[1,256,1024]{2,1,0:T(8,128)(2,1)S(1)}, u32[]{:S(2)}, u32[]{:S(2)}) collective-permute-start(bf16[1,256,1024]{2,1,0:T(8,128)(2,1)S(1)} %get-tuple-element.51), channel_id=1, source_target_pairs={{0,4},{4,0},{8,12},{12,8},{1,5},{5,1},{9,13},{13,9},{2,6},{6,2},{1... | collective-permute-start | bytes 1572872 | tf_op jit(solution)/shard_map/ppermute | solution.py:387
  81.9 23.0 %collective-permute-start.14 = (bf16[1,128,1024]{2,1,0:T(8,128)(2,1)S(1)}, bf16[1,128,1024]{2,1,0:T(8,128)(2,1)S(1)}, u32[]{:S(2)}, u32[]{:S(2)}) collective-permute-start(bf16[1,128,1024]{2,1,0:T(8,128)(2,1)S(1)} %add_convert_fusion.6), channel_id=1, source_target_pairs={{0,3},{1,0},{2,1},{3,2},{4,7},{5,4},{6,5},{7,6},{8,11},{9,8},{10,9... | collective-permute-start | bytes 786440 | tf_op jit(solution)/shard_map/ppermute | solution.py:390
  85.1 7.7 %collective-permute-start.25 = (bf16[1,128,1024]{2,1,0:T(8,128)(2,1)S(1)}, bf16[1,128,1024]{2,1,0:T(8,128)(2,1)S(1)}, u32[]{:S(2)}, u32[]{:S(2)}) collective-permute-start(bf16[1,128,1024]{2,1,0:T(8,128)(2,1)S(1)} %add_convert_fusion.3), channel_id=1, source_target_pairs={{0,8},{4,12},{8,0},{12,4},{1,9},{5,13},{9,1},{13,5},{2,10},{6,14},... | collective-permute-start | bytes 786440 | tf_op jit(solution)/shard_map/ppermute | solution.py:387
  86.6 18.3 %collective-permute-start.17 = (bf16[1,128,1024]{2,1,0:T(8,128)(2,1)S(1)}, bf16[1,128,1024]{2,1,0:T(8,128)(2,1)S(1)}, u32[]{:S(2)}, u32[]{:S(2)}) collective-permute-start(bf16[1,128,1024]{2,1,0:T(8,128)(2,1)S(1)} %add_convert_fusion.4), channel_id=1, source_target_pairs={{0,1},{1,2},{2,3},{3,0},{4,5},{5,6},{6,7},{7,4},{8,9},{9,10},{10,1... | collective-permute-start | bytes 786440 | tf_op jit(solution)/shard_map/ppermute | solution.py:390
  92.8 12.0 %collective-permute-start.28 = (bf16[1,128,1024]{2,1,0:T(8,128)(2,1)S(1)}, bf16[1,128,1024]{2,1,0:T(8,128)(2,1)S(1)}, u32[]{:S(2)}, u32[]{:S(2)}) collective-permute-start(bf16[1,128,1024]{2,1,0:T(8,128)(2,1)S(1)} %add_convert_fusion.1), channel_id=1, source_target_pairs={{0,8},{4,12},{8,0},{12,4},{1,9},{5,13},{9,1},{13,5},{2,10},{6,14},... | collective-permute-start | bytes 786440 | tf_op jit(solution)/shard_map/ppermute | solution.py:387
  95.0 14.1 %collective-permute-start.26 = (bf16[1,128,1024]{2,1,0:T(8,128)(2,1)S(1)}, bf16[1,128,1024]{2,1,0:T(8,128)(2,1)S(1)}, u32[]{:S(2)}, u32[]{:S(2)}) collective-permute-start(bf16[1,128,1024]{2,1,0:T(8,128)(2,1)S(1)} %add_convert_fusion.2), channel_id=1, source_target_pairs={{0,2},{1,3},{2,0},{3,1},{4,6},{5,7},{6,4},{7,5},{8,10},{9,11},{10,... | collective-permute-start | bytes 786440 | tf_op jit(solution)/shard_map/ppermute | solution.py:390
  (15 other events, 99.8 us)

commit v6 on v5

--- a/solution.py
+++ b/solution.py
@@ -17,8 +17,10 @@
 EXPERT_ROWS = 256
 EXTRA = 16
 VMEM = 14 * 2**20
-VMEM_EXPERTS = 40 * 2**20
-VMEM_SORT = 56 * 2**20
+VMEM_EXPERTS = 36 * 2**20
+VMEM_SORT = 52 * 2**20
+PIECES = 4
+DEPTH = 3
 PEAK = 1.1e9
 
 qk_scale = 192.0 ** (-0.5)
@@ -26,7 +28,7 @@
 TN = (((0,), (0,)), ((), ()))
 
 
-def call(kernel, micros, grid, in_specs, out_specs, out_shape, scratch, name, limit=VMEM):
+def call(kernel, micros, grid, in_specs, out_specs, out_shape, scratch, name, limit=VMEM, aliases={}):
     return pl.pallas_call(
         kernel,
         grid=grid,
@@ -34,6 +36,7 @@
         out_specs=out_specs,
         out_shape=out_shape,
         scratch_shapes=scratch,
+        input_output_aliases=aliases,
         compiler_params=pltpu.CompilerParams(
             dimension_semantics=("arbitrary",) * len(grid), vmem_limit_bytes=limit
         ),
@@ -113,7 +116,7 @@
 
 def dispatch(parts, top, base, rw, local, row=None, after=()):
     n_parts = len(parts)
-    n, width = parts[0].shape[0] // (BLOCK + EXTRA), parts[0].shape[1]
+    n, width = parts[0].shape[0] // (BLOCK + EXTRA), rw.shape[1]
     slots = n_parts * CAP
     in_specs = [
         pl.BlockSpec(memory_space=pltpu.SMEM),
@@ -148,26 +151,31 @@
     )(base, rw, *parts, *after, *extra)
 
 
-def fetch(sources, slots, sem, step, steps, first):
-    group = slots[0].shape[1]
+def fetch(sources, slots, sem, step, steps, first, start=0):
+    depth, group = slots[0].shape[:2]
 
     def copies(at):
-        slot = lax.rem(at, 2)
+        slot = lax.rem(at, depth)
         return [
             pltpu.make_async_copy(
-                source.at[pl.ds(at * group, group)], held.at[slot], sem.at[i, slot]
+                source.at[start + at * group + e], held.at[slot, e], sem.at[i, slot, e]
             )
             for i, (source, held) in enumerate(zip(sources, slots))
+            for e in range(group)
         ]
 
     @pl.when(first & (step == 0))
     def _():
-        for copy in copies(step):
-            copy.start()
-
-    @pl.when(first & (step + 1 < steps))
+        for ahead in range(depth - 1):
+
+            @pl.when(ahead < steps)
+            def _():
+                for copy in copies(step + ahead):
+                    copy.start()
+
+    @pl.when(first & (step + depth - 1 < steps))
     def _():
-        for copy in copies(step + 1):
+        for copy in copies(step + depth - 1):
             copy.start()
 
     @pl.when(first)
@@ -175,19 +183,21 @@
         for copy in copies(step):
             copy.wait()
 
-    return lax.rem(step, 2)
-
-
-def sort_kernel(gu_ref, out_ref, held, made, wide, in_sem, out_sem):
+    return lax.rem(step, depth)
+
+
+def sort_kernel(start, gu_ref, *refs):
+    out_ref, held, made, wide, in_sem, out_sem = refs[-6:]
     step, steps = pl.program_id(0), pl.num_programs(0)
     _, group, _, hidden, width = made.shape
     chunks = width // LANES
-    slot = fetch([gu_ref], [held], in_sem, step, steps, step >= 0)
+    slot = fetch([gu_ref], [held], in_sem, step, steps, step >= 0, start)
+    to = lax.rem(step, 2)
 
     def leave(at):
         to = lax.rem(at, 2)
         return pltpu.make_async_copy(
-            made.at[to], out_ref.at[pl.ds(at * group, group)], out_sem.at[to]
+            made.at[to], out_ref.at[pl.ds(start + at * group, group)], out_sem.at[to]
         )
 
     @pl.when(step >= 2)
@@ -199,7 +209,7 @@
         for z in range(2):
             for c in range(chunks):
                 part = wide[e, pl.ds(2 * c + z, hidden, stride=2 * chunks), :]
-                made[slot, e, z, :, c * LANES : (c + 1) * LANES] = part.astype(jnp.bfloat16)
+                made[to, e, z, :, c * LANES : (c + 1) * LANES] = part.astype(jnp.bfloat16)
     leave(step).start()
 
     @pl.when(step == steps - 1)
@@ -211,29 +221,37 @@
         leave(step).wait()
 
 
-def sort_rows(gate_up):
+def sort_rows(gate_up, behind):
     local, hidden, _, width = gate_up.shape
+    pieces = PIECES if local % (2 * PIECES) == 0 else 1
     group = 2 if local % 2 == 0 else 1
     chunks = width // LANES
     gu = gate_up.reshape(local, hidden, 2, chunks, LANES).swapaxes(2, 3)
     gu = gu.reshape(local, hidden * 2 * chunks, LANES)
-    return call(
-        sort_kernel,
-        8,
-        (local // group,),
-        [IN_HBM],
-        IN_HBM,
-        jax.ShapeDtypeStruct((local, 2, hidden, width), jnp.bfloat16),
-        [
-            pltpu.VMEM((2, group) + gu.shape[1:], jnp.bfloat16),
-            pltpu.VMEM((2, group, 2, hidden, width), jnp.bfloat16),
-            pltpu.VMEM((group,) + gu.shape[1:], jnp.float32),
-            pltpu.SemaphoreType.DMA((1, 2)),
-            pltpu.SemaphoreType.DMA((2,)),
-        ],
-        "sort",
-        VMEM_SORT,
-    )(gu)
+    done = ()
+    for j in range(pieces):
+        after = behind[j] if pieces > 1 else ()
+        done = (
+            call(
+                functools.partial(sort_kernel, j * local // pieces),
+                4,
+                (local // pieces // group,),
+                [IN_HBM] + [IN_HBM] * len(done) + [ANYWHERE] * len(after),
+                IN_HBM,
+                jax.ShapeDtypeStruct((local, 2, hidden, width), jnp.bfloat16),
+                [
+                    pltpu.VMEM((2, group) + gu.shape[1:], jnp.bfloat16),
+                    pltpu.VMEM((2, group, 2, hidden, width), jnp.bfloat16),
+                    pltpu.VMEM((group,) + gu.shape[1:], jnp.float32),
+                    pltpu.SemaphoreType.DMA((1, 2, group)),
+                    pltpu.SemaphoreType.DMA((2,)),
+                ],
+                "sort",
+                VMEM_SORT,
+                {1: 0} if done else {},
+            )(gu, *done, *after),
+        )
+    return done[0]
 
 
 def expert_kernel(n, *refs):
@@ -280,49 +298,52 @@
         [rows_spec] * n,
         [jax.ShapeDtypeStruct(r.shape, jnp.bfloat16) for r in rows],
         [
-            pltpu.VMEM((2, group, 2, hidden, width), jnp.bfloat16),
-            pltpu.VMEM((2, group, hidden, width), jnp.bfloat16),
-            pltpu.SemaphoreType.DMA((2, 2)),
+            pltpu.VMEM((DEPTH, group, 2, hidden, width), jnp.bfloat16),
+            pltpu.VMEM((DEPTH, group, hidden, width), jnp.bfloat16),
+            pltpu.SemaphoreType.DMA((2, DEPTH, group)),
         ],
         "experts",
         VMEM_EXPERTS,
     )(*rows, *weights, gu, down, *after)
 
 
-def combine_kernel(groups, picks_ref, made_ref, *outs):
-    local, _, width = made_ref.shape
-    per = outs[0].shape[1] // BLOCK
-    for p in range(picks_ref.shape[0]):
-        held = made_ref[:, p * CAP : (p + 1) * CAP, :].reshape(local * CAP, width)
-        mix = lax.dot_general(picks_ref[p], held, TN, preferred_element_type=jnp.float32)
-        out, at = outs[p // per], p % per
-        out[0, at * BLOCK : (at + 1) * BLOCK, :] = mix.astype(jnp.bfloat16)
-
-
-def combine(picks, made, n_parts):
-    n = picks.shape[0] // n_parts
-    local, _, width = made.shape
-    slots = n_parts * CAP
-    half = n_parts // 2 * BLOCK
+def combine_kernel(n, *refs):
+    picks, made, outs = refs[:n], refs[n : 2 * n], refs[-2:]
+    local, _, width = made[0].shape
+    parts = picks[0].shape[0]
+    half = parts // 2
+    for i in range(n):
+        for p in range(parts):
+            held = made[i][:, p * CAP : (p + 1) * CAP, :].reshape(local * CAP, width)
+            mix = lax.dot_general(picks[i][p], held, TN, preferred_element_type=jnp.float32)
+            at = ((p % half) * n + i) * BLOCK
+            outs[p // half][0, at : at + BLOCK, :] = mix.astype(jnp.bfloat16)
+
+
+def combine(picks, made, n_parts, after=()):
+    n = len(picks)
+    steps = picks[0].shape[0] // n_parts
+    local, _, width = made[0].shape
+    half = n_parts // 2 * n * BLOCK
     out = pl.BlockSpec((1, half, width), lambda i: (i, 0, 0))
     return call(
-        functools.partial(combine_kernel, 2),
-        2 * n,
-        (n,),
-        [
-            pl.BlockSpec((n_parts,) + picks.shape[1:], lambda i: (i, 0, 0)),
-            pl.BlockSpec((local, slots, width), lambda i: (0, i, 0)),
-        ],
+        functools.partial(combine_kernel, n),
+        2 * steps,
+        (steps,),
+        [pl.BlockSpec((n_parts,) + picks[0].shape[1:], lambda i: (i, 0, 0))] * n
+        + [pl.BlockSpec((local, n_parts * CAP, width), lambda i: (0, i, 0))] * n
+        + [ANYWHERE] * len(after),
         [out, out],
-        [jax.ShapeDtypeStruct((n, half, width), jnp.bfloat16)] * 2,
+        [jax.ShapeDtypeStruct((steps, half, width), jnp.bfloat16)] * 2,
         [],
         "combine",
-    )(picks, made)
-
-
-def attend_kernel(n, first_ref, last_ref, kpos_ref, q_ref, *refs):
+    )(*picks, *made, *after)
+
+
+def attend_kernel(n, kdim, first_ref, last_ref, kpos_ref, q_ref, *refs):
     parts, (out_ref, even, odd) = refs[:n], refs[n:]
-    rows, kdim = parts[0].shape
+    rows = q_ref.shape[0]
+    start = max(parts[0].shape[1] - even.shape[1], 0)
     wide = even.shape[1]
     half = wide - kdim
 
@@ -331,8 +352,9 @@
         pad = jnp.zeros((rows, half), jnp.bfloat16)
         for i in range(n):
             at = slice(i * rows, (i + 1) * rows)
-            even[at, :] = jnp.concatenate([parts[i][...], pad], axis=1)
-            odd[at, :] = jnp.concatenate([pad, parts[i][...]], axis=1)
+            keys = parts[i][:rows, start : start + kdim]
+            even[at, :] = jnp.concatenate([keys, pad], axis=1)
+            odd[at, :] = jnp.concatenate([pad, keys], axis=1)
 
     allowed = (kpos_ref[...] >= first_ref[...]) & (kpos_ref[...] <= last_ref[...])
     for i, keys in enumerate((even, odd)):
@@ -350,10 +372,10 @@
 
 def attend(queries, parts, first, last, kpos):
     n = len(parts)
-    rows, kdim = parts[0].shape
+    rows, kdim = queries.shape[0], queries.shape[1] // HEADS
     wide = -(-kdim // LANES) * LANES
     return call(
-        functools.partial(attend_kernel, n),
+        functools.partial(attend_kernel, n, kdim),
         6,
         (HEADS // 2,),
         [whole(first), whole(last), whole(kpos)]
@@ -403,12 +425,23 @@
     packed = jnp.concatenate([tokens, picks], axis=0)
 
     near_parts = along_exp(packed)
+    arrived = list(near_parts)
+    if near:
+        kdim = latent_kv.shape[2]
+        keys = jnp.pad(latent_kv[0], ((0, EXTRA), (0, -kdim % LANES)))
+        near_parts[0] = jnp.concatenate([packed, keys], axis=1)
     spread = [[a] for a in near_parts]
     spread = [held + [flip(a, 2) for a in held] for held in spread]
+    behind = [(), (), (), ()]
+    if len(shifts) == 4:
+        behind = [(), (arrived[1],), (arrived[2],), (spread[0][1],)]
     spread = [held + [flip(a, 1) for a in held] for held in spread]
-    kv = [latent_kv[0]]
-    for bit in flips:
-        kv = kv + [flip(a, bit) for a in kv]
+    if near:
+        kv = spread[0]
+    else:
+        kv = [latent_kv[0]]
+        for bit in flips:
+            kv = kv + [flip(a, bit) for a in kv]
 
     lengths = doc_lengths[0]
     ends = jnp.cumsum(lengths)
@@ -425,9 +458,9 @@
     base = (exp * local).reshape(1).astype(jnp.int32)
     rw = jnp.roll(router_weight.T, -exp * local, axis=0)
     balance = None
-    gu = sort_rows(gate_up)
+    gu = sort_rows(gate_up, behind)
     groups = [[1, 2], [3, 0]] if len(shifts) == 4 else [range(len(shifts))]
-    back, before, begun = [], (), []
+    back, before, begun, far = [], (), [], []
     for n, group in enumerate(groups):
         sent = []
         for i in group:
@@ -437,17 +470,23 @@
             if row is not None:
                 balance = out[3]
         if n + 1 < len(groups):
-            after = (near_parts[groups[n + 1][0]],)
+            after = (arrived[groups[n + 1][0]],)
         else:
             after = begun
         made = experts([a[0] for a in sent], [a[1] for a in sent], gu, w_down, after)
-        before, begun = (made[0],), []
-        for i, dispatched, part in zip(group, sent, made):
-            keep, give = combine(dispatched[2], part, n_ctx)
-            got = flip(give, 1)
-            far = added(keep[:, tok_rows:], got[:, tok_rows:])
-            begun.append(far)
-            terms = [keep[:, :tok_rows], got[:, :tok_rows], flip(far, 2)]
+        before = (made[0],)
+        keep, give = combine([a[2] for a in sent], made, n_ctx, tuple(far))
+        got = flip(give, 1)
+        size = len(group) * tok_rows
+        last = n + 1 == len(groups)
+        cuts = [slice(j * tok_rows, (j + 1) * tok_rows) for j in range(len(group))]
+        crossing = cuts if last else [slice(0, size)]
+        far = [added(keep[:, size + c.start : size + c.stop], got[:, size + c.start : size + c.stop]) for c in crossing]
+        begun = far
+        far = [flip(a, 2) for a in far]
+        for j, i in enumerate(group):
+            crossed = far[j] if last else far[0][:, cuts[j]]
+            terms = [keep[:, cuts[j]], got[:, cuts[j]], crossed]
             if i:
                 back.append(shift(added(*terms), -shifts[i]))
             else:

time: 111 us -> 125 us (1.13)
  starting transfers between devices: 25.5 us -> 33.3 us
  Pallas kernels: 52.1 us -> 59 us
  other arithmetic: 6.68 us -> 11.7 us
  waiting for transfers between devices: 20.7 us -> 16.3 us
    ppermute x6, starting transfers between devices: 12.2 us -> 23.2 us  [shift(): return lax.ppermute(a, 'exp', [(i, (i + d) % n_exp) for i in range(n_exp)])]
    ppermute x23 -> x17, waiting for transfers between devices: 16.4 us -> 8.17 us  [flip(): return lax.ppermute(a, 'ctx', [(i, i ^ bit) for i in range(n_ctx)])]
    pallas_call x6 -> x7, Pallas kernels: 23.1 us -> 30 us  [the longest x4 20.3 us: sort_rows(): call(functools.partial(sort_kernel, j * local // pieces), 4, (local // pi...]
    ppermute x6, waiting for transfers between devices: 4.23 us -> 8.14 us  [shift(): return lax.ppermute(a, 'exp', [(i, (i + d) % n_exp) for i in range(n_exp)])]
    ppermute x23 -> x17, starting transfers between devices: 13.3 us -> 10.1 us  [flip(): return lax.ppermute(a, 'ctx', [(i, i ^ bit) for i in range(n_ctx)])]
    convert_element_type x8 -> x5, other arithmetic: 4.44 us -> 7.55 us  [added(): return total.astype(jnp.bfloat16)]
    unnamed x23 -> x27, local copies, waits for them, and re-layouts: 3.17 us -> 2.72 us
  transfers between devices with their start and end apart: 29 -> 23, of which waited for: 5 -> 7; matrix products, arithmetic and copies ran while one was open for 5% -> 6% of each run, Pallas kernels for 47% -> 47%
where the time goes in v6:
time: 125 us
  Pallas kernels  59 us (47%)
  starting transfers between devices  33.3 us (27%)
  waiting for transfers between devices  16.3 us (13%)
  other arithmetic  11.7 us (9%)
  local copies, waits for them, and re-layouts  3.65 us (3%)
    ppermute x6, starting transfers between devices, shift(): return lax.ppermute(a, 'exp', [(i, (i + d) % n_exp) for i in range(n_exp)])  23.2 us
    pallas_call x2, Pallas kernels, experts(): call(functools.partial(expert_kernel, n), 6, (local // group, slots // si...  21.9 us
    pallas_call x4, Pallas kernels, sort_rows(): call(functools.partial(sort_kernel, j * local // pieces), 4, (local // pi...  20.3 us
    ppermute x17, starting transfers between devices, flip(): return lax.ppermute(a, 'ctx', [(i, i ^ bit) for i in range(n_ctx)])  10.1 us
    ppermute x17, waiting for transfers between devices, flip(): return lax.ppermute(a, 'ctx', [(i, i ^ bit) for i in range(n_ctx)])  8.17 us
    ppermute x6, waiting for transfers between devices, shift(): return lax.ppermute(a, 'exp', [(i, (i + d) % n_exp) for i in range(n_exp)])  8.14 us
    convert_element_type x5, other arithmetic, added(): return total.astype(jnp.bfloat16)  7.55 us
    pallas_call x1, Pallas kernels, attend(): call(functools.partial(attend_kernel, n, kdim), 6, (HEADS // 2,), [whole(...  7.19 us
  transfers between devices with their start and end apart: 23, of which 7 were waited for; matrix products, arithmetic and copies ran while one was open for 6% of the time, Pallas kernels for 47%

profile of v6, /device:TPU:0, one launch (start us, length us, event | category | flops | bytes accessed | tf_op | source)
XLA Modules:
  0.0 124.8 jit_solution(18187007746798927138)
XLA Ops:
  2.3 3.1 %collective-permute-start.3 = (bf16[144,1024]{1,0:T(8,128)(2,1)S(1)}, bf16[144,1024]{1,0:T(8,128)(2,1)S(1)}, u32[]{:S(2)}, u32[]{:S(2)}) collective-permute-start(bf16[144,1024]{1,0:T(8,128)(2,1)S(1)} %pad_maximum_fusion), channel_id=1, source_target_pairs={{0,1},{1,2},{2,3},{3,0},{4,5},{5,6},{6,7},{7,4},{8,9},{9,10},{10,1... | collective-permute-start | bytes 884744 | tf_op jit(solution)/shard_map/ppermute | solution.py:412
  5.4 2.1 %collective-permute-start.7 = (bf16[144,1024]{1,0:T(8,128)(2,1)S(1)}, bf16[144,1024]{1,0:T(8,128)(2,1)S(1)}, u32[]{:S(2)}, u32[]{:S(2)}) collective-permute-start(bf16[144,1024]{1,0:T(8,128)(2,1)S(1)} %pad_maximum_fusion), channel_id=1, source_target_pairs={{0,3},{1,0},{2,1},{3,2},{4,7},{5,4},{6,5},{7,6},{8,11},{9,8},{10,9... | collective-permute-start | bytes 884744 | tf_op jit(solution)/shard_map/ppermute | solution.py:412
  10.5 1.6 %collective-permute-start = (bf16[144,1664]{1,0:T(8,128)(2,1)S(1)}, bf16[144,1664]{1,0:T(8,128)(2,1)S(1)}, u32[]{:S(2)}, u32[]{:S(2)}) collective-permute-start(bf16[144,1664]{1,0:T(8,128)(2,1)S(1)} %fusion.1.refs_0_), channel_id=1, source_target_pairs={{0,8},{4,12},{8,0},{12,4},{1,9},{5,13},{9,1},{13,5},{2,10},{6,14},... | collective-permute-start | bytes 1437704 | tf_op jit(solution)/shard_map/ppermute | solution.py:409
  13.1 5.1 %sort.4.refs_0_ = bf16[16,2,176,1024]{3,2,1,0:T(8,128)(2,1)} custom-call(bf16[16,2816,128]{2,1,0:T(8,128)(2,1)} %bitcast.44), custom_call_target="tpu_custom_call" | custom-call | flops 4400000000 | tf_op jit(solution)/shard_map/sort/pallas_call | solution.py:235
  18.8 5.1 %sort.5.refs_0_ = bf16[16,2,176,1024]{3,2,1,0:T(8,128)(2,1)} custom-call(bf16[16,2816,128]{2,1,0:T(8,128)(2,1)} %bitcast.45, bf16[16,2,176,1024]{3,2,1,0:T(8,128)(2,1)} %sort.4.refs_0_, bf16[144,1024]{1,0:T(8,128)(2,1)S(1)} %collective-permute-done.3.refs_0_.refs_1_), custom_call_target="tpu_custom_call", output_to_operand_aliasing={{}: (1, {})} | custom-call | flops 4400000000 | tf_op jit(solution)/shard_map/sort/pallas_call | solution.py:235
  24.2 5.1 %sort.6.refs_0_ = bf16[16,2,176,1024]{3,2,1,0:T(8,128)(2,1)} custom-call(bf16[16,2816,128]{2,1,0:T(8,128)(2,1)} %bitcast.46, bf16[16,2,176,1024]{3,2,1,0:T(8,128)(2,1)} %sort.5.refs_0_, bf16[144,1024]{1,0:T(8,128)(2,1)S(1)} %collective-permute-done.7.refs_0_.refs_1_), custom_call_target="tpu_custom_call", output_to_operand_aliasing={{}: (1, {})} | custom-call | flops 4400000000 | tf_op jit(solution)/shard_map/sort/pallas_call | solution.py:235
  30.9 5.1 %sort.7.refs_4_ = bf16[16,2,176,1024]{3,2,1,0:T(8,128)(2,1)} custom-call(bf16[16,2816,128]{2,1,0:T(8,128)(2,1)} %bitcast.47, bf16[16,2,176,1024]{3,2,1,0:T(8,128)(2,1)} %sort.6.refs_0_, bf16[144,1664]{1,0:T(8,128)(2,1)S(1)} %collective-permute-done.refs_1_), custom_call_target="tpu_custom_call", output_to_operand_aliasing={{}: (1, {})} | custom-call | flops 4400000000 | tf_op jit(solution)/shard_map/sort/pallas_call | solution.py:235
  41.7 11.1 %experts.2 = (bf16[16,64,1024]{2,1,0:T(8,128)(2,1)S(1)}, bf16[16,64,1024]{2,1,0:T(8,128)(2,1)S(1)}) custom-call(bf16[16,64,1024]{2,1,0:T(8,128)(2,1)S(1)} %get-tuple-element.26.refs_0_, bf16[16,64,1024]{2,1,0:T(8,128)(2,1)S(1)} %get-tuple-element.27.refs_1_, f32[16,64,128]{2,1,0:T(8,128)S(1)} %get-tuple-element.28.refs_2_, ...), custom_call_target="tpu_custom_call" | custom-call | flops 6600000000 | tf_op jit(solution)/shard_map/experts/pallas_call | solution.py:293
  52.8 1.7 %combine.2 = (bf16[1,512,1024]{2,1,0:T(8,128)(2,1)S(1)}, bf16[1,512,1024]{2,1,0:T(8,128)(2,1)}) custom-call(bf16[4,256,128]{2,1,0:T(8,128)(2,1)S(1)} %get-tuple-element.24.refs_0_, bf16[4,256,128]{2,1,0:T(8,128)(2,1)S(1)} %get-tuple-element.25.refs_1_, bf16[16,64,1024]{2,1,0:T(8,128)(2,1)S(1)} %get-tuple-element.30.refs_2_.refs_4_, ...), custom_call_target="tpu_custom_call" | custom-call | flops 2200000000 | tf_op jit(solution)/shard_map/combine/pallas_call | solution.py:329
  55.9 1.8 %collective-permute-done.17.refs_2_ = bf16[144,1024]{1,0:T(8,128)(2,1)S(1)} collective-permute-done((bf16[144,1024]{1,0:T(8,128)(2,1)S(1)}, bf16[144,1024]{1,0:T(8,128)(2,1)S(1)}, u32[]{:S(2)}, u32[]{:S(2)}) %collective-permute-start.17) | collective-permute-done | bytes 294944 | tf_op jit(solution)/shard_map/ppermute | solution.py:409
  58.1 1.6 %copy-done.6 = bf16[16,64,1024]{2,1,0:T(8,128)(2,1)S(1)} copy-done((bf16[16,64,1024]{2,1,0:T(8,128)(2,1)S(1)}, bf16[16,64,1024]{2,1,0:T(8,128)(2,1)}, u32[]{:S(2)}) %copy-start.6) | copy-done | bytes 2097176
  61.3 2.7 %dispatch.7 = (bf16[16,64,1024]{2,1,0:T(8,128)(2,1)S(1)}, f32[16,64,128]{2,1,0:T(8,128)S(1)}, bf16[4,256,128]{2,1,0:T(8,128)(2,1)S(1)}, f32[8,128]{1,0:T(8,128)S(1)}) custom-call(s32[1]{0:T(128)} %bitcast.15.base_ref, bf16[64,1024]{1,0:T(8,128)(2,1)S(1)} %fusion.2.rw_ref, bf16[144,1664]{1,0:T(8,128)(2,1)S(1)} %fusion.1.refs_0_, ...), custom_call_target="tpu_custom_call" | custom-call | flops 3300000000 | tf_op jit(solution)/shard_map/dispatch/pallas_call | solution.py:142
  65.2 1.8 %collective-permute-start.13 = (bf16[1,256,1024]{2,1,0:T(8,128)(2,1)S(1)}, bf16[1,256,1024]{2,1,0:T(8,128)(2,1)S(1)}, u32[]{:S(2)}, u32[]{:S(2)}) collective-permute-start(bf16[1,256,1024]{2,1,0:T(8,128)(2,1)S(1)} %add_convert_fusion.refs_6_), channel_id=1, source_target_pairs={{0,8},{4,12},{8,0},{12,4},{1,9},{5,13},{9,1},{13,5},{2,10},{6,14},... | collective-permute-start | bytes 1572872 | tf_op jit(solution)/shard_map/ppermute | solution.py:409
  67.0 10.8 %experts.3 = (bf16[16,64,1024]{2,1,0:T(8,128)(2,1)S(1)}, bf16[16,64,1024]{2,1,0:T(8,128)(2,1)S(1)}) custom-call(bf16[16,64,1024]{2,1,0:T(8,128)(2,1)S(1)} %get-tuple-element.36.refs_0_, bf16[16,64,1024]{2,1,0:T(8,128)(2,1)S(1)} %get-tuple-element.37.refs_1_, f32[16,64,128]{2,1,0:T(8,128)S(1)} %get-tuple-element.38.refs_2_, ...), custom_call_target="tpu_custom_call" | custom-call | flops 6600000000 | tf_op jit(solution)/shard_map/experts/pallas_call | solution.py:293
  77.9 1.6 %collective-permute-done.13.refs_4_ = bf16[1,256,1024]{2,1,0:T(8,128)(2,1)S(1)} collective-permute-done((bf16[1,256,1024]{2,1,0:T(8,128)(2,1)S(1)}, bf16[1,256,1024]{2,1,0:T(8,128)(2,1)S(1)}, u32[]{:S(2)}, u32[]{:S(2)}) %collective-permute-start.13) | collective-permute-done | bytes 524320 | tf_op jit(solution)/shard_map/ppermute | solution.py:409
  80.3 2.8 %collective-permute-done.19 = bf16[1,512,1024]{2,1,0:T(8,128)(2,1)} collective-permute-done((bf16[1,512,1024]{2,1,0:T(8,128)(2,1)S(1)}, bf16[1,512,1024]{2,1,0:T(8,128)(2,1)}, u32[]{:S(2)}, u32[]{:S(2)}) %collective-permute-start.19) | collective-permute-done | bytes 1048608 | tf_op jit(solution)/shard_map/ppermute | solution.py:409
  83.1 1.7 %add_convert_fusion.4 = bf16[1,128,1024]{2,1,0:T(8,128)(2,1)} fusion(bf16[1,512,1024]{2,1,0:T(8,128)(2,1)} %collective-permute-done.19, bf16[1,512,1024]{2,1,0:T(8,128)(2,1)S(1)} %get-tuple-element.42), kind=kLoop, calls=%fused_computation.6 | loop fusion | flops 524288 | bytes 786432 | tf_op jit(solution)/shard_map/convert_element_type | solution.py:395
  84.8 1.7 %collective-permute-start.20 = (bf16[1,128,1024]{2,1,0:T(8,128)(2,1)}, bf16[1,128,1024]{2,1,0:T(8,128)(2,1)S(1)}, u32[]{:S(2)}, u32[]{:S(2)}) collective-permute-start(bf16[1,128,1024]{2,1,0:T(8,128)(2,1)} %add_convert_fusion.4), channel_id=1, source_target_pairs={{0,8},{4,12},{8,0},{12,4},{1,9},{5,13},{9,1},{13,5},{2,10},{6,14},... | collective-permute-start | bytes 786440 | tf_op jit(solution)/shard_map/ppermute | solution.py:409
  88.3 4.2 %collective-permute-start.14 = (bf16[1,128,1024]{2,1,0:T(8,128)(2,1)S(1)}, bf16[1,128,1024]{2,1,0:T(8,128)(2,1)S(1)}, u32[]{:S(2)}, u32[]{:S(2)}) collective-permute-start(bf16[1,128,1024]{2,1,0:T(8,128)(2,1)S(1)} %get-tuple-element.45), channel_id=1, source_target_pairs={{0,3},{1,0},{2,1},{3,2},{4,7},{5,4},{6,5},{7,6},{8,11},{9,8},{10,9... | collective-permute-start | bytes 786440 | tf_op jit(solution)/shard_map/ppermute | solution.py:412
  92.6 4.5 %collective-permute-start.15 = (bf16[1,128,1024]{2,1,0:T(8,128)(2,1)S(1)}, bf16[1,128,1024]{2,1,0:T(8,128)(2,1)S(1)}, u32[]{:S(2)}, u32[]{:S(2)}) collective-permute-start(bf16[1,128,1024]{2,1,0:T(8,128)(2,1)S(1)} %get-tuple-element.46), channel_id=1, source_target_pairs={{0,1},{1,2},{2,3},{3,0},{4,5},{5,6},{6,7},{7,4},{8,9},{9,10},{10,1... | collective-permute-start | bytes 786440 | tf_op jit(solution)/shard_map/ppermute | solution.py:412
  98.3 8.3 %collective-permute-start.21 = (bf16[1,128,1024]{2,1,0:T(8,128)(2,1)S(1)}, bf16[1,128,1024]{2,1,0:T(8,128)(2,1)S(1)}, u32[]{:S(2)}, u32[]{:S(2)}) collective-permute-start(bf16[1,128,1024]{2,1,0:T(8,128)(2,1)S(1)} %get-tuple-element.47), channel_id=1, source_target_pairs={{0,2},{1,3},{2,0},{3,1},{4,6},{5,7},{6,4},{7,5},{8,10},{9,11},{10,... | collective-permute-start | bytes 786440 | tf_op jit(solution)/shard_map/ppermute | solution.py:412
  107.0 7.2 %attention.1 = bf16[128,4096]{1,0:T(8,128)(2,1)} custom-call(s32[128,1]{1,0:T(8,128)S(1)} %copy.23.first_ref, s32[128,1]{1,0:T(8,128)S(1)} %copy.24.last_ref, s32[1,512]{1,0:T(1,128)S(1)} %bitcast.37, bf16[128,4608]{1,0:T(8,128)(2,1)S(1)} %bitcast.43, bf16[144,1664]{1,0:T(8,128)(2,1)S(1)} %fusion.1.refs_0_, bf16[144,1664]{1,0:T(8,128)(2,1)S(1)} %copy-done.1, ...), custom_call_target="tpu_custom_call" | custom-call | flops 6600000000 | tf_op jit(solution)/shard_map/attention/pallas_call | solution.py:377
  114.8 8.1 %collective-permute-done.21 = bf16[1,128,1024]{2,1,0:T(8,128)(2,1)S(1)} collective-permute-done((bf16[1,128,1024]{2,1,0:T(8,128)(2,1)S(1)}, bf16[1,128,1024]{2,1,0:T(8,128)(2,1)S(1)}, u32[]{:S(2)}, u32[]{:S(2)}) %collective-permute-start.21) | collective-permute-done | bytes 262176 | tf_op jit(solution)/shard_map/ppermute | solution.py:412
  122.9 1.9 %add_convert_fusion.1 = bf16[1,128,1024]{2,1,0:T(8,128)(2,1)} fusion(bf16[1,128,1024]{2,1,0:T(8,128)(2,1)S(1)} %collective-permute-done.22, bf16[1,128,1024]{2,1,0:T(8,128)(2,1)S(1)} %collective-permute-done.21, bf16[1,128,1024]{2,1,0:T(8,128)(2,1)S(1)} %collective-permute-done.15, bf16[1,128,1024]{2,1,0:T(8,128)(2,1)S(1)} %collective-permute-done.14, ...), kind=kLoop, calls=%fused_computation.3 | loop fusion | flops 1572864 | bytes 1835008 | tf_op jit(solution)/shard_map/convert_element_type | solution.py:395
  (85 shorter events, 23.3 us)
Async XLA Ops:
  2.3 15.8 %collective-permute-start.3 = (bf16[144,1024]{1,0:T(8,128)(2,1)S(1)}, bf16[144,1024]{1,0:T(8,128)(2,1)S(1)}, u32[]{:S(2)}, u32[]{:S(2)}) collective-permute-start(bf16[144,1024]{1,0:T(8,128)(2,1)S(1)} %pad_maximum_fusion), channel_id=1, source_target_pairs={{0,1},{1,2},{2,3},{3,0},{4,5},{5,6},{6,7},{7,4},{8,9},{9,10},{10,1... | collective-permute-start | bytes 884744 | tf_op jit(solution)/shard_map/ppermute | solution.py:412
  5.4 18.5 %collective-permute-start.7 = (bf16[144,1024]{1,0:T(8,128)(2,1)S(1)}, bf16[144,1024]{1,0:T(8,128)(2,1)S(1)}, u32[]{:S(2)}, u32[]{:S(2)}) collective-permute-start(bf16[144,1024]{1,0:T(8,128)(2,1)S(1)} %pad_maximum_fusion), channel_id=1, source_target_pairs={{0,3},{1,0},{2,1},{3,2},{4,7},{5,4},{6,5},{7,6},{8,11},{9,8},{10,9... | collective-permute-start | bytes 884744 | tf_op jit(solution)/shard_map/ppermute | solution.py:412
  7.5 28.5 %collective-permute-start.11 = (bf16[144,1024]{1,0:T(8,128)(2,1)S(1)}, bf16[144,1024]{1,0:T(8,128)(2,1)S(1)}, u32[]{:S(2)}, u32[]{:S(2)}) collective-permute-start(bf16[144,1024]{1,0:T(8,128)(2,1)S(1)} %pad_maximum_fusion), channel_id=1, source_target_pairs={{0,2},{1,3},{2,0},{3,1},{4,6},{5,7},{6,4},{7,5},{8,10},{9,11},{10,... | collective-permute-start | bytes 884744 | tf_op jit(solution)/shard_map/ppermute | solution.py:412
  10.5 18.8 %collective-permute-start = (bf16[144,1664]{1,0:T(8,128)(2,1)S(1)}, bf16[144,1664]{1,0:T(8,128)(2,1)S(1)}, u32[]{:S(2)}, u32[]{:S(2)}) collective-permute-start(bf16[144,1664]{1,0:T(8,128)(2,1)S(1)} %fusion.1.refs_0_), channel_id=1, source_target_pairs={{0,8},{4,12},{8,0},{12,4},{1,9},{5,13},{9,1},{13,5},{2,10},{6,14},... | collective-permute-start | bytes 1437704 | tf_op jit(solution)/shard_map/ppermute | solution.py:409
  12.0 49.1 %collective-permute-start.1 = (bf16[144,1664]{1,0:T(8,128)(2,1)S(1)}, bf16[144,1664]{1,0:T(8,128)(2,1)}, u32[]{:S(2)}, u32[]{:S(2)}) collective-permute-start(bf16[144,1664]{1,0:T(8,128)(2,1)S(1)} %fusion.1.refs_0_), channel_id=1, source_target_pairs={{0,4},{4,0},{8,12},{12,8},{1,5},{5,1},{9,13},{13,9},{2,6},{6,2},{1... | collective-permute-start | bytes 1437704 | tf_op jit(solution)/shard_map/ppermute | solution.py:409
  18.2 12.7 %collective-permute-start.4 = (bf16[144,1024]{1,0:T(8,128)(2,1)S(1)}, bf16[144,1024]{1,0:T(8,128)(2,1)S(1)}, u32[]{:S(2)}, u32[]{:S(2)}) collective-permute-start(bf16[144,1024]{1,0:T(8,128)(2,1)S(1)} %collective-permute-done.3.refs_0_.refs_1_), channel_id=1, source_target_pairs={{0,8},{4,12},{8,0},{12,4},{1,9},{5,13},{9,1},{13,5},{2,10},{6,14},... | collective-permute-start | bytes 884744 | tf_op jit(solution)/shard_map/ppermute | solution.py:409
  23.9 12.7 %collective-permute-start.5 = (bf16[144,1024]{1,0:T(8,128)(2,1)S(1)}, bf16[144,1024]{1,0:T(8,128)(2,1)S(1)}, u32[]{:S(2)}, u32[]{:S(2)}) collective-permute-start(bf16[144,1024]{1,0:T(8,128)(2,1)S(1)} %collective-permute-done.3.refs_0_.refs_1_), channel_id=1, source_target_pairs={{0,4},{4,0},{8,12},{12,8},{1,5},{5,1},{9,13},{13,9},{2,6},{6,2},{1... | collective-permute-start | bytes 884744 | tf_op jit(solution)/shard_map/ppermute | solution.py:409
  29.3 32.0 %copy-start = (bf16[144,1664]{1,0:T(8,128)(2,1)}, bf16[144,1664]{1,0:T(8,128)(2,1)S(1)}, u32[]{:S(2)}) copy-start(bf16[144,1664]{1,0:T(8,128)(2,1)S(1)} %collective-permute-done.refs_1_) | copy-start | bytes 1437700
  29.3 9.3 %collective-permute-start.8 = (bf16[144,1024]{1,0:T(8,128)(2,1)S(1)}, bf16[144,1024]{1,0:T(8,128)(2,1)S(1)}, u32[]{:S(2)}, u32[]{:S(2)}) collective-permute-start(bf16[144,1024]{1,0:T(8,128)(2,1)S(1)} %collective-permute-done.7.refs_0_.refs_1_), channel_id=1, source_target_pairs={{0,8},{4,12},{8,0},{12,4},{1,9},{5,13},{9,1},{13,5},{2,10},{6,14},... | collective-permute-start | bytes 884744 | tf_op jit(solution)/shard_map/ppermute | solution.py:409
  30.9 7.7 %collective-permute-start.6 = (bf16[144,1024]{1,0:T(8,128)(2,1)S(1)}, bf16[144,1024]{1,0:T(8,128)(2,1)S(1)}, u32[]{:S(2)}, u32[]{:S(2)}) collective-permute-start(bf16[144,1024]{1,0:T(8,128)(2,1)S(1)} %collective-permute-done.4.refs_1_), channel_id=1, source_target_pairs={{0,4},{4,0},{8,12},{12,8},{1,5},{5,1},{9,13},{13,9},{2,6},{6,2},{1... | collective-permute-start | bytes 884744 | tf_op jit(solution)/shard_map/ppermute | solution.py:409
  36.0 4.1 %collective-permute-start.9 = (bf16[144,1024]{1,0:T(8,128)(2,1)S(1)}, bf16[144,1024]{1,0:T(8,128)(2,1)S(1)}, u32[]{:S(2)}, u32[]{:S(2)}) collective-permute-start(bf16[144,1024]{1,0:T(8,128)(2,1)S(1)} %collective-permute-done.7.refs_0_.refs_1_), channel_id=1, source_target_pairs={{0,4},{4,0},{8,12},{12,8},{1,5},{5,1},{9,13},{13,9},{2,6},{6,2},{1... | collective-permute-start | bytes 884744 | tf_op jit(solution)/shard_map/ppermute | solution.py:409
  36.6 18.7 %collective-permute-start.16 = (bf16[144,1024]{1,0:T(8,128)(2,1)S(1)}, bf16[144,1024]{1,0:T(8,128)(2,1)S(1)}, u32[]{:S(2)}, u32[]{:S(2)}) collective-permute-start(bf16[144,1024]{1,0:T(8,128)(2,1)S(1)} %collective-permute-done.11.refs_6_.refs_0_), channel_id=1, source_target_pairs={{0,8},{4,12},{8,0},{12,4},{1,9},{5,13},{9,1},{13,5},{2,10},{6,14},... | collective-permute-start | bytes 884744 | tf_op jit(solution)/shard_map/ppermute | solution.py:409
  38.6 1.6 %collective-permute-start.10 = (bf16[144,1024]{1,0:T(8,128)(2,1)S(1)}, bf16[144,1024]{1,0:T(8,128)(2,1)S(1)}, u32[]{:S(2)}, u32[]{:S(2)}) collective-permute-start(bf16[144,1024]{1,0:T(8,128)(2,1)S(1)} %collective-permute-done.8.refs_1_), channel_id=1, source_target_pairs={{0,4},{4,0},{8,12},{12,8},{1,5},{5,1},{9,13},{13,9},{2,6},{6,2},{1... | collective-permute-start | bytes 884744 | tf_op jit(solution)/shard_map/ppermute | solution.py:409
  54.5 9.4 %collective-permute-start.12 = (bf16[1,512,1024]{2,1,0:T(8,128)(2,1)}, bf16[1,512,1024]{2,1,0:T(8,128)(2,1)}, u32[]{:S(2)}, u32[]{:S(2)}) collective-permute-start(bf16[1,512,1024]{2,1,0:T(8,128)(2,1)} %get-tuple-element.33), channel_id=1, source_target_pairs={{0,4},{4,0},{8,12},{12,8},{1,5},{5,1},{9,13},{13,9},{2,6},{6,2},{1... | collective-permute-start | bytes 3145736 | tf_op jit(solution)/shard_map/ppermute | solution.py:409
  55.2 2.5 %collective-permute-start.17 = (bf16[144,1024]{1,0:T(8,128)(2,1)S(1)}, bf16[144,1024]{1,0:T(8,128)(2,1)S(1)}, u32[]{:S(2)}, u32[]{:S(2)}) collective-permute-start(bf16[144,1024]{1,0:T(8,128)(2,1)S(1)} %collective-permute-done.11.refs_6_.refs_0_), channel_id=1, source_target_pairs={{0,4},{4,0},{8,12},{12,8},{1,5},{5,1},{9,13},{13,9},{2,6},{6,2},{1... | collective-permute-start | bytes 884744 | tf_op jit(solution)/shard_map/ppermute | solution.py:409
  55.3 2.8 %collective-permute-start.18 = (bf16[144,1024]{1,0:T(8,128)(2,1)S(1)}, bf16[144,1024]{1,0:T(8,128)(2,1)S(1)}, u32[]{:S(2)}, u32[]{:S(2)}) collective-permute-start(bf16[144,1024]{1,0:T(8,128)(2,1)S(1)} %collective-permute-done.16.refs_1_), channel_id=1, source_target_pairs={{0,4},{4,0},{8,12},{12,8},{1,5},{5,1},{9,13},{13,9},{2,6},{6,2},{1... | collective-permute-start | bytes 884744 | tf_op jit(solution)/shard_map/ppermute | solution.py:409
  55.8 5.4 %collective-permute-start.2 = (bf16[144,1664]{1,0:T(8,128)(2,1)S(1)}, bf16[144,1664]{1,0:T(8,128)(2,1)S(1)}, u32[]{:S(2)}, u32[]{:S(2)}) collective-permute-start(bf16[144,1664]{1,0:T(8,128)(2,1)S(1)} %collective-permute-done.refs_1_), channel_id=1, source_target_pairs={{0,4},{4,0},{8,12},{12,8},{1,5},{5,1},{9,13},{13,9},{2,6},{6,2},{1... | collective-permute-start | bytes 1437704 | tf_op jit(solution)/shard_map/ppermute | solution.py:409
  65.2 14.3 %collective-permute-start.13 = (bf16[1,256,1024]{2,1,0:T(8,128)(2,1)S(1)}, bf16[1,256,1024]{2,1,0:T(8,128)(2,1)S(1)}, u32[]{:S(2)}, u32[]{:S(2)}) collective-permute-start(bf16[1,256,1024]{2,1,0:T(8,128)(2,1)S(1)} %add_convert_fusion.refs_6_), channel_id=1, source_target_pairs={{0,8},{4,12},{8,0},{12,4},{1,9},{5,13},{9,1},{13,5},{2,10},{6,14},... | collective-permute-start | bytes 1572872 | tf_op jit(solution)/shard_map/ppermute | solution.py:409
  80.2 2.9 %collective-permute-start.19 = (bf16[1,512,1024]{2,1,0:T(8,128)(2,1)S(1)}, bf16[1,512,1024]{2,1,0:T(8,128)(2,1)}, u32[]{:S(2)}, u32[]{:S(2)}) collective-permute-start(bf16[1,512,1024]{2,1,0:T(8,128)(2,1)S(1)} %get-tuple-element.43), channel_id=1, source_target_pairs={{0,4},{4,0},{8,12},{12,8},{1,5},{5,1},{9,13},{13,9},{2,6},{6,2},{1... | collective-permute-start | bytes 3145736 | tf_op jit(solution)/shard_map/ppermute | solution.py:409
  84.8 12.3 %collective-permute-start.20 = (bf16[1,128,1024]{2,1,0:T(8,128)(2,1)}, bf16[1,128,1024]{2,1,0:T(8,128)(2,1)S(1)}, u32[]{:S(2)}, u32[]{:S(2)}) collective-permute-start(bf16[1,128,1024]{2,1,0:T(8,128)(2,1)} %add_convert_fusion.4), channel_id=1, source_target_pairs={{0,8},{4,12},{8,0},{12,4},{1,9},{5,13},{9,1},{13,5},{2,10},{6,14},... | collective-permute-start | bytes 786440 | tf_op jit(solution)/shard_map/ppermute | solution.py:409
  88.3 26.4 %collective-permute-start.14 = (bf16[1,128,1024]{2,1,0:T(8,128)(2,1)S(1)}, bf16[1,128,1024]{2,1,0:T(8,128)(2,1)S(1)}, u32[]{:S(2)}, u32[]{:S(2)}) collective-permute-start(bf16[1,128,1024]{2,1,0:T(8,128)(2,1)S(1)} %get-tuple-element.45), channel_id=1, source_target_pairs={{0,3},{1,0},{2,1},{3,2},{4,7},{5,4},{6,5},{7,6},{8,11},{9,8},{10,9... | collective-permute-start | bytes 786440 | tf_op jit(solution)/shard_map/ppermute | solution.py:412
  92.6 22.2 %collective-permute-start.15 = (bf16[1,128,1024]{2,1,0:T(8,128)(2,1)S(1)}, bf16[1,128,1024]{2,1,0:T(8,128)(2,1)S(1)}, u32[]{:S(2)}, u32[]{:S(2)}) collective-permute-start(bf16[1,128,1024]{2,1,0:T(8,128)(2,1)S(1)} %get-tuple-element.46), channel_id=1, source_target_pairs={{0,1},{1,2},{2,3},{3,0},{4,5},{5,6},{6,7},{7,4},{8,9},{9,10},{10,1... | collective-permute-start | bytes 786440 | tf_op jit(solution)/shard_map/ppermute | solution.py:412
  98.3 24.6 %collective-permute-start.21 = (bf16[1,128,1024]{2,1,0:T(8,128)(2,1)S(1)}, bf16[1,128,1024]{2,1,0:T(8,128)(2,1)S(1)}, u32[]{:S(2)}, u32[]{:S(2)}) collective-permute-start(bf16[1,128,1024]{2,1,0:T(8,128)(2,1)S(1)} %get-tuple-element.47), channel_id=1, source_target_pairs={{0,2},{1,3},{2,0},{3,1},{4,6},{5,7},{6,4},{7,5},{8,10},{9,11},{10,... | collective-permute-start | bytes 786440 | tf_op jit(solution)/shard_map/ppermute | solution.py:412
  106.7 16.2 %collective-permute-start.22 = (bf16[1,128,1024]{2,1,0:T(8,128)(2,1)S(1)}, bf16[1,128,1024]{2,1,0:T(8,128)(2,1)S(1)}, u32[]{:S(2)}, u32[]{:S(2)}) collective-permute-start(bf16[1,128,1024]{2,1,0:T(8,128)(2,1)S(1)} %get-tuple-element.48), channel_id=1, source_target_pairs={{0,8},{4,12},{8,0},{12,4},{1,9},{5,13},{9,1},{13,5},{2,10},{6,14},... | collective-permute-start | bytes 786440 | tf_op jit(solution)/shard_map/ppermute | solution.py:409
  (11 other events, 86.4 us)

commit v7 on v6

--- a/solution.py
+++ b/solution.py
@@ -400,8 +400,8 @@
     n_ctx, n_exp = lax.axis_size("ctx"), lax.axis_size("exp")
     ctx, exp = lax.axis_index("ctx"), lax.axis_index("exp")
     local = gate_up.shape[0]
-    near = n_exp <= 4
-    shifts = [0, 1, 3, 2][:n_exp] if near else [0]
+    near = n_exp == 4
+    shifts = [0, 1, 3, 2] if near else [0]
     flips = (2, 1)
     tokens = hidden_in[0]
 
@@ -409,11 +409,12 @@
         return lax.ppermute(a, "ctx", [(i, i ^ bit) for i in range(n_ctx)])
 
     def shift(a, d):
-        return lax.ppermute(a, "exp", [(i, (i + d) % n_exp) for i in range(n_exp)])
+        return lax.ppermute(a, "exp", [(i, i ^ d) for i in range(n_exp)])
 
     def along_exp(a):
         if near:
-            return [a if d == 0 else shift(a, d) for d in shifts]
+            beside, across = shift(a, 1), shift(a, 3)
+            return [a, beside, across, shift(across, 1)]
         return [lax.all_gather(a, "exp", axis=0, tiled=True)]
 
     masks = [0, 2, 1, 3]
@@ -434,7 +435,7 @@
     spread = [held + [flip(a, 2) for a in held] for held in spread]
     behind = [(), (), (), ()]
     if len(shifts) == 4:
-        behind = [(), (arrived[1],), (arrived[2],), (spread[0][1],)]
+        behind = [(), (arrived[1],), (arrived[2],), (arrived[3],)]
     spread = [held + [flip(a, 1) for a in held] for held in spread]
     if near:
         kv = spread[0]
@@ -461,6 +462,7 @@
     gu = sort_rows(gate_up, behind)
     groups = [[1, 2], [3, 0]] if len(shifts) == 4 else [range(len(shifts))]
     back, before, begun, far = [], (), [], []
+    late = (spread[3][1],) if near else ()
     for n, group in enumerate(groups):
         sent = []
         for i in group:
@@ -475,7 +477,7 @@
             after = begun
         made = experts([a[0] for a in sent], [a[1] for a in sent], gu, w_down, after)
         before = (made[0],)
-        keep, give = combine([a[2] for a in sent], made, n_ctx, tuple(far))
+        keep, give = combine([a[2] for a in sent], made, n_ctx, tuple(far) if n else late)
         got = flip(give, 1)
         size = len(group) * tok_rows
         last = n + 1 == len(groups)
@@ -488,7 +490,7 @@
             crossed = far[j] if last else far[0][:, cuts[j]]
             terms = [keep[:, cuts[j]], got[:, cuts[j]], crossed]
             if i:
-                back.append(shift(added(*terms), -shifts[i]))
+                back.append(shift(added(*terms), shifts[i]))
             else:
                 back = back + terms
     if near:

time: 125 us -> 116 us (0.928)
  starting transfers between devices: 33.3 us -> 27 us
  local copies, waits for them, and re-layouts: 3.65 us -> 2.1 us
  waiting for transfers between devices: 16.3 us -> 14.9 us
    ppermute x6, starting transfers between devices: 23.2 us -> 17.1 us  [shift(): return lax.ppermute(a, 'exp', [(i, i ^ d) for i in range(n_exp)])]
    ppermute x17, waiting for transfers between devices: 8.17 us -> 5.38 us  [flip(): return lax.ppermute(a, 'ctx', [(i, i ^ bit) for i in range(n_ctx)])]
    unnamed x27 -> x23, local copies, waits for them, and re-layouts: 2.72 us -> 1.16 us
    ppermute x6, waiting for transfers between devices: 8.14 us -> 9.54 us  [shift(): return lax.ppermute(a, 'exp', [(i, i ^ d) for i in range(n_exp)])]
  transfers between devices with their start and end apart: 23 -> 23, of which waited for: 7 -> 4; matrix products, arithmetic and copies ran while one was open for 6% -> 6% of each run, Pallas kernels for 47% -> 51%
where the time goes in v7:
time: 116 us
  Pallas kernels  59.3 us (51%)
  starting transfers between devices  27 us (23%)
  waiting for transfers between devices  14.9 us (13%)
  other arithmetic  11.7 us (10%)
  local copies, waits for them, and re-layouts  2.1 us (2%)
    pallas_call x2, Pallas kernels, experts(): call(functools.partial(expert_kernel, n), 6, (local // group, slots // si...  21.9 us
    pallas_call x4, Pallas kernels, sort_rows(): call(functools.partial(sort_kernel, j * local // pieces), 4, (local // pi...  20.4 us
    ppermute x6, starting transfers between devices, shift(): return lax.ppermute(a, 'exp', [(i, i ^ d) for i in range(n_exp)])  17.1 us
    ppermute x17, starting transfers between devices, flip(): return lax.ppermute(a, 'ctx', [(i, i ^ bit) for i in range(n_ctx)])  9.89 us
    ppermute x6, waiting for transfers between devices, shift(): return lax.ppermute(a, 'exp', [(i, i ^ d) for i in range(n_exp)])  9.54 us
    convert_element_type x5, other arithmetic, added(): return total.astype(jnp.bfloat16)  7.53 us
    pallas_call x1, Pallas kernels, attend(): call(functools.partial(attend_kernel, n, kdim), 6, (HEADS // 2,), [whole(...  7.35 us
    pallas_call x4, Pallas kernels, dispatch(): call(functools.partial(dispatch_kernel, n_parts, n_parts if row is not No...  7.24 us
  transfers between devices with their start and end apart: 23, of which 4 were waited for; matrix products, arithmetic and copies ran while one was open for 6% of the time, Pallas kernels for 51%

profile of v7, /device:TPU:0, one launch (start us, length us, event | category | flops | bytes accessed | tf_op | source)
XLA Modules:
  0.0 115.9 jit_solution(3991339169548780525)
XLA Ops:
  2.3 3.1 %collective-permute-start.3 = (bf16[144,1024]{1,0:T(8,128)(2,1)S(1)}, bf16[144,1024]{1,0:T(8,128)(2,1)S(1)}, u32[]{:S(2)}, u32[]{:S(2)}) collective-permute-start(bf16[144,1024]{1,0:T(8,128)(2,1)S(1)} %pad_maximum_fusion), channel_id=1, source_target_pairs={{0,1},{1,0},{2,3},{3,2},{4,5},{5,4},{6,7},{7,6},{8,9},{9,8},{10,11... | collective-permute-start | bytes 884744 | tf_op jit(solution)/shard_map/ppermute | solution.py:412
  5.4 2.5 %collective-permute-start.7 = (bf16[144,1024]{1,0:T(8,128)(2,1)S(1)}, bf16[144,1024]{1,0:T(8,128)(2,1)S(1)}, u32[]{:S(2)}, u32[]{:S(2)}) collective-permute-start(bf16[144,1024]{1,0:T(8,128)(2,1)S(1)} %pad_maximum_fusion), channel_id=1, source_target_pairs={{0,3},{1,2},{2,1},{3,0},{4,7},{5,6},{6,5},{7,4},{8,11},{9,10},{10,... | collective-permute-start | bytes 884744 | tf_op jit(solution)/shard_map/ppermute | solution.py:412
  9.9 1.6 %collective-permute-start = (bf16[144,1664]{1,0:T(8,128)(2,1)S(1)}, bf16[144,1664]{1,0:T(8,128)(2,1)S(1)}, u32[]{:S(2)}, u32[]{:S(2)}) collective-permute-start(bf16[144,1664]{1,0:T(8,128)(2,1)S(1)} %fusion.1.refs_0_), channel_id=1, source_target_pairs={{0,8},{4,12},{8,0},{12,4},{1,9},{5,13},{9,1},{13,5},{2,10},{6,14},... | collective-permute-start | bytes 1437704 | tf_op jit(solution)/shard_map/ppermute | solution.py:409
  12.5 5.1 %sort.4.refs_0_ = bf16[16,2,176,1024]{3,2,1,0:T(8,128)(2,1)} custom-call(bf16[16,2816,128]{2,1,0:T(8,128)(2,1)} %bitcast.44), custom_call_target="tpu_custom_call" | custom-call | flops 4400000000 | tf_op jit(solution)/shard_map/sort/pallas_call | solution.py:235
  18.4 5.1 %sort.5.refs_0_ = bf16[16,2,176,1024]{3,2,1,0:T(8,128)(2,1)} custom-call(bf16[16,2816,128]{2,1,0:T(8,128)(2,1)} %bitcast.45, bf16[16,2,176,1024]{3,2,1,0:T(8,128)(2,1)} %sort.4.refs_0_, bf16[144,1024]{1,0:T(8,128)(2,1)S(1)} %collective-permute-done.3.refs_0_.refs_1_), custom_call_target="tpu_custom_call", output_to_operand_aliasing={{}: (1, {})} | custom-call | flops 4400000000 | tf_op jit(solution)/shard_map/sort/pallas_call | solution.py:235
  24.3 5.2 %sort.6.refs_0_ = bf16[16,2,176,1024]{3,2,1,0:T(8,128)(2,1)} custom-call(bf16[16,2816,128]{2,1,0:T(8,128)(2,1)} %bitcast.46, bf16[16,2,176,1024]{3,2,1,0:T(8,128)(2,1)} %sort.5.refs_0_, bf16[144,1024]{1,0:T(8,128)(2,1)S(1)} %collective-permute-done.7.refs_0_.refs_1_), custom_call_target="tpu_custom_call", output_to_operand_aliasing={{}: (1, {})} | custom-call | flops 4400000000 | tf_op jit(solution)/shard_map/sort/pallas_call | solution.py:235
  29.5 1.6 %collective-permute-start.8 = (bf16[144,1024]{1,0:T(8,128)(2,1)S(1)}, bf16[144,1024]{1,0:T(8,128)(2,1)S(1)}, u32[]{:S(2)}, u32[]{:S(2)}) collective-permute-start(bf16[144,1024]{1,0:T(8,128)(2,1)S(1)} %collective-permute-done.7.refs_0_.refs_1_), channel_id=1, source_target_pairs={{0,8},{4,12},{8,0},{12,4},{1,9},{5,13},{9,1},{13,5},{2,10},{6,14},... | collective-permute-start | bytes 884744 | tf_op jit(solution)/shard_map/ppermute | solution.py:409
  31.0 1.8 %collective-permute-done.11.refs_1_.refs_6_.refs_0_ = bf16[144,1024]{1,0:T(8,128)(2,1)S(1)} collective-permute-done((bf16[144,1024]{1,0:T(8,128)(2,1)S(1)}, bf16[144,1024]{1,0:T(8,128)(2,1)S(1)}, u32[]{:S(2)}, u32[]{:S(2)}) %collective-permute-start.11) | collective-permute-done | bytes 294944 | tf_op jit(solution)/shard_map/ppermute | solution.py:412
  32.8 5.1 %sort.7.refs_4_ = bf16[16,2,176,1024]{3,2,1,0:T(8,128)(2,1)} custom-call(bf16[16,2816,128]{2,1,0:T(8,128)(2,1)} %bitcast.47, bf16[16,2,176,1024]{3,2,1,0:T(8,128)(2,1)} %sort.6.refs_0_, bf16[144,1024]{1,0:T(8,128)(2,1)S(1)} %collective-permute-done.11.refs_1_.refs_6_.refs_0_), custom_call_target="tpu_custom_call", output_to_operand_aliasing={{}: (1, {})} | custom-call | flops 4400000000 | tf_op jit(solution)/shard_map/sort/pallas_call | solution.py:235
  38.6 1.5 %collective-permute-start.12 = (bf16[144,1024]{1,0:T(8,128)(2,1)S(1)}, bf16[144,1024]{1,0:T(8,128)(2,1)S(1)}, u32[]{:S(2)}, u32[]{:S(2)}) collective-permute-start(bf16[144,1024]{1,0:T(8,128)(2,1)S(1)} %collective-permute-done.11.refs_1_.refs_6_.refs_0_), channel_id=1, source_target_pairs={{0,8},{4,12},{8,0},{12,4},{1,9},{5,13},{9,1},{13,5},{2,10},{6,14},... | collective-permute-start | bytes 884744 | tf_op jit(solution)/shard_map/ppermute | solution.py:409
  41.8 1.5 %dispatch.5 = (bf16[16,64,1024]{2,1,0:T(8,128)(2,1)S(1)}, f32[16,64,128]{2,1,0:T(8,128)S(1)}, bf16[4,256,128]{2,1,0:T(8,128)(2,1)S(1)}) custom-call(s32[1]{0:T(128)} %bitcast.15.base_ref, bf16[64,1024]{1,0:T(8,128)(2,1)S(1)} %fusion.2.rw_ref, bf16[144,1024]{1,0:T(8,128)(2,1)S(1)} %collective-permute-done.7.refs_0_.refs_1_, ...), custom_call_target="tpu_custom_call" | custom-call | flops 3300000000 | tf_op jit(solution)/shard_map/dispatch/pallas_call | solution.py:142
  43.3 11.0 %experts.2 = (bf16[16,64,1024]{2,1,0:T(8,128)(2,1)S(1)}, bf16[16,64,1024]{2,1,0:T(8,128)(2,1)S(1)}) custom-call(bf16[16,64,1024]{2,1,0:T(8,128)(2,1)S(1)} %get-tuple-element.26.refs_0_, bf16[16,64,1024]{2,1,0:T(8,128)(2,1)S(1)} %get-tuple-element.27.refs_1_, f32[16,64,128]{2,1,0:T(8,128)S(1)} %get-tuple-element.28.refs_2_, ...), custom_call_target="tpu_custom_call" | custom-call | flops 6600000000 | tf_op jit(solution)/shard_map/experts/pallas_call | solution.py:293
  54.4 1.7 %combine.2 = (bf16[1,512,1024]{2,1,0:T(8,128)(2,1)S(1)}, bf16[1,512,1024]{2,1,0:T(8,128)(2,1)}) custom-call(bf16[4,256,128]{2,1,0:T(8,128)(2,1)S(1)} %get-tuple-element.24.refs_0_, bf16[4,256,128]{2,1,0:T(8,128)(2,1)S(1)} %get-tuple-element.25.refs_1_, bf16[16,64,1024]{2,1,0:T(8,128)(2,1)S(1)} %get-tuple-element.30.refs_2_.refs_4_, ...), custom_call_target="tpu_custom_call" | custom-call | flops 2200000000 | tf_op jit(solution)/shard_map/combine/pallas_call | solution.py:329
  57.5 2.8 %dispatch.7 = (bf16[16,64,1024]{2,1,0:T(8,128)(2,1)S(1)}, f32[16,64,128]{2,1,0:T(8,128)S(1)}, bf16[4,256,128]{2,1,0:T(8,128)(2,1)S(1)}, f32[8,128]{1,0:T(8,128)S(1)}) custom-call(s32[1]{0:T(128)} %bitcast.15.base_ref, bf16[64,1024]{1,0:T(8,128)(2,1)S(1)} %fusion.2.rw_ref, bf16[144,1664]{1,0:T(8,128)(2,1)S(1)} %fusion.1.refs_0_, ...), custom_call_target="tpu_custom_call" | custom-call | flops 3300000000 | tf_op jit(solution)/shard_map/dispatch/pallas_call | solution.py:142
  63.7 10.8 %experts.3 = (bf16[16,64,1024]{2,1,0:T(8,128)(2,1)S(1)}, bf16[16,64,1024]{2,1,0:T(8,128)(2,1)S(1)}) custom-call(bf16[16,64,1024]{2,1,0:T(8,128)(2,1)S(1)} %get-tuple-element.36.refs_0_, bf16[16,64,1024]{2,1,0:T(8,128)(2,1)S(1)} %get-tuple-element.37.refs_1_, f32[16,64,128]{2,1,0:T(8,128)S(1)} %get-tuple-element.38.refs_2_, ...), custom_call_target="tpu_custom_call" | custom-call | flops 6600000000 | tf_op jit(solution)/shard_map/experts/pallas_call | solution.py:293
  74.5 2.6 %collective-permute-done.14.refs_4_ = bf16[1,256,1024]{2,1,0:T(8,128)(2,1)S(1)} collective-permute-done((bf16[1,256,1024]{2,1,0:T(8,128)(2,1)S(1)}, bf16[1,256,1024]{2,1,0:T(8,128)(2,1)S(1)}, u32[]{:S(2)}, u32[]{:S(2)}) %collective-permute-start.14) | collective-permute-done | bytes 524320 | tf_op jit(solution)/shard_map/ppermute | solution.py:409
  77.9 2.8 %collective-permute-done.19 = bf16[1,512,1024]{2,1,0:T(8,128)(2,1)} collective-permute-done((bf16[1,512,1024]{2,1,0:T(8,128)(2,1)S(1)}, bf16[1,512,1024]{2,1,0:T(8,128)(2,1)}, u32[]{:S(2)}, u32[]{:S(2)}) %collective-permute-start.19) | collective-permute-done | bytes 1048608 | tf_op jit(solution)/shard_map/ppermute | solution.py:409
  80.7 1.7 %add_convert_fusion.4 = bf16[1,128,1024]{2,1,0:T(8,128)(2,1)} fusion(bf16[1,512,1024]{2,1,0:T(8,128)(2,1)} %collective-permute-done.19, bf16[1,512,1024]{2,1,0:T(8,128)(2,1)S(1)} %get-tuple-element.42), kind=kLoop, calls=%fused_computation.6 | loop fusion | flops 524288 | bytes 786432 | tf_op jit(solution)/shard_map/convert_element_type | solution.py:395
  85.9 5.8 %collective-permute-start.16 = (bf16[1,128,1024]{2,1,0:T(8,128)(2,1)S(1)}, bf16[1,128,1024]{2,1,0:T(8,128)(2,1)S(1)}, u32[]{:S(2)}, u32[]{:S(2)}) collective-permute-start(bf16[1,128,1024]{2,1,0:T(8,128)(2,1)S(1)} %get-tuple-element.46), channel_id=1, source_target_pairs={{0,3},{1,2},{2,1},{3,0},{4,7},{5,6},{6,5},{7,4},{8,11},{9,10},{10,... | collective-permute-start | bytes 786440 | tf_op jit(solution)/shard_map/ppermute | solution.py:412
  92.9 3.8 %collective-permute-start.21 = (bf16[1,128,1024]{2,1,0:T(8,128)(2,1)S(1)}, bf16[1,128,1024]{2,1,0:T(8,128)(2,1)S(1)}, u32[]{:S(2)}, u32[]{:S(2)}) collective-permute-start(bf16[1,128,1024]{2,1,0:T(8,128)(2,1)S(1)} %get-tuple-element.47), channel_id=1, source_target_pairs={{0,2},{1,3},{2,0},{3,1},{4,6},{5,7},{6,4},{7,5},{8,10},{9,11},{10,... | collective-permute-start | bytes 786440 | tf_op jit(solution)/shard_map/ppermute | solution.py:412
  96.8 1.5 %collective-permute-start.22 = (bf16[1,128,1024]{2,1,0:T(8,128)(2,1)S(1)}, bf16[1,128,1024]{2,1,0:T(8,128)(2,1)S(1)}, u32[]{:S(2)}, u32[]{:S(2)}) collective-permute-start(bf16[1,128,1024]{2,1,0:T(8,128)(2,1)S(1)} %get-tuple-element.48), channel_id=1, source_target_pairs={{0,8},{4,12},{8,0},{12,4},{1,9},{5,13},{9,1},{13,5},{2,10},{6,14},... | collective-permute-start | bytes 786440 | tf_op jit(solution)/shard_map/ppermute | solution.py:409
  98.3 7.4 %attention.1 = bf16[128,4096]{1,0:T(8,128)(2,1)} custom-call(s32[128,1]{1,0:T(8,128)S(1)} %copy.23.first_ref, s32[128,1]{1,0:T(8,128)S(1)} %copy.24.last_ref, s32[1,512]{1,0:T(1,128)S(1)} %bitcast.37, bf16[128,4608]{1,0:T(8,128)(2,1)S(1)} %bitcast.43, bf16[144,1664]{1,0:T(8,128)(2,1)S(1)} %fusion.1.refs_0_, bf16[144,1664]{1,0:T(8,128)(2,1)S(1)} %copy-done.2, ...), custom_call_target="tpu_custom_call" | custom-call | flops 6600000000 | tf_op jit(solution)/shard_map/attention/pallas_call | solution.py:377
  106.3 7.7 %collective-permute-done.21 = bf16[1,128,1024]{2,1,0:T(8,128)(2,1)S(1)} collective-permute-done((bf16[1,128,1024]{2,1,0:T(8,128)(2,1)S(1)}, bf16[1,128,1024]{2,1,0:T(8,128)(2,1)S(1)}, u32[]{:S(2)}, u32[]{:S(2)}) %collective-permute-start.21) | collective-permute-done | bytes 262176 | tf_op jit(solution)/shard_map/ppermute | solution.py:412
  114.0 1.9 %add_convert_fusion.1 = bf16[1,128,1024]{2,1,0:T(8,128)(2,1)} fusion(bf16[1,128,1024]{2,1,0:T(8,128)(2,1)S(1)} %collective-permute-done.22, bf16[1,128,1024]{2,1,0:T(8,128)(2,1)S(1)} %collective-permute-done.21, bf16[1,128,1024]{2,1,0:T(8,128)(2,1)S(1)} %collective-permute-done.16, bf16[1,128,1024]{2,1,0:T(8,128)(2,1)S(1)} %collective-permute-done.15, ...), kind=kLoop, calls=%fused_computation.3 | loop fusion | flops 1572864 | bytes 1835008 | tf_op jit(solution)/shard_map/convert_element_type | solution.py:395
  (81 shorter events, 19.6 us)
Async XLA Ops:
  2.3 15.3 %collective-permute-start.3 = (bf16[144,1024]{1,0:T(8,128)(2,1)S(1)}, bf16[144,1024]{1,0:T(8,128)(2,1)S(1)}, u32[]{:S(2)}, u32[]{:S(2)}) collective-permute-start(bf16[144,1024]{1,0:T(8,128)(2,1)S(1)} %pad_maximum_fusion), channel_id=1, source_target_pairs={{0,1},{1,0},{2,3},{3,2},{4,5},{5,4},{6,7},{7,6},{8,9},{9,8},{10,11... | collective-permute-start | bytes 884744 | tf_op jit(solution)/shard_map/ppermute | solution.py:412
  5.4 18.1 %collective-permute-start.7 = (bf16[144,1024]{1,0:T(8,128)(2,1)S(1)}, bf16[144,1024]{1,0:T(8,128)(2,1)S(1)}, u32[]{:S(2)}, u32[]{:S(2)}) collective-permute-start(bf16[144,1024]{1,0:T(8,128)(2,1)S(1)} %pad_maximum_fusion), channel_id=1, source_target_pairs={{0,3},{1,2},{2,1},{3,0},{4,7},{5,6},{6,5},{7,4},{8,11},{9,10},{10,... | collective-permute-start | bytes 884744 | tf_op jit(solution)/shard_map/ppermute | solution.py:412
  9.9 28.0 %collective-permute-start = (bf16[144,1664]{1,0:T(8,128)(2,1)S(1)}, bf16[144,1664]{1,0:T(8,128)(2,1)S(1)}, u32[]{:S(2)}, u32[]{:S(2)}) collective-permute-start(bf16[144,1664]{1,0:T(8,128)(2,1)S(1)} %fusion.1.refs_0_), channel_id=1, source_target_pairs={{0,8},{4,12},{8,0},{12,4},{1,9},{5,13},{9,1},{13,5},{2,10},{6,14},... | collective-permute-start | bytes 1437704 | tf_op jit(solution)/shard_map/ppermute | solution.py:409
  11.5 45.9 %collective-permute-start.1 = (bf16[144,1664]{1,0:T(8,128)(2,1)S(1)}, bf16[144,1664]{1,0:T(8,128)(2,1)}, u32[]{:S(2)}, u32[]{:S(2)}) collective-permute-start(bf16[144,1664]{1,0:T(8,128)(2,1)S(1)} %fusion.1.refs_0_), channel_id=1, source_target_pairs={{0,4},{4,0},{8,12},{12,8},{1,5},{5,1},{9,13},{13,9},{2,6},{6,2},{1... | collective-permute-start | bytes 1437704 | tf_op jit(solution)/shard_map/ppermute | solution.py:409
  17.6 11.8 %collective-permute-start.4 = (bf16[144,1024]{1,0:T(8,128)(2,1)S(1)}, bf16[144,1024]{1,0:T(8,128)(2,1)S(1)}, u32[]{:S(2)}, u32[]{:S(2)}) collective-permute-start(bf16[144,1024]{1,0:T(8,128)(2,1)S(1)} %collective-permute-done.3.refs_0_.refs_1_), channel_id=1, source_target_pairs={{0,8},{4,12},{8,0},{12,4},{1,9},{5,13},{9,1},{13,5},{2,10},{6,14},... | collective-permute-start | bytes 884744 | tf_op jit(solution)/shard_map/ppermute | solution.py:409
  18.2 20.3 %collective-permute-start.5 = (bf16[144,1024]{1,0:T(8,128)(2,1)S(1)}, bf16[144,1024]{1,0:T(8,128)(2,1)S(1)}, u32[]{:S(2)}, u32[]{:S(2)}) collective-permute-start(bf16[144,1024]{1,0:T(8,128)(2,1)S(1)} %collective-permute-done.3.refs_0_.refs_1_), channel_id=1, source_target_pairs={{0,4},{4,0},{8,12},{12,8},{1,5},{5,1},{9,13},{13,9},{2,6},{6,2},{1... | collective-permute-start | bytes 884744 | tf_op jit(solution)/shard_map/ppermute | solution.py:409
  23.6 9.3 %collective-permute-start.11 = (bf16[144,1024]{1,0:T(8,128)(2,1)S(1)}, bf16[144,1024]{1,0:T(8,128)(2,1)S(1)}, u32[]{:S(2)}, u32[]{:S(2)}) collective-permute-start(bf16[144,1024]{1,0:T(8,128)(2,1)S(1)} %collective-permute-done.7.refs_0_.refs_1_), channel_id=1, source_target_pairs={{0,1},{1,0},{2,3},{3,2},{4,5},{5,4},{6,7},{7,6},{8,9},{9,8},{10,11... | collective-permute-start | bytes 884744 | tf_op jit(solution)/shard_map/ppermute | solution.py:412
  29.5 9.1 %collective-permute-start.8 = (bf16[144,1024]{1,0:T(8,128)(2,1)S(1)}, bf16[144,1024]{1,0:T(8,128)(2,1)S(1)}, u32[]{:S(2)}, u32[]{:S(2)}) collective-permute-start(bf16[144,1024]{1,0:T(8,128)(2,1)S(1)} %collective-permute-done.7.refs_0_.refs_1_), channel_id=1, source_target_pairs={{0,8},{4,12},{8,0},{12,4},{1,9},{5,13},{9,1},{13,5},{2,10},{6,14},... | collective-permute-start | bytes 884744 | tf_op jit(solution)/shard_map/ppermute | solution.py:409
  32.8 7.3 %collective-permute-start.6 = (bf16[144,1024]{1,0:T(8,128)(2,1)S(1)}, bf16[144,1024]{1,0:T(8,128)(2,1)S(1)}, u32[]{:S(2)}, u32[]{:S(2)}) collective-permute-start(bf16[144,1024]{1,0:T(8,128)(2,1)S(1)} %collective-permute-done.4.refs_1_), channel_id=1, source_target_pairs={{0,4},{4,0},{8,12},{12,8},{1,5},{5,1},{9,13},{13,9},{2,6},{6,2},{1... | collective-permute-start | bytes 884744 | tf_op jit(solution)/shard_map/ppermute | solution.py:409
  37.9 19.5 %copy-start.1 = (bf16[144,1664]{1,0:T(8,128)(2,1)}, bf16[144,1664]{1,0:T(8,128)(2,1)S(1)}, u32[]{:S(2)}) copy-start(bf16[144,1664]{1,0:T(8,128)(2,1)S(1)} %collective-permute-done.refs_1_) | copy-start | bytes 1437700
  37.9 3.8 %collective-permute-start.9 = (bf16[144,1024]{1,0:T(8,128)(2,1)S(1)}, bf16[144,1024]{1,0:T(8,128)(2,1)S(1)}, u32[]{:S(2)}, u32[]{:S(2)}) collective-permute-start(bf16[144,1024]{1,0:T(8,128)(2,1)S(1)} %collective-permute-done.7.refs_0_.refs_1_), channel_id=1, source_target_pairs={{0,4},{4,0},{8,12},{12,8},{1,5},{5,1},{9,13},{13,9},{2,6},{6,2},{1... | collective-permute-start | bytes 884744 | tf_op jit(solution)/shard_map/ppermute | solution.py:409
  38.5 18.9 %collective-permute-start.2 = (bf16[144,1664]{1,0:T(8,128)(2,1)S(1)}, bf16[144,1664]{1,0:T(8,128)(2,1)}, u32[]{:S(2)}, u32[]{:S(2)}) collective-permute-start(bf16[144,1664]{1,0:T(8,128)(2,1)S(1)} %collective-permute-done.refs_1_), channel_id=1, source_target_pairs={{0,4},{4,0},{8,12},{12,8},{1,5},{5,1},{9,13},{13,9},{2,6},{6,2},{1... | collective-permute-start | bytes 1437704 | tf_op jit(solution)/shard_map/ppermute | solution.py:409
  38.6 15.8 %collective-permute-start.12 = (bf16[144,1024]{1,0:T(8,128)(2,1)S(1)}, bf16[144,1024]{1,0:T(8,128)(2,1)S(1)}, u32[]{:S(2)}, u32[]{:S(2)}) collective-permute-start(bf16[144,1024]{1,0:T(8,128)(2,1)S(1)} %collective-permute-done.11.refs_1_.refs_6_.refs_0_), channel_id=1, source_target_pairs={{0,8},{4,12},{8,0},{12,4},{1,9},{5,13},{9,1},{13,5},{2,10},{6,14},... | collective-permute-start | bytes 884744 | tf_op jit(solution)/shard_map/ppermute | solution.py:409
  40.1 1.7 %collective-permute-start.10 = (bf16[144,1024]{1,0:T(8,128)(2,1)S(1)}, bf16[144,1024]{1,0:T(8,128)(2,1)S(1)}, u32[]{:S(2)}, u32[]{:S(2)}) collective-permute-start(bf16[144,1024]{1,0:T(8,128)(2,1)S(1)} %collective-permute-done.8.refs_1_), channel_id=1, source_target_pairs={{0,4},{4,0},{8,12},{12,8},{1,5},{5,1},{9,13},{13,9},{2,6},{6,2},{1... | collective-permute-start | bytes 884744 | tf_op jit(solution)/shard_map/ppermute | solution.py:409
  56.1 5.7 %collective-permute-start.13 = (bf16[1,512,1024]{2,1,0:T(8,128)(2,1)}, bf16[1,512,1024]{2,1,0:T(8,128)(2,1)}, u32[]{:S(2)}, u32[]{:S(2)}) collective-permute-start(bf16[1,512,1024]{2,1,0:T(8,128)(2,1)} %get-tuple-element.33), channel_id=1, source_target_pairs={{0,4},{4,0},{8,12},{12,8},{1,5},{5,1},{9,13},{13,9},{2,6},{6,2},{1... | collective-permute-start | bytes 3145736 | tf_op jit(solution)/shard_map/ppermute | solution.py:409
  56.8 3.5 %collective-permute-start.17 = (bf16[144,1024]{1,0:T(8,128)(2,1)S(1)}, bf16[144,1024]{1,0:T(8,128)(2,1)S(1)}, u32[]{:S(2)}, u32[]{:S(2)}) collective-permute-start(bf16[144,1024]{1,0:T(8,128)(2,1)S(1)} %collective-permute-done.11.refs_1_.refs_6_.refs_0_), channel_id=1, source_target_pairs={{0,4},{4,0},{8,12},{12,8},{1,5},{5,1},{9,13},{13,9},{2,6},{6,2},{1... | collective-permute-start | bytes 884744 | tf_op jit(solution)/shard_map/ppermute | solution.py:409
  57.0 3.2 %collective-permute-start.18 = (bf16[144,1024]{1,0:T(8,128)(2,1)S(1)}, bf16[144,1024]{1,0:T(8,128)(2,1)S(1)}, u32[]{:S(2)}, u32[]{:S(2)}) collective-permute-start(bf16[144,1024]{1,0:T(8,128)(2,1)S(1)} %collective-permute-done.12.refs_4_.refs_1_), channel_id=1, source_target_pairs={{0,4},{4,0},{8,12},{12,8},{1,5},{5,1},{9,13},{13,9},{2,6},{6,2},{1... | collective-permute-start | bytes 884744 | tf_op jit(solution)/shard_map/ppermute | solution.py:409
  63.0 14.1 %collective-permute-start.14 = (bf16[1,256,1024]{2,1,0:T(8,128)(2,1)S(1)}, bf16[1,256,1024]{2,1,0:T(8,128)(2,1)S(1)}, u32[]{:S(2)}, u32[]{:S(2)}) collective-permute-start(bf16[1,256,1024]{2,1,0:T(8,128)(2,1)S(1)} %add_convert_fusion.refs_6_), channel_id=1, source_target_pairs={{0,8},{4,12},{8,0},{12,4},{1,9},{5,13},{9,1},{13,5},{2,10},{6,14},... | collective-permute-start | bytes 1572872 | tf_op jit(solution)/shard_map/ppermute | solution.py:409
  77.8 2.9 %collective-permute-start.19 = (bf16[1,512,1024]{2,1,0:T(8,128)(2,1)S(1)}, bf16[1,512,1024]{2,1,0:T(8,128)(2,1)}, u32[]{:S(2)}, u32[]{:S(2)}) collective-permute-start(bf16[1,512,1024]{2,1,0:T(8,128)(2,1)S(1)} %get-tuple-element.43), channel_id=1, source_target_pairs={{0,4},{4,0},{8,12},{12,8},{1,5},{5,1},{9,13},{13,9},{2,6},{6,2},{1... | collective-permute-start | bytes 3145736 | tf_op jit(solution)/shard_map/ppermute | solution.py:409
  82.4 9.3 %collective-permute-start.20 = (bf16[1,128,1024]{2,1,0:T(8,128)(2,1)}, bf16[1,128,1024]{2,1,0:T(8,128)(2,1)S(1)}, u32[]{:S(2)}, u32[]{:S(2)}) collective-permute-start(bf16[1,128,1024]{2,1,0:T(8,128)(2,1)} %add_convert_fusion.4), channel_id=1, source_target_pairs={{0,8},{4,12},{8,0},{12,4},{1,9},{5,13},{9,1},{13,5},{2,10},{6,14},... | collective-permute-start | bytes 786440 | tf_op jit(solution)/shard_map/ppermute | solution.py:409
  84.7 21.6 %collective-permute-start.15 = (bf16[1,128,1024]{2,1,0:T(8,128)(2,1)S(1)}, bf16[1,128,1024]{2,1,0:T(8,128)(2,1)S(1)}, u32[]{:S(2)}, u32[]{:S(2)}) collective-permute-start(bf16[1,128,1024]{2,1,0:T(8,128)(2,1)S(1)} %get-tuple-element.45), channel_id=1, source_target_pairs={{0,1},{1,0},{2,3},{3,2},{4,5},{5,4},{6,7},{7,6},{8,9},{9,8},{10,11... | collective-permute-start | bytes 786440 | tf_op jit(solution)/shard_map/ppermute | solution.py:412
  85.9 20.4 %collective-permute-start.16 = (bf16[1,128,1024]{2,1,0:T(8,128)(2,1)S(1)}, bf16[1,128,1024]{2,1,0:T(8,128)(2,1)S(1)}, u32[]{:S(2)}, u32[]{:S(2)}) collective-permute-start(bf16[1,128,1024]{2,1,0:T(8,128)(2,1)S(1)} %get-tuple-element.46), channel_id=1, source_target_pairs={{0,3},{1,2},{2,1},{3,0},{4,7},{5,6},{6,5},{7,4},{8,11},{9,10},{10,... | collective-permute-start | bytes 786440 | tf_op jit(solution)/shard_map/ppermute | solution.py:412
  92.9 21.1 %collective-permute-start.21 = (bf16[1,128,1024]{2,1,0:T(8,128)(2,1)S(1)}, bf16[1,128,1024]{2,1,0:T(8,128)(2,1)S(1)}, u32[]{:S(2)}, u32[]{:S(2)}) collective-permute-start(bf16[1,128,1024]{2,1,0:T(8,128)(2,1)S(1)} %get-tuple-element.47), channel_id=1, source_target_pairs={{0,2},{1,3},{2,0},{3,1},{4,6},{5,7},{6,4},{7,5},{8,10},{9,11},{10,... | collective-permute-start | bytes 786440 | tf_op jit(solution)/shard_map/ppermute | solution.py:412
  96.8 17.2 %collective-permute-start.22 = (bf16[1,128,1024]{2,1,0:T(8,128)(2,1)S(1)}, bf16[1,128,1024]{2,1,0:T(8,128)(2,1)S(1)}, u32[]{:S(2)}, u32[]{:S(2)}) collective-permute-start(bf16[1,128,1024]{2,1,0:T(8,128)(2,1)S(1)} %get-tuple-element.48), channel_id=1, source_target_pairs={{0,8},{4,12},{8,0},{12,4},{1,9},{5,13},{9,1},{13,5},{2,10},{6,14},... | collective-permute-start | bytes 786440 | tf_op jit(solution)/shard_map/ppermute | solution.py:409
  (9 other events, 51.0 us)

commit v8 on v7

--- a/solution.py
+++ b/solution.py
@@ -17,7 +17,7 @@
 EXPERT_ROWS = 256
 EXTRA = 16
 VMEM = 14 * 2**20
-VMEM_EXPERTS = 36 * 2**20
+VMEM_EXPERTS = 24 * 2**20
 VMEM_SORT = 52 * 2**20
 PIECES = 4
 DEPTH = 3
@@ -114,14 +114,16 @@
     return pl.BlockSpec(a.shape, lambda *i: (0,) * a.ndim)
 
 
-def dispatch(parts, top, base, rw, local, row=None, after=()):
+def dispatch(parts, n, top, base, rw, local, row=None, after=()):
     n_parts = len(parts)
-    n, width = parts[0].shape[0] // (BLOCK + EXTRA), rw.shape[1]
+    width = rw.shape[1]
     slots = n_parts * CAP
     in_specs = [
         pl.BlockSpec(memory_space=pltpu.SMEM),
         whole(rw),
-    ] + [pl.BlockSpec((BLOCK + EXTRA, width), lambda i: (i, 0))] * n_parts
+    ] + [
+        pl.BlockSpec((BLOCK + EXTRA, width), lambda i, k=k: (k + i, 0)) for _, k in parts
+    ]
     in_specs += [ANYWHERE] * len(after)
     out_specs = [
         pl.BlockSpec((local, slots, width), lambda i: (0, i, 0)),
@@ -148,7 +150,7 @@
         out_shape,
         [],
         "dispatch",
-    )(base, rw, *parts, *after, *extra)
+    )(base, rw, *[a for a, _ in parts], *after, *extra)
 
 
 def fetch(sources, slots, sem, step, steps, first, start=0):
@@ -340,7 +342,8 @@
     )(*picks, *made, *after)
 
 
-def attend_kernel(n, kdim, first_ref, last_ref, kpos_ref, q_ref, *refs):
+def attend_kernel(starts, kdim, first_ref, last_ref, kpos_ref, q_ref, *refs):
+    n = len(starts)
     parts, (out_ref, even, odd) = refs[:n], refs[n:]
     rows = q_ref.shape[0]
     start = max(parts[0].shape[1] - even.shape[1], 0)
@@ -352,7 +355,7 @@
         pad = jnp.zeros((rows, half), jnp.bfloat16)
         for i in range(n):
             at = slice(i * rows, (i + 1) * rows)
-            keys = parts[i][:rows, start : start + kdim]
+            keys = parts[i][starts[i] : starts[i] + rows, start : start + kdim]
             even[at, :] = jnp.concatenate([keys, pad], axis=1)
             odd[at, :] = jnp.concatenate([pad, keys], axis=1)
 
@@ -375,17 +378,17 @@
     rows, kdim = queries.shape[0], queries.shape[1] // HEADS
     wide = -(-kdim // LANES) * LANES
     return call(
-        functools.partial(attend_kernel, n, kdim),
+        functools.partial(attend_kernel, [at for _, at in parts], kdim),
         6,
         (HEADS // 2,),
         [whole(first), whole(last), whole(kpos)]
         + [pl.BlockSpec((rows, 2 * kdim), lambda h: (0, h))]
-        + [whole(p) for p in parts],
+        + [whole(p) for p, _ in parts],
         pl.BlockSpec((rows, 2 * LATENT), lambda h: (0, h)),
         jax.ShapeDtypeStruct((rows, HEADS * LATENT), jnp.bfloat16),
         [pltpu.VMEM((n * rows, wide), jnp.bfloat16)] * 2,
         "attention",
-    )(first, last, kpos, queries, *parts)
+    )(first, last, kpos, queries, *[p for p, _ in parts])
 
 
 def added(*terms):
@@ -431,18 +434,24 @@
         kdim = latent_kv.shape[2]
         keys = jnp.pad(latent_kv[0], ((0, EXTRA), (0, -kdim % LANES)))
         near_parts[0] = jnp.concatenate([packed, keys], axis=1)
-    spread = [[a] for a in near_parts]
-    spread = [held + [flip(a, 2) for a in held] for held in spread]
-    behind = [(), (), (), ()]
-    if len(shifts) == 4:
-        behind = [(), (arrived[1],), (arrived[2],), (arrived[3],)]
-    spread = [held + [flip(a, 1) for a in held] for held in spread]
+    crossed = [flip(a, 2) for a in near_parts]
     if near:
-        kv = spread[0]
+        blocks = 1
+        pairs = [jnp.concatenate([a, b], axis=0) for a, b in zip(near_parts, crossed)]
+        flipped = [flip(a, 1) for a in pairs]
+        spread = [[(a, 0), (a, 1), (b, 0), (b, 1)] for a, b in zip(pairs, flipped)]
+        kv = [(a, k * (BLOCK + EXTRA)) for a, k in spread[0]]
     else:
+        blocks = near_parts[0].shape[0] // (BLOCK + EXTRA)
+        spread = [[(near_parts[0], 0), (crossed[0], 0)]]
+        spread[0] = spread[0] + [(flip(a, 1), 0) for a, _ in spread[0]]
         kv = [latent_kv[0]]
         for bit in flips:
             kv = kv + [flip(a, bit) for a in kv]
+        kv = [(a, 0) for a in kv]
+    behind = [()] * PIECES
+    if near:
+        behind = [(), (arrived[1],), (arrived[2], crossed[0]), (arrived[3],)]
 
     lengths = doc_lengths[0]
     ends = jnp.cumsum(lengths)
@@ -460,39 +469,24 @@
     rw = jnp.roll(router_weight.T, -exp * local, axis=0)
     balance = None
     gu = sort_rows(gate_up, behind)
-    groups = [[1, 2], [3, 0]] if len(shifts) == 4 else [range(len(shifts))]
-    back, before, begun, far = [], (), [], []
-    late = (spread[3][1],) if near else ()
-    for n, group in enumerate(groups):
-        sent = []
-        for i in group:
-            row = (seg.reshape(-1, 1, BLOCK), scale) if near and i == 0 else None
-            out = dispatch(spread[i], top, base, rw, local, row, before if i else ())
-            sent.append(out[:3])
-            if row is not None:
-                balance = out[3]
-        if n + 1 < len(groups):
-            after = (arrived[groups[n + 1][0]],)
+    sent = []
+    for i in range(len(shifts)):
+        row = (seg.reshape(-1, 1, BLOCK), scale) if near and i == 0 else None
+        out = dispatch(spread[i], blocks, top, base, rw, local, row)
+        sent.append(out[:3])
+        if row is not None:
+            balance = out[3]
+    made = experts([a[0] for a in sent], [a[1] for a in sent], gu, w_down)
+    back = []
+    for i in reversed(range(len(shifts))):
+        keep, give = combine([sent[i][2]], [made[i]], n_ctx)
+        got = flip(give, 1)
+        far = added(keep[:, tok_rows:], got[:, tok_rows:])
+        terms = [keep[:, :tok_rows], got[:, :tok_rows], flip(far, 2)]
+        if i:
+            back.append(shift(added(*terms), shifts[i]))
         else:
-            after = begun
-        made = experts([a[0] for a in sent], [a[1] for a in sent], gu, w_down, after)
-        before = (made[0],)
-        keep, give = combine([a[2] for a in sent], made, n_ctx, tuple(far) if n else late)
-        got = flip(give, 1)
-        size = len(group) * tok_rows
-        last = n + 1 == len(groups)
-        cuts = [slice(j * tok_rows, (j + 1) * tok_rows) for j in range(len(group))]
-        crossing = cuts if last else [slice(0, size)]
-        far = [added(keep[:, size + c.start : size + c.stop], got[:, size + c.start : size + c.stop]) for c in crossing]
-        begun = far
-        far = [flip(a, 2) for a in far]
-        for j, i in enumerate(group):
-            crossed = far[j] if last else far[0][:, cuts[j]]
-            terms = [keep[:, cuts[j]], got[:, cuts[j]], crossed]
-            if i:
-                back.append(shift(added(*terms), shifts[i]))
-            else:
-                back = back + terms
+            back = back + terms
     if near:
         expert_mix = added(*back)
     else:

time: 116 us -> 103 us (0.89)
  Pallas kernels: 59.3 us -> 47.4 us
  waiting for transfers between devices: 14.9 us -> 22.1 us
  other arithmetic: 11.7 us -> 4.93 us
  starting transfers between devices: 27 us -> 24.5 us
    ppermute x17 -> x16, waiting for transfers between devices: 5.38 us -> 16.6 us  [flip(): return lax.ppermute(a, 'ctx', [(i, i ^ bit) for i in range(n_ctx)])]
    pallas_call x2 -> x1, Pallas kernels: 21.9 us -> 12.8 us  [experts(): call(functools.partial(expert_kernel, n), 6, (local // group, slots // si...]
    convert_element_type x5 -> x8, other arithmetic: 7.53 us -> 1.59 us  [added(): return total.astype(jnp.bfloat16)]
    ppermute x6, waiting for transfers between devices: 9.54 us -> 5.49 us  [shift(): return lax.ppermute(a, 'exp', [(i, i ^ d) for i in range(n_exp)])]
    ppermute x6, starting transfers between devices: 17.1 us -> 14 us  [shift(): return lax.ppermute(a, 'exp', [(i, i ^ d) for i in range(n_exp)])]
    pallas_call x4, Pallas kernels: 7.24 us -> 6 us  [dispatch(): call(functools.partial(dispatch_kernel, n_parts, n_parts if row is not No...]
    pallas_call x1, Pallas kernels: 7.35 us -> 6.17 us  [attend(): call(functools.partial(attend_kernel, [at for _, at in parts], kdim), 6,...]
    ppermute x17 -> x16, starting transfers between devices: 9.89 us -> 10.6 us  [flip(): return lax.ppermute(a, 'ctx', [(i, i ^ bit) for i in range(n_ctx)])]
  transfers between devices with their start and end apart: 23 -> 22, of which waited for: 4 -> 7; matrix products, arithmetic and copies ran while one was open for 6% -> 4% of each run, Pallas kernels for 51% -> 32%
where the time goes in v8:
time: 103 us; the launch traced here: 102 us
  Pallas kernels  47.4 us (46%)
  starting transfers between devices  24.5 us (24%)
  waiting for transfers between devices  22.1 us (21%)
  other arithmetic  4.93 us (5%)
  local copies, waits for them, and re-layouts  2.23 us (2%)
    pallas_call x4, Pallas kernels, sort_rows(): call(functools.partial(sort_kernel, j * local // pieces), 4, (local // pi...  20.5 us
    ppermute x16, waiting for transfers between devices, flip(): return lax.ppermute(a, 'ctx', [(i, i ^ bit) for i in range(n_ctx)])  16.6 us
    ppermute x6, starting transfers between devices, shift(): return lax.ppermute(a, 'exp', [(i, i ^ d) for i in range(n_exp)])  14 us
    pallas_call x1, Pallas kernels, experts(): call(functools.partial(expert_kernel, n), 6, (local // group, slots // si...  12.8 us
    ppermute x16, starting transfers between devices, flip(): return lax.ppermute(a, 'ctx', [(i, i ^ bit) for i in range(n_ctx)])  10.6 us
    pallas_call x1, Pallas kernels, attend(): call(functools.partial(attend_kernel, [at for _, at in parts], kdim), 6,...  6.17 us
    pallas_call x4, Pallas kernels, dispatch(): call(functools.partial(dispatch_kernel, n_parts, n_parts if row is not No...  6 us
    ppermute x6, waiting for transfers between devices, shift(): return lax.ppermute(a, 'exp', [(i, i ^ d) for i in range(n_exp)])  5.49 us
  transfers between devices with their start and end apart: 22, of which 7 were waited for; matrix products, arithmetic and copies ran while one was open for 4% of the time, Pallas kernels for 32%

profile of v8, /device:TPU:0, one launch (start us, length us, event | category | flops | bytes accessed | tf_op | source)
XLA Modules:
  0.0 102.2 jit_solution(17030228643726639413)
XLA Ops:
  2.3 5.1 %collective-permute-start.2 = (bf16[144,1024]{1,0:T(8,128)(2,1)S(1)}, bf16[144,1024]{1,0:T(8,128)(2,1)S(1)}, u32[]{:S(2)}, u32[]{:S(2)}) collective-permute-start(bf16[144,1024]{1,0:T(8,128)(2,1)S(1)} %pad_maximum_fusion.2), channel_id=1, source_target_pairs={{0,3},{1,2},{2,1},{3,0},{4,7},{5,6},{6,5},{7,4},{8,11},{9,10},{10,... | collective-permute-start | bytes 884744 | tf_op jit(solution)/shard_map/ppermute | solution.py:415
  9.5 1.6 %collective-permute-start = (bf16[144,1664]{1,0:T(8,128)(2,1)S(1)}, bf16[144,1664]{1,0:T(8,128)(2,1)S(1)}, u32[]{:S(2)}, u32[]{:S(2)}) collective-permute-start(bf16[144,1664]{1,0:T(8,128)(2,1)S(1)} %pad_maximum_fusion.1), channel_id=1, source_target_pairs={{0,8},{4,12},{8,0},{12,4},{1,9},{5,13},{9,1},{13,5},{2,10},{6,14},... | collective-permute-start | bytes 1437704 | tf_op jit(solution)/shard_map/ppermute | solution.py:412
  11.8 5.1 %sort.4.refs_0_ = bf16[16,2,176,1024]{3,2,1,0:T(8,128)(2,1)} custom-call(bf16[16,2816,128]{2,1,0:T(8,128)(2,1)} %bitcast.42), custom_call_target="tpu_custom_call" | custom-call | flops 4400000000 | tf_op jit(solution)/shard_map/sort/pallas_call | solution.py:237
  17.7 4.3 %collective-permute-start.3 = (bf16[144,1024]{1,0:T(8,128)(2,1)S(1)}, bf16[144,1024]{1,0:T(8,128)(2,1)S(1)}, u32[]{:S(2)}, u32[]{:S(2)}) collective-permute-start(bf16[144,1024]{1,0:T(8,128)(2,1)S(1)} %collective-permute-done.2.refs_1_), channel_id=1, source_target_pairs={{0,1},{1,0},{2,3},{3,2},{4,5},{5,4},{6,7},{7,6},{8,9},{9,8},{10,11... | collective-permute-start | bytes 884744 | tf_op jit(solution)/shard_map/ppermute | solution.py:415
  22.6 5.1 %sort.5.refs_0_ = bf16[16,2,176,1024]{3,2,1,0:T(8,128)(2,1)} custom-call(bf16[16,2816,128]{2,1,0:T(8,128)(2,1)} %bitcast.43, bf16[16,2,176,1024]{3,2,1,0:T(8,128)(2,1)} %sort.4.refs_0_, bf16[144,1024]{1,0:T(8,128)(2,1)S(1)} %collective-permute-done.6.refs_1_), custom_call_target="tpu_custom_call", output_to_operand_aliasing={{}: (1, {})} | custom-call | flops 4400000000 | tf_op jit(solution)/shard_map/sort/pallas_call | solution.py:237
  27.9 5.2 %sort.6.refs_0_ = bf16[16,2,176,1024]{3,2,1,0:T(8,128)(2,1)} custom-call(bf16[16,2816,128]{2,1,0:T(8,128)(2,1)} %bitcast.44, bf16[16,2,176,1024]{3,2,1,0:T(8,128)(2,1)} %sort.5.refs_0_, bf16[144,1024]{1,0:T(8,128)(2,1)S(1)} %collective-permute-done.2.refs_1_, bf16[144,1664]{1,0:T(8,128)(2,1)S(1)} %collective-permute-done.refs_2_), custom_call_target="tpu_custom_call", output_to_operand_aliasing={{}: (1, {})} | custom-call | flops 4400000000 | tf_op jit(solution)/shard_map/sort/pallas_call | solution.py:237
  34.8 1.6 %collective-permute-start.4 = (bf16[144,1024]{1,0:T(8,128)(2,1)S(1)}, bf16[144,1024]{1,0:T(8,128)(2,1)S(1)}, u32[]{:S(2)}, u32[]{:S(2)}) collective-permute-start(bf16[144,1024]{1,0:T(8,128)(2,1)S(1)} %collective-permute-done.3.refs_1_), channel_id=1, source_target_pairs={{0,8},{4,12},{8,0},{12,4},{1,9},{5,13},{9,1},{13,5},{2,10},{6,14},... | collective-permute-start | bytes 884744 | tf_op jit(solution)/shard_map/ppermute | solution.py:412
  36.3 5.1 %sort.7.refs_8_ = bf16[16,2,176,1024]{3,2,1,0:T(8,128)(2,1)} custom-call(bf16[16,2816,128]{2,1,0:T(8,128)(2,1)} %bitcast.45, bf16[16,2,176,1024]{3,2,1,0:T(8,128)(2,1)} %sort.6.refs_0_, bf16[144,1024]{1,0:T(8,128)(2,1)S(1)} %collective-permute-done.3.refs_1_), custom_call_target="tpu_custom_call", output_to_operand_aliasing={{}: (1, {})} | custom-call | flops 4400000000 | tf_op jit(solution)/shard_map/sort/pallas_call | solution.py:237
  41.4 2.8 %collective-permute-done.4 = bf16[144,1024]{1,0:T(8,128)(2,1)S(1)} collective-permute-done((bf16[144,1024]{1,0:T(8,128)(2,1)S(1)}, bf16[144,1024]{1,0:T(8,128)(2,1)S(1)}, u32[]{:S(2)}, u32[]{:S(2)}) %collective-permute-start.4) | collective-permute-done | bytes 294944 | tf_op jit(solution)/shard_map/ppermute | solution.py:412
  44.3 1.5 %dispatch.6 = (bf16[16,64,1024]{2,1,0:T(8,128)(2,1)S(1)}, f32[16,64,128]{2,1,0:T(8,128)S(1)}, bf16[4,256,128]{2,1,0:T(8,128)(2,1)S(1)}) custom-call(s32[1]{0:T(128)} %bitcast.15.base_ref, bf16[64,1024]{1,0:T(8,128)(2,1)S(1)} %fusion.rw_ref, bf16[288,1024]{1,0:T(8,128)(2,1)S(1)} %constant_dynamic-update-slice_fusion.2.refs_0_.refs_1_, ...), custom_call_target="tpu_custom_call" | custom-call | flops 3300000000 | tf_op jit(solution)/shard_map/dispatch/pallas_call | solution.py:144
  45.8 1.5 %dispatch.7 = (bf16[16,64,1024]{2,1,0:T(8,128)(2,1)S(1)}, f32[16,64,128]{2,1,0:T(8,128)S(1)}, bf16[4,256,128]{2,1,0:T(8,128)(2,1)S(1)}) custom-call(s32[1]{0:T(128)} %bitcast.15.base_ref, bf16[64,1024]{1,0:T(8,128)(2,1)S(1)} %fusion.rw_ref, bf16[288,1024]{1,0:T(8,128)(2,1)S(1)} %constant_dynamic-update-slice_fusion.4.refs_0_.refs_1_, ...), custom_call_target="tpu_custom_call" | custom-call | flops 3300000000 | tf_op jit(solution)/shard_map/dispatch/pallas_call | solution.py:144
  47.4 1.6 %dispatch.5 = (bf16[16,64,1024]{2,1,0:T(8,128)(2,1)S(1)}, f32[16,64,128]{2,1,0:T(8,128)S(1)}, bf16[4,256,128]{2,1,0:T(8,128)(2,1)S(1)}, f32[8,128]{1,0:T(8,128)S(1)}) custom-call(s32[1]{0:T(128)} %bitcast.15.base_ref, bf16[64,1024]{1,0:T(8,128)(2,1)S(1)} %fusion.rw_ref, bf16[288,1664]{1,0:T(8,128)(2,1)S(1)} %pad_maximum_fusion.refs_0_.refs_1_, ...), custom_call_target="tpu_custom_call" | custom-call | flops 3300000000 | tf_op jit(solution)/shard_map/dispatch/pallas_call | solution.py:144
  48.9 1.5 %dispatch.4 = (bf16[16,64,1024]{2,1,0:T(8,128)(2,1)S(1)}, f32[16,64,128]{2,1,0:T(8,128)S(1)}, bf16[4,256,128]{2,1,0:T(8,128)(2,1)S(1)}) custom-call(s32[1]{0:T(128)} %bitcast.15.base_ref, bf16[64,1024]{1,0:T(8,128)(2,1)S(1)} %fusion.rw_ref, bf16[288,1024]{1,0:T(8,128)(2,1)S(1)} %constant_dynamic-update-slice_fusion.refs_0_.refs_1_, ...), custom_call_target="tpu_custom_call" | custom-call | flops 3300000000 | tf_op jit(solution)/shard_map/dispatch/pallas_call | solution.py:144
  50.5 12.8 %experts.1 = (bf16[16,64,1024]{2,1,0:T(8,128)(2,1)S(1)}, bf16[16,64,1024]{2,1,0:T(8,128)(2,1)S(1)}, bf16[16,64,1024]{2,1,0:T(8,128)(2,1)S(1)}, bf16[16,64,1024]{2,1,0:T(8,128)(2,1)S(1)}) custom-call(bf16[16,64,1024]{2,1,0:T(8,128)(2,1)S(1)} %get-tuple-element.29.refs_0_, bf16[16,64,1024]{2,1,0:T(8,128)(2,1)S(1)} %get-tuple-element.30.refs_1_, ...), custom_call_target="tpu_custom_call" | custom-call | flops 6600000000 | tf_op jit(solution)/shard_map/experts/pallas_call | solution.py:295
  66.6 1.6 %collective-permute-start.12 = (bf16[1,128,1024]{2,1,0:T(8,128)(2,1)S(1)}, bf16[1,128,1024]{2,1,0:T(8,128)(2,1)S(1)}, u32[]{:S(2)}, u32[]{:S(2)}) collective-permute-start(bf16[1,128,1024]{2,1,0:T(8,128)(2,1)S(1)} %add_convert_fusion.7), channel_id=1, source_target_pairs={{0,8},{4,12},{8,0},{12,4},{1,9},{5,13},{9,1},{13,5},{2,10},{6,14},... | collective-permute-start | bytes 786440 | tf_op jit(solution)/shard_map/ppermute | solution.py:412
  68.9 1.6 %collective-permute-start.18 = (bf16[1,128,1024]{2,1,0:T(8,128)(2,1)S(1)}, bf16[1,128,1024]{2,1,0:T(8,128)(2,1)S(1)}, u32[]{:S(2)}, u32[]{:S(2)}) collective-permute-start(bf16[1,128,1024]{2,1,0:T(8,128)(2,1)S(1)} %add_convert_fusion.3), channel_id=1, source_target_pairs={{0,8},{4,12},{8,0},{12,4},{1,9},{5,13},{9,1},{13,5},{2,10},{6,14},... | collective-permute-start | bytes 786440 | tf_op jit(solution)/shard_map/ppermute | solution.py:412
  71.1 4.6 %collective-permute-done.12 = bf16[1,128,1024]{2,1,0:T(8,128)(2,1)S(1)} collective-permute-done((bf16[1,128,1024]{2,1,0:T(8,128)(2,1)S(1)}, bf16[1,128,1024]{2,1,0:T(8,128)(2,1)S(1)}, u32[]{:S(2)}, u32[]{:S(2)}) %collective-permute-start.12) | collective-permute-done | bytes 262176 | tf_op jit(solution)/shard_map/ppermute | solution.py:412
  77.0 4.4 %collective-permute-done.15 = bf16[1,128,1024]{2,1,0:T(8,128)(2,1)S(1)} collective-permute-done((bf16[1,128,1024]{2,1,0:T(8,128)(2,1)S(1)}, bf16[1,128,1024]{2,1,0:T(8,128)(2,1)S(1)}, u32[]{:S(2)}, u32[]{:S(2)}) %collective-permute-start.15) | collective-permute-done | bytes 262176 | tf_op jit(solution)/shard_map/ppermute | solution.py:412
  81.5 1.6 %collective-permute-start.16 = (bf16[1,128,1024]{2,1,0:T(8,128)(2,1)S(1)}, bf16[1,128,1024]{2,1,0:T(8,128)(2,1)S(1)}, u32[]{:S(2)}, u32[]{:S(2)}) collective-permute-start(bf16[1,128,1024]{2,1,0:T(8,128)(2,1)S(1)} %add_convert_fusion.4), channel_id=1, source_target_pairs={{0,3},{1,2},{2,1},{3,0},{4,7},{5,6},{6,5},{7,4},{8,11},{9,10},{10,... | collective-permute-start | bytes 786440 | tf_op jit(solution)/shard_map/ppermute | solution.py:415
  83.1 3.9 %collective-permute-done.18 = bf16[1,128,1024]{2,1,0:T(8,128)(2,1)S(1)} collective-permute-done((bf16[1,128,1024]{2,1,0:T(8,128)(2,1)S(1)}, bf16[1,128,1024]{2,1,0:T(8,128)(2,1)S(1)}, u32[]{:S(2)}, u32[]{:S(2)}) %collective-permute-start.18) | collective-permute-done | bytes 262176 | tf_op jit(solution)/shard_map/ppermute | solution.py:412
  87.1 1.8 %collective-permute-start.19 = (bf16[1,128,1024]{2,1,0:T(8,128)(2,1)S(1)}, bf16[1,128,1024]{2,1,0:T(8,128)(2,1)S(1)}, u32[]{:S(2)}, u32[]{:S(2)}) collective-permute-start(bf16[1,128,1024]{2,1,0:T(8,128)(2,1)S(1)} %add_convert_fusion.2), channel_id=1, source_target_pairs={{0,1},{1,0},{2,3},{3,2},{4,5},{5,4},{6,7},{7,6},{8,9},{9,8},{10,11... | collective-permute-start | bytes 786440 | tf_op jit(solution)/shard_map/ppermute | solution.py:415
  88.9 6.2 %attention.1 = bf16[128,4096]{1,0:T(8,128)(2,1)} custom-call(s32[128,1]{1,0:T(8,128)S(1)} %copy.23.first_ref, s32[128,1]{1,0:T(8,128)S(1)} %copy.24.last_ref, s32[1,512]{1,0:T(1,128)S(1)} %bitcast.39, bf16[128,4608]{1,0:T(8,128)(2,1)S(1)} %bitcast.41, bf16[288,1664]{1,0:T(8,128)(2,1)S(1)} %pad_maximum_fusion.refs_0_.refs_1_, ...), custom_call_target="tpu_custom_call" | custom-call | flops 6600000000 | tf_op jit(solution)/shard_map/attention/pallas_call | solution.py:380
  95.7 1.3 %collective-permute-done.13 = bf16[1,128,1024]{2,1,0:T(8,128)(2,1)S(1)} collective-permute-done((bf16[1,128,1024]{2,1,0:T(8,128)(2,1)S(1)}, bf16[1,128,1024]{2,1,0:T(8,128)(2,1)S(1)}, u32[]{:S(2)}, u32[]{:S(2)}) %collective-permute-start.13) | collective-permute-done | bytes 262176 | tf_op jit(solution)/shard_map/ppermute | solution.py:415
  97.0 4.2 %collective-permute-done.19 = bf16[1,128,1024]{2,1,0:T(8,128)(2,1)S(1)} collective-permute-done((bf16[1,128,1024]{2,1,0:T(8,128)(2,1)S(1)}, bf16[1,128,1024]{2,1,0:T(8,128)(2,1)S(1)}, u32[]{:S(2)}, u32[]{:S(2)}) %collective-permute-start.19) | collective-permute-done | bytes 262176 | tf_op jit(solution)/shard_map/ppermute | solution.py:415
  (82 shorter events, 15.6 us)
Async XLA Ops:
  0.6 10.5 %copy-start.3 = (s32[1,8]{1,0:T(1,128)S(1)}, s32[1,8]{1,0:T(1,128)}, u32[]{:S(2)}) copy-start(s32[1,8]{1,0:T(1,128)} %param.10) | copy-start | bytes 100
  2.3 14.7 %collective-permute-start.2 = (bf16[144,1024]{1,0:T(8,128)(2,1)S(1)}, bf16[144,1024]{1,0:T(8,128)(2,1)S(1)}, u32[]{:S(2)}, u32[]{:S(2)}) collective-permute-start(bf16[144,1024]{1,0:T(8,128)(2,1)S(1)} %pad_maximum_fusion.2), channel_id=1, source_target_pairs={{0,3},{1,2},{2,1},{3,0},{4,7},{5,6},{6,5},{7,4},{8,11},{9,10},{10,... | collective-permute-start | bytes 884744 | tf_op jit(solution)/shard_map/ppermute | solution.py:415
  7.5 14.5 %collective-permute-start.6 = (bf16[144,1024]{1,0:T(8,128)(2,1)S(1)}, bf16[144,1024]{1,0:T(8,128)(2,1)S(1)}, u32[]{:S(2)}, u32[]{:S(2)}) collective-permute-start(bf16[144,1024]{1,0:T(8,128)(2,1)S(1)} %pad_maximum_fusion.2), channel_id=1, source_target_pairs={{0,1},{1,0},{2,3},{3,2},{4,5},{5,4},{6,7},{7,6},{8,9},{9,8},{10,11... | collective-permute-start | bytes 884744 | tf_op jit(solution)/shard_map/ppermute | solution.py:415
  9.5 18.2 %collective-permute-start = (bf16[144,1664]{1,0:T(8,128)(2,1)S(1)}, bf16[144,1664]{1,0:T(8,128)(2,1)S(1)}, u32[]{:S(2)}, u32[]{:S(2)}) collective-permute-start(bf16[144,1664]{1,0:T(8,128)(2,1)S(1)} %pad_maximum_fusion.1), channel_id=1, source_target_pairs={{0,8},{4,12},{8,0},{12,4},{1,9},{5,13},{9,1},{13,5},{2,10},{6,14},... | collective-permute-start | bytes 1437704 | tf_op jit(solution)/shard_map/ppermute | solution.py:412
  17.1 16.0 %collective-permute-start.9 = (bf16[144,1024]{1,0:T(8,128)(2,1)S(1)}, bf16[144,1024]{1,0:T(8,128)(2,1)S(1)}, u32[]{:S(2)}, u32[]{:S(2)}) collective-permute-start(bf16[144,1024]{1,0:T(8,128)(2,1)S(1)} %collective-permute-done.2.refs_1_), channel_id=1, source_target_pairs={{0,8},{4,12},{8,0},{12,4},{1,9},{5,13},{9,1},{13,5},{2,10},{6,14},... | collective-permute-start | bytes 884744 | tf_op jit(solution)/shard_map/ppermute | solution.py:412
  17.7 17.1 %collective-permute-start.3 = (bf16[144,1024]{1,0:T(8,128)(2,1)S(1)}, bf16[144,1024]{1,0:T(8,128)(2,1)S(1)}, u32[]{:S(2)}, u32[]{:S(2)}) collective-permute-start(bf16[144,1024]{1,0:T(8,128)(2,1)S(1)} %collective-permute-done.2.refs_1_), channel_id=1, source_target_pairs={{0,1},{1,0},{2,3},{3,2},{4,5},{5,4},{6,7},{7,6},{8,9},{9,8},{10,11... | collective-permute-start | bytes 884744 | tf_op jit(solution)/shard_map/ppermute | solution.py:415
  22.0 12.7 %collective-permute-start.7 = (bf16[144,1024]{1,0:T(8,128)(2,1)S(1)}, bf16[144,1024]{1,0:T(8,128)(2,1)S(1)}, u32[]{:S(2)}, u32[]{:S(2)}) collective-permute-start(bf16[144,1024]{1,0:T(8,128)(2,1)S(1)} %collective-permute-done.6.refs_1_), channel_id=1, source_target_pairs={{0,8},{4,12},{8,0},{12,4},{1,9},{5,13},{9,1},{13,5},{2,10},{6,14},... | collective-permute-start | bytes 884744 | tf_op jit(solution)/shard_map/ppermute | solution.py:412
  27.9 19.4 %collective-permute-start.1 = (bf16[288,1664]{1,0:T(8,128)(2,1)S(1)}, bf16[288,1664]{1,0:T(8,128)(2,1)S(1)}, u32[]{:S(2)}, u32[]{:S(2)}) collective-permute-start(bf16[288,1664]{1,0:T(8,128)(2,1)S(1)} %pad_maximum_fusion.refs_0_.refs_1_), channel_id=1, source_target_pairs={{0,4},{4,0},{8,12},{12,8},{1,5},{5,1},{9,13},{13,9},{2,6},{6,2},{1... | collective-permute-start | bytes 2875400 | tf_op jit(solution)/shard_map/ppermute | solution.py:412
  33.2 12.6 %collective-permute-start.10 = (bf16[288,1024]{1,0:T(8,128)(2,1)S(1)}, bf16[288,1024]{1,0:T(8,128)(2,1)S(1)}, u32[]{:S(2)}, u32[]{:S(2)}) collective-permute-start(bf16[288,1024]{1,0:T(8,128)(2,1)S(1)} %constant_dynamic-update-slice_fusion.4.refs_0_.refs_1_), channel_id=1, source_target_pairs={{0,4},{4,0},{8,12},{12,8},{1,5},{5,1},{9,13},{13,9},{2,6},{6,2},{1... | collective-permute-start | bytes 1769480 | tf_op jit(solution)/shard_map/ppermute | solution.py:412
  34.7 9.6 %collective-permute-start.8 = (bf16[288,1024]{1,0:T(8,128)(2,1)S(1)}, bf16[288,1024]{1,0:T(8,128)(2,1)S(1)}, u32[]{:S(2)}, u32[]{:S(2)}) collective-permute-start(bf16[288,1024]{1,0:T(8,128)(2,1)S(1)} %constant_dynamic-update-slice_fusion.2.refs_0_.refs_1_), channel_id=1, source_target_pairs={{0,4},{4,0},{8,12},{12,8},{1,5},{5,1},{9,13},{13,9},{2,6},{6,2},{1... | collective-permute-start | bytes 1769480 | tf_op jit(solution)/shard_map/ppermute | solution.py:412
  34.8 9.4 %collective-permute-start.4 = (bf16[144,1024]{1,0:T(8,128)(2,1)S(1)}, bf16[144,1024]{1,0:T(8,128)(2,1)S(1)}, u32[]{:S(2)}, u32[]{:S(2)}) collective-permute-start(bf16[144,1024]{1,0:T(8,128)(2,1)S(1)} %collective-permute-done.3.refs_1_), channel_id=1, source_target_pairs={{0,8},{4,12},{8,0},{12,4},{1,9},{5,13},{9,1},{13,5},{2,10},{6,14},... | collective-permute-start | bytes 884744 | tf_op jit(solution)/shard_map/ppermute | solution.py:412
  44.2 4.7 %collective-permute-start.5 = (bf16[288,1024]{1,0:T(8,128)(2,1)S(1)}, bf16[288,1024]{1,0:T(8,128)(2,1)S(1)}, u32[]{:S(2)}, u32[]{:S(2)}) collective-permute-start(bf16[288,1024]{1,0:T(8,128)(2,1)S(1)} %constant_dynamic-update-slice_fusion.refs_0_.refs_1_), channel_id=1, source_target_pairs={{0,4},{4,0},{8,12},{12,8},{1,5},{5,1},{9,13},{13,9},{2,6},{6,2},{1... | collective-permute-start | bytes 1769480 | tf_op jit(solution)/shard_map/ppermute | solution.py:412
  63.8 2.7 %collective-permute-start.11 = (bf16[1,256,1024]{2,1,0:T(8,128)(2,1)S(1)}, bf16[1,256,1024]{2,1,0:T(8,128)(2,1)S(1)}, u32[]{:S(2)}, u32[]{:S(2)}) collective-permute-start(bf16[1,256,1024]{2,1,0:T(8,128)(2,1)S(1)} %get-tuple-element.39), channel_id=1, source_target_pairs={{0,4},{4,0},{8,12},{12,8},{1,5},{5,1},{9,13},{13,9},{2,6},{6,2},{1... | collective-permute-start | bytes 1572872 | tf_op jit(solution)/shard_map/ppermute | solution.py:412
  64.8 3.3 %collective-permute-start.14 = (bf16[1,256,1024]{2,1,0:T(8,128)(2,1)S(1)}, bf16[1,256,1024]{2,1,0:T(8,128)(2,1)S(1)}, u32[]{:S(2)}, u32[]{:S(2)}) collective-permute-start(bf16[1,256,1024]{2,1,0:T(8,128)(2,1)S(1)} %get-tuple-element.43), channel_id=1, source_target_pairs={{0,4},{4,0},{8,12},{12,8},{1,5},{5,1},{9,13},{13,9},{2,6},{6,2},{1... | collective-permute-start | bytes 1572872 | tf_op jit(solution)/shard_map/ppermute | solution.py:412
  65.4 3.4 %collective-permute-start.17 = (bf16[1,256,1024]{2,1,0:T(8,128)(2,1)S(1)}, bf16[1,256,1024]{2,1,0:T(8,128)(2,1)S(1)}, u32[]{:S(2)}, u32[]{:S(2)}) collective-permute-start(bf16[1,256,1024]{2,1,0:T(8,128)(2,1)S(1)} %get-tuple-element.47), channel_id=1, source_target_pairs={{0,4},{4,0},{8,12},{12,8},{1,5},{5,1},{9,13},{13,9},{2,6},{6,2},{1... | collective-permute-start | bytes 1572872 | tf_op jit(solution)/shard_map/ppermute | solution.py:412
  66.4 4.0 %collective-permute-start.20 = (bf16[1,256,1024]{2,1,0:T(8,128)(2,1)S(1)}, bf16[1,256,1024]{2,1,0:T(8,128)(2,1)S(1)}, u32[]{:S(2)}, u32[]{:S(2)}) collective-permute-start(bf16[1,256,1024]{2,1,0:T(8,128)(2,1)S(1)} %get-tuple-element.51), channel_id=1, source_target_pairs={{0,4},{4,0},{8,12},{12,8},{1,5},{5,1},{9,13},{13,9},{2,6},{6,2},{1... | collective-permute-start | bytes 1572872 | tf_op jit(solution)/shard_map/ppermute | solution.py:412
  66.6 9.2 %collective-permute-start.12 = (bf16[1,128,1024]{2,1,0:T(8,128)(2,1)S(1)}, bf16[1,128,1024]{2,1,0:T(8,128)(2,1)S(1)}, u32[]{:S(2)}, u32[]{:S(2)}) collective-permute-start(bf16[1,128,1024]{2,1,0:T(8,128)(2,1)S(1)} %add_convert_fusion.7), channel_id=1, source_target_pairs={{0,8},{4,12},{8,0},{12,4},{1,9},{5,13},{9,1},{13,5},{2,10},{6,14},... | collective-permute-start | bytes 786440 | tf_op jit(solution)/shard_map/ppermute | solution.py:412
  68.2 13.2 %collective-permute-start.15 = (bf16[1,128,1024]{2,1,0:T(8,128)(2,1)S(1)}, bf16[1,128,1024]{2,1,0:T(8,128)(2,1)S(1)}, u32[]{:S(2)}, u32[]{:S(2)}) collective-permute-start(bf16[1,128,1024]{2,1,0:T(8,128)(2,1)S(1)} %add_convert_fusion.5), channel_id=1, source_target_pairs={{0,8},{4,12},{8,0},{12,4},{1,9},{5,13},{9,1},{13,5},{2,10},{6,14},... | collective-permute-start | bytes 786440 | tf_op jit(solution)/shard_map/ppermute | solution.py:412
  68.9 20.0 %copy-start = (bf16[1,128,4608]{2,1,0:T(8,128)(2,1)S(1)}, bf16[1,128,4608]{2,1,0:T(8,128)(2,1)}, u32[]{:S(2)}) copy-start(bf16[1,128,4608]{2,1,0:T(8,128)(2,1)} %param.8) | copy-start | bytes 3538948
  68.9 18.1 %collective-permute-start.18 = (bf16[1,128,1024]{2,1,0:T(8,128)(2,1)S(1)}, bf16[1,128,1024]{2,1,0:T(8,128)(2,1)S(1)}, u32[]{:S(2)}, u32[]{:S(2)}) collective-permute-start(bf16[1,128,1024]{2,1,0:T(8,128)(2,1)S(1)} %add_convert_fusion.3), channel_id=1, source_target_pairs={{0,8},{4,12},{8,0},{12,4},{1,9},{5,13},{9,1},{13,5},{2,10},{6,14},... | collective-permute-start | bytes 786440 | tf_op jit(solution)/shard_map/ppermute | solution.py:412
  70.5 25.2 %collective-permute-start.21 = (bf16[1,128,1024]{2,1,0:T(8,128)(2,1)S(1)}, bf16[1,128,1024]{2,1,0:T(8,128)(2,1)S(1)}, u32[]{:S(2)}, u32[]{:S(2)}) collective-permute-start(bf16[1,128,1024]{2,1,0:T(8,128)(2,1)S(1)} %add_convert_fusion.1), channel_id=1, source_target_pairs={{0,8},{4,12},{8,0},{12,4},{1,9},{5,13},{9,1},{13,5},{2,10},{6,14},... | collective-permute-start | bytes 786440 | tf_op jit(solution)/shard_map/ppermute | solution.py:412
  75.9 21.1 %collective-permute-start.13 = (bf16[1,128,1024]{2,1,0:T(8,128)(2,1)S(1)}, bf16[1,128,1024]{2,1,0:T(8,128)(2,1)S(1)}, u32[]{:S(2)}, u32[]{:S(2)}) collective-permute-start(bf16[1,128,1024]{2,1,0:T(8,128)(2,1)S(1)} %add_convert_fusion.6), channel_id=1, source_target_pairs={{0,2},{1,3},{2,0},{3,1},{4,6},{5,7},{6,4},{7,5},{8,10},{9,11},{10,... | collective-permute-start | bytes 786440 | tf_op jit(solution)/shard_map/ppermute | solution.py:415
  81.5 15.5 %collective-permute-start.16 = (bf16[1,128,1024]{2,1,0:T(8,128)(2,1)S(1)}, bf16[1,128,1024]{2,1,0:T(8,128)(2,1)S(1)}, u32[]{:S(2)}, u32[]{:S(2)}) collective-permute-start(bf16[1,128,1024]{2,1,0:T(8,128)(2,1)S(1)} %add_convert_fusion.4), channel_id=1, source_target_pairs={{0,3},{1,2},{2,1},{3,0},{4,7},{5,6},{6,5},{7,4},{8,11},{9,10},{10,... | collective-permute-start | bytes 786440 | tf_op jit(solution)/shard_map/ppermute | solution.py:415
  87.1 14.1 %collective-permute-start.19 = (bf16[1,128,1024]{2,1,0:T(8,128)(2,1)S(1)}, bf16[1,128,1024]{2,1,0:T(8,128)(2,1)S(1)}, u32[]{:S(2)}, u32[]{:S(2)}) collective-permute-start(bf16[1,128,1024]{2,1,0:T(8,128)(2,1)S(1)} %add_convert_fusion.2), channel_id=1, source_target_pairs={{0,1},{1,0},{2,3},{3,2},{4,5},{5,4},{6,7},{7,6},{8,9},{9,8},{10,11... | collective-permute-start | bytes 786440 | tf_op jit(solution)/shard_map/ppermute | solution.py:415
  (4 other events, 15.0 us)

commit v9 on v8

--- a/solution.py
+++ b/solution.py
@@ -17,9 +17,9 @@
 EXPERT_ROWS = 256
 EXTRA = 16
 VMEM = 14 * 2**20
-VMEM_EXPERTS = 24 * 2**20
+VMEM_EXPERTS = 20 * 2**20
 VMEM_SORT = 52 * 2**20
-PIECES = 4
+PIECES = 2
 DEPTH = 3
 PEAK = 1.1e9
 
@@ -47,8 +47,8 @@
     )
 
 
-def dispatch_kernel(n_parts, n_row, top, n_after, base_ref, rw_ref, *refs):
-    parts, refs = refs[:n_parts], refs[n_parts + n_after :]
+def dispatch_kernel(n_parts, n_row, top, n_carried, base_ref, rw_ref, *refs):
+    parts, carried, refs = refs[:n_parts], refs[n_parts : n_parts + n_carried], refs[n_parts + n_carried :]
     if n_row:
         seg_ref, scale_ref = refs[:2]
         refs = refs[2:]
@@ -90,6 +90,8 @@
         rows_ref[:, at, :] = taken.astype(jnp.bfloat16).reshape(local, CAP, width)
         hots.append(hot)
         probs.append(prob)
+    for source, target in zip(carried, refs[len(refs) - n_carried :]):
+        target[...] = source[...]
     if n_row:
         bal_ref = refs[3]
         for d in range(NDOC):
@@ -114,7 +116,7 @@
     return pl.BlockSpec(a.shape, lambda *i: (0,) * a.ndim)
 
 
-def dispatch(parts, n, top, base, rw, local, row=None, after=()):
+def dispatch(parts, n, top, base, rw, local, row=None, carried=()):
     n_parts = len(parts)
     width = rw.shape[1]
     slots = n_parts * CAP
@@ -124,7 +126,7 @@
     ] + [
         pl.BlockSpec((BLOCK + EXTRA, width), lambda i, k=k: (k + i, 0)) for _, k in parts
     ]
-    in_specs += [ANYWHERE] * len(after)
+    in_specs += [whole(a) for a in carried]
     out_specs = [
         pl.BlockSpec((local, slots, width), lambda i: (0, i, 0)),
         pl.BlockSpec((local, slots, LANES), lambda i: (0, i, 0)),
@@ -141,8 +143,10 @@
         in_specs += [whole(a) for a in row]
         out_specs.append(pl.BlockSpec((NDOC, LANES), lambda i: (0, 0)))
         out_shape.append(jax.ShapeDtypeStruct((NDOC, LANES), jnp.float32))
+    out_specs += [whole(a) for a in carried]
+    out_shape += [jax.ShapeDtypeStruct(a.shape, a.dtype) for a in carried]
     return call(
-        functools.partial(dispatch_kernel, n_parts, n_parts if row is not None else 0, top, len(after)),
+        functools.partial(dispatch_kernel, n_parts, n_parts if row is not None else 0, top, len(carried)),
         3 * n,
         (n,),
         in_specs,
@@ -150,7 +154,7 @@
         out_shape,
         [],
         "dispatch",
-    )(base, rw, *[a for a, _ in parts], *after, *extra)
+    )(base, rw, *[a for a, _ in parts], *carried, *extra)
 
 
 def fetch(sources, slots, sem, step, steps, first, start=0):
@@ -189,7 +193,8 @@
 
 
 def sort_kernel(start, gu_ref, *refs):
-    out_ref, held, made, wide, in_sem, out_sem = refs[-6:]
+    out_ref, token_ref, held, made, wide, in_sem, out_sem = refs[-7:]
+    token_ref[...] = jnp.zeros_like(token_ref)
     step, steps = pl.program_id(0), pl.num_programs(0)
     _, group, _, hidden, width = made.shape
     chunks = width // LANES
@@ -226,21 +231,24 @@
 def sort_rows(gate_up, behind):
     local, hidden, _, width = gate_up.shape
     pieces = PIECES if local % (2 * PIECES) == 0 else 1
-    group = 2 if local % 2 == 0 else 1
+    group = 1
     chunks = width // LANES
     gu = gate_up.reshape(local, hidden, 2, chunks, LANES).swapaxes(2, 3)
     gu = gu.reshape(local, hidden * 2 * chunks, LANES)
     done = ()
     for j in range(pieces):
         after = behind[j] if pieces > 1 else ()
-        done = (
+        *done, token = (
             call(
                 functools.partial(sort_kernel, j * local // pieces),
-                4,
+                8 // pieces,
                 (local // pieces // group,),
                 [IN_HBM] + [IN_HBM] * len(done) + [ANYWHERE] * len(after),
-                IN_HBM,
-                jax.ShapeDtypeStruct((local, 2, hidden, width), jnp.bfloat16),
+                [IN_HBM, pl.BlockSpec((8, LANES), lambda e: (0, 0))],
+                [
+                    jax.ShapeDtypeStruct((local, 2, hidden, width), jnp.bfloat16),
+                    jax.ShapeDtypeStruct((8, LANES), jnp.float32),
+                ],
                 [
                     pltpu.VMEM((2, group) + gu.shape[1:], jnp.bfloat16),
                     pltpu.VMEM((2, group, 2, hidden, width), jnp.bfloat16),
@@ -251,9 +259,29 @@
                 "sort",
                 VMEM_SORT,
                 {1: 0} if done else {},
-            )(gu, *done, *after),
+            )(gu, *done, *after)
         )
-    return done[0]
+    return done[0], token
+
+
+def stack_kernel(a_ref, b_ref, *refs):
+    rows = a_ref.shape[0]
+    refs[-1][:rows, :] = a_ref[...]
+    refs[-1][rows:, :] = b_ref[...]
+
+
+def stack(a, b, before):
+    rows, width = a.shape
+    return call(
+        stack_kernel,
+        1,
+        (1,),
+        [whole(a), whole(b)] + [ANYWHERE] * len(before),
+        pl.BlockSpec((2 * rows, width), lambda i: (0, 0)),
+        jax.ShapeDtypeStruct((2 * rows, width), a.dtype),
+        [],
+        "stack",
+    )(a, b, *before)
 
 
 def expert_kernel(n, *refs):
@@ -272,10 +300,12 @@
     )
     for e in range(group):
         held = jnp.concatenate([r[e] for r in rows], axis=0)
-        g = lax.dot_general(held, gu[slot, e, 0], NT, preferred_element_type=jnp.float32)
-        u = lax.dot_general(held, gu[slot, e, 1], NT, preferred_element_type=jnp.float32)
+        _, hidden, width = gu.shape[2:]
+        both = gu[slot, e].reshape(2 * hidden, width)
+        both = lax.dot_general(both, held, NT, preferred_element_type=jnp.float32)
+        g, u = both[:hidden], both[hidden:]
         inner = (g * lax.logistic(g) * u).astype(jnp.bfloat16)
-        made = jnp.dot(inner, down[slot, e], preferred_element_type=jnp.float32)
+        made = lax.dot_general(inner, down[slot, e], TN, preferred_element_type=jnp.float32)
         for i in range(n):
             w = weights[i][e]
             part = made[i * size : (i + 1) * size]
@@ -405,7 +435,6 @@
     local = gate_up.shape[0]
     near = n_exp == 4
     shifts = [0, 1, 3, 2] if near else [0]
-    flips = (2, 1)
     tokens = hidden_in[0]
 
     def flip(a, bit):
@@ -430,28 +459,16 @@
 
     near_parts = along_exp(packed)
     arrived = list(near_parts)
-    if near:
-        kdim = latent_kv.shape[2]
-        keys = jnp.pad(latent_kv[0], ((0, EXTRA), (0, -kdim % LANES)))
-        near_parts[0] = jnp.concatenate([packed, keys], axis=1)
     crossed = [flip(a, 2) for a in near_parts]
     if near:
         blocks = 1
-        pairs = [jnp.concatenate([a, b], axis=0) for a, b in zip(near_parts, crossed)]
+        pairs = [jnp.concatenate([a, b], axis=0) for a, b in zip(near_parts[:-1], crossed[:-1])]
         flipped = [flip(a, 1) for a in pairs]
         spread = [[(a, 0), (a, 1), (b, 0), (b, 1)] for a, b in zip(pairs, flipped)]
-        kv = [(a, k * (BLOCK + EXTRA)) for a, k in spread[0]]
     else:
         blocks = near_parts[0].shape[0] // (BLOCK + EXTRA)
         spread = [[(near_parts[0], 0), (crossed[0], 0)]]
         spread[0] = spread[0] + [(flip(a, 1), 0) for a, _ in spread[0]]
-        kv = [latent_kv[0]]
-        for bit in flips:
-            kv = kv + [flip(a, bit) for a in kv]
-        kv = [(a, 0) for a in kv]
-    behind = [()] * PIECES
-    if near:
-        behind = [(), (arrived[1],), (arrived[2], crossed[0]), (arrived[3],)]
 
     lengths = doc_lengths[0]
     ends = jnp.cumsum(lengths)
@@ -459,8 +476,6 @@
     pos = row_pos[0]
     passed = pos[:, None] >= ends[None, :]
     first = jnp.max(jnp.where(passed, ends[None, :], 0), axis=1)
-    context = attend(queries[0], kv, first[:, None], pos[:, None], row_pos.reshape(1, -1))
-
     seg = jnp.sum((row_pos[..., None] >= ends).astype(jnp.int32), axis=-1)
     sizes = lengths.astype(jnp.float32)
     scale = jnp.broadcast_to((EXPERTS / (top * sizes * sizes))[:, None], (NDOC, LANES))
@@ -468,18 +483,28 @@
     base = (exp * local).reshape(1).astype(jnp.int32)
     rw = jnp.roll(router_weight.T, -exp * local, axis=0)
     balance = None
-    gu = sort_rows(gate_up, behind)
-    sent = []
+    gu, token = sort_rows(gate_up, [(), (arrived[2],)] if near else [(), ()])
+    sent, keys = [], latent_kv[0]
     for i in range(len(shifts)):
+        if near and i + 1 == len(shifts):
+            before = [token] + [a[0] for a in sent]
+            pair = stack(near_parts[i], crossed[i], before)
+            flipped = flip(pair, 1)
+            spread.append([(pair, 0), (pair, 1), (flipped, 0), (flipped, 1)])
         row = (seg.reshape(-1, 1, BLOCK), scale) if near and i == 0 else None
-        out = dispatch(spread[i], blocks, top, base, rw, local, row)
+        carried = (keys,) if i + 1 == len(shifts) else ()
+        out = dispatch(spread[i], blocks, top, base, rw, local, row, carried)
         sent.append(out[:3])
         if row is not None:
             balance = out[3]
+        if carried:
+            keys = out[-1]
+    keys = jnp.concatenate([keys, flip(keys, 2)], axis=0)
+    keys = [keys, flip(keys, 1)]
     made = experts([a[0] for a in sent], [a[1] for a in sent], gu, w_down)
     back = []
     for i in reversed(range(len(shifts))):
-        keep, give = combine([sent[i][2]], [made[i]], n_ctx)
+        keep, give = combine([sent[i][2]], [made[i]], n_ctx, () if i else (keys[1],))
         got = flip(give, 1)
         far = added(keep[:, tok_rows:], got[:, tok_rows:])
         terms = [keep[:, :tok_rows], got[:, :tok_rows], flip(far, 2)]
@@ -487,6 +512,8 @@
             back.append(shift(added(*terms), shifts[i]))
         else:
             back = back + terms
+    kv = [(a, k * tok_rows) for a in keys for k in range(2)]
+    context = attend(queries[0], kv, first[:, None], pos[:, None], row_pos.reshape(1, -1))
     if near:
         expert_mix = added(*back)
     else:

time: 103 us -> 116 us (1.13)
  waiting for transfers between devices: 22.1 us -> 29 us
  Pallas kernels: 47.4 us -> 52.8 us
  local copies, waits for them, and re-layouts: 2.23 us -> 6.44 us
  starting transfers between devices: 24.5 us -> 22.3 us
    ppermute x16 -> x18, waiting for transfers between devices: 16.6 us -> 23.1 us  [flip(): return lax.ppermute(a, 'ctx', [(i, i ^ bit) for i in range(n_ctx)])]
    pallas_call x1, Pallas kernels: 12.8 us -> 17.7 us  [experts(): call(functools.partial(expert_kernel, n), 6, (local // group, slots // si...]
    ppermute x6, starting transfers between devices: 14 us -> 10.2 us  [shift(): return lax.ppermute(a, 'exp', [(i, i ^ d) for i in range(n_exp)])]
    unnamed x18 -> x48, local copies, waits for them, and re-layouts: 1.21 us -> 4.2 us
    ppermute x16 -> x18, starting transfers between devices: 10.6 us -> 12.1 us  [flip(): return lax.ppermute(a, 'ctx', [(i, i ^ bit) for i in range(n_ctx)])]
    pallas_call x4, Pallas kernels: 6 us -> 7.22 us  [dispatch(): call(functools.partial(dispatch_kernel, n_parts, n_parts if row is not No...]
    pallas_call x4 -> x3, Pallas kernels: 20.5 us -> 19.8 us  [the longest x2 19.7 us: sort_rows(): call(functools.partial(sort_kernel, j * local // pieces), 8 // pieces, (l...]
  transfers between devices with their start and end apart: 22 -> 24, of which waited for: 7 -> 8; matrix products, arithmetic and copies ran while one was open for 4% -> 4% of each run, Pallas kernels for 32% -> 43%
where the time goes in v9:
time: 116 us; the launch traced here: 115 us
  Pallas kernels  52.8 us (46%)
  waiting for transfers between devices  29 us (25%)
  starting transfers between devices  22.3 us (19%)
  local copies, waits for them, and re-layouts  6.44 us (6%)
  other arithmetic  3.88 us (3%)
    ppermute x18, waiting for transfers between devices, flip(): return lax.ppermute(a, 'ctx', [(i, i ^ bit) for i in range(n_ctx)])  23.1 us
    pallas_call x2, Pallas kernels, sort_rows(): call(functools.partial(sort_kernel, j * local // pieces), 8 // pieces, (l...  19.7 us
    pallas_call x1, Pallas kernels, experts(): call(functools.partial(expert_kernel, n), 6, (local // group, slots // si...  17.7 us
    ppermute x18, starting transfers between devices, flip(): return lax.ppermute(a, 'ctx', [(i, i ^ bit) for i in range(n_ctx)])  12.1 us
    ppermute x6, starting transfers between devices, shift(): return lax.ppermute(a, 'exp', [(i, i ^ d) for i in range(n_exp)])  10.2 us
    pallas_call x4, Pallas kernels, dispatch(): call(functools.partial(dispatch_kernel, n_parts, n_parts if row is not No...  7.22 us
    pallas_call x1, Pallas kernels, attend(): call(functools.partial(attend_kernel, [at for _, at in parts], kdim), 6,...  6.18 us
    ppermute x6, waiting for transfers between devices, shift(): return lax.ppermute(a, 'exp', [(i, i ^ d) for i in range(n_exp)])  5.96 us
  transfers between devices with their start and end apart: 24, of which 8 were waited for; matrix products, arithmetic and copies ran while one was open for 4% of the time, Pallas kernels for 43%

profile of v9, /device:TPU:0, one launch (start us, length us, event | category | flops | bytes accessed | tf_op | source)
XLA Modules:
  0.0 115.5 jit_solution(15168270247132908727)
XLA Ops:
  2.3 3.1 %collective-permute-start.5 = (bf16[144,1024]{1,0:T(8,128)(2,1)S(1)}, bf16[144,1024]{1,0:T(8,128)(2,1)S(1)}, u32[]{:S(2)}, u32[]{:S(2)}) collective-permute-start(bf16[144,1024]{1,0:T(8,128)(2,1)S(1)} %pad_maximum_fusion.1), channel_id=1, source_target_pairs={{0,1},{1,0},{2,3},{3,2},{4,5},{5,4},{6,7},{7,6},{8,9},{9,8},{10,11... | collective-permute-start | bytes 884744 | tf_op jit(solution)/shard_map/ppermute | solution.py:444
  5.4 2.5 %collective-permute-start = (bf16[144,1024]{1,0:T(8,128)(2,1)S(1)}, bf16[144,1024]{1,0:T(8,128)(2,1)S(1)}, u32[]{:S(2)}, u32[]{:S(2)}) collective-permute-start(bf16[144,1024]{1,0:T(8,128)(2,1)S(1)} %pad_maximum_fusion.1), channel_id=1, source_target_pairs={{0,3},{1,2},{2,1},{3,0},{4,7},{5,6},{6,5},{7,4},{8,11},{9,10},{10,... | collective-permute-start | bytes 884744 | tf_op jit(solution)/shard_map/ppermute | solution.py:444
  7.9 1.5 %collective-permute-start.3 = (bf16[144,1024]{1,0:T(8,128)(2,1)S(1)}, bf16[144,1024]{1,0:T(8,128)(2,1)S(1)}, u32[]{:S(2)}, u32[]{:S(2)}) collective-permute-start(bf16[144,1024]{1,0:T(8,128)(2,1)S(1)} %pad_maximum_fusion.1), channel_id=1, source_target_pairs={{0,8},{4,12},{8,0},{12,4},{1,9},{5,13},{9,1},{13,5},{2,10},{6,14},... | collective-permute-start | bytes 884744 | tf_op jit(solution)/shard_map/ppermute | solution.py:441
  9.5 10.2 %sort.2 = (bf16[16,2,176,1024]{3,2,1,0:T(8,128)(2,1)}, f32[8,128]{1,0:T(8,128)}) custom-call(bf16[16,2816,128]{2,1,0:T(8,128)(2,1)} %bitcast.41), custom_call_target="tpu_custom_call" | custom-call | flops 4400000000 | tf_op jit(solution)/shard_map/sort/pallas_call | solution.py:242
  21.0 1.5 %collective-permute-start.8 = (bf16[144,1024]{1,0:T(8,128)(2,1)S(1)}, bf16[144,1024]{1,0:T(8,128)(2,1)S(1)}, u32[]{:S(2)}, u32[]{:S(2)}) collective-permute-start(bf16[144,1024]{1,0:T(8,128)(2,1)S(1)} %collective-permute-done.refs_1_), channel_id=1, source_target_pairs={{0,8},{4,12},{8,0},{12,4},{1,9},{5,13},{9,1},{13,5},{2,10},{6,14},... | collective-permute-start | bytes 884744 | tf_op jit(solution)/shard_map/ppermute | solution.py:441
  23.1 6.9 %collective-permute-done.6 = bf16[144,1024]{1,0:T(8,128)(2,1)S(1)} collective-permute-done((bf16[144,1024]{1,0:T(8,128)(2,1)S(1)}, bf16[144,1024]{1,0:T(8,128)(2,1)S(1)}, u32[]{:S(2)}, u32[]{:S(2)}) %collective-permute-start.6) | collective-permute-done | bytes 294944 | tf_op jit(solution)/shard_map/ppermute | solution.py:441
  30.1 9.6 %sort.3 = (bf16[16,2,176,1024]{3,2,1,0:T(8,128)(2,1)}, f32[8,128]{1,0:T(8,128)S(1)}) custom-call(bf16[16,2816,128]{2,1,0:T(8,128)(2,1)} %bitcast.42, bf16[16,2,176,1024]{3,2,1,0:T(8,128)(2,1)} %get-tuple-element.32.refs_0_, bf16[144,1024]{1,0:T(8,128)(2,1)S(1)} %collective-permute-done.refs_1_), custom_call_target="tpu_custom_call", output_to_operand_aliasing={{0}: (1, {})} | custom-call | flops 4400000000 | tf_op jit(solution)/shard_map/sort/pallas_call | solution.py:242
  40.9 1.6 %dispatch.4 = (bf16[16,64,1024]{2,1,0:T(8,128)(2,1)S(1)}, f32[16,64,128]{2,1,0:T(8,128)S(1)}, bf16[4,256,128]{2,1,0:T(8,128)(2,1)S(1)}, f32[8,128]{1,0:T(8,128)S(1)}) custom-call(s32[1]{0:T(128)} %bitcast.11.base_ref, bf16[64,1024]{1,0:T(8,128)(2,1)S(1)} %fusion.rw_ref, bf16[288,1024]{1,0:T(8,128)(2,1)S(1)} %pad_maximum_fusion.refs_0_.refs_1_, ...), custom_call_target="tpu_custom_call" | custom-call | flops 3300000000 | tf_op jit(solution)/shard_map/dispatch/pallas_call | solution.py:148
  42.5 1.5 %dispatch.5 = (bf16[16,64,1024]{2,1,0:T(8,128)(2,1)S(1)}, f32[16,64,128]{2,1,0:T(8,128)S(1)}, bf16[4,256,128]{2,1,0:T(8,128)(2,1)S(1)}) custom-call(s32[1]{0:T(128)} %bitcast.11.base_ref, bf16[64,1024]{1,0:T(8,128)(2,1)S(1)} %fusion.rw_ref, bf16[288,1024]{1,0:T(8,128)(2,1)S(1)} %constant_dynamic-update-slice_fusion.refs_0_.refs_1_, ...), custom_call_target="tpu_custom_call" | custom-call | flops 3300000000 | tf_op jit(solution)/shard_map/dispatch/pallas_call | solution.py:148
  44.0 1.5 %dispatch.6 = (bf16[16,64,1024]{2,1,0:T(8,128)(2,1)S(1)}, f32[16,64,128]{2,1,0:T(8,128)S(1)}, bf16[4,256,128]{2,1,0:T(8,128)(2,1)S(1)}) custom-call(s32[1]{0:T(128)} %bitcast.11.base_ref, bf16[64,1024]{1,0:T(8,128)(2,1)S(1)} %fusion.rw_ref, bf16[288,1024]{1,0:T(8,128)(2,1)S(1)} %constant_dynamic-update-slice_fusion.2.refs_0_.refs_1_, ...), custom_call_target="tpu_custom_call" | custom-call | flops 3300000000 | tf_op jit(solution)/shard_map/dispatch/pallas_call | solution.py:148
  45.6 3.7 %collective-permute-done.2.b_ref = bf16[144,1024]{1,0:T(8,128)(2,1)S(1)} collective-permute-done((bf16[144,1024]{1,0:T(8,128)(2,1)S(1)}, bf16[144,1024]{1,0:T(8,128)(2,1)S(1)}, u32[]{:S(2)}, u32[]{:S(2)}) %collective-permute-start.2) | collective-permute-done | bytes 294944 | tf_op jit(solution)/shard_map/ppermute | solution.py:441
  49.5 1.1 copy.21
  52.7 2.7 %dispatch.7 = (bf16[16,64,1024]{2,1,0:T(8,128)(2,1)S(1)}, f32[16,64,128]{2,1,0:T(8,128)S(1)}, bf16[4,256,128]{2,1,0:T(8,128)(2,1)S(1)}, bf16[128,576]{1,0:T(8,128)(2,1)S(1)}) custom-call(s32[1]{0:T(128)} %bitcast.11.base_ref, bf16[64,1024]{1,0:T(8,128)(2,1)S(1)} %fusion.rw_ref, bf16[288,1024]{1,0:T(8,128)(2,1)S(1)} %stack.21.refs_0_.refs_1_, ...), custom_call_target="tpu_custom_call" | custom-call | flops 3300000000 | tf_op jit(solution)/shard_map/dispatch/pallas_call | solution.py:148
  56.1 2.6 %copy-done.4 = bf16[16,176,1024]{2,1,0:T(8,128)(2,1)S(1)} copy-done((bf16[16,176,1024]{2,1,0:T(8,128)(2,1)S(1)}, bf16[16,176,1024]{2,1,0:T(8,128)(2,1)}, u32[]{:S(2)}) %copy-start.4) | copy-done | bytes 5767192
  58.7 17.7 %experts.1 = (bf16[16,64,1024]{2,1,0:T(8,128)(2,1)S(1)}, bf16[16,64,1024]{2,1,0:T(8,128)(2,1)S(1)}, bf16[16,64,1024]{2,1,0:T(8,128)(2,1)S(1)}, bf16[16,64,1024]{2,1,0:T(8,128)(2,1)S(1)}) custom-call(bf16[16,64,1024]{2,1,0:T(8,128)(2,1)S(1)} %get-tuple-element.34.refs_1_.refs_0_, bf16[16,64,1024]{2,1,0:T(8,128)(2,1)S(1)} %copy-done.1, ...), custom_call_target="tpu_custom_call" | custom-call | flops 6600000000 | tf_op jit(solution)/shard_map/experts/pallas_call | solution.py:325
  80.3 1.5 %collective-permute-start.14 = (bf16[1,128,1024]{2,1,0:T(8,128)(2,1)S(1)}, bf16[1,128,1024]{2,1,0:T(8,128)(2,1)S(1)}, u32[]{:S(2)}, u32[]{:S(2)}) collective-permute-start(bf16[1,128,1024]{2,1,0:T(8,128)(2,1)S(1)} %add_convert_fusion.7), channel_id=1, source_target_pairs={{0,8},{4,12},{8,0},{12,4},{1,9},{5,13},{9,1},{13,5},{2,10},{6,14},... | collective-permute-start | bytes 786440 | tf_op jit(solution)/shard_map/ppermute | solution.py:441
  82.6 1.5 %collective-permute-start.20 = (bf16[1,128,1024]{2,1,0:T(8,128)(2,1)S(1)}, bf16[1,128,1024]{2,1,0:T(8,128)(2,1)S(1)}, u32[]{:S(2)}, u32[]{:S(2)}) collective-permute-start(bf16[1,128,1024]{2,1,0:T(8,128)(2,1)S(1)} %add_convert_fusion.3), channel_id=1, source_target_pairs={{0,8},{4,12},{8,0},{12,4},{1,9},{5,13},{9,1},{13,5},{2,10},{6,14},... | collective-permute-start | bytes 786440 | tf_op jit(solution)/shard_map/ppermute | solution.py:441
  84.2 5.3 %collective-permute-done.14 = bf16[1,128,1024]{2,1,0:T(8,128)(2,1)S(1)} collective-permute-done((bf16[1,128,1024]{2,1,0:T(8,128)(2,1)S(1)}, bf16[1,128,1024]{2,1,0:T(8,128)(2,1)S(1)}, u32[]{:S(2)}, u32[]{:S(2)}) %collective-permute-start.14) | collective-permute-done | bytes 262176 | tf_op jit(solution)/shard_map/ppermute | solution.py:441
  89.8 5.3 %collective-permute-done.17 = bf16[1,128,1024]{2,1,0:T(8,128)(2,1)S(1)} collective-permute-done((bf16[1,128,1024]{2,1,0:T(8,128)(2,1)S(1)}, bf16[1,128,1024]{2,1,0:T(8,128)(2,1)S(1)}, u32[]{:S(2)}, u32[]{:S(2)}) %collective-permute-start.17) | collective-permute-done | bytes 262176 | tf_op jit(solution)/shard_map/ppermute | solution.py:441
  95.2 3.1 %collective-permute-start.18 = (bf16[1,128,1024]{2,1,0:T(8,128)(2,1)S(1)}, bf16[1,128,1024]{2,1,0:T(8,128)(2,1)S(1)}, u32[]{:S(2)}, u32[]{:S(2)}) collective-permute-start(bf16[1,128,1024]{2,1,0:T(8,128)(2,1)S(1)} %add_convert_fusion.4), channel_id=1, source_target_pairs={{0,3},{1,2},{2,1},{3,0},{4,7},{5,6},{6,5},{7,4},{8,11},{9,10},{10,... | collective-permute-start | bytes 786440 | tf_op jit(solution)/shard_map/ppermute | solution.py:444
  98.3 1.8 %collective-permute-done.20 = bf16[1,128,1024]{2,1,0:T(8,128)(2,1)S(1)} collective-permute-done((bf16[1,128,1024]{2,1,0:T(8,128)(2,1)S(1)}, bf16[1,128,1024]{2,1,0:T(8,128)(2,1)S(1)}, u32[]{:S(2)}, u32[]{:S(2)}) %collective-permute-start.20) | collective-permute-done | bytes 262176 | tf_op jit(solution)/shard_map/ppermute | solution.py:441
  101.0 1.6 %collective-permute-start.23 = (bf16[1,128,1024]{2,1,0:T(8,128)(2,1)S(1)}, bf16[1,128,1024]{2,1,0:T(8,128)(2,1)S(1)}, u32[]{:S(2)}, u32[]{:S(2)}) collective-permute-start(bf16[1,128,1024]{2,1,0:T(8,128)(2,1)S(1)} %add_convert_fusion.1), channel_id=1, source_target_pairs={{0,8},{4,12},{8,0},{12,4},{1,9},{5,13},{9,1},{13,5},{2,10},{6,14},... | collective-permute-start | bytes 786440 | tf_op jit(solution)/shard_map/ppermute | solution.py:441
  102.6 6.2 %attention.1 = bf16[128,4096]{1,0:T(8,128)(2,1)} custom-call(s32[128,1]{1,0:T(8,128)S(1)} %copy-done.9, s32[128,1]{1,0:T(8,128)S(1)} %copy-done.10, s32[1,512]{1,0:T(1,128)S(1)} %bitcast.38, bf16[128,4608]{1,0:T(8,128)(2,1)S(1)} %bitcast.40, bf16[256,576]{1,0:T(8,128)(2,1)S(1)} %constant_dynamic-update-slice_fusion.4.refs_0_.refs_1_, ...), custom_call_target="tpu_custom_call" | custom-call | flops 6600000000 | tf_op jit(solution)/shard_map/attention/pallas_call | solution.py:410
  109.5 5.0 %collective-permute-done.21 = bf16[1,128,1024]{2,1,0:T(8,128)(2,1)S(1)} collective-permute-done((bf16[1,128,1024]{2,1,0:T(8,128)(2,1)S(1)}, bf16[1,128,1024]{2,1,0:T(8,128)(2,1)S(1)}, u32[]{:S(2)}, u32[]{:S(2)}) %collective-permute-start.21) | collective-permute-done | bytes 262176 | tf_op jit(solution)/shard_map/ppermute | solution.py:444
  (112 shorter events, 15.6 us)
Async XLA Ops:
  2.3 17.7 %collective-permute-start.5 = (bf16[144,1024]{1,0:T(8,128)(2,1)S(1)}, bf16[144,1024]{1,0:T(8,128)(2,1)S(1)}, u32[]{:S(2)}, u32[]{:S(2)}) collective-permute-start(bf16[144,1024]{1,0:T(8,128)(2,1)S(1)} %pad_maximum_fusion.1), channel_id=1, source_target_pairs={{0,1},{1,0},{2,3},{3,2},{4,5},{5,4},{6,7},{7,6},{8,9},{9,8},{10,11... | collective-permute-start | bytes 884744 | tf_op jit(solution)/shard_map/ppermute | solution.py:444
  5.4 15.6 %collective-permute-start = (bf16[144,1024]{1,0:T(8,128)(2,1)S(1)}, bf16[144,1024]{1,0:T(8,128)(2,1)S(1)}, u32[]{:S(2)}, u32[]{:S(2)}) collective-permute-start(bf16[144,1024]{1,0:T(8,128)(2,1)S(1)} %pad_maximum_fusion.1), channel_id=1, source_target_pairs={{0,3},{1,2},{2,1},{3,0},{4,7},{5,6},{6,5},{7,4},{8,11},{9,10},{10,... | collective-permute-start | bytes 884744 | tf_op jit(solution)/shard_map/ppermute | solution.py:444
  7.9 12.8 %collective-permute-start.3 = (bf16[144,1024]{1,0:T(8,128)(2,1)S(1)}, bf16[144,1024]{1,0:T(8,128)(2,1)S(1)}, u32[]{:S(2)}, u32[]{:S(2)}) collective-permute-start(bf16[144,1024]{1,0:T(8,128)(2,1)S(1)} %pad_maximum_fusion.1), channel_id=1, source_target_pairs={{0,8},{4,12},{8,0},{12,4},{1,9},{5,13},{9,1},{13,5},{2,10},{6,14},... | collective-permute-start | bytes 884744 | tf_op jit(solution)/shard_map/ppermute | solution.py:441
  20.1 9.9 %collective-permute-start.6 = (bf16[144,1024]{1,0:T(8,128)(2,1)S(1)}, bf16[144,1024]{1,0:T(8,128)(2,1)S(1)}, u32[]{:S(2)}, u32[]{:S(2)}) collective-permute-start(bf16[144,1024]{1,0:T(8,128)(2,1)S(1)} %collective-permute-done.5), channel_id=1, source_target_pairs={{0,8},{4,12},{8,0},{12,4},{1,9},{5,13},{9,1},{13,5},{2,10},{6,14},... | collective-permute-start | bytes 884744 | tf_op jit(solution)/shard_map/ppermute | solution.py:441
  20.7 20.1 %collective-permute-start.4 = (bf16[288,1024]{1,0:T(8,128)(2,1)S(1)}, bf16[288,1024]{1,0:T(8,128)(2,1)S(1)}, u32[]{:S(2)}, u32[]{:S(2)}) collective-permute-start(bf16[288,1024]{1,0:T(8,128)(2,1)S(1)} %pad_maximum_fusion.refs_0_.refs_1_), channel_id=1, source_target_pairs={{0,4},{4,0},{8,12},{12,8},{1,5},{5,1},{9,13},{13,9},{2,6},{6,2},{1... | collective-permute-start | bytes 1769480 | tf_op jit(solution)/shard_map/ppermute | solution.py:441
  21.0 18.7 %collective-permute-start.8 = (bf16[144,1024]{1,0:T(8,128)(2,1)S(1)}, bf16[144,1024]{1,0:T(8,128)(2,1)S(1)}, u32[]{:S(2)}, u32[]{:S(2)}) collective-permute-start(bf16[144,1024]{1,0:T(8,128)(2,1)S(1)} %collective-permute-done.refs_1_), channel_id=1, source_target_pairs={{0,8},{4,12},{8,0},{12,4},{1,9},{5,13},{9,1},{13,5},{2,10},{6,14},... | collective-permute-start | bytes 884744 | tf_op jit(solution)/shard_map/ppermute | solution.py:441
  22.5 17.8 %collective-permute-start.1 = (bf16[144,1024]{1,0:T(8,128)(2,1)S(1)}, bf16[144,1024]{1,0:T(8,128)(2,1)S(1)}, u32[]{:S(2)}, u32[]{:S(2)}) collective-permute-start(bf16[144,1024]{1,0:T(8,128)(2,1)S(1)} %collective-permute-done.refs_1_), channel_id=1, source_target_pairs={{0,1},{1,0},{2,3},{3,2},{4,5},{5,4},{6,7},{7,6},{8,9},{9,8},{10,11... | collective-permute-start | bytes 884744 | tf_op jit(solution)/shard_map/ppermute | solution.py:444
  30.0 12.4 %collective-permute-start.7 = (bf16[288,1024]{1,0:T(8,128)(2,1)S(1)}, bf16[288,1024]{1,0:T(8,128)(2,1)S(1)}, u32[]{:S(2)}, u32[]{:S(2)}) collective-permute-start(bf16[288,1024]{1,0:T(8,128)(2,1)S(1)} %constant_dynamic-update-slice_fusion.refs_0_.refs_1_), channel_id=1, source_target_pairs={{0,4},{4,0},{8,12},{12,8},{1,5},{5,1},{9,13},{13,9},{2,6},{6,2},{1... | collective-permute-start | bytes 1769480 | tf_op jit(solution)/shard_map/ppermute | solution.py:441
  39.8 4.3 %collective-permute-start.9 = (bf16[288,1024]{1,0:T(8,128)(2,1)S(1)}, bf16[288,1024]{1,0:T(8,128)(2,1)S(1)}, u32[]{:S(2)}, u32[]{:S(2)}) collective-permute-start(bf16[288,1024]{1,0:T(8,128)(2,1)S(1)} %constant_dynamic-update-slice_fusion.2.refs_0_.refs_1_), channel_id=1, source_target_pairs={{0,4},{4,0},{8,12},{12,8},{1,5},{5,1},{9,13},{13,9},{2,6},{6,2},{1... | collective-permute-start | bytes 1769480 | tf_op jit(solution)/shard_map/ppermute | solution.py:441
  40.3 9.0 %collective-permute-start.2 = (bf16[144,1024]{1,0:T(8,128)(2,1)S(1)}, bf16[144,1024]{1,0:T(8,128)(2,1)S(1)}, u32[]{:S(2)}, u32[]{:S(2)}) collective-permute-start(bf16[144,1024]{1,0:T(8,128)(2,1)S(1)} %collective-permute-done.1.a_ref), channel_id=1, source_target_pairs={{0,8},{4,12},{8,0},{12,4},{1,9},{5,13},{9,1},{13,5},{2,10},{6,14},... | collective-permute-start | bytes 884744 | tf_op jit(solution)/shard_map/ppermute | solution.py:441
  49.4 3.3 %collective-permute-start.10 = (bf16[288,1024]{1,0:T(8,128)(2,1)S(1)}, bf16[288,1024]{1,0:T(8,128)(2,1)}, u32[]{:S(2)}, u32[]{:S(2)}) collective-permute-start(bf16[288,1024]{1,0:T(8,128)(2,1)S(1)} %stack.21.refs_0_.refs_1_), channel_id=1, source_target_pairs={{0,4},{4,0},{8,12},{12,8},{1,5},{5,1},{9,13},{13,9},{2,6},{6,2},{1... | collective-permute-start | bytes 1769480 | tf_op jit(solution)/shard_map/ppermute | solution.py:441
  55.4 21.7 %collective-permute-start.11 = (bf16[128,576]{1,0:T(8,128)(2,1)S(1)}, bf16[128,576]{1,0:T(8,128)(2,1)S(1)}, u32[]{:S(2)}, u32[]{:S(2)}) collective-permute-start(bf16[128,576]{1,0:T(8,128)(2,1)S(1)} %get-tuple-element.37), channel_id=1, source_target_pairs={{0,8},{4,12},{8,0},{12,4},{1,9},{5,13},{9,1},{13,5},{2,10},{6,14},... | collective-permute-start | bytes 442376 | tf_op jit(solution)/shard_map/ppermute | solution.py:441
  76.9 3.4 %collective-permute-start.13 = (bf16[1,256,1024]{2,1,0:T(8,128)(2,1)S(1)}, bf16[1,256,1024]{2,1,0:T(8,128)(2,1)S(1)}, u32[]{:S(2)}, u32[]{:S(2)}) collective-permute-start(bf16[1,256,1024]{2,1,0:T(8,128)(2,1)S(1)} %get-tuple-element.47), channel_id=1, source_target_pairs={{0,4},{4,0},{8,12},{12,8},{1,5},{5,1},{9,13},{13,9},{2,6},{6,2},{1... | collective-permute-start | bytes 1572872 | tf_op jit(solution)/shard_map/ppermute | solution.py:441
  77.2 2.1 %collective-permute-start.12 = (bf16[256,576]{1,0:T(8,128)(2,1)S(1)}, bf16[256,576]{1,0:T(8,128)(2,1)S(1)}, u32[]{:S(2)}, u32[]{:S(2)}) collective-permute-start(bf16[256,576]{1,0:T(8,128)(2,1)S(1)} %constant_dynamic-update-slice_fusion.4.refs_0_.refs_1_), channel_id=1, source_target_pairs={{0,4},{4,0},{8,12},{12,8},{1,5},{5,1},{9,13},{13,9},{2,6},{6,2},{1... | collective-permute-start | bytes 884744 | tf_op jit(solution)/shard_map/ppermute | solution.py:441
  78.0 3.8 %collective-permute-start.16 = (bf16[1,256,1024]{2,1,0:T(8,128)(2,1)S(1)}, bf16[1,256,1024]{2,1,0:T(8,128)(2,1)S(1)}, u32[]{:S(2)}, u32[]{:S(2)}) collective-permute-start(bf16[1,256,1024]{2,1,0:T(8,128)(2,1)S(1)} %get-tuple-element.51), channel_id=1, source_target_pairs={{0,4},{4,0},{8,12},{12,8},{1,5},{5,1},{9,13},{13,9},{2,6},{6,2},{1... | collective-permute-start | bytes 1572872 | tf_op jit(solution)/shard_map/ppermute | solution.py:441
  79.0 3.5 %collective-permute-start.19 = (bf16[1,256,1024]{2,1,0:T(8,128)(2,1)S(1)}, bf16[1,256,1024]{2,1,0:T(8,128)(2,1)S(1)}, u32[]{:S(2)}, u32[]{:S(2)}) collective-permute-start(bf16[1,256,1024]{2,1,0:T(8,128)(2,1)S(1)} %get-tuple-element.55), channel_id=1, source_target_pairs={{0,4},{4,0},{8,12},{12,8},{1,5},{5,1},{9,13},{13,9},{2,6},{6,2},{1... | collective-permute-start | bytes 1572872 | tf_op jit(solution)/shard_map/ppermute | solution.py:441
  80.0 21.0 %collective-permute-start.22 = (bf16[1,256,1024]{2,1,0:T(8,128)(2,1)S(1)}, bf16[1,256,1024]{2,1,0:T(8,128)(2,1)S(1)}, u32[]{:S(2)}, u32[]{:S(2)}) collective-permute-start(bf16[1,256,1024]{2,1,0:T(8,128)(2,1)S(1)} %get-tuple-element.59), channel_id=1, source_target_pairs={{0,4},{4,0},{8,12},{12,8},{1,5},{5,1},{9,13},{13,9},{2,6},{6,2},{1... | collective-permute-start | bytes 1572872 | tf_op jit(solution)/shard_map/ppermute | solution.py:441
  80.3 9.2 %collective-permute-start.14 = (bf16[1,128,1024]{2,1,0:T(8,128)(2,1)S(1)}, bf16[1,128,1024]{2,1,0:T(8,128)(2,1)S(1)}, u32[]{:S(2)}, u32[]{:S(2)}) collective-permute-start(bf16[1,128,1024]{2,1,0:T(8,128)(2,1)S(1)} %add_convert_fusion.7), channel_id=1, source_target_pairs={{0,8},{4,12},{8,0},{12,4},{1,9},{5,13},{9,1},{13,5},{2,10},{6,14},... | collective-permute-start | bytes 786440 | tf_op jit(solution)/shard_map/ppermute | solution.py:441
  81.9 13.2 %collective-permute-start.17 = (bf16[1,128,1024]{2,1,0:T(8,128)(2,1)S(1)}, bf16[1,128,1024]{2,1,0:T(8,128)(2,1)S(1)}, u32[]{:S(2)}, u32[]{:S(2)}) collective-permute-start(bf16[1,128,1024]{2,1,0:T(8,128)(2,1)S(1)} %add_convert_fusion.5), channel_id=1, source_target_pairs={{0,8},{4,12},{8,0},{12,4},{1,9},{5,13},{9,1},{13,5},{2,10},{6,14},... | collective-permute-start | bytes 786440 | tf_op jit(solution)/shard_map/ppermute | solution.py:441
  82.6 17.5 %collective-permute-start.20 = (bf16[1,128,1024]{2,1,0:T(8,128)(2,1)S(1)}, bf16[1,128,1024]{2,1,0:T(8,128)(2,1)S(1)}, u32[]{:S(2)}, u32[]{:S(2)}) collective-permute-start(bf16[1,128,1024]{2,1,0:T(8,128)(2,1)S(1)} %add_convert_fusion.3), channel_id=1, source_target_pairs={{0,8},{4,12},{8,0},{12,4},{1,9},{5,13},{9,1},{13,5},{2,10},{6,14},... | collective-permute-start | bytes 786440 | tf_op jit(solution)/shard_map/ppermute | solution.py:441
  89.6 19.9 %collective-permute-start.15 = (bf16[1,128,1024]{2,1,0:T(8,128)(2,1)S(1)}, bf16[1,128,1024]{2,1,0:T(8,128)(2,1)S(1)}, u32[]{:S(2)}, u32[]{:S(2)}) collective-permute-start(bf16[1,128,1024]{2,1,0:T(8,128)(2,1)S(1)} %add_convert_fusion.6), channel_id=1, source_target_pairs={{0,2},{1,3},{2,0},{3,1},{4,6},{5,7},{6,4},{7,5},{8,10},{9,11},{10,... | collective-permute-start | bytes 786440 | tf_op jit(solution)/shard_map/ppermute | solution.py:444
  95.2 14.2 %collective-permute-start.18 = (bf16[1,128,1024]{2,1,0:T(8,128)(2,1)S(1)}, bf16[1,128,1024]{2,1,0:T(8,128)(2,1)S(1)}, u32[]{:S(2)}, u32[]{:S(2)}) collective-permute-start(bf16[1,128,1024]{2,1,0:T(8,128)(2,1)S(1)} %add_convert_fusion.4), channel_id=1, source_target_pairs={{0,3},{1,2},{2,1},{3,0},{4,7},{5,6},{6,5},{7,4},{8,11},{9,10},{10,... | collective-permute-start | bytes 786440 | tf_op jit(solution)/shard_map/ppermute | solution.py:444
  100.2 14.3 %collective-permute-start.21 = (bf16[1,128,1024]{2,1,0:T(8,128)(2,1)S(1)}, bf16[1,128,1024]{2,1,0:T(8,128)(2,1)S(1)}, u32[]{:S(2)}, u32[]{:S(2)}) collective-permute-start(bf16[1,128,1024]{2,1,0:T(8,128)(2,1)S(1)} %add_convert_fusion.2), channel_id=1, source_target_pairs={{0,1},{1,0},{2,3},{3,2},{4,5},{5,4},{6,7},{7,6},{8,9},{9,8},{10,11... | collective-permute-start | bytes 786440 | tf_op jit(solution)/shard_map/ppermute | solution.py:444
  101.0 13.5 %collective-permute-start.23 = (bf16[1,128,1024]{2,1,0:T(8,128)(2,1)S(1)}, bf16[1,128,1024]{2,1,0:T(8,128)(2,1)S(1)}, u32[]{:S(2)}, u32[]{:S(2)}) collective-permute-start(bf16[1,128,1024]{2,1,0:T(8,128)(2,1)S(1)} %add_convert_fusion.1), channel_id=1, source_target_pairs={{0,8},{4,12},{8,0},{12,4},{1,9},{5,13},{9,1},{13,5},{2,10},{6,14},... | collective-permute-start | bytes 786440 | tf_op jit(solution)/shard_map/ppermute | solution.py:441
  (21 other events, 131.9 us)

commit v10 on v9

--- a/solution.py
+++ b/solution.py
@@ -18,9 +18,6 @@
 EXTRA = 16
 VMEM = 14 * 2**20
 VMEM_EXPERTS = 20 * 2**20
-VMEM_SORT = 52 * 2**20
-PIECES = 2
-DEPTH = 3
 PEAK = 1.1e9
 
 qk_scale = 192.0 ** (-0.5)
@@ -28,7 +25,7 @@
 TN = (((0,), (0,)), ((), ()))
 
 
-def call(kernel, micros, grid, in_specs, out_specs, out_shape, scratch, name, limit=VMEM, aliases={}):
+def call(kernel, micros, grid, in_specs, out_specs, out_shape, scratch, name, limit=VMEM):
     return pl.pallas_call(
         kernel,
         grid=grid,
@@ -36,7 +33,6 @@
         out_specs=out_specs,
         out_shape=out_shape,
         scratch_shapes=scratch,
-        input_output_aliases=aliases,
         compiler_params=pltpu.CompilerParams(
             dimension_semantics=("arbitrary",) * len(grid), vmem_limit_bytes=limit
         ),
@@ -108,7 +104,6 @@
             )
 
 
-IN_HBM = pl.BlockSpec(memory_space=pltpu.HBM)
 ANYWHERE = pl.BlockSpec(memory_space=pl.ANY)
 
 
@@ -157,113 +152,6 @@
     )(base, rw, *[a for a, _ in parts], *carried, *extra)
 
 
-def fetch(sources, slots, sem, step, steps, first, start=0):
-    depth, group = slots[0].shape[:2]
-
-    def copies(at):
-        slot = lax.rem(at, depth)
-        return [
-            pltpu.make_async_copy(
-                source.at[start + at * group + e], held.at[slot, e], sem.at[i, slot, e]
-            )
-            for i, (source, held) in enumerate(zip(sources, slots))
-            for e in range(group)
-        ]
-
-    @pl.when(first & (step == 0))
-    def _():
-        for ahead in range(depth - 1):
-
-            @pl.when(ahead < steps)
-            def _():
-                for copy in copies(step + ahead):
-                    copy.start()
-
-    @pl.when(first & (step + depth - 1 < steps))
-    def _():
-        for copy in copies(step + depth - 1):
-            copy.start()
-
-    @pl.when(first)
-    def _():
-        for copy in copies(step):
-            copy.wait()
-
-    return lax.rem(step, depth)
-
-
-def sort_kernel(start, gu_ref, *refs):
-    out_ref, token_ref, held, made, wide, in_sem, out_sem = refs[-7:]
-    token_ref[...] = jnp.zeros_like(token_ref)
-    step, steps = pl.program_id(0), pl.num_programs(0)
-    _, group, _, hidden, width = made.shape
-    chunks = width // LANES
-    slot = fetch([gu_ref], [held], in_sem, step, steps, step >= 0, start)
-    to = lax.rem(step, 2)
-
-    def leave(at):
-        to = lax.rem(at, 2)
-        return pltpu.make_async_copy(
-            made.at[to], out_ref.at[pl.ds(start + at * group, group)], out_sem.at[to]
-        )
-
-    @pl.when(step >= 2)
-    def _():
-        leave(step - 2).wait()
-
-    for e in range(group):
-        wide[e] = held[slot, e].astype(jnp.float32)
-        for z in range(2):
-            for c in range(chunks):
-                part = wide[e, pl.ds(2 * c + z, hidden, stride=2 * chunks), :]
-                made[to, e, z, :, c * LANES : (c + 1) * LANES] = part.astype(jnp.bfloat16)
-    leave(step).start()
-
-    @pl.when(step == steps - 1)
-    def _():
-        @pl.when(step >= 1)
-        def _():
-            leave(step - 1).wait()
-
-        leave(step).wait()
-
-
-def sort_rows(gate_up, behind):
-    local, hidden, _, width = gate_up.shape
-    pieces = PIECES if local % (2 * PIECES) == 0 else 1
-    group = 1
-    chunks = width // LANES
-    gu = gate_up.reshape(local, hidden, 2, chunks, LANES).swapaxes(2, 3)
-    gu = gu.reshape(local, hidden * 2 * chunks, LANES)
-    done = ()
-    for j in range(pieces):
-        after = behind[j] if pieces > 1 else ()
-        *done, token = (
-            call(
-                functools.partial(sort_kernel, j * local // pieces),
-                8 // pieces,
-                (local // pieces // group,),
-                [IN_HBM] + [IN_HBM] * len(done) + [ANYWHERE] * len(after),
-                [IN_HBM, pl.BlockSpec((8, LANES), lambda e: (0, 0))],
-                [
-                    jax.ShapeDtypeStruct((local, 2, hidden, width), jnp.bfloat16),
-                    jax.ShapeDtypeStruct((8, LANES), jnp.float32),
-                ],
-                [
-                    pltpu.VMEM((2, group) + gu.shape[1:], jnp.bfloat16),
-                    pltpu.VMEM((2, group, 2, hidden, width), jnp.bfloat16),
-                    pltpu.VMEM((group,) + gu.shape[1:], jnp.float32),
-                    pltpu.SemaphoreType.DMA((1, 2, group)),
-                    pltpu.SemaphoreType.DMA((2,)),
-                ],
-                "sort",
-                VMEM_SORT,
-                {1: 0} if done else {},
-            )(gu, *done, *after)
-        )
-    return done[0], token
-
-
 def stack_kernel(a_ref, b_ref, *refs):
     rows = a_ref.shape[0]
     refs[-1][:rows, :] = a_ref[...]
@@ -287,56 +175,61 @@
 def expert_kernel(n, *refs):
     rows, weights = refs[:n], refs[n : 2 * n]
     gu_ref, down_ref = refs[2 * n : 2 * n + 2]
-    outs, (gu, down, sem) = refs[-3 - n : -3], refs[-3:]
-    group = gu.shape[1]
+    outs, wide = refs[2 * n + 2 : 3 * n + 2], refs[3 * n + 2]
+    group, hidden, width = down_ref.shape
     size = rows[0].shape[1]
-    slot = fetch(
-        [gu_ref, down_ref],
-        [gu, down],
-        sem,
-        pl.program_id(0),
-        pl.num_programs(0),
-        pl.program_id(1) == 0,
-    )
+    chunks = width // LANES
     for e in range(group):
+        wide[e] = gu_ref[e].astype(jnp.float32)
         held = jnp.concatenate([r[e] for r in rows], axis=0)
-        _, hidden, width = gu.shape[2:]
-        both = gu[slot, e].reshape(2 * hidden, width)
-        both = lax.dot_general(both, held, NT, preferred_element_type=jnp.float32)
-        g, u = both[:hidden], both[hidden:]
+        both = []
+        for z in range(2):
+            matrix = jnp.concatenate(
+                [
+                    wide[e, pl.ds(2 * c + z, hidden, stride=2 * chunks), :].astype(jnp.bfloat16)
+                    for c in range(chunks)
+                ],
+                axis=1,
+            )
+            both.append(lax.dot_general(held, matrix, NT, preferred_element_type=jnp.float32))
+        g, u = both
         inner = (g * lax.logistic(g) * u).astype(jnp.bfloat16)
-        made = lax.dot_general(inner, down[slot, e], TN, preferred_element_type=jnp.float32)
+        made = jnp.dot(inner, down_ref[e], preferred_element_type=jnp.float32)
         for i in range(n):
             w = weights[i][e]
             part = made[i * size : (i + 1) * size]
-            for c in range(part.shape[1] // LANES):
+            for c in range(chunks):
                 at = slice(c * LANES, (c + 1) * LANES)
                 outs[i][e, :, at] = (part[:, at] * w).astype(jnp.bfloat16)
 
 
-def experts(rows, weights, gu, down, after=()):
+def experts(rows, weights, gate_up, down):
     n = len(rows)
     local, slots, width = rows[0].shape
     size = min(slots, EXPERT_ROWS)
     hidden = down.shape[1]
     group = 2 if local % 2 == 0 else 1
+    chunks = width // LANES
+    gu = gate_up.reshape(local, hidden, 2, chunks, LANES).swapaxes(2, 3)
+    gu = gu.reshape(local, hidden * 2 * chunks, LANES)
     rows_spec = pl.BlockSpec((group, size, width), lambda e, i: (e, i, 0))
     weight_spec = pl.BlockSpec((group, size, LANES), lambda e, i: (e, i, 0))
     return call(
         functools.partial(expert_kernel, n),
-        6,
+        12,
         (local // group, slots // size),
-        [rows_spec] * n + [weight_spec] * n + [IN_HBM, IN_HBM] + [ANYWHERE] * len(after),
+        [rows_spec] * n
+        + [weight_spec] * n
+        + [
+            pl.BlockSpec((group,) + gu.shape[1:], lambda e, i: (e, 0, 0)),
+            pl.BlockSpec((group, hidden, width), lambda e, i: (e, 0, 0)),
+        ],
         [rows_spec] * n,
         [jax.ShapeDtypeStruct(r.shape, jnp.bfloat16) for r in rows],
-        [
-            pltpu.VMEM((DEPTH, group, 2, hidden, width), jnp.bfloat16),
-            pltpu.VMEM((DEPTH, group, hidden, width), jnp.bfloat16),
-            pltpu.SemaphoreType.DMA((2, DEPTH, group)),
-        ],
+        [pltpu.VMEM((group,) + gu.shape[1:], jnp.float32)],
         "experts",
         VMEM_EXPERTS,
-    )(*rows, *weights, gu, down, *after)
+    )(*rows, *weights, gu, down)
 
 
 def combine_kernel(n, *refs):
@@ -458,7 +351,6 @@
     packed = jnp.concatenate([tokens, picks], axis=0)
 
     near_parts = along_exp(packed)
-    arrived = list(near_parts)
     crossed = [flip(a, 2) for a in near_parts]
     if near:
         blocks = 1
@@ -483,11 +375,10 @@
     base = (exp * local).reshape(1).astype(jnp.int32)
     rw = jnp.roll(router_weight.T, -exp * local, axis=0)
     balance = None
-    gu, token = sort_rows(gate_up, [(), (arrived[2],)] if near else [(), ()])
     sent, keys = [], latent_kv[0]
     for i in range(len(shifts)):
         if near and i + 1 == len(shifts):
-            before = [token] + [a[0] for a in sent]
+            before = [a[0] for a in sent]
             pair = stack(near_parts[i], crossed[i], before)
             flipped = flip(pair, 1)
             spread.append([(pair, 0), (pair, 1), (flipped, 0), (flipped, 1)])
@@ -501,7 +392,7 @@
             keys = out[-1]
     keys = jnp.concatenate([keys, flip(keys, 2)], axis=0)
     keys = [keys, flip(keys, 1)]
-    made = experts([a[0] for a in sent], [a[1] for a in sent], gu, w_down)
+    made = experts([a[0] for a in sent], [a[1] for a in sent], gate_up, w_down)
     back = []
     for i in reversed(range(len(shifts))):
         keep, give = combine([sent[i][2]], [made[i]], n_ctx, () if i else (keys[1],))

time: 116 us -> 107 us (0.922)
  Pallas kernels: 52.8 us -> 32.1 us
  starting transfers between devices: 22.3 us -> 30.5 us
  local copies, waits for them, and re-layouts: 6.44 us -> 9.79 us
  other arithmetic: 3.88 us -> 7.02 us
  waiting for transfers between devices: 29 us -> 26.5 us
    pallas_call x3 -> x1, Pallas kernels: 37.4 us -> 15.4 us  [experts(): call(functools.partial(expert_kernel, n), 12, (local // group, slots // s...]
    ppermute x18, waiting for transfers between devices: 23.1 us -> 13.3 us  [flip(): return lax.ppermute(a, 'ctx', [(i, i ^ bit) for i in range(n_ctx)])]
    ppermute x6, starting transfers between devices: 10.2 us -> 18.2 us  [shift(): return lax.ppermute(a, 'exp', [(i, i ^ d) for i in range(n_exp)])]
    ppermute x6, waiting for transfers between devices: 5.96 us -> 13.1 us  [shift(): return lax.ppermute(a, 'exp', [(i, i ^ d) for i in range(n_exp)])]
    unnamed x48 -> x44, local copies, waits for them, and re-layouts: 4.2 us -> 8.08 us
    pallas_call x4, Pallas kernels: 7.22 us -> 8.58 us  [dispatch(): call(functools.partial(dispatch_kernel, n_parts, n_parts if row is not No...]
  transfers between devices with their start and end apart: 24 -> 24, of which waited for: 8 -> 11; matrix products, arithmetic and copies ran while one was open for 4% -> 7% of each run, Pallas kernels for 43% -> 27%
where the time goes in v10:
time: 107 us
  Pallas kernels  32.1 us (30%)
  starting transfers between devices  30.5 us (29%)
  waiting for transfers between devices  26.5 us (25%)
  local copies, waits for them, and re-layouts  9.79 us (9%)
  other arithmetic  7.02 us (7%)
    ppermute x6, starting transfers between devices, shift(): return lax.ppermute(a, 'exp', [(i, i ^ d) for i in range(n_exp)])  18.2 us
    pallas_call x1, Pallas kernels, experts(): call(functools.partial(expert_kernel, n), 12, (local // group, slots // s...  15.4 us
    ppermute x18, waiting for transfers between devices, flip(): return lax.ppermute(a, 'ctx', [(i, i ^ bit) for i in range(n_ctx)])  13.3 us
    ppermute x6, waiting for transfers between devices, shift(): return lax.ppermute(a, 'exp', [(i, i ^ d) for i in range(n_exp)])  13.1 us
    ppermute x18, starting transfers between devices, flip(): return lax.ppermute(a, 'ctx', [(i, i ^ bit) for i in range(n_ctx)])  12.4 us
    pallas_call x4, Pallas kernels, dispatch(): call(functools.partial(dispatch_kernel, n_parts, n_parts if row is not No...  8.58 us
    unnamed x44, local copies, waits for them, and re-layouts  8.08 us
    pallas_call x1, Pallas kernels, attend(): call(functools.partial(attend_kernel, [at for _, at in parts], kdim), 6,...  6.17 us
  transfers between devices with their start and end apart: 24, of which 11 were waited for; matrix products, arithmetic and copies ran while one was open for 7% of the time, Pallas kernels for 27%

profile of v10, /device:TPU:0, one launch (start us, length us, event | category | flops | bytes accessed | tf_op | source)
XLA Modules:
  0.0 106.9 jit_solution(3842142331368519369)
XLA Ops:
  2.3 3.1 %collective-permute-start.5 = (bf16[144,1024]{1,0:T(8,128)(2,1)S(1)}, bf16[144,1024]{1,0:T(8,128)(2,1)S(1)}, u32[]{:S(2)}, u32[]{:S(2)}) collective-permute-start(bf16[144,1024]{1,0:T(8,128)(2,1)S(1)} %pad_maximum_fusion.1), channel_id=1, source_target_pairs={{0,1},{1,0},{2,3},{3,2},{4,5},{5,4},{6,7},{7,6},{8,9},{9,8},{10,11... | collective-permute-start | bytes 884744 | tf_op jit(solution)/shard_map/ppermute | solution.py:337
  5.4 2.5 %collective-permute-start = (bf16[144,1024]{1,0:T(8,128)(2,1)S(1)}, bf16[144,1024]{1,0:T(8,128)(2,1)S(1)}, u32[]{:S(2)}, u32[]{:S(2)}) collective-permute-start(bf16[144,1024]{1,0:T(8,128)(2,1)S(1)} %pad_maximum_fusion.1), channel_id=1, source_target_pairs={{0,3},{1,2},{2,1},{3,0},{4,7},{5,6},{6,5},{7,4},{8,11},{9,10},{10,... | collective-permute-start | bytes 884744 | tf_op jit(solution)/shard_map/ppermute | solution.py:337
  7.9 1.5 %collective-permute-start.3 = (bf16[144,1024]{1,0:T(8,128)(2,1)S(1)}, bf16[144,1024]{1,0:T(8,128)(2,1)S(1)}, u32[]{:S(2)}, u32[]{:S(2)}) collective-permute-start(bf16[144,1024]{1,0:T(8,128)(2,1)S(1)} %pad_maximum_fusion.1), channel_id=1, source_target_pairs={{0,8},{4,12},{8,0},{12,4},{1,9},{5,13},{9,1},{13,5},{2,10},{6,14},... | collective-permute-start | bytes 884744 | tf_op jit(solution)/shard_map/ppermute | solution.py:334
  10.2 2.6 %collective-permute-done.5 = bf16[144,1024]{1,0:T(8,128)(2,1)S(1)} collective-permute-done((bf16[144,1024]{1,0:T(8,128)(2,1)S(1)}, bf16[144,1024]{1,0:T(8,128)(2,1)S(1)}, u32[]{:S(2)}, u32[]{:S(2)}) %collective-permute-start.5) | collective-permute-done | bytes 294944 | tf_op jit(solution)/shard_map/ppermute | solution.py:337
  12.8 1.5 %collective-permute-start.6 = (bf16[144,1024]{1,0:T(8,128)(2,1)S(1)}, bf16[144,1024]{1,0:T(8,128)(2,1)S(1)}, u32[]{:S(2)}, u32[]{:S(2)}) collective-permute-start(bf16[144,1024]{1,0:T(8,128)(2,1)S(1)} %collective-permute-done.5), channel_id=1, source_target_pairs={{0,8},{4,12},{8,0},{12,4},{1,9},{5,13},{9,1},{13,5},{2,10},{6,14},... | collective-permute-start | bytes 884744 | tf_op jit(solution)/shard_map/ppermute | solution.py:334
  16.1 1.7 %collective-permute-done.3 = bf16[144,1024]{1,0:T(8,128)(2,1)S(1)} collective-permute-done((bf16[144,1024]{1,0:T(8,128)(2,1)S(1)}, bf16[144,1024]{1,0:T(8,128)(2,1)S(1)}, u32[]{:S(2)}, u32[]{:S(2)}) %collective-permute-start.3) | collective-permute-done | bytes 294944 | tf_op jit(solution)/shard_map/ppermute | solution.py:334
  18.9 2.1 %collective-permute-done = bf16[144,1024]{1,0:T(8,128)(2,1)S(1)} collective-permute-done((bf16[144,1024]{1,0:T(8,128)(2,1)S(1)}, bf16[144,1024]{1,0:T(8,128)(2,1)S(1)}, u32[]{:S(2)}, u32[]{:S(2)}) %collective-permute-start) | collective-permute-done | bytes 294944 | tf_op jit(solution)/shard_map/ppermute | solution.py:337
  21.0 1.5 %collective-permute-start.8 = (bf16[144,1024]{1,0:T(8,128)(2,1)S(1)}, bf16[144,1024]{1,0:T(8,128)(2,1)S(1)}, u32[]{:S(2)}, u32[]{:S(2)}) collective-permute-start(bf16[144,1024]{1,0:T(8,128)(2,1)S(1)} %collective-permute-done), channel_id=1, source_target_pairs={{0,8},{4,12},{8,0},{12,4},{1,9},{5,13},{9,1},{13,5},{2,10},{6,14},... | collective-permute-start | bytes 884744 | tf_op jit(solution)/shard_map/ppermute | solution.py:334
  24.7 4.1 %collective-permute-done.8 = bf16[144,1024]{1,0:T(8,128)(2,1)S(1)} collective-permute-done((bf16[144,1024]{1,0:T(8,128)(2,1)S(1)}, bf16[144,1024]{1,0:T(8,128)(2,1)S(1)}, u32[]{:S(2)}, u32[]{:S(2)}) %collective-permute-start.8) | collective-permute-done | bytes 294944 | tf_op jit(solution)/shard_map/ppermute | solution.py:334
  32.5 1.5 %dispatch.4 = (bf16[16,64,1024]{2,1,0:T(8,128)(2,1)S(1)}, f32[16,64,128]{2,1,0:T(8,128)S(1)}, bf16[4,256,128]{2,1,0:T(8,128)(2,1)S(1)}, f32[8,128]{1,0:T(8,128)S(1)}) custom-call(s32[1]{0:T(128)} %bitcast.11.base_ref, bf16[64,1024]{1,0:T(8,128)(2,1)S(1)} %fusion.rw_ref, bf16[288,1024]{1,0:T(8,128)(2,1)S(1)} %pad_maximum_fusion.refs_0_.refs_1_, ...), custom_call_target="tpu_custom_call" | custom-call | flops 3300000000 | tf_op jit(solution)/shard_map/dispatch/pallas_call | solution.py:143
  34.1 2.9 %dispatch.5 = (bf16[16,64,1024]{2,1,0:T(8,128)(2,1)S(1)}, f32[16,64,128]{2,1,0:T(8,128)S(1)}, bf16[4,256,128]{2,1,0:T(8,128)(2,1)S(1)}) custom-call(s32[1]{0:T(128)} %bitcast.11.base_ref, bf16[64,1024]{1,0:T(8,128)(2,1)S(1)} %fusion.rw_ref, bf16[288,1024]{1,0:T(8,128)(2,1)} %constant_dynamic-update-slice_fusion.refs_0_.refs_1_, ...), custom_call_target="tpu_custom_call" | custom-call | flops 3300000000 | tf_op jit(solution)/shard_map/dispatch/pallas_call | solution.py:143
  37.7 1.5 %dispatch.6 = (bf16[16,64,1024]{2,1,0:T(8,128)(2,1)S(1)}, f32[16,64,128]{2,1,0:T(8,128)S(1)}, bf16[4,256,128]{2,1,0:T(8,128)(2,1)S(1)}) custom-call(s32[1]{0:T(128)} %bitcast.11.base_ref, bf16[64,1024]{1,0:T(8,128)(2,1)S(1)} %fusion.rw_ref, bf16[288,1024]{1,0:T(8,128)(2,1)S(1)} %constant_dynamic-update-slice_fusion.2.refs_0_.refs_1_, ...), custom_call_target="tpu_custom_call" | custom-call | flops 3300000000 | tf_op jit(solution)/shard_map/dispatch/pallas_call | solution.py:143
  43.0 2.7 %dispatch.7 = (bf16[16,64,1024]{2,1,0:T(8,128)(2,1)S(1)}, f32[16,64,128]{2,1,0:T(8,128)S(1)}, bf16[4,256,128]{2,1,0:T(8,128)(2,1)S(1)}, bf16[128,576]{1,0:T(8,128)(2,1)S(1)}) custom-call(s32[1]{0:T(128)} %bitcast.11.base_ref, bf16[64,1024]{1,0:T(8,128)(2,1)S(1)} %fusion.rw_ref, bf16[288,1024]{1,0:T(8,128)(2,1)S(1)} %stack.21.refs_0_.refs_1_, ...), custom_call_target="tpu_custom_call" | custom-call | flops 3300000000 | tf_op jit(solution)/shard_map/dispatch/pallas_call | solution.py:143
  45.7 1.6 %collective-permute-start.11 = (bf16[128,576]{1,0:T(8,128)(2,1)S(1)}, bf16[128,576]{1,0:T(8,128)(2,1)S(1)}, u32[]{:S(2)}, u32[]{:S(2)}) collective-permute-start(bf16[128,576]{1,0:T(8,128)(2,1)S(1)} %get-tuple-element.32), channel_id=1, source_target_pairs={{0,8},{4,12},{8,0},{12,4},{1,9},{5,13},{9,1},{13,5},{2,10},{6,14},... | collective-permute-start | bytes 442376 | tf_op jit(solution)/shard_map/ppermute | solution.py:334
  47.2 2.6 %copy-done.4 = bf16[16,176,1024]{2,1,0:T(8,128)(2,1)S(1)} copy-done((bf16[16,176,1024]{2,1,0:T(8,128)(2,1)S(1)}, bf16[16,176,1024]{2,1,0:T(8,128)(2,1)}, u32[]{:S(2)}) %copy-start.4) | copy-done | bytes 5767192
  49.9 15.4 %experts.1 = (bf16[16,64,1024]{2,1,0:T(8,128)(2,1)S(1)}, bf16[16,64,1024]{2,1,0:T(8,128)(2,1)S(1)}, bf16[16,64,1024]{2,1,0:T(8,128)(2,1)S(1)}, bf16[16,64,1024]{2,1,0:T(8,128)(2,1)S(1)}) custom-call(bf16[16,64,1024]{2,1,0:T(8,128)(2,1)S(1)} %get-tuple-element.29.refs_0_, bf16[16,64,1024]{2,1,0:T(8,128)(2,1)S(1)} %copy-done.1, ...), custom_call_target="tpu_custom_call" | custom-call | flops 13200000000 | tf_op jit(solution)/shard_map/experts/pallas_call | solution.py:217
  69.8 1.6 %collective-permute-start.17 = (bf16[1,128,1024]{2,1,0:T(8,128)(2,1)S(1)}, bf16[1,128,1024]{2,1,0:T(8,128)(2,1)S(1)}, u32[]{:S(2)}, u32[]{:S(2)}) collective-permute-start(bf16[1,128,1024]{2,1,0:T(8,128)(2,1)S(1)} %add_convert_fusion.5), channel_id=1, source_target_pairs={{0,8},{4,12},{8,0},{12,4},{1,9},{5,13},{9,1},{13,5},{2,10},{6,14},... | collective-permute-start | bytes 786440 | tf_op jit(solution)/shard_map/ppermute | solution.py:334
  72.1 6.3 %collective-permute-done.14 = bf16[1,128,1024]{2,1,0:T(8,128)(2,1)S(1)} collective-permute-done((bf16[1,128,1024]{2,1,0:T(8,128)(2,1)S(1)}, bf16[1,128,1024]{2,1,0:T(8,128)(2,1)S(1)}, u32[]{:S(2)}, u32[]{:S(2)}) %collective-permute-start.14) | collective-permute-done | bytes 262176 | tf_op jit(solution)/shard_map/ppermute | solution.py:334
  78.5 5.4 %collective-permute-start.15 = (bf16[1,128,1024]{2,1,0:T(8,128)(2,1)S(1)}, bf16[1,128,1024]{2,1,0:T(8,128)(2,1)S(1)}, u32[]{:S(2)}, u32[]{:S(2)}) collective-permute-start(bf16[1,128,1024]{2,1,0:T(8,128)(2,1)S(1)} %add_convert_fusion.6), channel_id=1, source_target_pairs={{0,2},{1,3},{2,0},{3,1},{4,6},{5,7},{6,4},{7,5},{8,10},{9,11},{10,... | collective-permute-start | bytes 786440 | tf_op jit(solution)/shard_map/ppermute | solution.py:337
  84.1 6.6 %collective-permute-start.18 = (bf16[1,128,1024]{2,1,0:T(8,128)(2,1)S(1)}, bf16[1,128,1024]{2,1,0:T(8,128)(2,1)S(1)}, u32[]{:S(2)}, u32[]{:S(2)}) collective-permute-start(bf16[1,128,1024]{2,1,0:T(8,128)(2,1)S(1)} %add_convert_fusion.4), channel_id=1, source_target_pairs={{0,3},{1,2},{2,1},{3,0},{4,7},{5,6},{6,5},{7,4},{8,11},{9,10},{10,... | collective-permute-start | bytes 786440 | tf_op jit(solution)/shard_map/ppermute | solution.py:337
  91.0 1.6 %collective-permute-start.23 = (bf16[1,128,1024]{2,1,0:T(8,128)(2,1)S(1)}, bf16[1,128,1024]{2,1,0:T(8,128)(2,1)S(1)}, u32[]{:S(2)}, u32[]{:S(2)}) collective-permute-start(bf16[1,128,1024]{2,1,0:T(8,128)(2,1)S(1)} %add_convert_fusion.1), channel_id=1, source_target_pairs={{0,8},{4,12},{8,0},{12,4},{1,9},{5,13},{9,1},{13,5},{2,10},{6,14},... | collective-permute-start | bytes 786440 | tf_op jit(solution)/shard_map/ppermute | solution.py:334
  92.5 6.2 %attention.1 = bf16[128,4096]{1,0:T(8,128)(2,1)} custom-call(s32[128,1]{1,0:T(8,128)S(1)} %copy.20.first_ref, s32[128,1]{1,0:T(8,128)S(1)} %copy.21.last_ref, s32[1,512]{1,0:T(1,128)S(1)} %bitcast.38, bf16[128,4608]{1,0:T(8,128)(2,1)S(1)} %bitcast.40, bf16[256,576]{1,0:T(8,128)(2,1)S(1)} %constant_dynamic-update-slice_fusion.4.refs_0_.refs_1_, ...), custom_call_target="tpu_custom_call" | custom-call | flops 6600000000 | tf_op jit(solution)/shard_map/attention/pallas_call | solution.py:303
  98.7 3.0 %collective-permute-done.15 = bf16[1,128,1024]{2,1,0:T(8,128)(2,1)S(1)} collective-permute-done((bf16[1,128,1024]{2,1,0:T(8,128)(2,1)S(1)}, bf16[1,128,1024]{2,1,0:T(8,128)(2,1)S(1)}, u32[]{:S(2)}, u32[]{:S(2)}) %collective-permute-start.15) | collective-permute-done | bytes 262176 | tf_op jit(solution)/shard_map/ppermute | solution.py:337
  101.7 4.3 %collective-permute-done.21 = bf16[1,128,1024]{2,1,0:T(8,128)(2,1)S(1)} collective-permute-done((bf16[1,128,1024]{2,1,0:T(8,128)(2,1)S(1)}, bf16[1,128,1024]{2,1,0:T(8,128)(2,1)S(1)}, u32[]{:S(2)}, u32[]{:S(2)}) %collective-permute-start.21) | collective-permute-done | bytes 262176 | tf_op jit(solution)/shard_map/ppermute | solution.py:337
  (106 shorter events, 22.2 us)
Async XLA Ops:
  2.3 10.5 %collective-permute-start.5 = (bf16[144,1024]{1,0:T(8,128)(2,1)S(1)}, bf16[144,1024]{1,0:T(8,128)(2,1)S(1)}, u32[]{:S(2)}, u32[]{:S(2)}) collective-permute-start(bf16[144,1024]{1,0:T(8,128)(2,1)S(1)} %pad_maximum_fusion.1), channel_id=1, source_target_pairs={{0,1},{1,0},{2,3},{3,2},{4,5},{5,4},{6,7},{7,6},{8,9},{9,8},{10,11... | collective-permute-start | bytes 884744 | tf_op jit(solution)/shard_map/ppermute | solution.py:337
  5.4 15.6 %collective-permute-start = (bf16[144,1024]{1,0:T(8,128)(2,1)S(1)}, bf16[144,1024]{1,0:T(8,128)(2,1)S(1)}, u32[]{:S(2)}, u32[]{:S(2)}) collective-permute-start(bf16[144,1024]{1,0:T(8,128)(2,1)S(1)} %pad_maximum_fusion.1), channel_id=1, source_target_pairs={{0,3},{1,2},{2,1},{3,0},{4,7},{5,6},{6,5},{7,4},{8,11},{9,10},{10,... | collective-permute-start | bytes 884744 | tf_op jit(solution)/shard_map/ppermute | solution.py:337
  7.9 9.9 %collective-permute-start.3 = (bf16[144,1024]{1,0:T(8,128)(2,1)S(1)}, bf16[144,1024]{1,0:T(8,128)(2,1)S(1)}, u32[]{:S(2)}, u32[]{:S(2)}) collective-permute-start(bf16[144,1024]{1,0:T(8,128)(2,1)S(1)} %pad_maximum_fusion.1), channel_id=1, source_target_pairs={{0,8},{4,12},{8,0},{12,4},{1,9},{5,13},{9,1},{13,5},{2,10},{6,14},... | collective-permute-start | bytes 884744 | tf_op jit(solution)/shard_map/ppermute | solution.py:334
  12.8 11.0 %collective-permute-start.6 = (bf16[144,1024]{1,0:T(8,128)(2,1)S(1)}, bf16[144,1024]{1,0:T(8,128)(2,1)S(1)}, u32[]{:S(2)}, u32[]{:S(2)}) collective-permute-start(bf16[144,1024]{1,0:T(8,128)(2,1)S(1)} %collective-permute-done.5), channel_id=1, source_target_pairs={{0,8},{4,12},{8,0},{12,4},{1,9},{5,13},{9,1},{13,5},{2,10},{6,14},... | collective-permute-start | bytes 884744 | tf_op jit(solution)/shard_map/ppermute | solution.py:334
  18.8 11.8 %collective-permute-start.4 = (bf16[288,1024]{1,0:T(8,128)(2,1)S(1)}, bf16[288,1024]{1,0:T(8,128)(2,1)S(1)}, u32[]{:S(2)}, u32[]{:S(2)}) collective-permute-start(bf16[288,1024]{1,0:T(8,128)(2,1)S(1)} %pad_maximum_fusion.refs_0_.refs_1_), channel_id=1, source_target_pairs={{0,4},{4,0},{8,12},{12,8},{1,5},{5,1},{9,13},{13,9},{2,6},{6,2},{1... | collective-permute-start | bytes 1769480 | tf_op jit(solution)/shard_map/ppermute | solution.py:334
  21.0 7.8 %collective-permute-start.8 = (bf16[144,1024]{1,0:T(8,128)(2,1)S(1)}, bf16[144,1024]{1,0:T(8,128)(2,1)S(1)}, u32[]{:S(2)}, u32[]{:S(2)}) collective-permute-start(bf16[144,1024]{1,0:T(8,128)(2,1)S(1)} %collective-permute-done), channel_id=1, source_target_pairs={{0,8},{4,12},{8,0},{12,4},{1,9},{5,13},{9,1},{13,5},{2,10},{6,14},... | collective-permute-start | bytes 884744 | tf_op jit(solution)/shard_map/ppermute | solution.py:334
  22.5 7.5 %collective-permute-start.1 = (bf16[144,1024]{1,0:T(8,128)(2,1)S(1)}, bf16[144,1024]{1,0:T(8,128)(2,1)S(1)}, u32[]{:S(2)}, u32[]{:S(2)}) collective-permute-start(bf16[144,1024]{1,0:T(8,128)(2,1)S(1)} %collective-permute-done), channel_id=1, source_target_pairs={{0,1},{1,0},{2,3},{3,2},{4,5},{5,4},{6,7},{7,6},{8,9},{9,8},{10,11... | collective-permute-start | bytes 884744 | tf_op jit(solution)/shard_map/ppermute | solution.py:337
  24.6 9.5 %collective-permute-start.7 = (bf16[288,1024]{1,0:T(8,128)(2,1)}, bf16[288,1024]{1,0:T(8,128)(2,1)}, u32[]{:S(2)}, u32[]{:S(2)}) collective-permute-start(bf16[288,1024]{1,0:T(8,128)(2,1)} %constant_dynamic-update-slice_fusion.refs_0_.refs_1_), channel_id=1, source_target_pairs={{0,4},{4,0},{8,12},{12,8},{1,5},{5,1},{9,13},{13,9},{2,6},{6,2},{1... | collective-permute-start | bytes 1769480 | tf_op jit(solution)/shard_map/ppermute | solution.py:334
  28.9 8.8 %collective-permute-start.9 = (bf16[288,1024]{1,0:T(8,128)(2,1)S(1)}, bf16[288,1024]{1,0:T(8,128)(2,1)S(1)}, u32[]{:S(2)}, u32[]{:S(2)}) collective-permute-start(bf16[288,1024]{1,0:T(8,128)(2,1)S(1)} %constant_dynamic-update-slice_fusion.2.refs_0_.refs_1_), channel_id=1, source_target_pairs={{0,4},{4,0},{8,12},{12,8},{1,5},{5,1},{9,13},{13,9},{2,6},{6,2},{1... | collective-permute-start | bytes 1769480 | tf_op jit(solution)/shard_map/ppermute | solution.py:334
  30.1 9.2 %collective-permute-start.2 = (bf16[144,1024]{1,0:T(8,128)(2,1)S(1)}, bf16[144,1024]{1,0:T(8,128)(2,1)S(1)}, u32[]{:S(2)}, u32[]{:S(2)}) collective-permute-start(bf16[144,1024]{1,0:T(8,128)(2,1)S(1)} %collective-permute-done.1.a_ref), channel_id=1, source_target_pairs={{0,8},{4,12},{8,0},{12,4},{1,9},{5,13},{9,1},{13,5},{2,10},{6,14},... | collective-permute-start | bytes 884744 | tf_op jit(solution)/shard_map/ppermute | solution.py:334
  40.8 2.1 %collective-permute-start.10 = (bf16[288,1024]{1,0:T(8,128)(2,1)S(1)}, bf16[288,1024]{1,0:T(8,128)(2,1)}, u32[]{:S(2)}, u32[]{:S(2)}) collective-permute-start(bf16[288,1024]{1,0:T(8,128)(2,1)S(1)} %stack.21.refs_0_.refs_1_), channel_id=1, source_target_pairs={{0,4},{4,0},{8,12},{12,8},{1,5},{5,1},{9,13},{13,9},{2,6},{6,2},{1... | collective-permute-start | bytes 1769480 | tf_op jit(solution)/shard_map/ppermute | solution.py:334
  45.7 20.3 %collective-permute-start.11 = (bf16[128,576]{1,0:T(8,128)(2,1)S(1)}, bf16[128,576]{1,0:T(8,128)(2,1)S(1)}, u32[]{:S(2)}, u32[]{:S(2)}) collective-permute-start(bf16[128,576]{1,0:T(8,128)(2,1)S(1)} %get-tuple-element.32), channel_id=1, source_target_pairs={{0,8},{4,12},{8,0},{12,4},{1,9},{5,13},{9,1},{13,5},{2,10},{6,14},... | collective-permute-start | bytes 442376 | tf_op jit(solution)/shard_map/ppermute | solution.py:334
  65.8 3.3 %collective-permute-start.13 = (bf16[1,256,1024]{2,1,0:T(8,128)(2,1)S(1)}, bf16[1,256,1024]{2,1,0:T(8,128)(2,1)S(1)}, u32[]{:S(2)}, u32[]{:S(2)}) collective-permute-start(bf16[1,256,1024]{2,1,0:T(8,128)(2,1)S(1)} %get-tuple-element.41), channel_id=1, source_target_pairs={{0,4},{4,0},{8,12},{12,8},{1,5},{5,1},{9,13},{13,9},{2,6},{6,2},{1... | collective-permute-start | bytes 1572872 | tf_op jit(solution)/shard_map/ppermute | solution.py:334
  66.0 2.3 %collective-permute-start.12 = (bf16[256,576]{1,0:T(8,128)(2,1)S(1)}, bf16[256,576]{1,0:T(8,128)(2,1)S(1)}, u32[]{:S(2)}, u32[]{:S(2)}) collective-permute-start(bf16[256,576]{1,0:T(8,128)(2,1)S(1)} %constant_dynamic-update-slice_fusion.4.refs_0_.refs_1_), channel_id=1, source_target_pairs={{0,4},{4,0},{8,12},{12,8},{1,5},{5,1},{9,13},{13,9},{2,6},{6,2},{1... | collective-permute-start | bytes 884744 | tf_op jit(solution)/shard_map/ppermute | solution.py:334
  67.0 2.8 %collective-permute-start.16 = (bf16[1,256,1024]{2,1,0:T(8,128)(2,1)S(1)}, bf16[1,256,1024]{2,1,0:T(8,128)(2,1)S(1)}, u32[]{:S(2)}, u32[]{:S(2)}) collective-permute-start(bf16[1,256,1024]{2,1,0:T(8,128)(2,1)S(1)} %get-tuple-element.45), channel_id=1, source_target_pairs={{0,4},{4,0},{8,12},{12,8},{1,5},{5,1},{9,13},{13,9},{2,6},{6,2},{1... | collective-permute-start | bytes 1572872 | tf_op jit(solution)/shard_map/ppermute | solution.py:334
  67.9 3.4 %collective-permute-start.19 = (bf16[1,256,1024]{2,1,0:T(8,128)(2,1)S(1)}, bf16[1,256,1024]{2,1,0:T(8,128)(2,1)S(1)}, u32[]{:S(2)}, u32[]{:S(2)}) collective-permute-start(bf16[1,256,1024]{2,1,0:T(8,128)(2,1)S(1)} %get-tuple-element.49), channel_id=1, source_target_pairs={{0,4},{4,0},{8,12},{12,8},{1,5},{5,1},{9,13},{13,9},{2,6},{6,2},{1... | collective-permute-start | bytes 1572872 | tf_op jit(solution)/shard_map/ppermute | solution.py:334
  68.7 22.1 %collective-permute-start.22 = (bf16[1,256,1024]{2,1,0:T(8,128)(2,1)S(1)}, bf16[1,256,1024]{2,1,0:T(8,128)(2,1)S(1)}, u32[]{:S(2)}, u32[]{:S(2)}) collective-permute-start(bf16[1,256,1024]{2,1,0:T(8,128)(2,1)S(1)} %get-tuple-element.53), channel_id=1, source_target_pairs={{0,4},{4,0},{8,12},{12,8},{1,5},{5,1},{9,13},{13,9},{2,6},{6,2},{1... | collective-permute-start | bytes 1572872 | tf_op jit(solution)/shard_map/ppermute | solution.py:334
  69.1 9.2 %collective-permute-start.14 = (bf16[1,128,1024]{2,1,0:T(8,128)(2,1)S(1)}, bf16[1,128,1024]{2,1,0:T(8,128)(2,1)S(1)}, u32[]{:S(2)}, u32[]{:S(2)}) collective-permute-start(bf16[1,128,1024]{2,1,0:T(8,128)(2,1)S(1)} %add_convert_fusion.7), channel_id=1, source_target_pairs={{0,8},{4,12},{8,0},{12,4},{1,9},{5,13},{9,1},{13,5},{2,10},{6,14},... | collective-permute-start | bytes 786440 | tf_op jit(solution)/shard_map/ppermute | solution.py:334
  69.8 14.1 %collective-permute-start.17 = (bf16[1,128,1024]{2,1,0:T(8,128)(2,1)S(1)}, bf16[1,128,1024]{2,1,0:T(8,128)(2,1)S(1)}, u32[]{:S(2)}, u32[]{:S(2)}) collective-permute-start(bf16[1,128,1024]{2,1,0:T(8,128)(2,1)S(1)} %add_convert_fusion.5), channel_id=1, source_target_pairs={{0,8},{4,12},{8,0},{12,4},{1,9},{5,13},{9,1},{13,5},{2,10},{6,14},... | collective-permute-start | bytes 786440 | tf_op jit(solution)/shard_map/ppermute | solution.py:334
  71.5 19.2 %collective-permute-start.20 = (bf16[1,128,1024]{2,1,0:T(8,128)(2,1)S(1)}, bf16[1,128,1024]{2,1,0:T(8,128)(2,1)S(1)}, u32[]{:S(2)}, u32[]{:S(2)}) collective-permute-start(bf16[1,128,1024]{2,1,0:T(8,128)(2,1)S(1)} %add_convert_fusion.3), channel_id=1, source_target_pairs={{0,8},{4,12},{8,0},{12,4},{1,9},{5,13},{9,1},{13,5},{2,10},{6,14},... | collective-permute-start | bytes 786440 | tf_op jit(solution)/shard_map/ppermute | solution.py:334
  78.5 23.2 %collective-permute-start.15 = (bf16[1,128,1024]{2,1,0:T(8,128)(2,1)S(1)}, bf16[1,128,1024]{2,1,0:T(8,128)(2,1)S(1)}, u32[]{:S(2)}, u32[]{:S(2)}) collective-permute-start(bf16[1,128,1024]{2,1,0:T(8,128)(2,1)S(1)} %add_convert_fusion.6), channel_id=1, source_target_pairs={{0,2},{1,3},{2,0},{3,1},{4,6},{5,7},{6,4},{7,5},{8,10},{9,11},{10,... | collective-permute-start | bytes 786440 | tf_op jit(solution)/shard_map/ppermute | solution.py:337
  84.1 17.6 %collective-permute-start.18 = (bf16[1,128,1024]{2,1,0:T(8,128)(2,1)S(1)}, bf16[1,128,1024]{2,1,0:T(8,128)(2,1)S(1)}, u32[]{:S(2)}, u32[]{:S(2)}) collective-permute-start(bf16[1,128,1024]{2,1,0:T(8,128)(2,1)S(1)} %add_convert_fusion.4), channel_id=1, source_target_pairs={{0,3},{1,2},{2,1},{3,0},{4,7},{5,6},{6,5},{7,4},{8,11},{9,10},{10,... | collective-permute-start | bytes 786440 | tf_op jit(solution)/shard_map/ppermute | solution.py:337
  90.8 15.2 %collective-permute-start.21 = (bf16[1,128,1024]{2,1,0:T(8,128)(2,1)S(1)}, bf16[1,128,1024]{2,1,0:T(8,128)(2,1)S(1)}, u32[]{:S(2)}, u32[]{:S(2)}) collective-permute-start(bf16[1,128,1024]{2,1,0:T(8,128)(2,1)S(1)} %add_convert_fusion.2), channel_id=1, source_target_pairs={{0,1},{1,0},{2,3},{3,2},{4,5},{5,4},{6,7},{7,6},{8,9},{9,8},{10,11... | collective-permute-start | bytes 786440 | tf_op jit(solution)/shard_map/ppermute | solution.py:337
  91.0 15.0 %collective-permute-start.23 = (bf16[1,128,1024]{2,1,0:T(8,128)(2,1)S(1)}, bf16[1,128,1024]{2,1,0:T(8,128)(2,1)S(1)}, u32[]{:S(2)}, u32[]{:S(2)}) collective-permute-start(bf16[1,128,1024]{2,1,0:T(8,128)(2,1)S(1)} %add_convert_fusion.1), channel_id=1, source_target_pairs={{0,8},{4,12},{8,0},{12,4},{1,9},{5,13},{9,1},{13,5},{2,10},{6,14},... | collective-permute-start | bytes 786440 | tf_op jit(solution)/shard_map/ppermute | solution.py:334
  (19 other events, 61.7 us)

commit v11 on v8

--- a/solution.py
+++ b/solution.py
@@ -405,7 +405,6 @@
     local = gate_up.shape[0]
     near = n_exp == 4
     shifts = [0, 1, 3, 2] if near else [0]
-    flips = (2, 1)
     tokens = hidden_in[0]
 
     def flip(a, bit):
@@ -428,30 +427,26 @@
     picks = jnp.pad(picks, ((0, EXTRA - 1), (0, width - top * tok_rows)))
     packed = jnp.concatenate([tokens, picks], axis=0)
 
+    keys = latent_kv[0]
+    keys = jnp.concatenate([keys, flip(keys, 2)], axis=0)
     near_parts = along_exp(packed)
-    arrived = list(near_parts)
+    arrived = near_parts
+    crossed = [flip(a, 2) for a in near_parts[:3]]
     if near:
-        kdim = latent_kv.shape[2]
-        keys = jnp.pad(latent_kv[0], ((0, EXTRA), (0, -kdim % LANES)))
-        near_parts[0] = jnp.concatenate([packed, keys], axis=1)
-    crossed = [flip(a, 2) for a in near_parts]
+        crossed.append(shift(crossed[2], 1))
+    kv = [(a, k * tok_rows) for a in (keys, flip(keys, 1)) for k in range(2)]
     if near:
         blocks = 1
         pairs = [jnp.concatenate([a, b], axis=0) for a, b in zip(near_parts, crossed)]
         flipped = [flip(a, 1) for a in pairs]
         spread = [[(a, 0), (a, 1), (b, 0), (b, 1)] for a, b in zip(pairs, flipped)]
-        kv = [(a, k * (BLOCK + EXTRA)) for a, k in spread[0]]
     else:
         blocks = near_parts[0].shape[0] // (BLOCK + EXTRA)
         spread = [[(near_parts[0], 0), (crossed[0], 0)]]
         spread[0] = spread[0] + [(flip(a, 1), 0) for a, _ in spread[0]]
-        kv = [latent_kv[0]]
-        for bit in flips:
-            kv = kv + [flip(a, bit) for a in kv]
-        kv = [(a, 0) for a in kv]
     behind = [()] * PIECES
     if near:
-        behind = [(), (arrived[1],), (arrived[2], crossed[0]), (arrived[3],)]
+        behind = [(), (arrived[1],), (arrived[2],), (crossed[2],)]
 
     lengths = doc_lengths[0]
     ends = jnp.cumsum(lengths)
@@ -483,8 +478,10 @@
         got = flip(give, 1)
         far = added(keep[:, tok_rows:], got[:, tok_rows:])
         terms = [keep[:, :tok_rows], got[:, :tok_rows], flip(far, 2)]
-        if i:
-            back.append(shift(added(*terms), shifts[i]))
+        if shifts[i] == 2:
+            joining = [shift(added(*terms), 1)]
+        elif i:
+            back.append(shift(added(*terms, *(joining if shifts[i] == 3 else [])), shifts[i]))
         else:
             back = back + terms
     if near:

time: 103 us -> 103 us (level)
    ppermute x6 -> x7, starting transfers between devices: 14 us -> 12.7 us  [shift(): return lax.ppermute(a, 'exp', [(i, i ^ d) for i in range(n_exp)])]
    ppermute x16 -> x17, starting transfers between devices: 10.6 us -> 11.7 us  [flip(): return lax.ppermute(a, 'ctx', [(i, i ^ bit) for i in range(n_ctx)])]
    ppermute x6 -> x7, waiting for transfers between devices: 5.49 us -> 6.39 us  [shift(): return lax.ppermute(a, 'exp', [(i, i ^ d) for i in range(n_exp)])]
    ppermute x16 -> x17, waiting for transfers between devices: 16.6 us -> 15.7 us  [flip(): return lax.ppermute(a, 'ctx', [(i, i ^ bit) for i in range(n_ctx)])]
  transfers between devices with their start and end apart: 22 -> 24, of which waited for: 7 -> 7; matrix products, arithmetic and copies ran while one was open for 4% -> 5% of each run, Pallas kernels for 32% -> 46%
where the time goes in v11:
time: 103 us; the launch traced here: 102 us
  Pallas kernels  47.3 us (46%)
  starting transfers between devices  24.4 us (24%)
  waiting for transfers between devices  22.1 us (21%)
  other arithmetic  5.22 us (5%)
  local copies, waits for them, and re-layouts  2.21 us (2%)
    pallas_call x4, Pallas kernels, sort_rows(): call(functools.partial(sort_kernel, j * local // pieces), 4, (local // pi...  20.4 us
    ppermute x17, waiting for transfers between devices, flip(): return lax.ppermute(a, 'ctx', [(i, i ^ bit) for i in range(n_ctx)])  15.7 us
    pallas_call x1, Pallas kernels, experts(): call(functools.partial(expert_kernel, n), 6, (local // group, slots // si...  12.8 us
    ppermute x7, starting transfers between devices, shift(): return lax.ppermute(a, 'exp', [(i, i ^ d) for i in range(n_exp)])  12.7 us
    ppermute x17, starting transfers between devices, flip(): return lax.ppermute(a, 'ctx', [(i, i ^ bit) for i in range(n_ctx)])  11.7 us
    ppermute x7, waiting for transfers between devices, shift(): return lax.ppermute(a, 'exp', [(i, i ^ d) for i in range(n_exp)])  6.39 us
    pallas_call x1, Pallas kernels, attend(): call(functools.partial(attend_kernel, [at for _, at in parts], kdim), 6,...  6.17 us
    pallas_call x4, Pallas kernels, dispatch(): call(functools.partial(dispatch_kernel, n_parts, n_parts if row is not No...  6.01 us
  transfers between devices with their start and end apart: 24, of which 7 were waited for; matrix products, arithmetic and copies ran while one was open for 5% of the time, Pallas kernels for 46%

profile of v11, /device:TPU:0, one launch (start us, length us, event | category | flops | bytes accessed | tf_op | source)
XLA Modules:
  0.0 102.2 jit_solution(10611624578841886018)
XLA Ops:
  2.3 5.1 %collective-permute-start.2 = (bf16[144,1024]{1,0:T(8,128)(2,1)S(1)}, bf16[144,1024]{1,0:T(8,128)(2,1)S(1)}, u32[]{:S(2)}, u32[]{:S(2)}) collective-permute-start(bf16[144,1024]{1,0:T(8,128)(2,1)S(1)} %pad_maximum_fusion.2), channel_id=1, source_target_pairs={{0,3},{1,2},{2,1},{3,0},{4,7},{5,6},{6,5},{7,4},{8,11},{9,10},{10,... | collective-permute-start | bytes 884744 | tf_op jit(solution)/shard_map/ppermute | solution.py:414
  7.4 1.5 %collective-permute-start.5 = (bf16[144,1024]{1,0:T(8,128)(2,1)S(1)}, bf16[144,1024]{1,0:T(8,128)(2,1)S(1)}, u32[]{:S(2)}, u32[]{:S(2)}) collective-permute-start(bf16[144,1024]{1,0:T(8,128)(2,1)S(1)} %pad_maximum_fusion.2), channel_id=1, source_target_pairs={{0,8},{4,12},{8,0},{12,4},{1,9},{5,13},{9,1},{13,5},{2,10},{6,14},... | collective-permute-start | bytes 884744 | tf_op jit(solution)/shard_map/ppermute | solution.py:411
  12.2 5.1 %sort.4.refs_0_ = bf16[16,2,176,1024]{3,2,1,0:T(8,128)(2,1)} custom-call(bf16[16,2816,128]{2,1,0:T(8,128)(2,1)} %bitcast.42), custom_call_target="tpu_custom_call" | custom-call | flops 4400000000 | tf_op jit(solution)/shard_map/sort/pallas_call | solution.py:237
  17.9 1.5 %collective-permute-done = bf16[128,576]{1,0:T(8,128)(2,1)S(1)} collective-permute-done((bf16[128,576]{1,0:T(8,128)(2,1)S(1)}, bf16[128,576]{1,0:T(8,128)(2,1)S(1)}, u32[]{:S(2)}, u32[]{:S(2)}) %collective-permute-start) | collective-permute-done | bytes 147488 | tf_op jit(solution)/shard_map/ppermute | solution.py:411
  20.1 1.5 %collective-permute-start.3 = (bf16[144,1024]{1,0:T(8,128)(2,1)S(1)}, bf16[144,1024]{1,0:T(8,128)(2,1)S(1)}, u32[]{:S(2)}, u32[]{:S(2)}) collective-permute-start(bf16[144,1024]{1,0:T(8,128)(2,1)S(1)} %collective-permute-done.2.refs_1_), channel_id=1, source_target_pairs={{0,8},{4,12},{8,0},{12,4},{1,9},{5,13},{9,1},{13,5},{2,10},{6,14},... | collective-permute-start | bytes 884744 | tf_op jit(solution)/shard_map/ppermute | solution.py:411
  21.6 1.7 %collective-permute-start.10 = (bf16[144,1024]{1,0:T(8,128)(2,1)S(1)}, bf16[144,1024]{1,0:T(8,128)(2,1)S(1)}, u32[]{:S(2)}, u32[]{:S(2)}) collective-permute-start(bf16[144,1024]{1,0:T(8,128)(2,1)S(1)} %collective-permute-done.2.refs_1_), channel_id=1, source_target_pairs={{0,1},{1,0},{2,3},{3,2},{4,5},{5,4},{6,7},{7,6},{8,9},{9,8},{10,11... | collective-permute-start | bytes 884744 | tf_op jit(solution)/shard_map/ppermute | solution.py:414
  23.9 5.1 %sort.5.refs_0_ = bf16[16,2,176,1024]{3,2,1,0:T(8,128)(2,1)} custom-call(bf16[16,2816,128]{2,1,0:T(8,128)(2,1)} %bitcast.43, bf16[16,2,176,1024]{3,2,1,0:T(8,128)(2,1)} %sort.4.refs_0_, bf16[144,1024]{1,0:T(8,128)(2,1)S(1)} %collective-permute-done.7.refs_1_), custom_call_target="tpu_custom_call", output_to_operand_aliasing={{}: (1, {})} | custom-call | flops 4400000000 | tf_op jit(solution)/shard_map/sort/pallas_call | solution.py:237
  29.0 5.2 %sort.6.refs_0_ = bf16[16,2,176,1024]{3,2,1,0:T(8,128)(2,1)} custom-call(bf16[16,2816,128]{2,1,0:T(8,128)(2,1)} %bitcast.44, bf16[16,2,176,1024]{3,2,1,0:T(8,128)(2,1)} %sort.5.refs_0_, bf16[144,1024]{1,0:T(8,128)(2,1)S(1)} %collective-permute-done.2.refs_1_), custom_call_target="tpu_custom_call", output_to_operand_aliasing={{}: (1, {})} | custom-call | flops 4400000000 | tf_op jit(solution)/shard_map/sort/pallas_call | solution.py:237
  35.6 1.8 %collective-permute-start.11 = (bf16[144,1024]{1,0:T(8,128)(2,1)S(1)}, bf16[144,1024]{1,0:T(8,128)(2,1)S(1)}, u32[]{:S(2)}, u32[]{:S(2)}) collective-permute-start(bf16[144,1024]{1,0:T(8,128)(2,1)S(1)} %collective-permute-done.3.refs_1_), channel_id=1, source_target_pairs={{0,1},{1,0},{2,3},{3,2},{4,5},{5,4},{6,7},{7,6},{8,9},{9,8},{10,11... | collective-permute-start | bytes 884744 | tf_op jit(solution)/shard_map/ppermute | solution.py:414
  37.4 5.1 %sort.7.refs_8_ = bf16[16,2,176,1024]{3,2,1,0:T(8,128)(2,1)} custom-call(bf16[16,2816,128]{2,1,0:T(8,128)(2,1)} %bitcast.45, bf16[16,2,176,1024]{3,2,1,0:T(8,128)(2,1)} %sort.6.refs_0_, bf16[144,1024]{1,0:T(8,128)(2,1)S(1)} %collective-permute-done.3.refs_1_), custom_call_target="tpu_custom_call", output_to_operand_aliasing={{}: (1, {})} | custom-call | flops 4400000000 | tf_op jit(solution)/shard_map/sort/pallas_call | solution.py:237
  42.8 2.2 %collective-permute-done.11 = bf16[144,1024]{1,0:T(8,128)(2,1)S(1)} collective-permute-done((bf16[144,1024]{1,0:T(8,128)(2,1)S(1)}, bf16[144,1024]{1,0:T(8,128)(2,1)S(1)}, u32[]{:S(2)}, u32[]{:S(2)}) %collective-permute-start.11) | collective-permute-done | bytes 294944 | tf_op jit(solution)/shard_map/ppermute | solution.py:414
  45.2 1.5 %dispatch.5 = (bf16[16,64,1024]{2,1,0:T(8,128)(2,1)S(1)}, f32[16,64,128]{2,1,0:T(8,128)S(1)}, bf16[4,256,128]{2,1,0:T(8,128)(2,1)S(1)}, f32[8,128]{1,0:T(8,128)S(1)}) custom-call(s32[1]{0:T(128)} %bitcast.13.base_ref, bf16[64,1024]{1,0:T(8,128)(2,1)S(1)} %fusion.rw_ref, bf16[288,1024]{1,0:T(8,128)(2,1)S(1)} %pad_maximum_fusion.refs_0_.refs_1_, ...), custom_call_target="tpu_custom_call" | custom-call | flops 3300000000 | tf_op jit(solution)/shard_map/dispatch/pallas_call | solution.py:144
  48.2 1.5 %dispatch.4 = (bf16[16,64,1024]{2,1,0:T(8,128)(2,1)S(1)}, f32[16,64,128]{2,1,0:T(8,128)S(1)}, bf16[4,256,128]{2,1,0:T(8,128)(2,1)S(1)}) custom-call(s32[1]{0:T(128)} %bitcast.13.base_ref, bf16[64,1024]{1,0:T(8,128)(2,1)S(1)} %fusion.rw_ref, bf16[288,1024]{1,0:T(8,128)(2,1)S(1)} %constant_dynamic-update-slice_fusion.refs_0_.refs_1_, ...), custom_call_target="tpu_custom_call" | custom-call | flops 3300000000 | tf_op jit(solution)/shard_map/dispatch/pallas_call | solution.py:144
  49.8 1.5 %dispatch.7 = (bf16[16,64,1024]{2,1,0:T(8,128)(2,1)S(1)}, f32[16,64,128]{2,1,0:T(8,128)S(1)}, bf16[4,256,128]{2,1,0:T(8,128)(2,1)S(1)}) custom-call(s32[1]{0:T(128)} %bitcast.13.base_ref, bf16[64,1024]{1,0:T(8,128)(2,1)S(1)} %fusion.rw_ref, bf16[288,1024]{1,0:T(8,128)(2,1)S(1)} %constant_dynamic-update-slice_fusion.4.refs_0_.refs_1_, ...), custom_call_target="tpu_custom_call" | custom-call | flops 3300000000 | tf_op jit(solution)/shard_map/dispatch/pallas_call | solution.py:144
  51.3 12.8 %experts.1 = (bf16[16,64,1024]{2,1,0:T(8,128)(2,1)S(1)}, bf16[16,64,1024]{2,1,0:T(8,128)(2,1)S(1)}, bf16[16,64,1024]{2,1,0:T(8,128)(2,1)S(1)}, bf16[16,64,1024]{2,1,0:T(8,128)(2,1)S(1)}) custom-call(bf16[16,64,1024]{2,1,0:T(8,128)(2,1)S(1)} %get-tuple-element.29.refs_0_, bf16[16,64,1024]{2,1,0:T(8,128)(2,1)S(1)} %get-tuple-element.30.refs_1_, ...), custom_call_target="tpu_custom_call" | custom-call | flops 6600000000 | tf_op jit(solution)/shard_map/experts/pallas_call | solution.py:295
  67.4 1.6 %collective-permute-start.16 = (bf16[1,128,1024]{2,1,0:T(8,128)(2,1)S(1)}, bf16[1,128,1024]{2,1,0:T(8,128)(2,1)S(1)}, u32[]{:S(2)}, u32[]{:S(2)}) collective-permute-start(bf16[1,128,1024]{2,1,0:T(8,128)(2,1)S(1)} %add_convert_fusion.6), channel_id=1, source_target_pairs={{0,8},{4,12},{8,0},{12,4},{1,9},{5,13},{9,1},{13,5},{2,10},{6,14},... | collective-permute-start | bytes 786440 | tf_op jit(solution)/shard_map/ppermute | solution.py:411
  69.7 1.6 %collective-permute-start.20 = (bf16[1,128,1024]{2,1,0:T(8,128)(2,1)S(1)}, bf16[1,128,1024]{2,1,0:T(8,128)(2,1)S(1)}, u32[]{:S(2)}, u32[]{:S(2)}) collective-permute-start(bf16[1,128,1024]{2,1,0:T(8,128)(2,1)S(1)} %add_convert_fusion.3), channel_id=1, source_target_pairs={{0,8},{4,12},{8,0},{12,4},{1,9},{5,13},{9,1},{13,5},{2,10},{6,14},... | collective-permute-start | bytes 786440 | tf_op jit(solution)/shard_map/ppermute | solution.py:411
  71.3 5.3 %collective-permute-done.16 = bf16[1,128,1024]{2,1,0:T(8,128)(2,1)S(1)} collective-permute-done((bf16[1,128,1024]{2,1,0:T(8,128)(2,1)S(1)}, bf16[1,128,1024]{2,1,0:T(8,128)(2,1)S(1)}, u32[]{:S(2)}, u32[]{:S(2)}) %collective-permute-start.16) | collective-permute-done | bytes 262176 | tf_op jit(solution)/shard_map/ppermute | solution.py:411
  76.7 1.8 %collective-permute-start.17 = (bf16[1,128,1024]{2,1,0:T(8,128)(2,1)S(1)}, bf16[1,128,1024]{2,1,0:T(8,128)(2,1)S(1)}, u32[]{:S(2)}, u32[]{:S(2)}) collective-permute-start(bf16[1,128,1024]{2,1,0:T(8,128)(2,1)S(1)} %add_convert_fusion.5), channel_id=1, source_target_pairs={{0,1},{1,0},{2,3},{3,2},{4,5},{5,4},{6,7},{7,6},{8,9},{9,8},{10,11... | collective-permute-start | bytes 786440 | tf_op jit(solution)/shard_map/ppermute | solution.py:414
  78.6 1.6 %collective-permute-start.23 = (bf16[1,128,1024]{2,1,0:T(8,128)(2,1)S(1)}, bf16[1,128,1024]{2,1,0:T(8,128)(2,1)S(1)}, u32[]{:S(2)}, u32[]{:S(2)}) collective-permute-start(bf16[1,128,1024]{2,1,0:T(8,128)(2,1)S(1)} %add_convert_fusion.1), channel_id=1, source_target_pairs={{0,8},{4,12},{8,0},{12,4},{1,9},{5,13},{9,1},{13,5},{2,10},{6,14},... | collective-permute-start | bytes 786440 | tf_op jit(solution)/shard_map/ppermute | solution.py:411
  80.1 7.7 %collective-permute-done.20 = bf16[1,128,1024]{2,1,0:T(8,128)(2,1)S(1)} collective-permute-done((bf16[1,128,1024]{2,1,0:T(8,128)(2,1)S(1)}, bf16[1,128,1024]{2,1,0:T(8,128)(2,1)S(1)}, u32[]{:S(2)}, u32[]{:S(2)}) %collective-permute-start.20) | collective-permute-done | bytes 262176 | tf_op jit(solution)/shard_map/ppermute | solution.py:411
  87.9 1.8 %collective-permute-start.21 = (bf16[1,128,1024]{2,1,0:T(8,128)(2,1)S(1)}, bf16[1,128,1024]{2,1,0:T(8,128)(2,1)S(1)}, u32[]{:S(2)}, u32[]{:S(2)}) collective-permute-start(bf16[1,128,1024]{2,1,0:T(8,128)(2,1)S(1)} %add_convert_fusion.2), channel_id=1, source_target_pairs={{0,1},{1,0},{2,3},{3,2},{4,5},{5,4},{6,7},{7,6},{8,9},{9,8},{10,11... | collective-permute-start | bytes 786440 | tf_op jit(solution)/shard_map/ppermute | solution.py:414
  90.4 6.2 %attention.1 = bf16[128,4096]{1,0:T(8,128)(2,1)} custom-call(s32[128,1]{1,0:T(8,128)S(1)} %copy.23.first_ref, s32[128,1]{1,0:T(8,128)S(1)} %copy.24.last_ref, s32[1,512]{1,0:T(1,128)S(1)} %bitcast.39, bf16[128,4608]{1,0:T(8,128)(2,1)S(1)} %bitcast.41, bf16[256,576]{1,0:T(8,128)(2,1)S(1)} %pad_maximum_fusion.1.refs_0_.refs_1_, ...), custom_call_target="tpu_custom_call" | custom-call | flops 6600000000 | tf_op jit(solution)/shard_map/attention/pallas_call | solution.py:380
  97.2 4.1 %collective-permute-done.18 = bf16[1,128,1024]{2,1,0:T(8,128)(2,1)S(1)} collective-permute-done((bf16[1,128,1024]{2,1,0:T(8,128)(2,1)S(1)}, bf16[1,128,1024]{2,1,0:T(8,128)(2,1)S(1)}, u32[]{:S(2)}, u32[]{:S(2)}) %collective-permute-start.18) | collective-permute-done | bytes 262176 | tf_op jit(solution)/shard_map/ppermute | solution.py:414
  (83 shorter events, 16.6 us)
Async XLA Ops:
  2.3 17.8 %collective-permute-start.2 = (bf16[144,1024]{1,0:T(8,128)(2,1)S(1)}, bf16[144,1024]{1,0:T(8,128)(2,1)S(1)}, u32[]{:S(2)}, u32[]{:S(2)}) collective-permute-start(bf16[144,1024]{1,0:T(8,128)(2,1)S(1)} %pad_maximum_fusion.2), channel_id=1, source_target_pairs={{0,3},{1,2},{2,1},{3,0},{4,7},{5,6},{6,5},{7,4},{8,11},{9,10},{10,... | collective-permute-start | bytes 884744 | tf_op jit(solution)/shard_map/ppermute | solution.py:414
  7.4 16.0 %collective-permute-start.7 = (bf16[144,1024]{1,0:T(8,128)(2,1)S(1)}, bf16[144,1024]{1,0:T(8,128)(2,1)S(1)}, u32[]{:S(2)}, u32[]{:S(2)}) collective-permute-start(bf16[144,1024]{1,0:T(8,128)(2,1)S(1)} %pad_maximum_fusion.2), channel_id=1, source_target_pairs={{0,1},{1,0},{2,3},{3,2},{4,5},{5,4},{6,7},{7,6},{8,9},{9,8},{10,11... | collective-permute-start | bytes 884744 | tf_op jit(solution)/shard_map/ppermute | solution.py:414
  7.4 12.1 %collective-permute-start.5 = (bf16[144,1024]{1,0:T(8,128)(2,1)S(1)}, bf16[144,1024]{1,0:T(8,128)(2,1)S(1)}, u32[]{:S(2)}, u32[]{:S(2)}) collective-permute-start(bf16[144,1024]{1,0:T(8,128)(2,1)S(1)} %pad_maximum_fusion.2), channel_id=1, source_target_pairs={{0,8},{4,12},{8,0},{12,4},{1,9},{5,13},{9,1},{13,5},{2,10},{6,14},... | collective-permute-start | bytes 884744 | tf_op jit(solution)/shard_map/ppermute | solution.py:411
  10.0 9.4 %collective-permute-start = (bf16[128,576]{1,0:T(8,128)(2,1)S(1)}, bf16[128,576]{1,0:T(8,128)(2,1)S(1)}, u32[]{:S(2)}, u32[]{:S(2)}) collective-permute-start(bf16[128,576]{1,0:T(8,128)(2,1)S(1)} %bitcast.48), channel_id=1, source_target_pairs={{0,8},{4,12},{8,0},{12,4},{1,9},{5,13},{9,1},{13,5},{2,10},{6,14},... | collective-permute-start | bytes 442376 | tf_op jit(solution)/shard_map/ppermute | solution.py:411
  19.5 70.9 %collective-permute-start.1 = (bf16[256,576]{1,0:T(8,128)(2,1)S(1)}, bf16[256,576]{1,0:T(8,128)(2,1)S(1)}, u32[]{:S(2)}, u32[]{:S(2)}) collective-permute-start(bf16[256,576]{1,0:T(8,128)(2,1)S(1)} %pad_maximum_fusion.1.refs_0_.refs_1_), channel_id=1, source_target_pairs={{0,4},{4,0},{8,12},{12,8},{1,5},{5,1},{9,13},{13,9},{2,6},{6,2},{1... | collective-permute-start | bytes 884744 | tf_op jit(solution)/shard_map/ppermute | solution.py:411
  19.6 25.5 %collective-permute-start.6 = (bf16[288,1024]{1,0:T(8,128)(2,1)S(1)}, bf16[288,1024]{1,0:T(8,128)(2,1)S(1)}, u32[]{:S(2)}, u32[]{:S(2)}) collective-permute-start(bf16[288,1024]{1,0:T(8,128)(2,1)S(1)} %pad_maximum_fusion.refs_0_.refs_1_), channel_id=1, source_target_pairs={{0,4},{4,0},{8,12},{12,8},{1,5},{5,1},{9,13},{13,9},{2,6},{6,2},{1... | collective-permute-start | bytes 1769480 | tf_op jit(solution)/shard_map/ppermute | solution.py:411
  20.1 15.4 %collective-permute-start.3 = (bf16[144,1024]{1,0:T(8,128)(2,1)S(1)}, bf16[144,1024]{1,0:T(8,128)(2,1)S(1)}, u32[]{:S(2)}, u32[]{:S(2)}) collective-permute-start(bf16[144,1024]{1,0:T(8,128)(2,1)S(1)} %collective-permute-done.2.refs_1_), channel_id=1, source_target_pairs={{0,8},{4,12},{8,0},{12,4},{1,9},{5,13},{9,1},{13,5},{2,10},{6,14},... | collective-permute-start | bytes 884744 | tf_op jit(solution)/shard_map/ppermute | solution.py:411
  21.6 20.9 %collective-permute-start.10 = (bf16[144,1024]{1,0:T(8,128)(2,1)S(1)}, bf16[144,1024]{1,0:T(8,128)(2,1)S(1)}, u32[]{:S(2)}, u32[]{:S(2)}) collective-permute-start(bf16[144,1024]{1,0:T(8,128)(2,1)S(1)} %collective-permute-done.2.refs_1_), channel_id=1, source_target_pairs={{0,1},{1,0},{2,3},{3,2},{4,5},{5,4},{6,7},{7,6},{8,9},{9,8},{10,11... | collective-permute-start | bytes 884744 | tf_op jit(solution)/shard_map/ppermute | solution.py:414
  23.4 12.1 %collective-permute-start.8 = (bf16[144,1024]{1,0:T(8,128)(2,1)S(1)}, bf16[144,1024]{1,0:T(8,128)(2,1)S(1)}, u32[]{:S(2)}, u32[]{:S(2)}) collective-permute-start(bf16[144,1024]{1,0:T(8,128)(2,1)S(1)} %collective-permute-done.7.refs_1_), channel_id=1, source_target_pairs={{0,8},{4,12},{8,0},{12,4},{1,9},{5,13},{9,1},{13,5},{2,10},{6,14},... | collective-permute-start | bytes 884744 | tf_op jit(solution)/shard_map/ppermute | solution.py:411
  35.5 11.2 %collective-permute-start.9 = (bf16[288,1024]{1,0:T(8,128)(2,1)S(1)}, bf16[288,1024]{1,0:T(8,128)(2,1)S(1)}, u32[]{:S(2)}, u32[]{:S(2)}) collective-permute-start(bf16[288,1024]{1,0:T(8,128)(2,1)S(1)} %constant_dynamic-update-slice_fusion.2.refs_0_.refs_1_), channel_id=1, source_target_pairs={{0,4},{4,0},{8,12},{12,8},{1,5},{5,1},{9,13},{13,9},{2,6},{6,2},{1... | collective-permute-start | bytes 1769480 | tf_op jit(solution)/shard_map/ppermute | solution.py:411
  35.6 9.4 %collective-permute-start.11 = (bf16[144,1024]{1,0:T(8,128)(2,1)S(1)}, bf16[144,1024]{1,0:T(8,128)(2,1)S(1)}, u32[]{:S(2)}, u32[]{:S(2)}) collective-permute-start(bf16[144,1024]{1,0:T(8,128)(2,1)S(1)} %collective-permute-done.3.refs_1_), channel_id=1, source_target_pairs={{0,1},{1,0},{2,3},{3,2},{4,5},{5,4},{6,7},{7,6},{8,9},{9,8},{10,11... | collective-permute-start | bytes 884744 | tf_op jit(solution)/shard_map/ppermute | solution.py:414
  42.5 5.7 %collective-permute-start.4 = (bf16[288,1024]{1,0:T(8,128)(2,1)S(1)}, bf16[288,1024]{1,0:T(8,128)(2,1)S(1)}, u32[]{:S(2)}, u32[]{:S(2)}) collective-permute-start(bf16[288,1024]{1,0:T(8,128)(2,1)S(1)} %constant_dynamic-update-slice_fusion.refs_0_.refs_1_), channel_id=1, source_target_pairs={{0,4},{4,0},{8,12},{12,8},{1,5},{5,1},{9,13},{13,9},{2,6},{6,2},{1... | collective-permute-start | bytes 1769480 | tf_op jit(solution)/shard_map/ppermute | solution.py:411
  45.0 4.7 %collective-permute-start.12 = (bf16[288,1024]{1,0:T(8,128)(2,1)S(1)}, bf16[288,1024]{1,0:T(8,128)(2,1)S(1)}, u32[]{:S(2)}, u32[]{:S(2)}) collective-permute-start(bf16[288,1024]{1,0:T(8,128)(2,1)S(1)} %constant_dynamic-update-slice_fusion.4.refs_0_.refs_1_), channel_id=1, source_target_pairs={{0,4},{4,0},{8,12},{12,8},{1,5},{5,1},{9,13},{13,9},{2,6},{6,2},{1... | collective-permute-start | bytes 1769480 | tf_op jit(solution)/shard_map/ppermute | solution.py:411
  64.6 2.7 %collective-permute-start.15 = (bf16[1,256,1024]{2,1,0:T(8,128)(2,1)S(1)}, bf16[1,256,1024]{2,1,0:T(8,128)(2,1)S(1)}, u32[]{:S(2)}, u32[]{:S(2)}) collective-permute-start(bf16[1,256,1024]{2,1,0:T(8,128)(2,1)S(1)} %get-tuple-element.43), channel_id=1, source_target_pairs={{0,4},{4,0},{8,12},{12,8},{1,5},{5,1},{9,13},{13,9},{2,6},{6,2},{1... | collective-permute-start | bytes 1572872 | tf_op jit(solution)/shard_map/ppermute | solution.py:411
  65.6 3.3 %collective-permute-start.13 = (bf16[1,256,1024]{2,1,0:T(8,128)(2,1)S(1)}, bf16[1,256,1024]{2,1,0:T(8,128)(2,1)S(1)}, u32[]{:S(2)}, u32[]{:S(2)}) collective-permute-start(bf16[1,256,1024]{2,1,0:T(8,128)(2,1)S(1)} %get-tuple-element.39), channel_id=1, source_target_pairs={{0,4},{4,0},{8,12},{12,8},{1,5},{5,1},{9,13},{13,9},{2,6},{6,2},{1... | collective-permute-start | bytes 1572872 | tf_op jit(solution)/shard_map/ppermute | solution.py:411
  66.2 3.4 %collective-permute-start.19 = (bf16[1,256,1024]{2,1,0:T(8,128)(2,1)S(1)}, bf16[1,256,1024]{2,1,0:T(8,128)(2,1)S(1)}, u32[]{:S(2)}, u32[]{:S(2)}) collective-permute-start(bf16[1,256,1024]{2,1,0:T(8,128)(2,1)S(1)} %get-tuple-element.47), channel_id=1, source_target_pairs={{0,4},{4,0},{8,12},{12,8},{1,5},{5,1},{9,13},{13,9},{2,6},{6,2},{1... | collective-permute-start | bytes 1572872 | tf_op jit(solution)/shard_map/ppermute | solution.py:411
  67.2 11.3 %collective-permute-start.22 = (bf16[1,256,1024]{2,1,0:T(8,128)(2,1)S(1)}, bf16[1,256,1024]{2,1,0:T(8,128)(2,1)S(1)}, u32[]{:S(2)}, u32[]{:S(2)}) collective-permute-start(bf16[1,256,1024]{2,1,0:T(8,128)(2,1)S(1)} %get-tuple-element.51), channel_id=1, source_target_pairs={{0,4},{4,0},{8,12},{12,8},{1,5},{5,1},{9,13},{13,9},{2,6},{6,2},{1... | collective-permute-start | bytes 1572872 | tf_op jit(solution)/shard_map/ppermute | solution.py:411
  67.4 9.2 %collective-permute-start.16 = (bf16[1,128,1024]{2,1,0:T(8,128)(2,1)S(1)}, bf16[1,128,1024]{2,1,0:T(8,128)(2,1)S(1)}, u32[]{:S(2)}, u32[]{:S(2)}) collective-permute-start(bf16[1,128,1024]{2,1,0:T(8,128)(2,1)S(1)} %add_convert_fusion.6), channel_id=1, source_target_pairs={{0,8},{4,12},{8,0},{12,4},{1,9},{5,13},{9,1},{13,5},{2,10},{6,14},... | collective-permute-start | bytes 786440 | tf_op jit(solution)/shard_map/ppermute | solution.py:411
  69.0 20.7 %collective-permute-start.14 = (bf16[1,128,1024]{2,1,0:T(8,128)(2,1)S(1)}, bf16[1,128,1024]{2,1,0:T(8,128)(2,1)S(1)}, u32[]{:S(2)}, u32[]{:S(2)}) collective-permute-start(bf16[1,128,1024]{2,1,0:T(8,128)(2,1)S(1)} %add_convert_fusion.7), channel_id=1, source_target_pairs={{0,8},{4,12},{8,0},{12,4},{1,9},{5,13},{9,1},{13,5},{2,10},{6,14},... | collective-permute-start | bytes 786440 | tf_op jit(solution)/shard_map/ppermute | solution.py:411
  69.7 18.1 %collective-permute-start.20 = (bf16[1,128,1024]{2,1,0:T(8,128)(2,1)S(1)}, bf16[1,128,1024]{2,1,0:T(8,128)(2,1)S(1)}, u32[]{:S(2)}, u32[]{:S(2)}) collective-permute-start(bf16[1,128,1024]{2,1,0:T(8,128)(2,1)S(1)} %add_convert_fusion.3), channel_id=1, source_target_pairs={{0,8},{4,12},{8,0},{12,4},{1,9},{5,13},{9,1},{13,5},{2,10},{6,14},... | collective-permute-start | bytes 786440 | tf_op jit(solution)/shard_map/ppermute | solution.py:411
  76.7 13.0 %collective-permute-start.17 = (bf16[1,128,1024]{2,1,0:T(8,128)(2,1)S(1)}, bf16[1,128,1024]{2,1,0:T(8,128)(2,1)S(1)}, u32[]{:S(2)}, u32[]{:S(2)}) collective-permute-start(bf16[1,128,1024]{2,1,0:T(8,128)(2,1)S(1)} %add_convert_fusion.5), channel_id=1, source_target_pairs={{0,1},{1,0},{2,3},{3,2},{4,5},{5,4},{6,7},{7,6},{8,9},{9,8},{10,11... | collective-permute-start | bytes 786440 | tf_op jit(solution)/shard_map/ppermute | solution.py:414
  78.6 18.6 %collective-permute-start.23 = (bf16[1,128,1024]{2,1,0:T(8,128)(2,1)S(1)}, bf16[1,128,1024]{2,1,0:T(8,128)(2,1)S(1)}, u32[]{:S(2)}, u32[]{:S(2)}) collective-permute-start(bf16[1,128,1024]{2,1,0:T(8,128)(2,1)S(1)} %add_convert_fusion.1), channel_id=1, source_target_pairs={{0,8},{4,12},{8,0},{12,4},{1,9},{5,13},{9,1},{13,5},{2,10},{6,14},... | collective-permute-start | bytes 786440 | tf_op jit(solution)/shard_map/ppermute | solution.py:411
  87.9 9.3 %collective-permute-start.21 = (bf16[1,128,1024]{2,1,0:T(8,128)(2,1)S(1)}, bf16[1,128,1024]{2,1,0:T(8,128)(2,1)S(1)}, u32[]{:S(2)}, u32[]{:S(2)}) collective-permute-start(bf16[1,128,1024]{2,1,0:T(8,128)(2,1)S(1)} %add_convert_fusion.2), channel_id=1, source_target_pairs={{0,1},{1,0},{2,3},{3,2},{4,5},{5,4},{6,7},{7,6},{8,9},{9,8},{10,11... | collective-permute-start | bytes 786440 | tf_op jit(solution)/shard_map/ppermute | solution.py:414
  89.9 11.4 %collective-permute-start.18 = (bf16[1,128,1024]{2,1,0:T(8,128)(2,1)S(1)}, bf16[1,128,1024]{2,1,0:T(8,128)(2,1)S(1)}, u32[]{:S(2)}, u32[]{:S(2)}) collective-permute-start(bf16[1,128,1024]{2,1,0:T(8,128)(2,1)S(1)} %add_convert_fusion.4), channel_id=1, source_target_pairs={{0,3},{1,2},{2,1},{3,0},{4,7},{5,6},{6,5},{7,4},{8,11},{9,10},{10,... | collective-permute-start | bytes 786440 | tf_op jit(solution)/shard_map/ppermute | solution.py:414
  (5 other events, 37.7 us)

commit v12 on v11

--- a/solution.py
+++ b/solution.py
@@ -19,7 +19,7 @@
 VMEM = 14 * 2**20
 VMEM_EXPERTS = 24 * 2**20
 VMEM_SORT = 52 * 2**20
-PIECES = 4
+PIECES = 2
 DEPTH = 3
 PEAK = 1.1e9
 
@@ -189,7 +189,8 @@
 
 
 def sort_kernel(start, gu_ref, *refs):
-    out_ref, held, made, wide, in_sem, out_sem = refs[-6:]
+    out_ref, token_ref, held, made, wide, in_sem, out_sem = refs[-7:]
+    token_ref[...] = jnp.zeros_like(token_ref)
     step, steps = pl.program_id(0), pl.num_programs(0)
     _, group, _, hidden, width = made.shape
     chunks = width // LANES
@@ -233,14 +234,17 @@
     done = ()
     for j in range(pieces):
         after = behind[j] if pieces > 1 else ()
-        done = (
+        *done, token = (
             call(
                 functools.partial(sort_kernel, j * local // pieces),
-                4,
+                8,
                 (local // pieces // group,),
                 [IN_HBM] + [IN_HBM] * len(done) + [ANYWHERE] * len(after),
-                IN_HBM,
-                jax.ShapeDtypeStruct((local, 2, hidden, width), jnp.bfloat16),
+                [IN_HBM, pl.BlockSpec((8, LANES), lambda e: (0, 0))],
+                [
+                    jax.ShapeDtypeStruct((local, 2, hidden, width), jnp.bfloat16),
+                    jax.ShapeDtypeStruct((8, LANES), jnp.float32),
+                ],
                 [
                     pltpu.VMEM((2, group) + gu.shape[1:], jnp.bfloat16),
                     pltpu.VMEM((2, group, 2, hidden, width), jnp.bfloat16),
@@ -251,9 +255,29 @@
                 "sort",
                 VMEM_SORT,
                 {1: 0} if done else {},
-            )(gu, *done, *after),
+            )(gu, *done, *after)
         )
-    return done[0]
+    return done[0], token
+
+
+def stack_kernel(a_ref, b_ref, *refs):
+    rows = a_ref.shape[0]
+    refs[-1][:rows, :] = a_ref[...]
+    refs[-1][rows:, :] = b_ref[...]
+
+
+def stack(a, b, before):
+    rows, width = a.shape
+    return call(
+        stack_kernel,
+        1,
+        (1,),
+        [whole(a), whole(b)] + [ANYWHERE] * len(before),
+        pl.BlockSpec((2 * rows, width), lambda i: (0, 0)),
+        jax.ShapeDtypeStruct((2 * rows, width), a.dtype),
+        [],
+        "stack",
+    )(a, b, *before)
 
 
 def expert_kernel(n, *refs):
@@ -437,17 +461,18 @@
     kv = [(a, k * tok_rows) for a in (keys, flip(keys, 1)) for k in range(2)]
     if near:
         blocks = 1
-        pairs = [jnp.concatenate([a, b], axis=0) for a, b in zip(near_parts, crossed)]
+        gu, token = sort_rows(gate_up, [(), (crossed[2],)])
+        pairs = [
+            stack(a, b, (token,)) if i == 1 else jnp.concatenate([a, b], axis=0)
+            for i, (a, b) in enumerate(zip(near_parts, crossed))
+        ]
         flipped = [flip(a, 1) for a in pairs]
         spread = [[(a, 0), (a, 1), (b, 0), (b, 1)] for a, b in zip(pairs, flipped)]
     else:
+        gu, _ = sort_rows(gate_up, [(), ()])
         blocks = near_parts[0].shape[0] // (BLOCK + EXTRA)
         spread = [[(near_parts[0], 0), (crossed[0], 0)]]
         spread[0] = spread[0] + [(flip(a, 1), 0) for a, _ in spread[0]]
-    behind = [()] * PIECES
-    if near:
-        behind = [(), (arrived[1],), (arrived[2],), (crossed[2],)]
-
     lengths = doc_lengths[0]
     ends = jnp.cumsum(lengths)
     row_pos = order[:, None] * tok_rows + jnp.arange(tok_rows, dtype=jnp.int32)[None, :]
@@ -463,7 +488,6 @@
     base = (exp * local).reshape(1).astype(jnp.int32)
     rw = jnp.roll(router_weight.T, -exp * local, axis=0)
     balance = None
-    gu = sort_rows(gate_up, behind)
     sent = []
     for i in range(len(shifts)):
         row = (seg.reshape(-1, 1, BLOCK), scale) if near and i == 0 else None
@@ -473,7 +497,7 @@
             balance = out[3]
     made = experts([a[0] for a in sent], [a[1] for a in sent], gu, w_down)
     back = []
-    for i in reversed(range(len(shifts))):
+    for i in [3, 1, 2, 0][-len(shifts) :]:
         keep, give = combine([sent[i][2]], [made[i]], n_ctx)
         got = flip(give, 1)
         far = added(keep[:, tok_rows:], got[:, tok_rows:])

time: 103 us -> 96.1 us (0.933)
  Pallas kernels: 47.3 us -> 44.3 us
  starting transfers between devices: 24.4 us -> 22.8 us
  other arithmetic: 5.22 us -> 3.91 us
  waiting for transfers between devices: 22.1 us -> 21 us
    ppermute x7, waiting for transfers between devices: 6.39 us -> 2.18 us  [shift(): return lax.ppermute(a, 'exp', [(i, i ^ d) for i in range(n_exp)])]
    pallas_call x4 -> x3, Pallas kernels: 20.4 us -> 17.4 us  [the longest x2 17.3 us: sort_rows(): call(functools.partial(sort_kernel, j * local // pieces), 8, (local // pi...]
    ppermute x17, waiting for transfers between devices: 15.7 us -> 18.8 us  [flip(): return lax.ppermute(a, 'ctx', [(i, i ^ bit) for i in range(n_ctx)])]
    ppermute x7, starting transfers between devices: 12.7 us -> 10.7 us  [shift(): return lax.ppermute(a, 'exp', [(i, i ^ d) for i in range(n_exp)])]
  transfers between devices with their start and end apart: 24 -> 24, of which waited for: 7 -> 5; matrix products, arithmetic and copies ran while one was open for 5% -> 4% of each run, Pallas kernels for 46% -> 47%
where the time goes in v12:
time: 96.1 us; the launch traced here: 95 us
  Pallas kernels  44.3 us (46%)
  starting transfers between devices  22.8 us (24%)
  waiting for transfers between devices  21 us (22%)
  other arithmetic  3.91 us (4%)
  local copies, waits for them, and re-layouts  2.17 us (2%)
    ppermute x17, waiting for transfers between devices, flip(): return lax.ppermute(a, 'ctx', [(i, i ^ bit) for i in range(n_ctx)])  18.8 us
    pallas_call x2, Pallas kernels, sort_rows(): call(functools.partial(sort_kernel, j * local // pieces), 8, (local // pi...  17.3 us
    pallas_call x1, Pallas kernels, experts(): call(functools.partial(expert_kernel, n), 6, (local // group, slots // si...  12.8 us
    ppermute x17, starting transfers between devices, flip(): return lax.ppermute(a, 'ctx', [(i, i ^ bit) for i in range(n_ctx)])  12.1 us
    ppermute x7, starting transfers between devices, shift(): return lax.ppermute(a, 'exp', [(i, i ^ d) for i in range(n_exp)])  10.7 us
    pallas_call x1, Pallas kernels, attend(): call(functools.partial(attend_kernel, [at for _, at in parts], kdim), 6,...  6.17 us
    pallas_call x4, Pallas kernels, dispatch(): call(functools.partial(dispatch_kernel, n_parts, n_parts if row is not No...  6.01 us
    ppermute x7, waiting for transfers between devices, shift(): return lax.ppermute(a, 'exp', [(i, i ^ d) for i in range(n_exp)])  2.18 us
  transfers between devices with their start and end apart: 24, of which 5 were waited for; matrix products, arithmetic and copies ran while one was open for 4% of the time, Pallas kernels for 47%

profile of v12, /device:TPU:0, one launch (start us, length us, event | category | flops | bytes accessed | tf_op | source)
XLA Modules:
  0.0 95.0 jit_solution(2233371673940589458)
XLA Ops:
  1.3 1.0 %pad_maximum_fusion.2 = bf16[144,1024]{1,0:T(8,128)(2,1)S(1)} fusion(bf16[16,1024]{1,0:T(8,128)(2,1)S(1)} %pad.4, bf16[128,1024]{1,0:T(8,128)(2,1)} %bitcast.42), kind=kLoop, calls=%fused_computation.10 | loop fusion | flops 589824 | bytes 589824 | tf_op jit(solution)/shard_map/concatenate | solution.py:452
  2.3 5.1 %collective-permute-start.4 = (bf16[144,1024]{1,0:T(8,128)(2,1)S(1)}, bf16[144,1024]{1,0:T(8,128)(2,1)S(1)}, u32[]{:S(2)}, u32[]{:S(2)}) collective-permute-start(bf16[144,1024]{1,0:T(8,128)(2,1)S(1)} %pad_maximum_fusion.2), channel_id=1, source_target_pairs={{0,3},{1,2},{2,1},{3,0},{4,7},{5,6},{6,5},{7,4},{8,11},{9,10},{10,... | collective-permute-start | bytes 884744 | tf_op jit(solution)/shard_map/ppermute | solution.py:438
  7.4 1.5 %collective-permute-start.7 = (bf16[144,1024]{1,0:T(8,128)(2,1)S(1)}, bf16[144,1024]{1,0:T(8,128)(2,1)S(1)}, u32[]{:S(2)}, u32[]{:S(2)}) collective-permute-start(bf16[144,1024]{1,0:T(8,128)(2,1)S(1)} %pad_maximum_fusion.2), channel_id=1, source_target_pairs={{0,8},{4,12},{8,0},{12,4},{1,9},{5,13},{9,1},{13,5},{2,10},{6,14},... | collective-permute-start | bytes 884744 | tf_op jit(solution)/shard_map/ppermute | solution.py:435
  8.9 1.1 %copy.20 = bf16[1,128,576]{2,1,0:T(8,128)(2,1)S(1)} copy(bf16[1,128,576]{1,2,0:T(8,128)(2,1)} %param.9) | data formatting | bytes 294912 | tf_op args[1]
  10.6 9.0 %sort.2 = (bf16[16,2,176,1024]{3,2,1,0:T(8,128)(2,1)}, f32[8,128]{1,0:T(8,128)}) custom-call(bf16[16,2816,128]{2,1,0:T(8,128)(2,1)} %bitcast.53), custom_call_target="tpu_custom_call" | custom-call | flops 8800000000 | tf_op jit(solution)/shard_map/sort/pallas_call | solution.py:238
  20.4 1.6 %collective-permute-start.5 = (bf16[144,1024]{1,0:T(8,128)(2,1)S(1)}, bf16[144,1024]{1,0:T(8,128)(2,1)S(1)}, u32[]{:S(2)}, u32[]{:S(2)}) collective-permute-start(bf16[144,1024]{1,0:T(8,128)(2,1)S(1)} %collective-permute-done.4), channel_id=1, source_target_pairs={{0,8},{4,12},{8,0},{12,4},{1,9},{5,13},{9,1},{13,5},{2,10},{6,14},... | collective-permute-start | bytes 884744 | tf_op jit(solution)/shard_map/ppermute | solution.py:435
  22.7 2.0 %collective-permute-start.10 = (bf16[144,1024]{1,0:T(8,128)(2,1)S(1)}, bf16[144,1024]{1,0:T(8,128)(2,1)S(1)}, u32[]{:S(2)}, u32[]{:S(2)}) collective-permute-start(bf16[144,1024]{1,0:T(8,128)(2,1)S(1)} %collective-permute-done.4), channel_id=1, source_target_pairs={{0,1},{1,0},{2,3},{3,2},{4,5},{5,4},{6,7},{7,6},{8,9},{9,8},{10,11... | collective-permute-start | bytes 884744 | tf_op jit(solution)/shard_map/ppermute | solution.py:438
  25.3 4.3 %collective-permute-done.5.refs_1_ = bf16[144,1024]{1,0:T(8,128)(2,1)S(1)} collective-permute-done((bf16[144,1024]{1,0:T(8,128)(2,1)S(1)}, bf16[144,1024]{1,0:T(8,128)(2,1)S(1)}, u32[]{:S(2)}, u32[]{:S(2)}) %collective-permute-start.5) | collective-permute-done | bytes 294944 | tf_op jit(solution)/shard_map/ppermute | solution.py:435
  29.6 2.9 %collective-permute-start.11 = (bf16[144,1024]{1,0:T(8,128)(2,1)S(1)}, bf16[144,1024]{1,0:T(8,128)(2,1)S(1)}, u32[]{:S(2)}, u32[]{:S(2)}) collective-permute-start(bf16[144,1024]{1,0:T(8,128)(2,1)S(1)} %collective-permute-done.5.refs_1_), channel_id=1, source_target_pairs={{0,1},{1,0},{2,3},{3,2},{4,5},{5,4},{6,7},{7,6},{8,9},{9,8},{10,11... | collective-permute-start | bytes 884744 | tf_op jit(solution)/shard_map/ppermute | solution.py:438
  32.5 8.3 %sort.3 = (bf16[16,2,176,1024]{3,2,1,0:T(8,128)(2,1)}, f32[8,128]{1,0:T(8,128)S(1)}) custom-call(bf16[16,2816,128]{2,1,0:T(8,128)(2,1)} %bitcast.54, bf16[16,2,176,1024]{3,2,1,0:T(8,128)(2,1)} %get-tuple-element.31.refs_0_, bf16[144,1024]{1,0:T(8,128)(2,1)S(1)} %collective-permute-done.5.refs_1_), custom_call_target="tpu_custom_call", output_to_operand_aliasing={{0}: (1, {})} | custom-call | flops 8800000000 | tf_op jit(solution)/shard_map/sort/pallas_call | solution.py:238
  41.8 1.6 %dispatch.5 = (bf16[16,64,1024]{2,1,0:T(8,128)(2,1)S(1)}, f32[16,64,128]{2,1,0:T(8,128)S(1)}, bf16[4,256,128]{2,1,0:T(8,128)(2,1)S(1)}, f32[8,128]{1,0:T(8,128)S(1)}) custom-call(s32[1]{0:T(128)} %bitcast.13.base_ref, bf16[64,1024]{1,0:T(8,128)(2,1)S(1)} %fusion.rw_ref, bf16[288,1024]{1,0:T(8,128)(2,1)S(1)} %pad_maximum_fusion.refs_0_.refs_1_, ...), custom_call_target="tpu_custom_call" | custom-call | flops 3300000000 | tf_op jit(solution)/shard_map/dispatch/pallas_call | solution.py:144
  43.3 1.5 %dispatch.4 = (bf16[16,64,1024]{2,1,0:T(8,128)(2,1)S(1)}, f32[16,64,128]{2,1,0:T(8,128)S(1)}, bf16[4,256,128]{2,1,0:T(8,128)(2,1)S(1)}) custom-call(s32[1]{0:T(128)} %bitcast.13.base_ref, bf16[64,1024]{1,0:T(8,128)(2,1)S(1)} %fusion.rw_ref, bf16[288,1024]{1,0:T(8,128)(2,1)S(1)} %stack.21.refs_0_.refs_1_, bf16[288,1024]{1,0:T(8,128)(2,1)S(1)} %stack.21.refs_0_.refs_1_, ...), custom_call_target="tpu_custom_call" | custom-call | flops 3300000000 | tf_op jit(solution)/shard_map/dispatch/pallas_call | solution.py:144
  44.8 1.5 %dispatch.6 = (bf16[16,64,1024]{2,1,0:T(8,128)(2,1)S(1)}, f32[16,64,128]{2,1,0:T(8,128)S(1)}, bf16[4,256,128]{2,1,0:T(8,128)(2,1)S(1)}) custom-call(s32[1]{0:T(128)} %bitcast.13.base_ref, bf16[64,1024]{1,0:T(8,128)(2,1)S(1)} %fusion.rw_ref, bf16[288,1024]{1,0:T(8,128)(2,1)S(1)} %constant_dynamic-update-slice_fusion.refs_0_.refs_1_, ...), custom_call_target="tpu_custom_call" | custom-call | flops 3300000000 | tf_op jit(solution)/shard_map/dispatch/pallas_call | solution.py:144
  46.4 1.5 %dispatch.7 = (bf16[16,64,1024]{2,1,0:T(8,128)(2,1)S(1)}, f32[16,64,128]{2,1,0:T(8,128)S(1)}, bf16[4,256,128]{2,1,0:T(8,128)(2,1)S(1)}) custom-call(s32[1]{0:T(128)} %bitcast.13.base_ref, bf16[64,1024]{1,0:T(8,128)(2,1)S(1)} %fusion.rw_ref, bf16[288,1024]{1,0:T(8,128)(2,1)S(1)} %constant_dynamic-update-slice_fusion.2.refs_0_.refs_1_, ...), custom_call_target="tpu_custom_call" | custom-call | flops 3300000000 | tf_op jit(solution)/shard_map/dispatch/pallas_call | solution.py:144
  47.9 12.8 %experts.1 = (bf16[16,64,1024]{2,1,0:T(8,128)(2,1)S(1)}, bf16[16,64,1024]{2,1,0:T(8,128)(2,1)S(1)}, bf16[16,64,1024]{2,1,0:T(8,128)(2,1)S(1)}, bf16[16,64,1024]{2,1,0:T(8,128)(2,1)S(1)}) custom-call(bf16[16,64,1024]{2,1,0:T(8,128)(2,1)S(1)} %get-tuple-element.34.refs_0_, bf16[16,64,1024]{2,1,0:T(8,128)(2,1)S(1)} %get-tuple-element.35.refs_1_, ...), custom_call_target="tpu_custom_call" | custom-call | flops 6600000000 | tf_op jit(solution)/shard_map/experts/pallas_call | solution.py:319
  64.0 1.6 %collective-permute-start.19 = (bf16[1,128,1024]{2,1,0:T(8,128)(2,1)S(1)}, bf16[1,128,1024]{2,1,0:T(8,128)(2,1)S(1)}, u32[]{:S(2)}, u32[]{:S(2)}) collective-permute-start(bf16[1,128,1024]{2,1,0:T(8,128)(2,1)S(1)} %add_convert_fusion.4), channel_id=1, source_target_pairs={{0,8},{4,12},{8,0},{12,4},{1,9},{5,13},{9,1},{13,5},{2,10},{6,14},... | collective-permute-start | bytes 786440 | tf_op jit(solution)/shard_map/ppermute | solution.py:435
  66.3 1.6 %collective-permute-start.17 = (bf16[1,128,1024]{2,1,0:T(8,128)(2,1)S(1)}, bf16[1,128,1024]{2,1,0:T(8,128)(2,1)S(1)}, u32[]{:S(2)}, u32[]{:S(2)}) collective-permute-start(bf16[1,128,1024]{2,1,0:T(8,128)(2,1)S(1)} %add_convert_fusion.5), channel_id=1, source_target_pairs={{0,8},{4,12},{8,0},{12,4},{1,9},{5,13},{9,1},{13,5},{2,10},{6,14},... | collective-permute-start | bytes 786440 | tf_op jit(solution)/shard_map/ppermute | solution.py:435
  67.9 5.3 %collective-permute-done.19 = bf16[1,128,1024]{2,1,0:T(8,128)(2,1)S(1)} collective-permute-done((bf16[1,128,1024]{2,1,0:T(8,128)(2,1)S(1)}, bf16[1,128,1024]{2,1,0:T(8,128)(2,1)S(1)}, u32[]{:S(2)}, u32[]{:S(2)}) %collective-permute-start.19) | collective-permute-done | bytes 262176 | tf_op jit(solution)/shard_map/ppermute | solution.py:435
  73.5 1.6 %collective-permute-start.23 = (bf16[1,128,1024]{2,1,0:T(8,128)(2,1)S(1)}, bf16[1,128,1024]{2,1,0:T(8,128)(2,1)S(1)}, u32[]{:S(2)}, u32[]{:S(2)}) collective-permute-start(bf16[1,128,1024]{2,1,0:T(8,128)(2,1)S(1)} %add_convert_fusion.1), channel_id=1, source_target_pairs={{0,8},{4,12},{8,0},{12,4},{1,9},{5,13},{9,1},{13,5},{2,10},{6,14},... | collective-permute-start | bytes 786440 | tf_op jit(solution)/shard_map/ppermute | solution.py:435
  75.1 3.8 %collective-permute-done.14 = bf16[1,128,1024]{2,1,0:T(8,128)(2,1)S(1)} collective-permute-done((bf16[1,128,1024]{2,1,0:T(8,128)(2,1)S(1)}, bf16[1,128,1024]{2,1,0:T(8,128)(2,1)S(1)}, u32[]{:S(2)}, u32[]{:S(2)}) %collective-permute-start.14) | collective-permute-done | bytes 262176 | tf_op jit(solution)/shard_map/ppermute | solution.py:435
  79.0 5.4 %collective-permute-done.17 = bf16[1,128,1024]{2,1,0:T(8,128)(2,1)S(1)} collective-permute-done((bf16[1,128,1024]{2,1,0:T(8,128)(2,1)S(1)}, bf16[1,128,1024]{2,1,0:T(8,128)(2,1)S(1)}, u32[]{:S(2)}, u32[]{:S(2)}) %collective-permute-start.17) | collective-permute-done | bytes 262176 | tf_op jit(solution)/shard_map/ppermute | solution.py:435
  85.1 6.2 %attention.1 = bf16[128,4096]{1,0:T(8,128)(2,1)} custom-call(s32[128,1]{1,0:T(8,128)S(1)} %copy.21.first_ref, s32[128,1]{1,0:T(8,128)S(1)} %copy.22.last_ref, s32[1,512]{1,0:T(1,128)S(1)} %bitcast.39, bf16[128,4608]{1,0:T(8,128)(2,1)S(1)} %bitcast.41, bf16[256,576]{1,0:T(8,128)(2,1)S(1)} %pad_maximum_fusion.1.refs_0_.refs_1_, ...), custom_call_target="tpu_custom_call" | custom-call | flops 6600000000 | tf_op jit(solution)/shard_map/attention/pallas_call | solution.py:404
  91.9 2.2 %collective-permute-done.21 = bf16[1,128,1024]{2,1,0:T(8,128)(2,1)S(1)} collective-permute-done((bf16[1,128,1024]{2,1,0:T(8,128)(2,1)S(1)}, bf16[1,128,1024]{2,1,0:T(8,128)(2,1)S(1)}, u32[]{:S(2)}, u32[]{:S(2)}) %collective-permute-start.21) | collective-permute-done | bytes 262176 | tf_op jit(solution)/shard_map/ppermute | solution.py:438
  94.1 0.9 add_convert_fusion
  (82 shorter events, 10.2 us)
Async XLA Ops:
  2.3 18.1 %collective-permute-start.4 = (bf16[144,1024]{1,0:T(8,128)(2,1)S(1)}, bf16[144,1024]{1,0:T(8,128)(2,1)S(1)}, u32[]{:S(2)}, u32[]{:S(2)}) collective-permute-start(bf16[144,1024]{1,0:T(8,128)(2,1)S(1)} %pad_maximum_fusion.2), channel_id=1, source_target_pairs={{0,3},{1,2},{2,1},{3,0},{4,7},{5,6},{6,5},{7,4},{8,11},{9,10},{10,... | collective-permute-start | bytes 884744 | tf_op jit(solution)/shard_map/ppermute | solution.py:438
  7.4 17.3 %collective-permute-start.2 = (bf16[144,1024]{1,0:T(8,128)(2,1)S(1)}, bf16[144,1024]{1,0:T(8,128)(2,1)S(1)}, u32[]{:S(2)}, u32[]{:S(2)}) collective-permute-start(bf16[144,1024]{1,0:T(8,128)(2,1)S(1)} %pad_maximum_fusion.2), channel_id=1, source_target_pairs={{0,1},{1,0},{2,3},{3,2},{4,5},{5,4},{6,7},{7,6},{8,9},{9,8},{10,11... | collective-permute-start | bytes 884744 | tf_op jit(solution)/shard_map/ppermute | solution.py:438
  7.4 14.7 %collective-permute-start.7 = (bf16[144,1024]{1,0:T(8,128)(2,1)S(1)}, bf16[144,1024]{1,0:T(8,128)(2,1)S(1)}, u32[]{:S(2)}, u32[]{:S(2)}) collective-permute-start(bf16[144,1024]{1,0:T(8,128)(2,1)S(1)} %pad_maximum_fusion.2), channel_id=1, source_target_pairs={{0,8},{4,12},{8,0},{12,4},{1,9},{5,13},{9,1},{13,5},{2,10},{6,14},... | collective-permute-start | bytes 884744 | tf_op jit(solution)/shard_map/ppermute | solution.py:435
  10.0 12.0 %collective-permute-start = (bf16[128,576]{1,0:T(8,128)(2,1)S(1)}, bf16[128,576]{1,0:T(8,128)(2,1)S(1)}, u32[]{:S(2)}, u32[]{:S(2)}) collective-permute-start(bf16[128,576]{1,0:T(8,128)(2,1)S(1)} %bitcast.44), channel_id=1, source_target_pairs={{0,8},{4,12},{8,0},{12,4},{1,9},{5,13},{9,1},{13,5},{2,10},{6,14},... | collective-permute-start | bytes 442376 | tf_op jit(solution)/shard_map/ppermute | solution.py:435
  20.4 9.2 %collective-permute-start.5 = (bf16[144,1024]{1,0:T(8,128)(2,1)S(1)}, bf16[144,1024]{1,0:T(8,128)(2,1)S(1)}, u32[]{:S(2)}, u32[]{:S(2)}) collective-permute-start(bf16[144,1024]{1,0:T(8,128)(2,1)S(1)} %collective-permute-done.4), channel_id=1, source_target_pairs={{0,8},{4,12},{8,0},{12,4},{1,9},{5,13},{9,1},{13,5},{2,10},{6,14},... | collective-permute-start | bytes 884744 | tf_op jit(solution)/shard_map/ppermute | solution.py:435
  22.0 63.1 %collective-permute-start.1 = (bf16[256,576]{1,0:T(8,128)(2,1)S(1)}, bf16[256,576]{1,0:T(8,128)(2,1)S(1)}, u32[]{:S(2)}, u32[]{:S(2)}) collective-permute-start(bf16[256,576]{1,0:T(8,128)(2,1)S(1)} %pad_maximum_fusion.1.refs_0_.refs_1_), channel_id=1, source_target_pairs={{0,4},{4,0},{8,12},{12,8},{1,5},{5,1},{9,13},{13,9},{2,6},{6,2},{1... | collective-permute-start | bytes 884744 | tf_op jit(solution)/shard_map/ppermute | solution.py:435
  22.2 19.5 %collective-permute-start.8 = (bf16[288,1024]{1,0:T(8,128)(2,1)S(1)}, bf16[288,1024]{1,0:T(8,128)(2,1)S(1)}, u32[]{:S(2)}, u32[]{:S(2)}) collective-permute-start(bf16[288,1024]{1,0:T(8,128)(2,1)S(1)} %pad_maximum_fusion.refs_0_.refs_1_), channel_id=1, source_target_pairs={{0,4},{4,0},{8,12},{12,8},{1,5},{5,1},{9,13},{13,9},{2,6},{6,2},{1... | collective-permute-start | bytes 1769480 | tf_op jit(solution)/shard_map/ppermute | solution.py:435
  22.7 18.3 %collective-permute-start.10 = (bf16[144,1024]{1,0:T(8,128)(2,1)S(1)}, bf16[144,1024]{1,0:T(8,128)(2,1)S(1)}, u32[]{:S(2)}, u32[]{:S(2)}) collective-permute-start(bf16[144,1024]{1,0:T(8,128)(2,1)S(1)} %collective-permute-done.4), channel_id=1, source_target_pairs={{0,1},{1,0},{2,3},{3,2},{4,5},{5,4},{6,7},{7,6},{8,9},{9,8},{10,11... | collective-permute-start | bytes 884744 | tf_op jit(solution)/shard_map/ppermute | solution.py:438
  24.7 16.1 %collective-permute-start.3 = (bf16[144,1024]{1,0:T(8,128)(2,1)S(1)}, bf16[144,1024]{1,0:T(8,128)(2,1)S(1)}, u32[]{:S(2)}, u32[]{:S(2)}) collective-permute-start(bf16[144,1024]{1,0:T(8,128)(2,1)S(1)} %collective-permute-done.2.a_ref), channel_id=1, source_target_pairs={{0,8},{4,12},{8,0},{12,4},{1,9},{5,13},{9,1},{13,5},{2,10},{6,14},... | collective-permute-start | bytes 884744 | tf_op jit(solution)/shard_map/ppermute | solution.py:435
  29.6 12.0 %collective-permute-start.11 = (bf16[144,1024]{1,0:T(8,128)(2,1)S(1)}, bf16[144,1024]{1,0:T(8,128)(2,1)S(1)}, u32[]{:S(2)}, u32[]{:S(2)}) collective-permute-start(bf16[144,1024]{1,0:T(8,128)(2,1)S(1)} %collective-permute-done.5.refs_1_), channel_id=1, source_target_pairs={{0,1},{1,0},{2,3},{3,2},{4,5},{5,4},{6,7},{7,6},{8,9},{9,8},{10,11... | collective-permute-start | bytes 884744 | tf_op jit(solution)/shard_map/ppermute | solution.py:438
  40.9 2.5 %collective-permute-start.6 = (bf16[288,1024]{1,0:T(8,128)(2,1)S(1)}, bf16[288,1024]{1,0:T(8,128)(2,1)S(1)}, u32[]{:S(2)}, u32[]{:S(2)}) collective-permute-start(bf16[288,1024]{1,0:T(8,128)(2,1)S(1)} %stack.21.refs_0_.refs_1_), channel_id=1, source_target_pairs={{0,4},{4,0},{8,12},{12,8},{1,5},{5,1},{9,13},{13,9},{2,6},{6,2},{1... | collective-permute-start | bytes 1769480 | tf_op jit(solution)/shard_map/ppermute | solution.py:435
  41.0 3.8 %collective-permute-start.9 = (bf16[288,1024]{1,0:T(8,128)(2,1)S(1)}, bf16[288,1024]{1,0:T(8,128)(2,1)S(1)}, u32[]{:S(2)}, u32[]{:S(2)}) collective-permute-start(bf16[288,1024]{1,0:T(8,128)(2,1)S(1)} %constant_dynamic-update-slice_fusion.refs_0_.refs_1_), channel_id=1, source_target_pairs={{0,4},{4,0},{8,12},{12,8},{1,5},{5,1},{9,13},{13,9},{2,6},{6,2},{1... | collective-permute-start | bytes 1769480 | tf_op jit(solution)/shard_map/ppermute | solution.py:435
  41.6 4.7 %collective-permute-start.12 = (bf16[288,1024]{1,0:T(8,128)(2,1)S(1)}, bf16[288,1024]{1,0:T(8,128)(2,1)S(1)}, u32[]{:S(2)}, u32[]{:S(2)}) collective-permute-start(bf16[288,1024]{1,0:T(8,128)(2,1)S(1)} %constant_dynamic-update-slice_fusion.2.refs_0_.refs_1_), channel_id=1, source_target_pairs={{0,4},{4,0},{8,12},{12,8},{1,5},{5,1},{9,13},{13,9},{2,6},{6,2},{1... | collective-permute-start | bytes 1769480 | tf_op jit(solution)/shard_map/ppermute | solution.py:435
  61.2 2.7 %collective-permute-start.18 = (bf16[1,256,1024]{2,1,0:T(8,128)(2,1)S(1)}, bf16[1,256,1024]{2,1,0:T(8,128)(2,1)S(1)}, u32[]{:S(2)}, u32[]{:S(2)}) collective-permute-start(bf16[1,256,1024]{2,1,0:T(8,128)(2,1)S(1)} %get-tuple-element.53), channel_id=1, source_target_pairs={{0,4},{4,0},{8,12},{12,8},{1,5},{5,1},{9,13},{13,9},{2,6},{6,2},{1... | collective-permute-start | bytes 1572872 | tf_op jit(solution)/shard_map/ppermute | solution.py:435
  62.2 3.4 %collective-permute-start.13 = (bf16[1,256,1024]{2,1,0:T(8,128)(2,1)S(1)}, bf16[1,256,1024]{2,1,0:T(8,128)(2,1)S(1)}, u32[]{:S(2)}, u32[]{:S(2)}) collective-permute-start(bf16[1,256,1024]{2,1,0:T(8,128)(2,1)S(1)} %get-tuple-element.45), channel_id=1, source_target_pairs={{0,4},{4,0},{8,12},{12,8},{1,5},{5,1},{9,13},{13,9},{2,6},{6,2},{1... | collective-permute-start | bytes 1572872 | tf_op jit(solution)/shard_map/ppermute | solution.py:435
  62.8 3.4 %collective-permute-start.16 = (bf16[1,256,1024]{2,1,0:T(8,128)(2,1)S(1)}, bf16[1,256,1024]{2,1,0:T(8,128)(2,1)S(1)}, u32[]{:S(2)}, u32[]{:S(2)}) collective-permute-start(bf16[1,256,1024]{2,1,0:T(8,128)(2,1)S(1)} %get-tuple-element.49), channel_id=1, source_target_pairs={{0,4},{4,0},{8,12},{12,8},{1,5},{5,1},{9,13},{13,9},{2,6},{6,2},{1... | collective-permute-start | bytes 1572872 | tf_op jit(solution)/shard_map/ppermute | solution.py:435
  63.9 9.6 %collective-permute-start.22 = (bf16[1,256,1024]{2,1,0:T(8,128)(2,1)S(1)}, bf16[1,256,1024]{2,1,0:T(8,128)(2,1)S(1)}, u32[]{:S(2)}, u32[]{:S(2)}) collective-permute-start(bf16[1,256,1024]{2,1,0:T(8,128)(2,1)S(1)} %get-tuple-element.57), channel_id=1, source_target_pairs={{0,4},{4,0},{8,12},{12,8},{1,5},{5,1},{9,13},{13,9},{2,6},{6,2},{1... | collective-permute-start | bytes 1572872 | tf_op jit(solution)/shard_map/ppermute | solution.py:435
  64.0 9.2 %collective-permute-start.19 = (bf16[1,128,1024]{2,1,0:T(8,128)(2,1)S(1)}, bf16[1,128,1024]{2,1,0:T(8,128)(2,1)S(1)}, u32[]{:S(2)}, u32[]{:S(2)}) collective-permute-start(bf16[1,128,1024]{2,1,0:T(8,128)(2,1)S(1)} %add_convert_fusion.4), channel_id=1, source_target_pairs={{0,8},{4,12},{8,0},{12,4},{1,9},{5,13},{9,1},{13,5},{2,10},{6,14},... | collective-permute-start | bytes 786440 | tf_op jit(solution)/shard_map/ppermute | solution.py:435
  65.7 13.1 %collective-permute-start.14 = (bf16[1,128,1024]{2,1,0:T(8,128)(2,1)S(1)}, bf16[1,128,1024]{2,1,0:T(8,128)(2,1)S(1)}, u32[]{:S(2)}, u32[]{:S(2)}) collective-permute-start(bf16[1,128,1024]{2,1,0:T(8,128)(2,1)S(1)} %add_convert_fusion.7), channel_id=1, source_target_pairs={{0,8},{4,12},{8,0},{12,4},{1,9},{5,13},{9,1},{13,5},{2,10},{6,14},... | collective-permute-start | bytes 786440 | tf_op jit(solution)/shard_map/ppermute | solution.py:435
  66.3 18.1 %collective-permute-start.17 = (bf16[1,128,1024]{2,1,0:T(8,128)(2,1)S(1)}, bf16[1,128,1024]{2,1,0:T(8,128)(2,1)S(1)}, u32[]{:S(2)}, u32[]{:S(2)}) collective-permute-start(bf16[1,128,1024]{2,1,0:T(8,128)(2,1)S(1)} %add_convert_fusion.5), channel_id=1, source_target_pairs={{0,8},{4,12},{8,0},{12,4},{1,9},{5,13},{9,1},{13,5},{2,10},{6,14},... | collective-permute-start | bytes 786440 | tf_op jit(solution)/shard_map/ppermute | solution.py:435
  73.3 11.1 %collective-permute-start.20 = (bf16[1,128,1024]{2,1,0:T(8,128)(2,1)S(1)}, bf16[1,128,1024]{2,1,0:T(8,128)(2,1)S(1)}, u32[]{:S(2)}, u32[]{:S(2)}) collective-permute-start(bf16[1,128,1024]{2,1,0:T(8,128)(2,1)S(1)} %add_convert_fusion.3), channel_id=1, source_target_pairs={{0,1},{1,0},{2,3},{3,2},{4,5},{5,4},{6,7},{7,6},{8,9},{9,8},{10,11... | collective-permute-start | bytes 786440 | tf_op jit(solution)/shard_map/ppermute | solution.py:438
  73.5 18.4 %collective-permute-start.23 = (bf16[1,128,1024]{2,1,0:T(8,128)(2,1)S(1)}, bf16[1,128,1024]{2,1,0:T(8,128)(2,1)S(1)}, u32[]{:S(2)}, u32[]{:S(2)}) collective-permute-start(bf16[1,128,1024]{2,1,0:T(8,128)(2,1)S(1)} %add_convert_fusion.1), channel_id=1, source_target_pairs={{0,8},{4,12},{8,0},{12,4},{1,9},{5,13},{9,1},{13,5},{2,10},{6,14},... | collective-permute-start | bytes 786440 | tf_op jit(solution)/shard_map/ppermute | solution.py:435
  78.9 13.0 %collective-permute-start.15 = (bf16[1,128,1024]{2,1,0:T(8,128)(2,1)S(1)}, bf16[1,128,1024]{2,1,0:T(8,128)(2,1)S(1)}, u32[]{:S(2)}, u32[]{:S(2)}) collective-permute-start(bf16[1,128,1024]{2,1,0:T(8,128)(2,1)S(1)} %add_convert_fusion.6), channel_id=1, source_target_pairs={{0,1},{1,0},{2,3},{3,2},{4,5},{5,4},{6,7},{7,6},{8,9},{9,8},{10,11... | collective-permute-start | bytes 786440 | tf_op jit(solution)/shard_map/ppermute | solution.py:438
  84.6 9.5 %collective-permute-start.21 = (bf16[1,128,1024]{2,1,0:T(8,128)(2,1)S(1)}, bf16[1,128,1024]{2,1,0:T(8,128)(2,1)S(1)}, u32[]{:S(2)}, u32[]{:S(2)}) collective-permute-start(bf16[1,128,1024]{2,1,0:T(8,128)(2,1)S(1)} %add_convert_fusion.2), channel_id=1, source_target_pairs={{0,3},{1,2},{2,1},{3,0},{4,7},{5,6},{6,5},{7,4},{8,11},{9,10},{10,... | collective-permute-start | bytes 786440 | tf_op jit(solution)/shard_map/ppermute | solution.py:438
  (6 other events, 53.4 us)

commit v13 on v12

--- a/solution.py
+++ b/solution.py
@@ -19,7 +19,7 @@
 VMEM = 14 * 2**20
 VMEM_EXPERTS = 24 * 2**20
 VMEM_SORT = 52 * 2**20
-PIECES = 2
+PIECES = (0.5, 0.75, 1.0)
 DEPTH = 3
 PEAK = 1.1e9
 
@@ -38,7 +38,7 @@
         scratch_shapes=scratch,
         input_output_aliases=aliases,
         compiler_params=pltpu.CompilerParams(
-            dimension_semantics=("arbitrary",) * len(grid), vmem_limit_bytes=limit
+            dimension_semantics=("arbitrary",) * len(grid) if grid else None, vmem_limit_bytes=limit
         ),
         cost_estimate=pl.CostEstimate(
             flops=int(micros * PEAK), bytes_accessed=0, transcendentals=0
@@ -47,8 +47,9 @@
     )
 
 
-def dispatch_kernel(n_parts, n_row, top, n_after, base_ref, rw_ref, *refs):
-    parts, refs = refs[:n_parts], refs[n_parts + n_after :]
+def dispatch_kernel(starts, n_row, top, base_ref, rw_ref, *refs):
+    n_parts = len(starts)
+    parts, refs = refs[:n_parts], refs[n_parts:]
     if n_row:
         seg_ref, scale_ref = refs[:2]
         refs = refs[2:]
@@ -64,8 +65,9 @@
     slot = lax.broadcasted_iota(jnp.int32, (local, CAP, BLOCK), 1).astype(jnp.float32)
     hots, probs = [], []
     for p in range(n_parts):
-        x = parts[p][:BLOCK, :]
-        ids = parts[p][BLOCK : BLOCK + EXTRA, :].astype(jnp.float32)[0:1] - base
+        s = starts[p]
+        x = parts[p][s : s + BLOCK, :]
+        ids = parts[p][s + BLOCK : s + BLOCK + EXTRA, :].astype(jnp.float32)[0:1] - base
         ids = jnp.where(ids < 0.0, ids + EXPERTS, ids)
         logits = lax.dot_general(rw_ref[...], x, NT, preferred_element_type=jnp.float32)
         expo = jnp.exp(logits - jnp.max(logits, axis=0, keepdims=True))
@@ -110,11 +112,14 @@
 ANYWHERE = pl.BlockSpec(memory_space=pl.ANY)
 
 
+IN_VMEM = pl.BlockSpec(memory_space=pltpu.VMEM)
+
+
 def whole(a):
     return pl.BlockSpec(a.shape, lambda *i: (0,) * a.ndim)
 
 
-def dispatch(parts, n, top, base, rw, local, row=None, after=()):
+def dispatch(parts, n, top, base, rw, local, row=None):
     n_parts = len(parts)
     width = rw.shape[1]
     slots = n_parts * CAP
@@ -124,7 +129,6 @@
     ] + [
         pl.BlockSpec((BLOCK + EXTRA, width), lambda i, k=k: (k + i, 0)) for _, k in parts
     ]
-    in_specs += [ANYWHERE] * len(after)
     out_specs = [
         pl.BlockSpec((local, slots, width), lambda i: (0, i, 0)),
         pl.BlockSpec((local, slots, LANES), lambda i: (0, i, 0)),
@@ -141,16 +145,21 @@
         in_specs += [whole(a) for a in row]
         out_specs.append(pl.BlockSpec((NDOC, LANES), lambda i: (0, 0)))
         out_shape.append(jax.ShapeDtypeStruct((NDOC, LANES), jnp.float32))
+    grid, starts = (n,), [0] * n_parts
+    if n == 1:
+        grid, starts = (), [k * (BLOCK + EXTRA) for _, k in parts]
+        in_specs = in_specs[:1] + [IN_VMEM] * (len(in_specs) - 1)
+        out_specs = [IN_VMEM] * len(out_specs)
     return call(
-        functools.partial(dispatch_kernel, n_parts, n_parts if row is not None else 0, top, len(after)),
+        functools.partial(dispatch_kernel, starts, n_parts if row is not None else 0, top),
         3 * n,
-        (n,),
+        grid,
         in_specs,
         out_specs,
         out_shape,
         [],
         "dispatch",
-    )(base, rw, *[a for a, _ in parts], *after, *extra)
+    )(base, rw, *[a for a, _ in parts], *extra)
 
 
 def fetch(sources, slots, sem, step, steps, first, start=0):
@@ -226,19 +235,20 @@
 
 def sort_rows(gate_up, behind):
     local, hidden, _, width = gate_up.shape
-    pieces = PIECES if local % (2 * PIECES) == 0 else 1
+    ends = [int(local * p) for p in PIECES] if local % 8 == 0 else [local]
     group = 2 if local % 2 == 0 else 1
     chunks = width // LANES
     gu = gate_up.reshape(local, hidden, 2, chunks, LANES).swapaxes(2, 3)
     gu = gu.reshape(local, hidden * 2 * chunks, LANES)
     done = ()
-    for j in range(pieces):
-        after = behind[j] if pieces > 1 else ()
+    for j, end in enumerate(ends):
+        start = ends[j - 1] if j else 0
+        after = behind[j] if len(ends) > 1 else ()
         *done, token = (
             call(
-                functools.partial(sort_kernel, j * local // pieces),
+                functools.partial(sort_kernel, start),
                 8,
-                (local // pieces // group,),
+                ((end - start) // group,),
                 [IN_HBM] + [IN_HBM] * len(done) + [ANYWHERE] * len(after),
                 [IN_HBM, pl.BlockSpec((8, LANES), lambda e: (0, 0))],
                 [
@@ -461,7 +471,7 @@
     kv = [(a, k * tok_rows) for a in (keys, flip(keys, 1)) for k in range(2)]
     if near:
         blocks = 1
-        gu, token = sort_rows(gate_up, [(), (crossed[2],)])
+        gu, token = sort_rows(gate_up, [(), (arrived[1],), (crossed[2],)])
         pairs = [
             stack(a, b, (token,)) if i == 1 else jnp.concatenate([a, b], axis=0)
             for i, (a, b) in enumerate(zip(near_parts, crossed))
@@ -469,7 +479,7 @@
         flipped = [flip(a, 1) for a in pairs]
         spread = [[(a, 0), (a, 1), (b, 0), (b, 1)] for a, b in zip(pairs, flipped)]
     else:
-        gu, _ = sort_rows(gate_up, [(), ()])
+        gu, _ = sort_rows(gate_up, [(), (), ()])
         blocks = near_parts[0].shape[0] // (BLOCK + EXTRA)
         spread = [[(near_parts[0], 0), (crossed[0], 0)]]
         spread[0] = spread[0] + [(flip(a, 1), 0) for a, _ in spread[0]]

time: 96.1 us -> 94.2 us (0.980)
  the two profiles are of different devices: /device:TPU:0 before, /device:TPU:8 now
where the time goes in v13:
time: 94.2 us; the launch traced here: 93.8 us
  Pallas kernels  46.7 us (50%)
  starting transfers between devices  20.8 us (22%)
  waiting for transfers between devices  19.3 us (20%)
  other arithmetic  3.91 us (4%)
  local copies, waits for them, and re-layouts  2.17 us (2%)
  between operations  0.97 us (1%)
    pallas_call x3, Pallas kernels, sort_rows(): call(functools.partial(sort_kernel, start), 8, ((end - start) // group,),...  19.8 us
    ppermute x17, waiting for transfers between devices, flip(): return lax.ppermute(a, 'ctx', [(i, i ^ bit) for i in range(n_ctx)])  13 us
    pallas_call x1, Pallas kernels, experts(): call(functools.partial(expert_kernel, n), 6, (local // group, slots // si...  12.8 us
    ppermute x17, starting transfers between devices, flip(): return lax.ppermute(a, 'ctx', [(i, i ^ bit) for i in range(n_ctx)])  12 us
    ppermute x7, starting transfers between devices, shift(): return lax.ppermute(a, 'exp', [(i, i ^ d) for i in range(n_exp)])  8.78 us
    ppermute x7, waiting for transfers between devices, shift(): return lax.ppermute(a, 'exp', [(i, i ^ d) for i in range(n_exp)])  6.24 us
    pallas_call x1, Pallas kernels, attend(): call(functools.partial(attend_kernel, [at for _, at in parts], kdim), 6,...  6.17 us
    pallas_call x4, Pallas kernels, dispatch(): call(functools.partial(dispatch_kernel, starts, n_parts if row is not Non...  6.01 us
  transfers between devices with their start and end apart: 24, of which 6 were waited for; matrix products, arithmetic and copies ran while one was open for 4% of the time, Pallas kernels for 50%

profile of v13, /device:TPU:8, one launch (start us, length us, event | category | flops | bytes accessed | tf_op | source)
XLA Modules:
  0.0 93.8 jit_solution(9018894170322744511)
XLA Ops:
  2.4 3.1 %collective-permute-start.4 = (bf16[144,1024]{1,0:T(8,128)(2,1)S(1)}, bf16[144,1024]{1,0:T(8,128)(2,1)S(1)}, u32[]{:S(2)}, u32[]{:S(2)}) collective-permute-start(bf16[144,1024]{1,0:T(8,128)(2,1)S(1)} %pad_maximum_fusion.2), channel_id=1, source_target_pairs={{0,3},{1,2},{2,1},{3,0},{4,7},{5,6},{6,5},{7,4},{8,11},{9,10},{10,... | collective-permute-start | bytes 884744 | tf_op jit(solution)/shard_map/ppermute | solution.py:448
  5.5 1.5 %collective-permute-start.7 = (bf16[144,1024]{1,0:T(8,128)(2,1)S(1)}, bf16[144,1024]{1,0:T(8,128)(2,1)S(1)}, u32[]{:S(2)}, u32[]{:S(2)}) collective-permute-start(bf16[144,1024]{1,0:T(8,128)(2,1)S(1)} %pad_maximum_fusion.2), channel_id=1, source_target_pairs={{0,8},{4,12},{8,0},{12,4},{1,9},{5,13},{9,1},{13,5},{2,10},{6,14},... | collective-permute-start | bytes 884744 | tf_op jit(solution)/shard_map/ppermute | solution.py:445
  7.0 1.1 %copy.21 = bf16[1,128,576]{2,1,0:T(8,128)(2,1)S(1)} copy(bf16[1,128,576]{1,2,0:T(8,128)(2,1)} %param.9) | data formatting | bytes 294912 | tf_op args[1]
  8.7 9.0 %sort.3 = (bf16[16,2,176,1024]{3,2,1,0:T(8,128)(2,1)}, f32[8,128]{1,0:T(8,128)}) custom-call(bf16[16,2816,128]{2,1,0:T(8,128)(2,1)} %bitcast.53), custom_call_target="tpu_custom_call" | custom-call | flops 8800000000 | tf_op jit(solution)/shard_map/sort/pallas_call | solution.py:248
  19.3 1.5 %collective-permute-start.5 = (bf16[144,1024]{1,0:T(8,128)(2,1)S(1)}, bf16[144,1024]{1,0:T(8,128)(2,1)S(1)}, u32[]{:S(2)}, u32[]{:S(2)}) collective-permute-start(bf16[144,1024]{1,0:T(8,128)(2,1)S(1)} %collective-permute-done.4), channel_id=1, source_target_pairs={{0,8},{4,12},{8,0},{12,4},{1,9},{5,13},{9,1},{13,5},{2,10},{6,14},... | collective-permute-start | bytes 884744 | tf_op jit(solution)/shard_map/ppermute | solution.py:445
  20.8 1.3 %collective-permute-start.10 = (bf16[144,1024]{1,0:T(8,128)(2,1)S(1)}, bf16[144,1024]{1,0:T(8,128)(2,1)S(1)}, u32[]{:S(2)}, u32[]{:S(2)}) collective-permute-start(bf16[144,1024]{1,0:T(8,128)(2,1)S(1)} %collective-permute-done.4), channel_id=1, source_target_pairs={{0,1},{1,0},{2,3},{3,2},{4,5},{5,4},{6,7},{7,6},{8,9},{9,8},{10,11... | collective-permute-start | bytes 884744 | tf_op jit(solution)/shard_map/ppermute | solution.py:448
  22.6 5.8 %sort.4 = (bf16[16,2,176,1024]{3,2,1,0:T(8,128)(2,1)}, f32[8,128]{1,0:T(8,128)}) custom-call(bf16[16,2816,128]{2,1,0:T(8,128)(2,1)} %bitcast.54, bf16[16,2,176,1024]{3,2,1,0:T(8,128)(2,1)} %get-tuple-element.32.refs_0_, bf16[144,1024]{1,0:T(8,128)(2,1)S(1)} %collective-permute-done.2.refs_1_.a_ref), custom_call_target="tpu_custom_call", output_to_operand_aliasing={{0}: (1, {})} | custom-call | flops 8800000000 | tf_op jit(solution)/shard_map/sort/pallas_call | solution.py:248
  29.1 1.3 %collective-permute-start.11 = (bf16[144,1024]{1,0:T(8,128)(2,1)S(1)}, bf16[144,1024]{1,0:T(8,128)(2,1)S(1)}, u32[]{:S(2)}, u32[]{:S(2)}) collective-permute-start(bf16[144,1024]{1,0:T(8,128)(2,1)S(1)} %collective-permute-done.5.refs_1_), channel_id=1, source_target_pairs={{0,1},{1,0},{2,3},{3,2},{4,5},{5,4},{6,7},{7,6},{8,9},{9,8},{10,11... | collective-permute-start | bytes 884744 | tf_op jit(solution)/shard_map/ppermute | solution.py:448
  30.5 5.1 %sort.5 = (bf16[16,2,176,1024]{3,2,1,0:T(8,128)(2,1)}, f32[8,128]{1,0:T(8,128)S(1)}) custom-call(bf16[16,2816,128]{2,1,0:T(8,128)(2,1)} %bitcast.55, bf16[16,2,176,1024]{3,2,1,0:T(8,128)(2,1)} %get-tuple-element.33.refs_0_, bf16[144,1024]{1,0:T(8,128)(2,1)S(1)} %collective-permute-done.5.refs_1_), custom_call_target="tpu_custom_call", output_to_operand_aliasing={{0}: (1, {})} | custom-call | flops 8800000000 | tf_op jit(solution)/shard_map/sort/pallas_call | solution.py:248
  36.9 1.6 %dispatch.5 = (bf16[16,64,1024]{2,1,0:T(8,128)(2,1)S(1)}, f32[16,64,128]{2,1,0:T(8,128)S(1)}, bf16[4,256,128]{2,1,0:T(8,128)(2,1)S(1)}, f32[8,128]{1,0:T(8,128)S(1)}) custom-call(s32[1]{0:T(128)} %bitcast.13.base_ref, bf16[64,1024]{1,0:T(8,128)(2,1)S(1)} %fusion.rw_ref, bf16[288,1024]{1,0:T(8,128)(2,1)S(1)} %pad_maximum_fusion.refs_0_.refs_1_, ...), custom_call_target="tpu_custom_call" | custom-call | flops 3300000000 | tf_op jit(solution)/shard_map/dispatch/pallas_call | solution.py:153
  38.4 1.5 %dispatch.4 = (bf16[16,64,1024]{2,1,0:T(8,128)(2,1)S(1)}, f32[16,64,128]{2,1,0:T(8,128)S(1)}, bf16[4,256,128]{2,1,0:T(8,128)(2,1)S(1)}) custom-call(s32[1]{0:T(128)} %bitcast.13.base_ref, bf16[64,1024]{1,0:T(8,128)(2,1)S(1)} %fusion.rw_ref, bf16[288,1024]{1,0:T(8,128)(2,1)S(1)} %stack.21.refs_0_.refs_1_, bf16[288,1024]{1,0:T(8,128)(2,1)S(1)} %stack.21.refs_0_.refs_1_, ...), custom_call_target="tpu_custom_call" | custom-call | flops 3300000000 | tf_op jit(solution)/shard_map/dispatch/pallas_call | solution.py:153
  39.9 1.5 %dispatch.6 = (bf16[16,64,1024]{2,1,0:T(8,128)(2,1)S(1)}, f32[16,64,128]{2,1,0:T(8,128)S(1)}, bf16[4,256,128]{2,1,0:T(8,128)(2,1)S(1)}) custom-call(s32[1]{0:T(128)} %bitcast.13.base_ref, bf16[64,1024]{1,0:T(8,128)(2,1)S(1)} %fusion.rw_ref, bf16[288,1024]{1,0:T(8,128)(2,1)S(1)} %constant_dynamic-update-slice_fusion.refs_0_.refs_1_, ...), custom_call_target="tpu_custom_call" | custom-call | flops 3300000000 | tf_op jit(solution)/shard_map/dispatch/pallas_call | solution.py:153
  41.5 1.5 %dispatch.7 = (bf16[16,64,1024]{2,1,0:T(8,128)(2,1)S(1)}, f32[16,64,128]{2,1,0:T(8,128)S(1)}, bf16[4,256,128]{2,1,0:T(8,128)(2,1)S(1)}) custom-call(s32[1]{0:T(128)} %bitcast.13.base_ref, bf16[64,1024]{1,0:T(8,128)(2,1)S(1)} %fusion.rw_ref, bf16[288,1024]{1,0:T(8,128)(2,1)S(1)} %constant_dynamic-update-slice_fusion.2.refs_0_.refs_1_, ...), custom_call_target="tpu_custom_call" | custom-call | flops 3300000000 | tf_op jit(solution)/shard_map/dispatch/pallas_call | solution.py:153
  43.0 12.8 %experts.1 = (bf16[16,64,1024]{2,1,0:T(8,128)(2,1)S(1)}, bf16[16,64,1024]{2,1,0:T(8,128)(2,1)S(1)}, bf16[16,64,1024]{2,1,0:T(8,128)(2,1)S(1)}, bf16[16,64,1024]{2,1,0:T(8,128)(2,1)S(1)}) custom-call(bf16[16,64,1024]{2,1,0:T(8,128)(2,1)S(1)} %get-tuple-element.36.refs_0_, bf16[16,64,1024]{2,1,0:T(8,128)(2,1)S(1)} %get-tuple-element.37.refs_1_, ...), custom_call_target="tpu_custom_call" | custom-call | flops 6600000000 | tf_op jit(solution)/shard_map/experts/pallas_call | solution.py:329
  59.1 1.6 %collective-permute-start.19 = (bf16[1,128,1024]{2,1,0:T(8,128)(2,1)S(1)}, bf16[1,128,1024]{2,1,0:T(8,128)(2,1)S(1)}, u32[]{:S(2)}, u32[]{:S(2)}) collective-permute-start(bf16[1,128,1024]{2,1,0:T(8,128)(2,1)S(1)} %add_convert_fusion.4), channel_id=1, source_target_pairs={{0,8},{4,12},{8,0},{12,4},{1,9},{5,13},{9,1},{13,5},{2,10},{6,14},... | collective-permute-start | bytes 786440 | tf_op jit(solution)/shard_map/ppermute | solution.py:445
  61.4 1.6 %collective-permute-start.17 = (bf16[1,128,1024]{2,1,0:T(8,128)(2,1)S(1)}, bf16[1,128,1024]{2,1,0:T(8,128)(2,1)S(1)}, u32[]{:S(2)}, u32[]{:S(2)}) collective-permute-start(bf16[1,128,1024]{2,1,0:T(8,128)(2,1)S(1)} %add_convert_fusion.5), channel_id=1, source_target_pairs={{0,8},{4,12},{8,0},{12,4},{1,9},{5,13},{9,1},{13,5},{2,10},{6,14},... | collective-permute-start | bytes 786440 | tf_op jit(solution)/shard_map/ppermute | solution.py:445
  63.0 5.3 %collective-permute-done.19 = bf16[1,128,1024]{2,1,0:T(8,128)(2,1)S(1)} collective-permute-done((bf16[1,128,1024]{2,1,0:T(8,128)(2,1)S(1)}, bf16[1,128,1024]{2,1,0:T(8,128)(2,1)S(1)}, u32[]{:S(2)}, u32[]{:S(2)}) %collective-permute-start.19) | collective-permute-done | bytes 262176 | tf_op jit(solution)/shard_map/ppermute | solution.py:445
  68.4 1.2 %collective-permute-start.20 = (bf16[1,128,1024]{2,1,0:T(8,128)(2,1)S(1)}, bf16[1,128,1024]{2,1,0:T(8,128)(2,1)S(1)}, u32[]{:S(2)}, u32[]{:S(2)}) collective-permute-start(bf16[1,128,1024]{2,1,0:T(8,128)(2,1)S(1)} %add_convert_fusion.3), channel_id=1, source_target_pairs={{0,1},{1,0},{2,3},{3,2},{4,5},{5,4},{6,7},{7,6},{8,9},{9,8},{10,11... | collective-permute-start | bytes 786440 | tf_op jit(solution)/shard_map/ppermute | solution.py:448
  69.7 1.5 %collective-permute-start.23 = (bf16[1,128,1024]{2,1,0:T(8,128)(2,1)S(1)}, bf16[1,128,1024]{2,1,0:T(8,128)(2,1)S(1)}, u32[]{:S(2)}, u32[]{:S(2)}) collective-permute-start(bf16[1,128,1024]{2,1,0:T(8,128)(2,1)S(1)} %add_convert_fusion.1), channel_id=1, source_target_pairs={{0,8},{4,12},{8,0},{12,4},{1,9},{5,13},{9,1},{13,5},{2,10},{6,14},... | collective-permute-start | bytes 786440 | tf_op jit(solution)/shard_map/ppermute | solution.py:445
  71.2 2.7 %collective-permute-done.14 = bf16[1,128,1024]{2,1,0:T(8,128)(2,1)S(1)} collective-permute-done((bf16[1,128,1024]{2,1,0:T(8,128)(2,1)S(1)}, bf16[1,128,1024]{2,1,0:T(8,128)(2,1)S(1)}, u32[]{:S(2)}, u32[]{:S(2)}) %collective-permute-start.14) | collective-permute-done | bytes 262176 | tf_op jit(solution)/shard_map/ppermute | solution.py:445
  74.0 1.2 %collective-permute-start.15 = (bf16[1,128,1024]{2,1,0:T(8,128)(2,1)S(1)}, bf16[1,128,1024]{2,1,0:T(8,128)(2,1)S(1)}, u32[]{:S(2)}, u32[]{:S(2)}) collective-permute-start(bf16[1,128,1024]{2,1,0:T(8,128)(2,1)S(1)} %add_convert_fusion.6), channel_id=1, source_target_pairs={{0,1},{1,0},{2,3},{3,2},{4,5},{5,4},{6,7},{7,6},{8,9},{9,8},{10,11... | collective-permute-start | bytes 786440 | tf_op jit(solution)/shard_map/ppermute | solution.py:448
  75.2 4.3 %collective-permute-done.17 = bf16[1,128,1024]{2,1,0:T(8,128)(2,1)S(1)} collective-permute-done((bf16[1,128,1024]{2,1,0:T(8,128)(2,1)S(1)}, bf16[1,128,1024]{2,1,0:T(8,128)(2,1)S(1)}, u32[]{:S(2)}, u32[]{:S(2)}) %collective-permute-start.17) | collective-permute-done | bytes 262176 | tf_op jit(solution)/shard_map/ppermute | solution.py:445
  80.2 6.2 %attention.1 = bf16[128,4096]{1,0:T(8,128)(2,1)} custom-call(s32[128,1]{1,0:T(8,128)S(1)} %copy.22.first_ref, s32[128,1]{1,0:T(8,128)S(1)} %copy.23.last_ref, s32[1,512]{1,0:T(1,128)S(1)} %bitcast.39, bf16[128,4608]{1,0:T(8,128)(2,1)S(1)} %bitcast.41, bf16[256,576]{1,0:T(8,128)(2,1)S(1)} %pad_maximum_fusion.1.refs_0_.refs_1_, ...), custom_call_target="tpu_custom_call" | custom-call | flops 6600000000 | tf_op jit(solution)/shard_map/attention/pallas_call | solution.py:414
  87.0 5.9 %collective-permute-done.21 = bf16[1,128,1024]{2,1,0:T(8,128)(2,1)S(1)} collective-permute-done((bf16[1,128,1024]{2,1,0:T(8,128)(2,1)S(1)}, bf16[1,128,1024]{2,1,0:T(8,128)(2,1)S(1)}, u32[]{:S(2)}, u32[]{:S(2)}) %collective-permute-start.21) | collective-permute-done | bytes 262176 | tf_op jit(solution)/shard_map/ppermute | solution.py:448
  (83 shorter events, 13.0 us)
Async XLA Ops:
  2.3 19.8 %collective-permute-start.2 = (bf16[144,1024]{1,0:T(8,128)(2,1)S(1)}, bf16[144,1024]{1,0:T(8,128)(2,1)S(1)}, u32[]{:S(2)}, u32[]{:S(2)}) collective-permute-start(bf16[144,1024]{1,0:T(8,128)(2,1)S(1)} %pad_maximum_fusion.2), channel_id=1, source_target_pairs={{0,1},{1,0},{2,3},{3,2},{4,5},{5,4},{6,7},{7,6},{8,9},{9,8},{10,11... | collective-permute-start | bytes 884744 | tf_op jit(solution)/shard_map/ppermute | solution.py:448
  2.4 16.9 %collective-permute-start.4 = (bf16[144,1024]{1,0:T(8,128)(2,1)S(1)}, bf16[144,1024]{1,0:T(8,128)(2,1)S(1)}, u32[]{:S(2)}, u32[]{:S(2)}) collective-permute-start(bf16[144,1024]{1,0:T(8,128)(2,1)S(1)} %pad_maximum_fusion.2), channel_id=1, source_target_pairs={{0,3},{1,2},{2,1},{3,0},{4,7},{5,6},{6,5},{7,4},{8,11},{9,10},{10,... | collective-permute-start | bytes 884744 | tf_op jit(solution)/shard_map/ppermute | solution.py:448
  5.5 13.1 %collective-permute-start.7 = (bf16[144,1024]{1,0:T(8,128)(2,1)S(1)}, bf16[144,1024]{1,0:T(8,128)(2,1)S(1)}, u32[]{:S(2)}, u32[]{:S(2)}) collective-permute-start(bf16[144,1024]{1,0:T(8,128)(2,1)S(1)} %pad_maximum_fusion.2), channel_id=1, source_target_pairs={{0,8},{4,12},{8,0},{12,4},{1,9},{5,13},{9,1},{13,5},{2,10},{6,14},... | collective-permute-start | bytes 884744 | tf_op jit(solution)/shard_map/ppermute | solution.py:445
  8.1 10.4 %collective-permute-start = (bf16[128,576]{1,0:T(8,128)(2,1)S(1)}, bf16[128,576]{1,0:T(8,128)(2,1)S(1)}, u32[]{:S(2)}, u32[]{:S(2)}) collective-permute-start(bf16[128,576]{1,0:T(8,128)(2,1)S(1)} %bitcast.44), channel_id=1, source_target_pairs={{0,8},{4,12},{8,0},{12,4},{1,9},{5,13},{9,1},{13,5},{2,10},{6,14},... | collective-permute-start | bytes 442376 | tf_op jit(solution)/shard_map/ppermute | solution.py:445
  18.6 61.6 %collective-permute-start.1 = (bf16[256,576]{1,0:T(8,128)(2,1)S(1)}, bf16[256,576]{1,0:T(8,128)(2,1)S(1)}, u32[]{:S(2)}, u32[]{:S(2)}) collective-permute-start(bf16[256,576]{1,0:T(8,128)(2,1)S(1)} %pad_maximum_fusion.1.refs_0_.refs_1_), channel_id=1, source_target_pairs={{0,4},{4,0},{8,12},{12,8},{1,5},{5,1},{9,13},{13,9},{2,6},{6,2},{1... | collective-permute-start | bytes 884744 | tf_op jit(solution)/shard_map/ppermute | solution.py:445
  18.7 18.1 %collective-permute-start.8 = (bf16[288,1024]{1,0:T(8,128)(2,1)S(1)}, bf16[288,1024]{1,0:T(8,128)(2,1)S(1)}, u32[]{:S(2)}, u32[]{:S(2)}) collective-permute-start(bf16[288,1024]{1,0:T(8,128)(2,1)S(1)} %pad_maximum_fusion.refs_0_.refs_1_), channel_id=1, source_target_pairs={{0,4},{4,0},{8,12},{12,8},{1,5},{5,1},{9,13},{13,9},{2,6},{6,2},{1... | collective-permute-start | bytes 1769480 | tf_op jit(solution)/shard_map/ppermute | solution.py:445
  19.3 9.9 %collective-permute-start.5 = (bf16[144,1024]{1,0:T(8,128)(2,1)S(1)}, bf16[144,1024]{1,0:T(8,128)(2,1)S(1)}, u32[]{:S(2)}, u32[]{:S(2)}) collective-permute-start(bf16[144,1024]{1,0:T(8,128)(2,1)S(1)} %collective-permute-done.4), channel_id=1, source_target_pairs={{0,8},{4,12},{8,0},{12,4},{1,9},{5,13},{9,1},{13,5},{2,10},{6,14},... | collective-permute-start | bytes 884744 | tf_op jit(solution)/shard_map/ppermute | solution.py:445
  20.8 15.0 %collective-permute-start.10 = (bf16[144,1024]{1,0:T(8,128)(2,1)S(1)}, bf16[144,1024]{1,0:T(8,128)(2,1)S(1)}, u32[]{:S(2)}, u32[]{:S(2)}) collective-permute-start(bf16[144,1024]{1,0:T(8,128)(2,1)S(1)} %collective-permute-done.4), channel_id=1, source_target_pairs={{0,1},{1,0},{2,3},{3,2},{4,5},{5,4},{6,7},{7,6},{8,9},{9,8},{10,11... | collective-permute-start | bytes 884744 | tf_op jit(solution)/shard_map/ppermute | solution.py:448
  22.1 13.5 %collective-permute-start.3 = (bf16[144,1024]{1,0:T(8,128)(2,1)S(1)}, bf16[144,1024]{1,0:T(8,128)(2,1)S(1)}, u32[]{:S(2)}, u32[]{:S(2)}) collective-permute-start(bf16[144,1024]{1,0:T(8,128)(2,1)S(1)} %collective-permute-done.2.refs_1_.a_ref), channel_id=1, source_target_pairs={{0,8},{4,12},{8,0},{12,4},{1,9},{5,13},{9,1},{13,5},{2,10},{6,14},... | collective-permute-start | bytes 884744 | tf_op jit(solution)/shard_map/ppermute | solution.py:445
  29.1 7.5 %collective-permute-start.11 = (bf16[144,1024]{1,0:T(8,128)(2,1)S(1)}, bf16[144,1024]{1,0:T(8,128)(2,1)S(1)}, u32[]{:S(2)}, u32[]{:S(2)}) collective-permute-start(bf16[144,1024]{1,0:T(8,128)(2,1)S(1)} %collective-permute-done.5.refs_1_), channel_id=1, source_target_pairs={{0,1},{1,0},{2,3},{3,2},{4,5},{5,4},{6,7},{7,6},{8,9},{9,8},{10,11... | collective-permute-start | bytes 884744 | tf_op jit(solution)/shard_map/ppermute | solution.py:448
  35.6 2.8 %collective-permute-start.6 = (bf16[288,1024]{1,0:T(8,128)(2,1)S(1)}, bf16[288,1024]{1,0:T(8,128)(2,1)S(1)}, u32[]{:S(2)}, u32[]{:S(2)}) collective-permute-start(bf16[288,1024]{1,0:T(8,128)(2,1)S(1)} %stack.21.refs_0_.refs_1_), channel_id=1, source_target_pairs={{0,4},{4,0},{8,12},{12,8},{1,5},{5,1},{9,13},{13,9},{2,6},{6,2},{1... | collective-permute-start | bytes 1769480 | tf_op jit(solution)/shard_map/ppermute | solution.py:445
  35.7 4.2 %collective-permute-start.9 = (bf16[288,1024]{1,0:T(8,128)(2,1)S(1)}, bf16[288,1024]{1,0:T(8,128)(2,1)S(1)}, u32[]{:S(2)}, u32[]{:S(2)}) collective-permute-start(bf16[288,1024]{1,0:T(8,128)(2,1)S(1)} %constant_dynamic-update-slice_fusion.refs_0_.refs_1_), channel_id=1, source_target_pairs={{0,4},{4,0},{8,12},{12,8},{1,5},{5,1},{9,13},{13,9},{2,6},{6,2},{1... | collective-permute-start | bytes 1769480 | tf_op jit(solution)/shard_map/ppermute | solution.py:445
  36.7 4.7 %collective-permute-start.12 = (bf16[288,1024]{1,0:T(8,128)(2,1)S(1)}, bf16[288,1024]{1,0:T(8,128)(2,1)S(1)}, u32[]{:S(2)}, u32[]{:S(2)}) collective-permute-start(bf16[288,1024]{1,0:T(8,128)(2,1)S(1)} %constant_dynamic-update-slice_fusion.2.refs_0_.refs_1_), channel_id=1, source_target_pairs={{0,4},{4,0},{8,12},{12,8},{1,5},{5,1},{9,13},{13,9},{2,6},{6,2},{1... | collective-permute-start | bytes 1769480 | tf_op jit(solution)/shard_map/ppermute | solution.py:445
  56.3 2.7 %collective-permute-start.18 = (bf16[1,256,1024]{2,1,0:T(8,128)(2,1)S(1)}, bf16[1,256,1024]{2,1,0:T(8,128)(2,1)S(1)}, u32[]{:S(2)}, u32[]{:S(2)}) collective-permute-start(bf16[1,256,1024]{2,1,0:T(8,128)(2,1)S(1)} %get-tuple-element.55), channel_id=1, source_target_pairs={{0,4},{4,0},{8,12},{12,8},{1,5},{5,1},{9,13},{13,9},{2,6},{6,2},{1... | collective-permute-start | bytes 1572872 | tf_op jit(solution)/shard_map/ppermute | solution.py:445
  57.3 3.3 %collective-permute-start.13 = (bf16[1,256,1024]{2,1,0:T(8,128)(2,1)S(1)}, bf16[1,256,1024]{2,1,0:T(8,128)(2,1)S(1)}, u32[]{:S(2)}, u32[]{:S(2)}) collective-permute-start(bf16[1,256,1024]{2,1,0:T(8,128)(2,1)S(1)} %get-tuple-element.47), channel_id=1, source_target_pairs={{0,4},{4,0},{8,12},{12,8},{1,5},{5,1},{9,13},{13,9},{2,6},{6,2},{1... | collective-permute-start | bytes 1572872 | tf_op jit(solution)/shard_map/ppermute | solution.py:445
  57.9 3.4 %collective-permute-start.16 = (bf16[1,256,1024]{2,1,0:T(8,128)(2,1)S(1)}, bf16[1,256,1024]{2,1,0:T(8,128)(2,1)S(1)}, u32[]{:S(2)}, u32[]{:S(2)}) collective-permute-start(bf16[1,256,1024]{2,1,0:T(8,128)(2,1)S(1)} %get-tuple-element.51), channel_id=1, source_target_pairs={{0,4},{4,0},{8,12},{12,8},{1,5},{5,1},{9,13},{13,9},{2,6},{6,2},{1... | collective-permute-start | bytes 1572872 | tf_op jit(solution)/shard_map/ppermute | solution.py:445
  58.9 10.6 %collective-permute-start.22 = (bf16[1,256,1024]{2,1,0:T(8,128)(2,1)S(1)}, bf16[1,256,1024]{2,1,0:T(8,128)(2,1)S(1)}, u32[]{:S(2)}, u32[]{:S(2)}) collective-permute-start(bf16[1,256,1024]{2,1,0:T(8,128)(2,1)S(1)} %get-tuple-element.59), channel_id=1, source_target_pairs={{0,4},{4,0},{8,12},{12,8},{1,5},{5,1},{9,13},{13,9},{2,6},{6,2},{1... | collective-permute-start | bytes 1572872 | tf_op jit(solution)/shard_map/ppermute | solution.py:445
  59.1 9.2 %collective-permute-start.19 = (bf16[1,128,1024]{2,1,0:T(8,128)(2,1)S(1)}, bf16[1,128,1024]{2,1,0:T(8,128)(2,1)S(1)}, u32[]{:S(2)}, u32[]{:S(2)}) collective-permute-start(bf16[1,128,1024]{2,1,0:T(8,128)(2,1)S(1)} %add_convert_fusion.4), channel_id=1, source_target_pairs={{0,8},{4,12},{8,0},{12,4},{1,9},{5,13},{9,1},{13,5},{2,10},{6,14},... | collective-permute-start | bytes 786440 | tf_op jit(solution)/shard_map/ppermute | solution.py:445
  60.7 13.2 %collective-permute-start.14 = (bf16[1,128,1024]{2,1,0:T(8,128)(2,1)S(1)}, bf16[1,128,1024]{2,1,0:T(8,128)(2,1)S(1)}, u32[]{:S(2)}, u32[]{:S(2)}) collective-permute-start(bf16[1,128,1024]{2,1,0:T(8,128)(2,1)S(1)} %add_convert_fusion.7), channel_id=1, source_target_pairs={{0,8},{4,12},{8,0},{12,4},{1,9},{5,13},{9,1},{13,5},{2,10},{6,14},... | collective-permute-start | bytes 786440 | tf_op jit(solution)/shard_map/ppermute | solution.py:445
  61.4 18.1 %collective-permute-start.17 = (bf16[1,128,1024]{2,1,0:T(8,128)(2,1)S(1)}, bf16[1,128,1024]{2,1,0:T(8,128)(2,1)S(1)}, u32[]{:S(2)}, u32[]{:S(2)}) collective-permute-start(bf16[1,128,1024]{2,1,0:T(8,128)(2,1)S(1)} %add_convert_fusion.5), channel_id=1, source_target_pairs={{0,8},{4,12},{8,0},{12,4},{1,9},{5,13},{9,1},{13,5},{2,10},{6,14},... | collective-permute-start | bytes 786440 | tf_op jit(solution)/shard_map/ppermute | solution.py:445
  68.4 11.1 %collective-permute-start.20 = (bf16[1,128,1024]{2,1,0:T(8,128)(2,1)S(1)}, bf16[1,128,1024]{2,1,0:T(8,128)(2,1)S(1)}, u32[]{:S(2)}, u32[]{:S(2)}) collective-permute-start(bf16[1,128,1024]{2,1,0:T(8,128)(2,1)S(1)} %add_convert_fusion.3), channel_id=1, source_target_pairs={{0,1},{1,0},{2,3},{3,2},{4,5},{5,4},{6,7},{7,6},{8,9},{9,8},{10,11... | collective-permute-start | bytes 786440 | tf_op jit(solution)/shard_map/ppermute | solution.py:448
  69.7 17.4 %collective-permute-start.23 = (bf16[1,128,1024]{2,1,0:T(8,128)(2,1)S(1)}, bf16[1,128,1024]{2,1,0:T(8,128)(2,1)S(1)}, u32[]{:S(2)}, u32[]{:S(2)}) collective-permute-start(bf16[1,128,1024]{2,1,0:T(8,128)(2,1)S(1)} %add_convert_fusion.1), channel_id=1, source_target_pairs={{0,8},{4,12},{8,0},{12,4},{1,9},{5,13},{9,1},{13,5},{2,10},{6,14},... | collective-permute-start | bytes 786440 | tf_op jit(solution)/shard_map/ppermute | solution.py:445
  74.0 13.0 %collective-permute-start.15 = (bf16[1,128,1024]{2,1,0:T(8,128)(2,1)S(1)}, bf16[1,128,1024]{2,1,0:T(8,128)(2,1)S(1)}, u32[]{:S(2)}, u32[]{:S(2)}) collective-permute-start(bf16[1,128,1024]{2,1,0:T(8,128)(2,1)S(1)} %add_convert_fusion.6), channel_id=1, source_target_pairs={{0,1},{1,0},{2,3},{3,2},{4,5},{5,4},{6,7},{7,6},{8,9},{9,8},{10,11... | collective-permute-start | bytes 786440 | tf_op jit(solution)/shard_map/ppermute | solution.py:448
  79.7 13.2 %collective-permute-start.21 = (bf16[1,128,1024]{2,1,0:T(8,128)(2,1)S(1)}, bf16[1,128,1024]{2,1,0:T(8,128)(2,1)S(1)}, u32[]{:S(2)}, u32[]{:S(2)}) collective-permute-start(bf16[1,128,1024]{2,1,0:T(8,128)(2,1)S(1)} %add_convert_fusion.2), channel_id=1, source_target_pairs={{0,3},{1,2},{2,1},{3,0},{4,7},{5,6},{6,5},{7,4},{8,11},{9,10},{10,... | collective-permute-start | bytes 786440 | tf_op jit(solution)/shard_map/ppermute | solution.py:448
  (6 other events, 51.9 us)

commit v14 on v13

--- a/solution.py
+++ b/solution.py
@@ -256,10 +256,10 @@
                     jax.ShapeDtypeStruct((8, LANES), jnp.float32),
                 ],
                 [
-                    pltpu.VMEM((2, group) + gu.shape[1:], jnp.bfloat16),
+                    pltpu.VMEM((DEPTH, group) + gu.shape[1:], jnp.bfloat16),
                     pltpu.VMEM((2, group, 2, hidden, width), jnp.bfloat16),
                     pltpu.VMEM((group,) + gu.shape[1:], jnp.float32),
-                    pltpu.SemaphoreType.DMA((1, 2, group)),
+                    pltpu.SemaphoreType.DMA((1, DEPTH, group)),
                     pltpu.SemaphoreType.DMA((2,)),
                 ],
                 "sort",
@@ -374,6 +374,25 @@
         [],
         "combine",
     )(*picks, *made, *after)
+
+
+def join_kernel(a_ref, b_ref, c_ref, *refs):
+    rows = c_ref.shape[1]
+    total = a_ref[:, :rows, :].astype(jnp.float32) + b_ref[:, :rows, :].astype(jnp.float32)
+    refs[-1][...] = (total + c_ref[...].astype(jnp.float32)).astype(jnp.bfloat16)
+
+
+def join(a, b, c, before):
+    return call(
+        join_kernel,
+        1,
+        (),
+        [IN_VMEM] * 3 + [ANYWHERE] * len(before),
+        IN_VMEM,
+        jax.ShapeDtypeStruct(c.shape, c.dtype),
+        [],
+        "join",
+    )(a, b, c, *before)
 
 
 def attend_kernel(starts, kdim, first_ref, last_ref, kpos_ref, q_ref, *refs):
@@ -507,15 +526,19 @@
             balance = out[3]
     made = experts([a[0] for a in sent], [a[1] for a in sent], gu, w_down)
     back = []
-    for i in [3, 1, 2, 0][-len(shifts) :]:
+    for i in reversed(range(len(shifts))):
         keep, give = combine([sent[i][2]], [made[i]], n_ctx)
         got = flip(give, 1)
         far = added(keep[:, tok_rows:], got[:, tok_rows:])
-        terms = [keep[:, :tok_rows], got[:, :tok_rows], flip(far, 2)]
+        crossed_sum = flip(far, 2)
+        terms = [keep[:, :tok_rows], got[:, :tok_rows], crossed_sum]
         if shifts[i] == 2:
-            joining = [shift(added(*terms), 1)]
+            joining = shift(added(*terms), 1)
+        elif shifts[i] == 3:
+            across = added(*terms, joining)
+            back.append(shift(across, 3))
         elif i:
-            back.append(shift(added(*terms, *(joining if shifts[i] == 3 else [])), shifts[i]))
+            back.append(shift(join(keep, got, crossed_sum, (across,)), 1))
         else:
             back = back + terms
     if near:

time: 94.2 us -> 92.2 us (0.979)
  the two profiles are of different devices: /device:TPU:8 before, /device:TPU:0 now
where the time goes in v14:
time: 92.2 us; the launch traced here: 91.9 us
  Pallas kernels  46.3 us (50%)
  starting transfers between devices  22.2 us (24%)
  waiting for transfers between devices  16.5 us (18%)
  other arithmetic  3.8 us (4%)
  local copies, waits for them, and re-layouts  2.17 us (2%)
  between operations  0.96 us (1%)
    pallas_call x3, Pallas kernels, sort_rows(): call(functools.partial(sort_kernel, start), 8, ((end - start) // group,),...  19.3 us
    pallas_call x1, Pallas kernels, experts(): call(functools.partial(expert_kernel, n), 6, (local // group, slots // si...  12.8 us
    ppermute x7, starting transfers between devices, shift(): return lax.ppermute(a, 'exp', [(i, i ^ d) for i in range(n_exp)])  11.4 us
    ppermute x17, starting transfers between devices, flip(): return lax.ppermute(a, 'ctx', [(i, i ^ bit) for i in range(n_ctx)])  10.8 us
    ppermute x17, waiting for transfers between devices, flip(): return lax.ppermute(a, 'ctx', [(i, i ^ bit) for i in range(n_ctx)])  10.7 us
    pallas_call x1, Pallas kernels, attend(): call(functools.partial(attend_kernel, [at for _, at in parts], kdim), 6,...  6.17 us
    pallas_call x4, Pallas kernels, dispatch(): call(functools.partial(dispatch_kernel, starts, n_parts if row is not Non...  6.03 us
    ppermute x7, waiting for transfers between devices, shift(): return lax.ppermute(a, 'exp', [(i, i ^ d) for i in range(n_exp)])  5.82 us
  transfers between devices with their start and end apart: 24, of which 8 were waited for; matrix products, arithmetic and copies ran while one was open for 4% of the time, Pallas kernels for 50%

profile of v14, /device:TPU:0, one launch (start us, length us, event | category | flops | bytes accessed | tf_op | source)
XLA Modules:
  0.0 91.9 jit_solution(9484100614121081036)
XLA Ops:
  2.3 3.1 %collective-permute-start.7 = (bf16[144,1024]{1,0:T(8,128)(2,1)S(1)}, bf16[144,1024]{1,0:T(8,128)(2,1)S(1)}, u32[]{:S(2)}, u32[]{:S(2)}) collective-permute-start(bf16[144,1024]{1,0:T(8,128)(2,1)S(1)} %pad_maximum_fusion.2), channel_id=1, source_target_pairs={{0,1},{1,0},{2,3},{3,2},{4,5},{5,4},{6,7},{7,6},{8,9},{9,8},{10,11... | collective-permute-start | bytes 884744 | tf_op jit(solution)/shard_map/ppermute | solution.py:467
  5.4 2.5 %collective-permute-start.2 = (bf16[144,1024]{1,0:T(8,128)(2,1)S(1)}, bf16[144,1024]{1,0:T(8,128)(2,1)S(1)}, u32[]{:S(2)}, u32[]{:S(2)}) collective-permute-start(bf16[144,1024]{1,0:T(8,128)(2,1)S(1)} %pad_maximum_fusion.2), channel_id=1, source_target_pairs={{0,3},{1,2},{2,1},{3,0},{4,7},{5,6},{6,5},{7,4},{8,11},{9,10},{10,... | collective-permute-start | bytes 884744 | tf_op jit(solution)/shard_map/ppermute | solution.py:467
  7.9 1.5 %collective-permute-start.5 = (bf16[144,1024]{1,0:T(8,128)(2,1)S(1)}, bf16[144,1024]{1,0:T(8,128)(2,1)S(1)}, u32[]{:S(2)}, u32[]{:S(2)}) collective-permute-start(bf16[144,1024]{1,0:T(8,128)(2,1)S(1)} %pad_maximum_fusion.2), channel_id=1, source_target_pairs={{0,8},{4,12},{8,0},{12,4},{1,9},{5,13},{9,1},{13,5},{2,10},{6,14},... | collective-permute-start | bytes 884744 | tf_op jit(solution)/shard_map/ppermute | solution.py:464
  9.4 1.1 %copy.21 = bf16[1,128,576]{2,1,0:T(8,128)(2,1)S(1)} copy(bf16[1,128,576]{1,2,0:T(8,128)(2,1)} %param.9) | data formatting | bytes 294912 | tf_op args[1]
  11.0 8.4 %sort.3 = (bf16[16,2,176,1024]{3,2,1,0:T(8,128)(2,1)}, f32[8,128]{1,0:T(8,128)}) custom-call(bf16[16,2816,128]{2,1,0:T(8,128)(2,1)} %bitcast.53), custom_call_target="tpu_custom_call" | custom-call | flops 8800000000 | tf_op jit(solution)/shard_map/sort/pallas_call | solution.py:248
  21.0 1.5 %collective-permute-start.3 = (bf16[144,1024]{1,0:T(8,128)(2,1)S(1)}, bf16[144,1024]{1,0:T(8,128)(2,1)S(1)}, u32[]{:S(2)}, u32[]{:S(2)}) collective-permute-start(bf16[144,1024]{1,0:T(8,128)(2,1)S(1)} %collective-permute-done.2), channel_id=1, source_target_pairs={{0,8},{4,12},{8,0},{12,4},{1,9},{5,13},{9,1},{13,5},{2,10},{6,14},... | collective-permute-start | bytes 884744 | tf_op jit(solution)/shard_map/ppermute | solution.py:464
  23.6 5.8 %sort.4 = (bf16[16,2,176,1024]{3,2,1,0:T(8,128)(2,1)}, f32[8,128]{1,0:T(8,128)}) custom-call(bf16[16,2816,128]{2,1,0:T(8,128)(2,1)} %bitcast.54, bf16[16,2,176,1024]{3,2,1,0:T(8,128)(2,1)} %get-tuple-element.34.refs_0_, bf16[144,1024]{1,0:T(8,128)(2,1)S(1)} %collective-permute-done.7.refs_1_.a_ref), custom_call_target="tpu_custom_call", output_to_operand_aliasing={{0}: (1, {})} | custom-call | flops 8800000000 | tf_op jit(solution)/shard_map/sort/pallas_call | solution.py:248
  29.5 1.5 %collective-permute-done.3.refs_1_ = bf16[144,1024]{1,0:T(8,128)(2,1)S(1)} collective-permute-done((bf16[144,1024]{1,0:T(8,128)(2,1)S(1)}, bf16[144,1024]{1,0:T(8,128)(2,1)S(1)}, u32[]{:S(2)}, u32[]{:S(2)}) %collective-permute-start.3) | collective-permute-done | bytes 294944 | tf_op jit(solution)/shard_map/ppermute | solution.py:464
  31.5 5.1 %sort.5 = (bf16[16,2,176,1024]{3,2,1,0:T(8,128)(2,1)}, f32[8,128]{1,0:T(8,128)S(1)}) custom-call(bf16[16,2816,128]{2,1,0:T(8,128)(2,1)} %bitcast.55, bf16[16,2,176,1024]{3,2,1,0:T(8,128)(2,1)} %get-tuple-element.35.refs_0_, bf16[144,1024]{1,0:T(8,128)(2,1)S(1)} %collective-permute-done.3.refs_1_), custom_call_target="tpu_custom_call", output_to_operand_aliasing={{0}: (1, {})} | custom-call | flops 8800000000 | tf_op jit(solution)/shard_map/sort/pallas_call | solution.py:248
  38.0 1.6 %dispatch.5 = (bf16[16,64,1024]{2,1,0:T(8,128)(2,1)S(1)}, f32[16,64,128]{2,1,0:T(8,128)S(1)}, bf16[4,256,128]{2,1,0:T(8,128)(2,1)S(1)}, f32[8,128]{1,0:T(8,128)S(1)}) custom-call(s32[1]{0:T(128)} %bitcast.13.base_ref, bf16[64,1024]{1,0:T(8,128)(2,1)S(1)} %fusion.rw_ref, bf16[288,1024]{1,0:T(8,128)(2,1)S(1)} %pad_maximum_fusion.refs_0_.refs_1_, ...), custom_call_target="tpu_custom_call" | custom-call | flops 3300000000 | tf_op jit(solution)/shard_map/dispatch/pallas_call | solution.py:153
  39.6 1.5 %dispatch.6 = (bf16[16,64,1024]{2,1,0:T(8,128)(2,1)S(1)}, f32[16,64,128]{2,1,0:T(8,128)S(1)}, bf16[4,256,128]{2,1,0:T(8,128)(2,1)S(1)}) custom-call(s32[1]{0:T(128)} %bitcast.13.base_ref, bf16[64,1024]{1,0:T(8,128)(2,1)S(1)} %fusion.rw_ref, bf16[288,1024]{1,0:T(8,128)(2,1)S(1)} %stack.21.refs_0_.refs_1_, bf16[288,1024]{1,0:T(8,128)(2,1)S(1)} %stack.21.refs_0_.refs_1_, ...), custom_call_target="tpu_custom_call" | custom-call | flops 3300000000 | tf_op jit(solution)/shard_map/dispatch/pallas_call | solution.py:153
  41.1 1.5 %dispatch.4 = (bf16[16,64,1024]{2,1,0:T(8,128)(2,1)S(1)}, f32[16,64,128]{2,1,0:T(8,128)S(1)}, bf16[4,256,128]{2,1,0:T(8,128)(2,1)S(1)}) custom-call(s32[1]{0:T(128)} %bitcast.13.base_ref, bf16[64,1024]{1,0:T(8,128)(2,1)S(1)} %fusion.rw_ref, bf16[288,1024]{1,0:T(8,128)(2,1)S(1)} %constant_dynamic-update-slice_fusion.refs_0_.refs_1_, ...), custom_call_target="tpu_custom_call" | custom-call | flops 3300000000 | tf_op jit(solution)/shard_map/dispatch/pallas_call | solution.py:153
  42.6 1.5 %dispatch.7 = (bf16[16,64,1024]{2,1,0:T(8,128)(2,1)S(1)}, f32[16,64,128]{2,1,0:T(8,128)S(1)}, bf16[4,256,128]{2,1,0:T(8,128)(2,1)S(1)}) custom-call(s32[1]{0:T(128)} %bitcast.13.base_ref, bf16[64,1024]{1,0:T(8,128)(2,1)S(1)} %fusion.rw_ref, bf16[288,1024]{1,0:T(8,128)(2,1)S(1)} %constant_dynamic-update-slice_fusion.2.refs_0_.refs_1_, ...), custom_call_target="tpu_custom_call" | custom-call | flops 3300000000 | tf_op jit(solution)/shard_map/dispatch/pallas_call | solution.py:153
  44.2 12.8 %experts.1 = (bf16[16,64,1024]{2,1,0:T(8,128)(2,1)S(1)}, bf16[16,64,1024]{2,1,0:T(8,128)(2,1)S(1)}, bf16[16,64,1024]{2,1,0:T(8,128)(2,1)S(1)}, bf16[16,64,1024]{2,1,0:T(8,128)(2,1)S(1)}) custom-call(bf16[16,64,1024]{2,1,0:T(8,128)(2,1)S(1)} %get-tuple-element.33.refs_0_, bf16[16,64,1024]{2,1,0:T(8,128)(2,1)S(1)} %get-tuple-element.37.refs_1_, ...), custom_call_target="tpu_custom_call" | custom-call | flops 6600000000 | tf_op jit(solution)/shard_map/experts/pallas_call | solution.py:329
  59.8 1.5 %collective-permute-start.16 = (bf16[1,128,1024]{2,1,0:T(8,128)(2,1)S(1)}, bf16[1,128,1024]{2,1,0:T(8,128)(2,1)S(1)}, u32[]{:S(2)}, u32[]{:S(2)}) collective-permute-start(bf16[1,128,1024]{2,1,0:T(8,128)(2,1)S(1)} %add_convert_fusion.5), channel_id=1, source_target_pairs={{0,8},{4,12},{8,0},{12,4},{1,9},{5,13},{9,1},{13,5},{2,10},{6,14},... | collective-permute-start | bytes 786440 | tf_op jit(solution)/shard_map/ppermute | solution.py:464
  62.8 6.2 %collective-permute-done.16 = bf16[1,128,1024]{2,1,0:T(8,128)(2,1)S(1)} collective-permute-done((bf16[1,128,1024]{2,1,0:T(8,128)(2,1)S(1)}, bf16[1,128,1024]{2,1,0:T(8,128)(2,1)S(1)}, u32[]{:S(2)}, u32[]{:S(2)}) %collective-permute-start.16) | collective-permute-done | bytes 262176 | tf_op jit(solution)/shard_map/ppermute | solution.py:464
  69.1 1.2 %collective-permute-start.17 = (bf16[1,128,1024]{2,1,0:T(8,128)(2,1)S(1)}, bf16[1,128,1024]{2,1,0:T(8,128)(2,1)S(1)}, u32[]{:S(2)}, u32[]{:S(2)}) collective-permute-start(bf16[1,128,1024]{2,1,0:T(8,128)(2,1)S(1)} %add_convert_fusion.4), channel_id=1, source_target_pairs={{0,1},{1,0},{2,3},{3,2},{4,5},{5,4},{6,7},{7,6},{8,9},{9,8},{10,11... | collective-permute-start | bytes 786440 | tf_op jit(solution)/shard_map/ppermute | solution.py:467
  70.4 1.5 %collective-permute-start.20 = (bf16[1,128,1024]{2,1,0:T(8,128)(2,1)S(1)}, bf16[1,128,1024]{2,1,0:T(8,128)(2,1)S(1)}, u32[]{:S(2)}, u32[]{:S(2)}) collective-permute-start(bf16[1,128,1024]{2,1,0:T(8,128)(2,1)S(1)} %add_convert_fusion.2), channel_id=1, source_target_pairs={{0,8},{4,12},{8,0},{12,4},{1,9},{5,13},{9,1},{13,5},{2,10},{6,14},... | collective-permute-start | bytes 786440 | tf_op jit(solution)/shard_map/ppermute | solution.py:464
  72.6 2.0 %collective-permute-done.14 = bf16[1,128,1024]{2,1,0:T(8,128)(2,1)S(1)} collective-permute-done((bf16[1,128,1024]{2,1,0:T(8,128)(2,1)S(1)}, bf16[1,128,1024]{2,1,0:T(8,128)(2,1)S(1)}, u32[]{:S(2)}, u32[]{:S(2)}) %collective-permute-start.14) | collective-permute-done | bytes 262176 | tf_op jit(solution)/shard_map/ppermute | solution.py:464
  74.6 2.1 %collective-permute-done.17 = bf16[1,128,1024]{2,1,0:T(8,128)(2,1)S(1)} collective-permute-done((bf16[1,128,1024]{2,1,0:T(8,128)(2,1)S(1)}, bf16[1,128,1024]{2,1,0:T(8,128)(2,1)S(1)}, u32[]{:S(2)}, u32[]{:S(2)}) %collective-permute-start.17) | collective-permute-done | bytes 262176 | tf_op jit(solution)/shard_map/ppermute | solution.py:467
  76.9 2.3 %collective-permute-start.18 = (bf16[1,128,1024]{2,1,0:T(8,128)(2,1)S(1)}, bf16[1,128,1024]{2,1,0:T(8,128)(2,1)S(1)}, u32[]{:S(2)}, u32[]{:S(2)}) collective-permute-start(bf16[1,128,1024]{2,1,0:T(8,128)(2,1)S(1)} %add_convert_fusion.3.refs_0_), channel_id=1, source_target_pairs={{0,3},{1,2},{2,1},{3,0},{4,7},{5,6},{6,5},{7,4},{8,11},{9,10},{10,... | collective-permute-start | bytes 786440 | tf_op jit(solution)/shard_map/ppermute | solution.py:467
  80.3 1.2 %collective-permute-start.21 = (bf16[1,128,1024]{2,1,0:T(8,128)(2,1)S(1)}, bf16[1,128,1024]{2,1,0:T(8,128)(2,1)S(1)}, u32[]{:S(2)}, u32[]{:S(2)}) collective-permute-start(bf16[1,128,1024]{2,1,0:T(8,128)(2,1)S(1)} %join.1), channel_id=1, source_target_pairs={{0,1},{1,0},{2,3},{3,2},{4,5},{5,4},{6,7},{7,6},{8,9},{9,8},{10,11... | collective-permute-start | bytes 786440 | tf_op jit(solution)/shard_map/ppermute | solution.py:467
  81.5 6.2 %attention.1 = bf16[128,4096]{1,0:T(8,128)(2,1)} custom-call(s32[128,1]{1,0:T(8,128)S(1)} %copy.22.first_ref, s32[128,1]{1,0:T(8,128)S(1)} %copy.23.last_ref, s32[1,512]{1,0:T(1,128)S(1)} %bitcast.39, bf16[128,4608]{1,0:T(8,128)(2,1)S(1)} %bitcast.41, bf16[256,576]{1,0:T(8,128)(2,1)S(1)} %pad_maximum_fusion.1.refs_0_.refs_1_, ...), custom_call_target="tpu_custom_call" | custom-call | flops 6600000000 | tf_op jit(solution)/shard_map/attention/pallas_call | solution.py:433
  88.3 2.7 %collective-permute-done.21 = bf16[1,128,1024]{2,1,0:T(8,128)(2,1)S(1)} collective-permute-done((bf16[1,128,1024]{2,1,0:T(8,128)(2,1)S(1)}, bf16[1,128,1024]{2,1,0:T(8,128)(2,1)S(1)}, u32[]{:S(2)}, u32[]{:S(2)}) %collective-permute-start.21) | collective-permute-done | bytes 262176 | tf_op jit(solution)/shard_map/ppermute | solution.py:467
  (83 shorter events, 15.0 us)
Async XLA Ops:
  2.3 20.8 %collective-permute-start.7 = (bf16[144,1024]{1,0:T(8,128)(2,1)S(1)}, bf16[144,1024]{1,0:T(8,128)(2,1)S(1)}, u32[]{:S(2)}, u32[]{:S(2)}) collective-permute-start(bf16[144,1024]{1,0:T(8,128)(2,1)S(1)} %pad_maximum_fusion.2), channel_id=1, source_target_pairs={{0,1},{1,0},{2,3},{3,2},{4,5},{5,4},{6,7},{7,6},{8,9},{9,8},{10,11... | collective-permute-start | bytes 884744 | tf_op jit(solution)/shard_map/ppermute | solution.py:467
  5.4 15.6 %collective-permute-start.2 = (bf16[144,1024]{1,0:T(8,128)(2,1)S(1)}, bf16[144,1024]{1,0:T(8,128)(2,1)S(1)}, u32[]{:S(2)}, u32[]{:S(2)}) collective-permute-start(bf16[144,1024]{1,0:T(8,128)(2,1)S(1)} %pad_maximum_fusion.2), channel_id=1, source_target_pairs={{0,3},{1,2},{2,1},{3,0},{4,7},{5,6},{6,5},{7,4},{8,11},{9,10},{10,... | collective-permute-start | bytes 884744 | tf_op jit(solution)/shard_map/ppermute | solution.py:467
  7.9 12.4 %collective-permute-start.5 = (bf16[144,1024]{1,0:T(8,128)(2,1)S(1)}, bf16[144,1024]{1,0:T(8,128)(2,1)S(1)}, u32[]{:S(2)}, u32[]{:S(2)}) collective-permute-start(bf16[144,1024]{1,0:T(8,128)(2,1)S(1)} %pad_maximum_fusion.2), channel_id=1, source_target_pairs={{0,8},{4,12},{8,0},{12,4},{1,9},{5,13},{9,1},{13,5},{2,10},{6,14},... | collective-permute-start | bytes 884744 | tf_op jit(solution)/shard_map/ppermute | solution.py:464
  10.4 47.6 %collective-permute-start = (bf16[128,576]{1,0:T(8,128)(2,1)S(1)}, bf16[128,576]{1,0:T(8,128)(2,1)S(1)}, u32[]{:S(2)}, u32[]{:S(2)}) collective-permute-start(bf16[128,576]{1,0:T(8,128)(2,1)S(1)} %bitcast.44), channel_id=1, source_target_pairs={{0,8},{4,12},{8,0},{12,4},{1,9},{5,13},{9,1},{13,5},{2,10},{6,14},... | collective-permute-start | bytes 442376 | tf_op jit(solution)/shard_map/ppermute | solution.py:464
  20.4 17.6 %collective-permute-start.6 = (bf16[288,1024]{1,0:T(8,128)(2,1)S(1)}, bf16[288,1024]{1,0:T(8,128)(2,1)S(1)}, u32[]{:S(2)}, u32[]{:S(2)}) collective-permute-start(bf16[288,1024]{1,0:T(8,128)(2,1)S(1)} %pad_maximum_fusion.refs_0_.refs_1_), channel_id=1, source_target_pairs={{0,4},{4,0},{8,12},{12,8},{1,5},{5,1},{9,13},{13,9},{2,6},{6,2},{1... | collective-permute-start | bytes 1769480 | tf_op jit(solution)/shard_map/ppermute | solution.py:464
  21.0 9.9 %collective-permute-start.3 = (bf16[144,1024]{1,0:T(8,128)(2,1)S(1)}, bf16[144,1024]{1,0:T(8,128)(2,1)S(1)}, u32[]{:S(2)}, u32[]{:S(2)}) collective-permute-start(bf16[144,1024]{1,0:T(8,128)(2,1)S(1)} %collective-permute-done.2), channel_id=1, source_target_pairs={{0,8},{4,12},{8,0},{12,4},{1,9},{5,13},{9,1},{13,5},{2,10},{6,14},... | collective-permute-start | bytes 884744 | tf_op jit(solution)/shard_map/ppermute | solution.py:464
  22.5 14.2 %collective-permute-start.10 = (bf16[144,1024]{1,0:T(8,128)(2,1)S(1)}, bf16[144,1024]{1,0:T(8,128)(2,1)S(1)}, u32[]{:S(2)}, u32[]{:S(2)}) collective-permute-start(bf16[144,1024]{1,0:T(8,128)(2,1)S(1)} %collective-permute-done.2), channel_id=1, source_target_pairs={{0,1},{1,0},{2,3},{3,2},{4,5},{5,4},{6,7},{7,6},{8,9},{9,8},{10,11... | collective-permute-start | bytes 884744 | tf_op jit(solution)/shard_map/ppermute | solution.py:467
  23.1 13.5 %collective-permute-start.8 = (bf16[144,1024]{1,0:T(8,128)(2,1)S(1)}, bf16[144,1024]{1,0:T(8,128)(2,1)S(1)}, u32[]{:S(2)}, u32[]{:S(2)}) collective-permute-start(bf16[144,1024]{1,0:T(8,128)(2,1)S(1)} %collective-permute-done.7.refs_1_.a_ref), channel_id=1, source_target_pairs={{0,8},{4,12},{8,0},{12,4},{1,9},{5,13},{9,1},{13,5},{2,10},{6,14},... | collective-permute-start | bytes 884744 | tf_op jit(solution)/shard_map/ppermute | solution.py:464
  30.9 6.9 %collective-permute-start.11 = (bf16[144,1024]{1,0:T(8,128)(2,1)S(1)}, bf16[144,1024]{1,0:T(8,128)(2,1)S(1)}, u32[]{:S(2)}, u32[]{:S(2)}) collective-permute-start(bf16[144,1024]{1,0:T(8,128)(2,1)S(1)} %collective-permute-done.3.refs_1_), channel_id=1, source_target_pairs={{0,1},{1,0},{2,3},{3,2},{4,5},{5,4},{6,7},{7,6},{8,9},{9,8},{10,11... | collective-permute-start | bytes 884744 | tf_op jit(solution)/shard_map/ppermute | solution.py:467
  36.6 2.9 %collective-permute-start.9 = (bf16[288,1024]{1,0:T(8,128)(2,1)S(1)}, bf16[288,1024]{1,0:T(8,128)(2,1)S(1)}, u32[]{:S(2)}, u32[]{:S(2)}) collective-permute-start(bf16[288,1024]{1,0:T(8,128)(2,1)S(1)} %stack.21.refs_0_.refs_1_), channel_id=1, source_target_pairs={{0,4},{4,0},{8,12},{12,8},{1,5},{5,1},{9,13},{13,9},{2,6},{6,2},{1... | collective-permute-start | bytes 1769480 | tf_op jit(solution)/shard_map/ppermute | solution.py:464
  36.8 4.3 %collective-permute-start.4 = (bf16[288,1024]{1,0:T(8,128)(2,1)S(1)}, bf16[288,1024]{1,0:T(8,128)(2,1)S(1)}, u32[]{:S(2)}, u32[]{:S(2)}) collective-permute-start(bf16[288,1024]{1,0:T(8,128)(2,1)S(1)} %constant_dynamic-update-slice_fusion.refs_0_.refs_1_), channel_id=1, source_target_pairs={{0,4},{4,0},{8,12},{12,8},{1,5},{5,1},{9,13},{13,9},{2,6},{6,2},{1... | collective-permute-start | bytes 1769480 | tf_op jit(solution)/shard_map/ppermute | solution.py:464
  37.8 4.8 %collective-permute-start.12 = (bf16[288,1024]{1,0:T(8,128)(2,1)S(1)}, bf16[288,1024]{1,0:T(8,128)(2,1)S(1)}, u32[]{:S(2)}, u32[]{:S(2)}) collective-permute-start(bf16[288,1024]{1,0:T(8,128)(2,1)S(1)} %constant_dynamic-update-slice_fusion.2.refs_0_.refs_1_), channel_id=1, source_target_pairs={{0,4},{4,0},{8,12},{12,8},{1,5},{5,1},{9,13},{13,9},{2,6},{6,2},{1... | collective-permute-start | bytes 1769480 | tf_op jit(solution)/shard_map/ppermute | solution.py:464
  57.5 2.3 %collective-permute-start.15 = (bf16[1,256,1024]{2,1,0:T(8,128)(2,1)S(1)}, bf16[1,256,1024]{2,1,0:T(8,128)(2,1)S(1)}, u32[]{:S(2)}, u32[]{:S(2)}) collective-permute-start(bf16[1,256,1024]{2,1,0:T(8,128)(2,1)S(1)} %get-tuple-element.51), channel_id=1, source_target_pairs={{0,4},{4,0},{8,12},{12,8},{1,5},{5,1},{9,13},{13,9},{2,6},{6,2},{1... | collective-permute-start | bytes 1572872 | tf_op jit(solution)/shard_map/ppermute | solution.py:464
  58.1 23.5 %collective-permute-start.1 = (bf16[256,576]{1,0:T(8,128)(2,1)S(1)}, bf16[256,576]{1,0:T(8,128)(2,1)S(1)}, u32[]{:S(2)}, u32[]{:S(2)}) collective-permute-start(bf16[256,576]{1,0:T(8,128)(2,1)S(1)} %pad_maximum_fusion.1.refs_0_.refs_1_), channel_id=1, source_target_pairs={{0,4},{4,0},{8,12},{12,8},{1,5},{5,1},{9,13},{13,9},{2,6},{6,2},{1... | collective-permute-start | bytes 884744 | tf_op jit(solution)/shard_map/ppermute | solution.py:464
  58.6 3.5 %collective-permute-start.13 = (bf16[1,256,1024]{2,1,0:T(8,128)(2,1)S(1)}, bf16[1,256,1024]{2,1,0:T(8,128)(2,1)S(1)}, u32[]{:S(2)}, u32[]{:S(2)}) collective-permute-start(bf16[1,256,1024]{2,1,0:T(8,128)(2,1)S(1)} %get-tuple-element.47), channel_id=1, source_target_pairs={{0,4},{4,0},{8,12},{12,8},{1,5},{5,1},{9,13},{13,9},{2,6},{6,2},{1... | collective-permute-start | bytes 1572872 | tf_op jit(solution)/shard_map/ppermute | solution.py:464
  59.7 10.7 %collective-permute-start.19 = (bf16[1,256,1024]{2,1,0:T(8,128)(2,1)S(1)}, bf16[1,256,1024]{2,1,0:T(8,128)(2,1)S(1)}, u32[]{:S(2)}, u32[]{:S(2)}) collective-permute-start(bf16[1,256,1024]{2,1,0:T(8,128)(2,1)S(1)} %get-tuple-element.55), channel_id=1, source_target_pairs={{0,4},{4,0},{8,12},{12,8},{1,5},{5,1},{9,13},{13,9},{2,6},{6,2},{1... | collective-permute-start | bytes 1572872 | tf_op jit(solution)/shard_map/ppermute | solution.py:464
  59.8 9.2 %collective-permute-start.16 = (bf16[1,128,1024]{2,1,0:T(8,128)(2,1)S(1)}, bf16[1,128,1024]{2,1,0:T(8,128)(2,1)S(1)}, u32[]{:S(2)}, u32[]{:S(2)}) collective-permute-start(bf16[1,128,1024]{2,1,0:T(8,128)(2,1)S(1)} %add_convert_fusion.5), channel_id=1, source_target_pairs={{0,8},{4,12},{8,0},{12,4},{1,9},{5,13},{9,1},{13,5},{2,10},{6,14},... | collective-permute-start | bytes 786440 | tf_op jit(solution)/shard_map/ppermute | solution.py:464
  61.9 10.1 %collective-permute-start.22 = (bf16[1,256,1024]{2,1,0:T(8,128)(2,1)S(1)}, bf16[1,256,1024]{2,1,0:T(8,128)(2,1)S(1)}, u32[]{:S(2)}, u32[]{:S(2)}) collective-permute-start(bf16[1,256,1024]{2,1,0:T(8,128)(2,1)S(1)} %get-tuple-element.59), channel_id=1, source_target_pairs={{0,4},{4,0},{8,12},{12,8},{1,5},{5,1},{9,13},{13,9},{2,6},{6,2},{1... | collective-permute-start | bytes 1572872 | tf_op jit(solution)/shard_map/ppermute | solution.py:464
  62.2 12.4 %collective-permute-start.14 = (bf16[1,128,1024]{2,1,0:T(8,128)(2,1)S(1)}, bf16[1,128,1024]{2,1,0:T(8,128)(2,1)S(1)}, u32[]{:S(2)}, u32[]{:S(2)}) collective-permute-start(bf16[1,128,1024]{2,1,0:T(8,128)(2,1)S(1)} %add_convert_fusion.6), channel_id=1, source_target_pairs={{0,8},{4,12},{8,0},{12,4},{1,9},{5,13},{9,1},{13,5},{2,10},{6,14},... | collective-permute-start | bytes 786440 | tf_op jit(solution)/shard_map/ppermute | solution.py:464
  69.1 7.6 %collective-permute-start.17 = (bf16[1,128,1024]{2,1,0:T(8,128)(2,1)S(1)}, bf16[1,128,1024]{2,1,0:T(8,128)(2,1)S(1)}, u32[]{:S(2)}, u32[]{:S(2)}) collective-permute-start(bf16[1,128,1024]{2,1,0:T(8,128)(2,1)S(1)} %add_convert_fusion.4), channel_id=1, source_target_pairs={{0,1},{1,0},{2,3},{3,2},{4,5},{5,4},{6,7},{7,6},{8,9},{9,8},{10,11... | collective-permute-start | bytes 786440 | tf_op jit(solution)/shard_map/ppermute | solution.py:467
  70.4 9.8 %collective-permute-start.20 = (bf16[1,128,1024]{2,1,0:T(8,128)(2,1)S(1)}, bf16[1,128,1024]{2,1,0:T(8,128)(2,1)S(1)}, u32[]{:S(2)}, u32[]{:S(2)}) collective-permute-start(bf16[1,128,1024]{2,1,0:T(8,128)(2,1)S(1)} %add_convert_fusion.2), channel_id=1, source_target_pairs={{0,8},{4,12},{8,0},{12,4},{1,9},{5,13},{9,1},{13,5},{2,10},{6,14},... | collective-permute-start | bytes 786440 | tf_op jit(solution)/shard_map/ppermute | solution.py:464
  72.0 16.3 %collective-permute-start.23 = (bf16[1,128,1024]{2,1,0:T(8,128)(2,1)S(1)}, bf16[1,128,1024]{2,1,0:T(8,128)(2,1)S(1)}, u32[]{:S(2)}, u32[]{:S(2)}) collective-permute-start(bf16[1,128,1024]{2,1,0:T(8,128)(2,1)S(1)} %add_convert_fusion.1), channel_id=1, source_target_pairs={{0,8},{4,12},{8,0},{12,4},{1,9},{5,13},{9,1},{13,5},{2,10},{6,14},... | collective-permute-start | bytes 786440 | tf_op jit(solution)/shard_map/ppermute | solution.py:464
  76.9 14.1 %collective-permute-start.18 = (bf16[1,128,1024]{2,1,0:T(8,128)(2,1)S(1)}, bf16[1,128,1024]{2,1,0:T(8,128)(2,1)S(1)}, u32[]{:S(2)}, u32[]{:S(2)}) collective-permute-start(bf16[1,128,1024]{2,1,0:T(8,128)(2,1)S(1)} %add_convert_fusion.3.refs_0_), channel_id=1, source_target_pairs={{0,3},{1,2},{2,1},{3,0},{4,7},{5,6},{6,5},{7,4},{8,11},{9,10},{10,... | collective-permute-start | bytes 786440 | tf_op jit(solution)/shard_map/ppermute | solution.py:467
  80.3 10.7 %collective-permute-start.21 = (bf16[1,128,1024]{2,1,0:T(8,128)(2,1)S(1)}, bf16[1,128,1024]{2,1,0:T(8,128)(2,1)S(1)}, u32[]{:S(2)}, u32[]{:S(2)}) collective-permute-start(bf16[1,128,1024]{2,1,0:T(8,128)(2,1)S(1)} %join.1), channel_id=1, source_target_pairs={{0,1},{1,0},{2,3},{3,2},{4,5},{5,4},{6,7},{7,6},{8,9},{9,8},{10,11... | collective-permute-start | bytes 786440 | tf_op jit(solution)/shard_map/ppermute | solution.py:467
  (6 other events, 36.3 us)

commit v15 on v14

--- a/solution.py
+++ b/solution.py
@@ -165,15 +165,19 @@
 def fetch(sources, slots, sem, step, steps, first, start=0):
     depth, group = slots[0].shape[:2]
 
-    def copies(at):
+    def copies(at, e):
         slot = lax.rem(at, depth)
         return [
             pltpu.make_async_copy(
                 source.at[start + at * group + e], held.at[slot, e], sem.at[i, slot, e]
             )
             for i, (source, held) in enumerate(zip(sources, slots))
-            for e in range(group)
         ]
+
+    def begin(at):
+        for e in range(group):
+            for copy in copies(at, e):
+                copy.start()
 
     @pl.when(first & (step == 0))
     def _():
@@ -181,20 +185,24 @@
 
             @pl.when(ahead < steps)
             def _():
-                for copy in copies(step + ahead):
-                    copy.start()
+                begin(step + ahead)
 
     @pl.when(first & (step + depth - 1 < steps))
     def _():
-        for copy in copies(step + depth - 1):
-            copy.start()
-
-    @pl.when(first)
-    def _():
-        for copy in copies(step):
-            copy.wait()
-
-    return lax.rem(step, depth)
+        begin(step + depth - 1)
+
+    def ready(e):
+        if first is True:
+            for copy in copies(step, e):
+                copy.wait()
+            return
+
+        @pl.when(first)
+        def _():
+            for copy in copies(step, e):
+                copy.wait()
+
+    return lax.rem(step, depth), ready
 
 
 def sort_kernel(start, gu_ref, *refs):
@@ -203,34 +211,38 @@
     step, steps = pl.program_id(0), pl.num_programs(0)
     _, group, _, hidden, width = made.shape
     chunks = width // LANES
-    slot = fetch([gu_ref], [held], in_sem, step, steps, step >= 0, start)
+    slot, ready = fetch([gu_ref], [held], in_sem, step, steps, True, start)
     to = lax.rem(step, 2)
 
-    def leave(at):
+    def leave(at, e):
         to = lax.rem(at, 2)
         return pltpu.make_async_copy(
-            made.at[to], out_ref.at[pl.ds(start + at * group, group)], out_sem.at[to]
+            made.at[to, e], out_ref.at[start + at * group + e], out_sem.at[to, e]
         )
 
     @pl.when(step >= 2)
     def _():
-        leave(step - 2).wait()
+        for e in range(group):
+            leave(step - 2, e).wait()
 
     for e in range(group):
+        ready(e)
         wide[e] = held[slot, e].astype(jnp.float32)
         for z in range(2):
             for c in range(chunks):
                 part = wide[e, pl.ds(2 * c + z, hidden, stride=2 * chunks), :]
                 made[to, e, z, :, c * LANES : (c + 1) * LANES] = part.astype(jnp.bfloat16)
-    leave(step).start()
+        leave(step, e).start()
 
     @pl.when(step == steps - 1)
     def _():
         @pl.when(step >= 1)
         def _():
-            leave(step - 1).wait()
-
-        leave(step).wait()
+            for e in range(group):
+                leave(step - 1, e).wait()
+
+        for e in range(group):
+            leave(step, e).wait()
 
 
 def sort_rows(gate_up, behind):
@@ -260,7 +272,7 @@
                     pltpu.VMEM((2, group, 2, hidden, width), jnp.bfloat16),
                     pltpu.VMEM((group,) + gu.shape[1:], jnp.float32),
                     pltpu.SemaphoreType.DMA((1, DEPTH, group)),
-                    pltpu.SemaphoreType.DMA((2,)),
+                    pltpu.SemaphoreType.DMA((2, group)),
                 ],
                 "sort",
                 VMEM_SORT,
@@ -296,7 +308,7 @@
     outs, (gu, down, sem) = refs[-3 - n : -3], refs[-3:]
     group = gu.shape[1]
     size = rows[0].shape[1]
-    slot = fetch(
+    slot, ready = fetch(
         [gu_ref, down_ref],
         [gu, down],
         sem,
@@ -304,6 +316,8 @@
         pl.num_programs(0),
         pl.program_id(1) == 0,
     )
+    for e in range(group):
+        ready(e)
     for e in range(group):
         held = jnp.concatenate([r[e] for r in rows], axis=0)
         g = lax.dot_general(held, gu[slot, e, 0], NT, preferred_element_type=jnp.float32)
@@ -323,7 +337,7 @@
     local, slots, width = rows[0].shape
     size = min(slots, EXPERT_ROWS)
     hidden = down.shape[1]
-    group = 2 if local % 2 == 0 else 1
+    group = 4 if local % 4 == 0 else 1
     rows_spec = pl.BlockSpec((group, size, width), lambda e, i: (e, i, 0))
     weight_spec = pl.BlockSpec((group, size, LANES), lambda e, i: (e, i, 0))
     return call(
@@ -334,9 +348,9 @@
         [rows_spec] * n,
         [jax.ShapeDtypeStruct(r.shape, jnp.bfloat16) for r in rows],
         [
-            pltpu.VMEM((DEPTH, group, 2, hidden, width), jnp.bfloat16),
-            pltpu.VMEM((DEPTH, group, hidden, width), jnp.bfloat16),
-            pltpu.SemaphoreType.DMA((2, DEPTH, group)),
+            pltpu.VMEM((2, group, 2, hidden, width), jnp.bfloat16),
+            pltpu.VMEM((2, group, hidden, width), jnp.bfloat16),
+            pltpu.SemaphoreType.DMA((2, 2, group)),
         ],
         "experts",
         VMEM_EXPERTS,

time: 92.2 us -> 91.6 us (level)
  waiting for transfers between devices: 16.5 us -> 19 us
  Pallas kernels: 46.3 us -> 44.4 us
  starting transfers between devices: 22.2 us -> 21 us
    pallas_call x3, Pallas kernels: 19.3 us -> 17.9 us  [sort_rows(): call(functools.partial(sort_kernel, start), 8, ((end - start) // group,),...]
    ppermute x17, waiting for transfers between devices: 10.7 us -> 12 us  [flip(): return lax.ppermute(a, 'ctx', [(i, i ^ bit) for i in range(n_ctx)])]
    ppermute x7, starting transfers between devices: 11.4 us -> 10.2 us  [shift(): return lax.ppermute(a, 'exp', [(i, i ^ d) for i in range(n_exp)])]
    ppermute x7, waiting for transfers between devices: 5.82 us -> 7.01 us  [shift(): return lax.ppermute(a, 'exp', [(i, i ^ d) for i in range(n_exp)])]
  transfers between devices with their start and end apart: 24 -> 24, of which waited for: 8 -> 8; matrix products, arithmetic and copies ran while one was open for 4% -> 4% of each run, Pallas kernels for 50% -> 49%
where the time goes in v15:
time: 91.6 us; the launch traced here: 91.3 us
  Pallas kernels  44.4 us (48%)
  starting transfers between devices  21 us (23%)
  waiting for transfers between devices  19 us (21%)
  other arithmetic  3.8 us (4%)
  local copies, waits for them, and re-layouts  2.17 us (2%)
  between operations  0.97 us (1%)
    pallas_call x3, Pallas kernels, sort_rows(): call(functools.partial(sort_kernel, start), 8, ((end - start) // group,),...  17.9 us
    pallas_call x1, Pallas kernels, experts(): call(functools.partial(expert_kernel, n), 6, (local // group, slots // si...  12.2 us
    ppermute x17, waiting for transfers between devices, flip(): return lax.ppermute(a, 'ctx', [(i, i ^ bit) for i in range(n_ctx)])  12 us
    ppermute x17, starting transfers between devices, flip(): return lax.ppermute(a, 'ctx', [(i, i ^ bit) for i in range(n_ctx)])  10.8 us
    ppermute x7, starting transfers between devices, shift(): return lax.ppermute(a, 'exp', [(i, i ^ d) for i in range(n_exp)])  10.2 us
    ppermute x7, waiting for transfers between devices, shift(): return lax.ppermute(a, 'exp', [(i, i ^ d) for i in range(n_exp)])  7.01 us
    pallas_call x1, Pallas kernels, attend(): call(functools.partial(attend_kernel, [at for _, at in parts], kdim), 6,...  6.17 us
    pallas_call x4, Pallas kernels, dispatch(): call(functools.partial(dispatch_kernel, starts, n_parts if row is not Non...  6.03 us
  transfers between devices with their start and end apart: 24, of which 8 were waited for; matrix products, arithmetic and copies ran while one was open for 4% of the time, Pallas kernels for 49%

profile of v15, /device:TPU:0, one launch (start us, length us, event | category | flops | bytes accessed | tf_op | source)
XLA Modules:
  0.0 91.3 jit_solution(8493487201930478706)
XLA Ops:
  2.3 3.1 %collective-permute-start.7 = (bf16[144,1024]{1,0:T(8,128)(2,1)S(1)}, bf16[144,1024]{1,0:T(8,128)(2,1)S(1)}, u32[]{:S(2)}, u32[]{:S(2)}) collective-permute-start(bf16[144,1024]{1,0:T(8,128)(2,1)S(1)} %pad_maximum_fusion.2), channel_id=1, source_target_pairs={{0,1},{1,0},{2,3},{3,2},{4,5},{5,4},{6,7},{7,6},{8,9},{9,8},{10,11... | collective-permute-start | bytes 884744 | tf_op jit(solution)/shard_map/ppermute | solution.py:481
  5.4 2.5 %collective-permute-start.2 = (bf16[144,1024]{1,0:T(8,128)(2,1)S(1)}, bf16[144,1024]{1,0:T(8,128)(2,1)S(1)}, u32[]{:S(2)}, u32[]{:S(2)}) collective-permute-start(bf16[144,1024]{1,0:T(8,128)(2,1)S(1)} %pad_maximum_fusion.2), channel_id=1, source_target_pairs={{0,3},{1,2},{2,1},{3,0},{4,7},{5,6},{6,5},{7,4},{8,11},{9,10},{10,... | collective-permute-start | bytes 884744 | tf_op jit(solution)/shard_map/ppermute | solution.py:481
  7.9 1.5 %collective-permute-start.5 = (bf16[144,1024]{1,0:T(8,128)(2,1)S(1)}, bf16[144,1024]{1,0:T(8,128)(2,1)S(1)}, u32[]{:S(2)}, u32[]{:S(2)}) collective-permute-start(bf16[144,1024]{1,0:T(8,128)(2,1)S(1)} %pad_maximum_fusion.2), channel_id=1, source_target_pairs={{0,8},{4,12},{8,0},{12,4},{1,9},{5,13},{9,1},{13,5},{2,10},{6,14},... | collective-permute-start | bytes 884744 | tf_op jit(solution)/shard_map/ppermute | solution.py:478
  9.4 1.1 %copy.21 = bf16[1,128,576]{2,1,0:T(8,128)(2,1)S(1)} copy(bf16[1,128,576]{1,2,0:T(8,128)(2,1)} %param.9) | data formatting | bytes 294912 | tf_op args[1]
  11.0 8.0 %sort.3 = (bf16[16,2,176,1024]{3,2,1,0:T(8,128)(2,1)}, f32[8,128]{1,0:T(8,128)}) custom-call(bf16[16,2816,128]{2,1,0:T(8,128)(2,1)} %bitcast.53), custom_call_target="tpu_custom_call" | custom-call | flops 8800000000 | tf_op jit(solution)/shard_map/sort/pallas_call | solution.py:260
  20.0 1.0 %collective-permute-done.2 = bf16[144,1024]{1,0:T(8,128)(2,1)S(1)} collective-permute-done((bf16[144,1024]{1,0:T(8,128)(2,1)S(1)}, bf16[144,1024]{1,0:T(8,128)(2,1)S(1)}, u32[]{:S(2)}, u32[]{:S(2)}) %collective-permute-start.2) | collective-permute-done | bytes 294944 | tf_op jit(solution)/shard_map/ppermute | solution.py:481
  21.0 1.5 %collective-permute-start.3 = (bf16[144,1024]{1,0:T(8,128)(2,1)S(1)}, bf16[144,1024]{1,0:T(8,128)(2,1)S(1)}, u32[]{:S(2)}, u32[]{:S(2)}) collective-permute-start(bf16[144,1024]{1,0:T(8,128)(2,1)S(1)} %collective-permute-done.2), channel_id=1, source_target_pairs={{0,8},{4,12},{8,0},{12,4},{1,9},{5,13},{9,1},{13,5},{2,10},{6,14},... | collective-permute-start | bytes 884744 | tf_op jit(solution)/shard_map/ppermute | solution.py:478
  23.6 5.3 %sort.4 = (bf16[16,2,176,1024]{3,2,1,0:T(8,128)(2,1)}, f32[8,128]{1,0:T(8,128)}) custom-call(bf16[16,2816,128]{2,1,0:T(8,128)(2,1)} %bitcast.54, bf16[16,2,176,1024]{3,2,1,0:T(8,128)(2,1)} %get-tuple-element.34.refs_0_, bf16[144,1024]{1,0:T(8,128)(2,1)S(1)} %collective-permute-done.7.refs_1_.a_ref), custom_call_target="tpu_custom_call", output_to_operand_aliasing={{0}: (1, {})} | custom-call | flops 8800000000 | tf_op jit(solution)/shard_map/sort/pallas_call | solution.py:260
  29.0 2.0 %collective-permute-done.3.refs_1_ = bf16[144,1024]{1,0:T(8,128)(2,1)S(1)} collective-permute-done((bf16[144,1024]{1,0:T(8,128)(2,1)S(1)}, bf16[144,1024]{1,0:T(8,128)(2,1)S(1)}, u32[]{:S(2)}, u32[]{:S(2)}) %collective-permute-start.3) | collective-permute-done | bytes 294944 | tf_op jit(solution)/shard_map/ppermute | solution.py:478
  31.5 4.6 %sort.5 = (bf16[16,2,176,1024]{3,2,1,0:T(8,128)(2,1)}, f32[8,128]{1,0:T(8,128)S(1)}) custom-call(bf16[16,2816,128]{2,1,0:T(8,128)(2,1)} %bitcast.55, bf16[16,2,176,1024]{3,2,1,0:T(8,128)(2,1)} %get-tuple-element.35.refs_0_, bf16[144,1024]{1,0:T(8,128)(2,1)S(1)} %collective-permute-done.3.refs_1_), custom_call_target="tpu_custom_call", output_to_operand_aliasing={{0}: (1, {})} | custom-call | flops 8800000000 | tf_op jit(solution)/shard_map/sort/pallas_call | solution.py:260
  37.9 1.6 %dispatch.5 = (bf16[16,64,1024]{2,1,0:T(8,128)(2,1)S(1)}, f32[16,64,128]{2,1,0:T(8,128)S(1)}, bf16[4,256,128]{2,1,0:T(8,128)(2,1)S(1)}, f32[8,128]{1,0:T(8,128)S(1)}) custom-call(s32[1]{0:T(128)} %bitcast.13.base_ref, bf16[64,1024]{1,0:T(8,128)(2,1)S(1)} %fusion.rw_ref, bf16[288,1024]{1,0:T(8,128)(2,1)S(1)} %pad_maximum_fusion.refs_0_.refs_1_, ...), custom_call_target="tpu_custom_call" | custom-call | flops 3300000000 | tf_op jit(solution)/shard_map/dispatch/pallas_call | solution.py:153
  39.5 1.5 %dispatch.6 = (bf16[16,64,1024]{2,1,0:T(8,128)(2,1)S(1)}, f32[16,64,128]{2,1,0:T(8,128)S(1)}, bf16[4,256,128]{2,1,0:T(8,128)(2,1)S(1)}) custom-call(s32[1]{0:T(128)} %bitcast.13.base_ref, bf16[64,1024]{1,0:T(8,128)(2,1)S(1)} %fusion.rw_ref, bf16[288,1024]{1,0:T(8,128)(2,1)S(1)} %stack.21.refs_0_.refs_1_, bf16[288,1024]{1,0:T(8,128)(2,1)S(1)} %stack.21.refs_0_.refs_1_, ...), custom_call_target="tpu_custom_call" | custom-call | flops 3300000000 | tf_op jit(solution)/shard_map/dispatch/pallas_call | solution.py:153
  41.0 1.5 %dispatch.4 = (bf16[16,64,1024]{2,1,0:T(8,128)(2,1)S(1)}, f32[16,64,128]{2,1,0:T(8,128)S(1)}, bf16[4,256,128]{2,1,0:T(8,128)(2,1)S(1)}) custom-call(s32[1]{0:T(128)} %bitcast.13.base_ref, bf16[64,1024]{1,0:T(8,128)(2,1)S(1)} %fusion.rw_ref, bf16[288,1024]{1,0:T(8,128)(2,1)S(1)} %constant_dynamic-update-slice_fusion.refs_0_.refs_1_, ...), custom_call_target="tpu_custom_call" | custom-call | flops 3300000000 | tf_op jit(solution)/shard_map/dispatch/pallas_call | solution.py:153
  42.5 1.5 %dispatch.7 = (bf16[16,64,1024]{2,1,0:T(8,128)(2,1)S(1)}, f32[16,64,128]{2,1,0:T(8,128)S(1)}, bf16[4,256,128]{2,1,0:T(8,128)(2,1)S(1)}) custom-call(s32[1]{0:T(128)} %bitcast.13.base_ref, bf16[64,1024]{1,0:T(8,128)(2,1)S(1)} %fusion.rw_ref, bf16[288,1024]{1,0:T(8,128)(2,1)S(1)} %constant_dynamic-update-slice_fusion.2.refs_0_.refs_1_, ...), custom_call_target="tpu_custom_call" | custom-call | flops 3300000000 | tf_op jit(solution)/shard_map/dispatch/pallas_call | solution.py:153
  44.1 12.2 %experts.1 = (bf16[16,64,1024]{2,1,0:T(8,128)(2,1)S(1)}, bf16[16,64,1024]{2,1,0:T(8,128)(2,1)S(1)}, bf16[16,64,1024]{2,1,0:T(8,128)(2,1)S(1)}, bf16[16,64,1024]{2,1,0:T(8,128)(2,1)S(1)}) custom-call(bf16[16,64,1024]{2,1,0:T(8,128)(2,1)S(1)} %get-tuple-element.33.refs_0_, bf16[16,64,1024]{2,1,0:T(8,128)(2,1)S(1)} %get-tuple-element.37.refs_1_, ...), custom_call_target="tpu_custom_call" | custom-call | flops 6600000000 | tf_op jit(solution)/shard_map/experts/pallas_call | solution.py:343
  59.2 1.6 %collective-permute-start.16 = (bf16[1,128,1024]{2,1,0:T(8,128)(2,1)S(1)}, bf16[1,128,1024]{2,1,0:T(8,128)(2,1)S(1)}, u32[]{:S(2)}, u32[]{:S(2)}) collective-permute-start(bf16[1,128,1024]{2,1,0:T(8,128)(2,1)S(1)} %add_convert_fusion.5), channel_id=1, source_target_pairs={{0,8},{4,12},{8,0},{12,4},{1,9},{5,13},{9,1},{13,5},{2,10},{6,14},... | collective-permute-start | bytes 786440 | tf_op jit(solution)/shard_map/ppermute | solution.py:478
  62.2 6.2 %collective-permute-done.16 = bf16[1,128,1024]{2,1,0:T(8,128)(2,1)S(1)} collective-permute-done((bf16[1,128,1024]{2,1,0:T(8,128)(2,1)S(1)}, bf16[1,128,1024]{2,1,0:T(8,128)(2,1)S(1)}, u32[]{:S(2)}, u32[]{:S(2)}) %collective-permute-start.16) | collective-permute-done | bytes 262176 | tf_op jit(solution)/shard_map/ppermute | solution.py:478
  69.3 1.6 %collective-permute-start.20 = (bf16[1,128,1024]{2,1,0:T(8,128)(2,1)S(1)}, bf16[1,128,1024]{2,1,0:T(8,128)(2,1)S(1)}, u32[]{:S(2)}, u32[]{:S(2)}) collective-permute-start(bf16[1,128,1024]{2,1,0:T(8,128)(2,1)S(1)} %add_convert_fusion.2), channel_id=1, source_target_pairs={{0,8},{4,12},{8,0},{12,4},{1,9},{5,13},{9,1},{13,5},{2,10},{6,14},... | collective-permute-start | bytes 786440 | tf_op jit(solution)/shard_map/ppermute | solution.py:478
  71.6 2.4 %collective-permute-done.14 = bf16[1,128,1024]{2,1,0:T(8,128)(2,1)S(1)} collective-permute-done((bf16[1,128,1024]{2,1,0:T(8,128)(2,1)S(1)}, bf16[1,128,1024]{2,1,0:T(8,128)(2,1)S(1)}, u32[]{:S(2)}, u32[]{:S(2)}) %collective-permute-start.14) | collective-permute-done | bytes 262176 | tf_op jit(solution)/shard_map/ppermute | solution.py:478
  73.9 2.1 %collective-permute-done.17 = bf16[1,128,1024]{2,1,0:T(8,128)(2,1)S(1)} collective-permute-done((bf16[1,128,1024]{2,1,0:T(8,128)(2,1)S(1)}, bf16[1,128,1024]{2,1,0:T(8,128)(2,1)S(1)}, u32[]{:S(2)}, u32[]{:S(2)}) %collective-permute-start.17) | collective-permute-done | bytes 262176 | tf_op jit(solution)/shard_map/ppermute | solution.py:481
  76.2 1.9 %collective-permute-start.18 = (bf16[1,128,1024]{2,1,0:T(8,128)(2,1)S(1)}, bf16[1,128,1024]{2,1,0:T(8,128)(2,1)S(1)}, u32[]{:S(2)}, u32[]{:S(2)}) collective-permute-start(bf16[1,128,1024]{2,1,0:T(8,128)(2,1)S(1)} %add_convert_fusion.3.refs_0_), channel_id=1, source_target_pairs={{0,3},{1,2},{2,1},{3,0},{4,7},{5,6},{6,5},{7,4},{8,11},{9,10},{10,... | collective-permute-start | bytes 786440 | tf_op jit(solution)/shard_map/ppermute | solution.py:481
  78.2 1.4 %collective-permute-done.20.c_ref = bf16[1,128,1024]{2,1,0:T(8,128)(2,1)S(1)} collective-permute-done((bf16[1,128,1024]{2,1,0:T(8,128)(2,1)S(1)}, bf16[1,128,1024]{2,1,0:T(8,128)(2,1)S(1)}, u32[]{:S(2)}, u32[]{:S(2)}) %collective-permute-start.20) | collective-permute-done | bytes 262176 | tf_op jit(solution)/shard_map/ppermute | solution.py:478
  80.5 6.2 %attention.1 = bf16[128,4096]{1,0:T(8,128)(2,1)} custom-call(s32[128,1]{1,0:T(8,128)S(1)} %copy.22.first_ref, s32[128,1]{1,0:T(8,128)S(1)} %copy.23.last_ref, s32[1,512]{1,0:T(1,128)S(1)} %bitcast.39, bf16[128,4608]{1,0:T(8,128)(2,1)S(1)} %bitcast.41, bf16[256,576]{1,0:T(8,128)(2,1)S(1)} %pad_maximum_fusion.1.refs_0_.refs_1_, ...), custom_call_target="tpu_custom_call" | custom-call | flops 6600000000 | tf_op jit(solution)/shard_map/attention/pallas_call | solution.py:447
  87.3 3.1 %collective-permute-done.21 = bf16[1,128,1024]{2,1,0:T(8,128)(2,1)S(1)} collective-permute-done((bf16[1,128,1024]{2,1,0:T(8,128)(2,1)S(1)}, bf16[1,128,1024]{2,1,0:T(8,128)(2,1)S(1)}, u32[]{:S(2)}, u32[]{:S(2)}) %collective-permute-start.21) | collective-permute-done | bytes 262176 | tf_op jit(solution)/shard_map/ppermute | solution.py:481
  (83 shorter events, 15.1 us)
Async XLA Ops:
  2.3 20.8 %collective-permute-start.7 = (bf16[144,1024]{1,0:T(8,128)(2,1)S(1)}, bf16[144,1024]{1,0:T(8,128)(2,1)S(1)}, u32[]{:S(2)}, u32[]{:S(2)}) collective-permute-start(bf16[144,1024]{1,0:T(8,128)(2,1)S(1)} %pad_maximum_fusion.2), channel_id=1, source_target_pairs={{0,1},{1,0},{2,3},{3,2},{4,5},{5,4},{6,7},{7,6},{8,9},{9,8},{10,11... | collective-permute-start | bytes 884744 | tf_op jit(solution)/shard_map/ppermute | solution.py:481
  5.4 15.6 %collective-permute-start.2 = (bf16[144,1024]{1,0:T(8,128)(2,1)S(1)}, bf16[144,1024]{1,0:T(8,128)(2,1)S(1)}, u32[]{:S(2)}, u32[]{:S(2)}) collective-permute-start(bf16[144,1024]{1,0:T(8,128)(2,1)S(1)} %pad_maximum_fusion.2), channel_id=1, source_target_pairs={{0,3},{1,2},{2,1},{3,0},{4,7},{5,6},{6,5},{7,4},{8,11},{9,10},{10,... | collective-permute-start | bytes 884744 | tf_op jit(solution)/shard_map/ppermute | solution.py:481
  7.9 12.0 %collective-permute-start.5 = (bf16[144,1024]{1,0:T(8,128)(2,1)S(1)}, bf16[144,1024]{1,0:T(8,128)(2,1)S(1)}, u32[]{:S(2)}, u32[]{:S(2)}) collective-permute-start(bf16[144,1024]{1,0:T(8,128)(2,1)S(1)} %pad_maximum_fusion.2), channel_id=1, source_target_pairs={{0,8},{4,12},{8,0},{12,4},{1,9},{5,13},{9,1},{13,5},{2,10},{6,14},... | collective-permute-start | bytes 884744 | tf_op jit(solution)/shard_map/ppermute | solution.py:478
  10.4 46.9 %collective-permute-start = (bf16[128,576]{1,0:T(8,128)(2,1)S(1)}, bf16[128,576]{1,0:T(8,128)(2,1)S(1)}, u32[]{:S(2)}, u32[]{:S(2)}) collective-permute-start(bf16[128,576]{1,0:T(8,128)(2,1)S(1)} %bitcast.44), channel_id=1, source_target_pairs={{0,8},{4,12},{8,0},{12,4},{1,9},{5,13},{9,1},{13,5},{2,10},{6,14},... | collective-permute-start | bytes 442376 | tf_op jit(solution)/shard_map/ppermute | solution.py:478
  19.9 17.9 %collective-permute-start.6 = (bf16[288,1024]{1,0:T(8,128)(2,1)S(1)}, bf16[288,1024]{1,0:T(8,128)(2,1)S(1)}, u32[]{:S(2)}, u32[]{:S(2)}) collective-permute-start(bf16[288,1024]{1,0:T(8,128)(2,1)S(1)} %pad_maximum_fusion.refs_0_.refs_1_), channel_id=1, source_target_pairs={{0,4},{4,0},{8,12},{12,8},{1,5},{5,1},{9,13},{13,9},{2,6},{6,2},{1... | collective-permute-start | bytes 1769480 | tf_op jit(solution)/shard_map/ppermute | solution.py:478
  21.0 9.9 %collective-permute-start.3 = (bf16[144,1024]{1,0:T(8,128)(2,1)S(1)}, bf16[144,1024]{1,0:T(8,128)(2,1)S(1)}, u32[]{:S(2)}, u32[]{:S(2)}) collective-permute-start(bf16[144,1024]{1,0:T(8,128)(2,1)S(1)} %collective-permute-done.2), channel_id=1, source_target_pairs={{0,8},{4,12},{8,0},{12,4},{1,9},{5,13},{9,1},{13,5},{2,10},{6,14},... | collective-permute-start | bytes 884744 | tf_op jit(solution)/shard_map/ppermute | solution.py:478
  22.5 13.8 %collective-permute-start.10 = (bf16[144,1024]{1,0:T(8,128)(2,1)S(1)}, bf16[144,1024]{1,0:T(8,128)(2,1)S(1)}, u32[]{:S(2)}, u32[]{:S(2)}) collective-permute-start(bf16[144,1024]{1,0:T(8,128)(2,1)S(1)} %collective-permute-done.2), channel_id=1, source_target_pairs={{0,1},{1,0},{2,3},{3,2},{4,5},{5,4},{6,7},{7,6},{8,9},{9,8},{10,11... | collective-permute-start | bytes 884744 | tf_op jit(solution)/shard_map/ppermute | solution.py:481
  23.1 13.1 %collective-permute-start.8 = (bf16[144,1024]{1,0:T(8,128)(2,1)S(1)}, bf16[144,1024]{1,0:T(8,128)(2,1)S(1)}, u32[]{:S(2)}, u32[]{:S(2)}) collective-permute-start(bf16[144,1024]{1,0:T(8,128)(2,1)S(1)} %collective-permute-done.7.refs_1_.a_ref), channel_id=1, source_target_pairs={{0,8},{4,12},{8,0},{12,4},{1,9},{5,13},{9,1},{13,5},{2,10},{6,14},... | collective-permute-start | bytes 884744 | tf_op jit(solution)/shard_map/ppermute | solution.py:478
  31.0 6.7 %collective-permute-start.11 = (bf16[144,1024]{1,0:T(8,128)(2,1)S(1)}, bf16[144,1024]{1,0:T(8,128)(2,1)S(1)}, u32[]{:S(2)}, u32[]{:S(2)}) collective-permute-start(bf16[144,1024]{1,0:T(8,128)(2,1)S(1)} %collective-permute-done.3.refs_1_), channel_id=1, source_target_pairs={{0,1},{1,0},{2,3},{3,2},{4,5},{5,4},{6,7},{7,6},{8,9},{9,8},{10,11... | collective-permute-start | bytes 884744 | tf_op jit(solution)/shard_map/ppermute | solution.py:481
  36.3 3.2 %collective-permute-start.9 = (bf16[288,1024]{1,0:T(8,128)(2,1)S(1)}, bf16[288,1024]{1,0:T(8,128)(2,1)S(1)}, u32[]{:S(2)}, u32[]{:S(2)}) collective-permute-start(bf16[288,1024]{1,0:T(8,128)(2,1)S(1)} %stack.21.refs_0_.refs_1_), channel_id=1, source_target_pairs={{0,4},{4,0},{8,12},{12,8},{1,5},{5,1},{9,13},{13,9},{2,6},{6,2},{1... | collective-permute-start | bytes 1769480 | tf_op jit(solution)/shard_map/ppermute | solution.py:478
  36.4 4.6 %collective-permute-start.4 = (bf16[288,1024]{1,0:T(8,128)(2,1)S(1)}, bf16[288,1024]{1,0:T(8,128)(2,1)S(1)}, u32[]{:S(2)}, u32[]{:S(2)}) collective-permute-start(bf16[288,1024]{1,0:T(8,128)(2,1)S(1)} %constant_dynamic-update-slice_fusion.refs_0_.refs_1_), channel_id=1, source_target_pairs={{0,4},{4,0},{8,12},{12,8},{1,5},{5,1},{9,13},{13,9},{2,6},{6,2},{1... | collective-permute-start | bytes 1769480 | tf_op jit(solution)/shard_map/ppermute | solution.py:478
  37.7 4.8 %collective-permute-start.12 = (bf16[288,1024]{1,0:T(8,128)(2,1)S(1)}, bf16[288,1024]{1,0:T(8,128)(2,1)S(1)}, u32[]{:S(2)}, u32[]{:S(2)}) collective-permute-start(bf16[288,1024]{1,0:T(8,128)(2,1)S(1)} %constant_dynamic-update-slice_fusion.2.refs_0_.refs_1_), channel_id=1, source_target_pairs={{0,4},{4,0},{8,12},{12,8},{1,5},{5,1},{9,13},{13,9},{2,6},{6,2},{1... | collective-permute-start | bytes 1769480 | tf_op jit(solution)/shard_map/ppermute | solution.py:478
  56.8 2.3 %collective-permute-start.15 = (bf16[1,256,1024]{2,1,0:T(8,128)(2,1)S(1)}, bf16[1,256,1024]{2,1,0:T(8,128)(2,1)S(1)}, u32[]{:S(2)}, u32[]{:S(2)}) collective-permute-start(bf16[1,256,1024]{2,1,0:T(8,128)(2,1)S(1)} %get-tuple-element.51), channel_id=1, source_target_pairs={{0,4},{4,0},{8,12},{12,8},{1,5},{5,1},{9,13},{13,9},{2,6},{6,2},{1... | collective-permute-start | bytes 1572872 | tf_op jit(solution)/shard_map/ppermute | solution.py:478
  57.4 23.0 %collective-permute-start.1 = (bf16[256,576]{1,0:T(8,128)(2,1)S(1)}, bf16[256,576]{1,0:T(8,128)(2,1)S(1)}, u32[]{:S(2)}, u32[]{:S(2)}) collective-permute-start(bf16[256,576]{1,0:T(8,128)(2,1)S(1)} %pad_maximum_fusion.1.refs_0_.refs_1_), channel_id=1, source_target_pairs={{0,4},{4,0},{8,12},{12,8},{1,5},{5,1},{9,13},{13,9},{2,6},{6,2},{1... | collective-permute-start | bytes 884744 | tf_op jit(solution)/shard_map/ppermute | solution.py:478
  58.0 3.5 %collective-permute-start.13 = (bf16[1,256,1024]{2,1,0:T(8,128)(2,1)S(1)}, bf16[1,256,1024]{2,1,0:T(8,128)(2,1)S(1)}, u32[]{:S(2)}, u32[]{:S(2)}) collective-permute-start(bf16[1,256,1024]{2,1,0:T(8,128)(2,1)S(1)} %get-tuple-element.47), channel_id=1, source_target_pairs={{0,4},{4,0},{8,12},{12,8},{1,5},{5,1},{9,13},{13,9},{2,6},{6,2},{1... | collective-permute-start | bytes 1572872 | tf_op jit(solution)/shard_map/ppermute | solution.py:478
  59.0 10.3 %collective-permute-start.19 = (bf16[1,256,1024]{2,1,0:T(8,128)(2,1)S(1)}, bf16[1,256,1024]{2,1,0:T(8,128)(2,1)S(1)}, u32[]{:S(2)}, u32[]{:S(2)}) collective-permute-start(bf16[1,256,1024]{2,1,0:T(8,128)(2,1)S(1)} %get-tuple-element.55), channel_id=1, source_target_pairs={{0,4},{4,0},{8,12},{12,8},{1,5},{5,1},{9,13},{13,9},{2,6},{6,2},{1... | collective-permute-start | bytes 1572872 | tf_op jit(solution)/shard_map/ppermute | solution.py:478
  59.2 9.2 %collective-permute-start.16 = (bf16[1,128,1024]{2,1,0:T(8,128)(2,1)S(1)}, bf16[1,128,1024]{2,1,0:T(8,128)(2,1)S(1)}, u32[]{:S(2)}, u32[]{:S(2)}) collective-permute-start(bf16[1,128,1024]{2,1,0:T(8,128)(2,1)S(1)} %add_convert_fusion.5), channel_id=1, source_target_pairs={{0,8},{4,12},{8,0},{12,4},{1,9},{5,13},{9,1},{13,5},{2,10},{6,14},... | collective-permute-start | bytes 786440 | tf_op jit(solution)/shard_map/ppermute | solution.py:478
  61.2 9.7 %collective-permute-start.22 = (bf16[1,256,1024]{2,1,0:T(8,128)(2,1)S(1)}, bf16[1,256,1024]{2,1,0:T(8,128)(2,1)S(1)}, u32[]{:S(2)}, u32[]{:S(2)}) collective-permute-start(bf16[1,256,1024]{2,1,0:T(8,128)(2,1)S(1)} %get-tuple-element.59), channel_id=1, source_target_pairs={{0,4},{4,0},{8,12},{12,8},{1,5},{5,1},{9,13},{13,9},{2,6},{6,2},{1... | collective-permute-start | bytes 1572872 | tf_op jit(solution)/shard_map/ppermute | solution.py:478
  61.6 12.4 %collective-permute-start.14 = (bf16[1,128,1024]{2,1,0:T(8,128)(2,1)S(1)}, bf16[1,128,1024]{2,1,0:T(8,128)(2,1)S(1)}, u32[]{:S(2)}, u32[]{:S(2)}) collective-permute-start(bf16[1,128,1024]{2,1,0:T(8,128)(2,1)S(1)} %add_convert_fusion.6), channel_id=1, source_target_pairs={{0,8},{4,12},{8,0},{12,4},{1,9},{5,13},{9,1},{13,5},{2,10},{6,14},... | collective-permute-start | bytes 786440 | tf_op jit(solution)/shard_map/ppermute | solution.py:478
  68.5 7.6 %collective-permute-start.17 = (bf16[1,128,1024]{2,1,0:T(8,128)(2,1)S(1)}, bf16[1,128,1024]{2,1,0:T(8,128)(2,1)S(1)}, u32[]{:S(2)}, u32[]{:S(2)}) collective-permute-start(bf16[1,128,1024]{2,1,0:T(8,128)(2,1)S(1)} %add_convert_fusion.4), channel_id=1, source_target_pairs={{0,1},{1,0},{2,3},{3,2},{4,5},{5,4},{6,7},{7,6},{8,9},{9,8},{10,11... | collective-permute-start | bytes 786440 | tf_op jit(solution)/shard_map/ppermute | solution.py:481
  69.3 10.2 %collective-permute-start.20 = (bf16[1,128,1024]{2,1,0:T(8,128)(2,1)S(1)}, bf16[1,128,1024]{2,1,0:T(8,128)(2,1)S(1)}, u32[]{:S(2)}, u32[]{:S(2)}) collective-permute-start(bf16[1,128,1024]{2,1,0:T(8,128)(2,1)S(1)} %add_convert_fusion.2), channel_id=1, source_target_pairs={{0,8},{4,12},{8,0},{12,4},{1,9},{5,13},{9,1},{13,5},{2,10},{6,14},... | collective-permute-start | bytes 786440 | tf_op jit(solution)/shard_map/ppermute | solution.py:478
  71.0 16.3 %collective-permute-start.23 = (bf16[1,128,1024]{2,1,0:T(8,128)(2,1)S(1)}, bf16[1,128,1024]{2,1,0:T(8,128)(2,1)S(1)}, u32[]{:S(2)}, u32[]{:S(2)}) collective-permute-start(bf16[1,128,1024]{2,1,0:T(8,128)(2,1)S(1)} %add_convert_fusion.1), channel_id=1, source_target_pairs={{0,8},{4,12},{8,0},{12,4},{1,9},{5,13},{9,1},{13,5},{2,10},{6,14},... | collective-permute-start | bytes 786440 | tf_op jit(solution)/shard_map/ppermute | solution.py:478
  76.2 14.2 %collective-permute-start.18 = (bf16[1,128,1024]{2,1,0:T(8,128)(2,1)S(1)}, bf16[1,128,1024]{2,1,0:T(8,128)(2,1)S(1)}, u32[]{:S(2)}, u32[]{:S(2)}) collective-permute-start(bf16[1,128,1024]{2,1,0:T(8,128)(2,1)S(1)} %add_convert_fusion.3.refs_0_), channel_id=1, source_target_pairs={{0,3},{1,2},{2,1},{3,0},{4,7},{5,6},{6,5},{7,4},{8,11},{9,10},{10,... | collective-permute-start | bytes 786440 | tf_op jit(solution)/shard_map/ppermute | solution.py:481
  79.7 10.7 %collective-permute-start.21 = (bf16[1,128,1024]{2,1,0:T(8,128)(2,1)S(1)}, bf16[1,128,1024]{2,1,0:T(8,128)(2,1)S(1)}, u32[]{:S(2)}, u32[]{:S(2)}) collective-permute-start(bf16[1,128,1024]{2,1,0:T(8,128)(2,1)S(1)} %join.1), channel_id=1, source_target_pairs={{0,1},{1,0},{2,3},{3,2},{4,5},{5,4},{6,7},{7,6},{8,9},{9,8},{10,11... | collective-permute-start | bytes 786440 | tf_op jit(solution)/shard_map/ppermute | solution.py:481
  (6 other events, 34.6 us)

commit v16 on v15

--- a/solution.py
+++ b/solution.py
@@ -19,7 +19,7 @@
 VMEM = 14 * 2**20
 VMEM_EXPERTS = 24 * 2**20
 VMEM_SORT = 52 * 2**20
-PIECES = (0.5, 0.75, 1.0)
+PIECES = (0.625, 0.875, 1.0)
 DEPTH = 3
 PEAK = 1.1e9
 

time: 91.6 us -> 93.2 us (1.017)
  waiting for transfers between devices: 19 us -> 21 us
    ppermute x17, waiting for transfers between devices: 12 us -> 14.2 us  [flip(): return lax.ppermute(a, 'ctx', [(i, i ^ bit) for i in range(n_ctx)])]
  transfers between devices with their start and end apart: 24 -> 24, of which waited for: 8 -> 8; matrix products, arithmetic and copies ran while one was open for 4% -> 4% of each run, Pallas kernels for 49% -> 48%
where the time goes in v16:
time: 93.2 us; the launch traced here: 92.9 us
  Pallas kernels  44.3 us (48%)
  waiting for transfers between devices  21 us (23%)
  starting transfers between devices  20.7 us (22%)
  other arithmetic  3.8 us (4%)
  local copies, waits for them, and re-layouts  2.17 us (2%)
  between operations  0.96 us (1%)
    pallas_call x3, Pallas kernels, sort_rows(): call(functools.partial(sort_kernel, start), 8, ((end - start) // group,),...  17.8 us
    ppermute x17, waiting for transfers between devices, flip(): return lax.ppermute(a, 'ctx', [(i, i ^ bit) for i in range(n_ctx)])  14.2 us
    pallas_call x1, Pallas kernels, experts(): call(functools.partial(expert_kernel, n), 6, (local // group, slots // si...  12.2 us
    ppermute x17, starting transfers between devices, flip(): return lax.ppermute(a, 'ctx', [(i, i ^ bit) for i in range(n_ctx)])  10.8 us
    ppermute x7, starting transfers between devices, shift(): return lax.ppermute(a, 'exp', [(i, i ^ d) for i in range(n_exp)])  9.84 us
    ppermute x7, waiting for transfers between devices, shift(): return lax.ppermute(a, 'exp', [(i, i ^ d) for i in range(n_exp)])  6.77 us
    pallas_call x1, Pallas kernels, attend(): call(functools.partial(attend_kernel, [at for _, at in parts], kdim), 6,...  6.17 us
    pallas_call x4, Pallas kernels, dispatch(): call(functools.partial(dispatch_kernel, starts, n_parts if row is not Non...  6.04 us
  transfers between devices with their start and end apart: 24, of which 8 were waited for; matrix products, arithmetic and copies ran while one was open for 4% of the time, Pallas kernels for 48%

profile of v16, /device:TPU:0, one launch (start us, length us, event | category | flops | bytes accessed | tf_op | source)
XLA Modules:
  0.0 92.9 jit_solution(8837302315420716480)
XLA Ops:
  2.3 3.1 %collective-permute-start.7 = (bf16[144,1024]{1,0:T(8,128)(2,1)S(1)}, bf16[144,1024]{1,0:T(8,128)(2,1)S(1)}, u32[]{:S(2)}, u32[]{:S(2)}) collective-permute-start(bf16[144,1024]{1,0:T(8,128)(2,1)S(1)} %pad_maximum_fusion.2), channel_id=1, source_target_pairs={{0,1},{1,0},{2,3},{3,2},{4,5},{5,4},{6,7},{7,6},{8,9},{9,8},{10,11... | collective-permute-start | bytes 884744 | tf_op jit(solution)/shard_map/ppermute | solution.py:481
  5.4 2.5 %collective-permute-start.2 = (bf16[144,1024]{1,0:T(8,128)(2,1)S(1)}, bf16[144,1024]{1,0:T(8,128)(2,1)S(1)}, u32[]{:S(2)}, u32[]{:S(2)}) collective-permute-start(bf16[144,1024]{1,0:T(8,128)(2,1)S(1)} %pad_maximum_fusion.2), channel_id=1, source_target_pairs={{0,3},{1,2},{2,1},{3,0},{4,7},{5,6},{6,5},{7,4},{8,11},{9,10},{10,... | collective-permute-start | bytes 884744 | tf_op jit(solution)/shard_map/ppermute | solution.py:481
  7.9 1.5 %collective-permute-start.5 = (bf16[144,1024]{1,0:T(8,128)(2,1)S(1)}, bf16[144,1024]{1,0:T(8,128)(2,1)S(1)}, u32[]{:S(2)}, u32[]{:S(2)}) collective-permute-start(bf16[144,1024]{1,0:T(8,128)(2,1)S(1)} %pad_maximum_fusion.2), channel_id=1, source_target_pairs={{0,8},{4,12},{8,0},{12,4},{1,9},{5,13},{9,1},{13,5},{2,10},{6,14},... | collective-permute-start | bytes 884744 | tf_op jit(solution)/shard_map/ppermute | solution.py:478
  11.0 9.3 %sort.3 = (bf16[16,2,176,1024]{3,2,1,0:T(8,128)(2,1)}, f32[8,128]{1,0:T(8,128)}) custom-call(bf16[16,2816,128]{2,1,0:T(8,128)(2,1)} %bitcast.53), custom_call_target="tpu_custom_call" | custom-call | flops 8800000000 | tf_op jit(solution)/shard_map/sort/pallas_call | solution.py:260
  21.3 1.6 %collective-permute-start.3 = (bf16[144,1024]{1,0:T(8,128)(2,1)S(1)}, bf16[144,1024]{1,0:T(8,128)(2,1)S(1)}, u32[]{:S(2)}, u32[]{:S(2)}) collective-permute-start(bf16[144,1024]{1,0:T(8,128)(2,1)S(1)} %collective-permute-done.2), channel_id=1, source_target_pairs={{0,8},{4,12},{8,0},{12,4},{1,9},{5,13},{9,1},{13,5},{2,10},{6,14},... | collective-permute-start | bytes 884744 | tf_op jit(solution)/shard_map/ppermute | solution.py:478
  24.1 5.2 %sort.4 = (bf16[16,2,176,1024]{3,2,1,0:T(8,128)(2,1)}, f32[8,128]{1,0:T(8,128)}) custom-call(bf16[16,2816,128]{2,1,0:T(8,128)(2,1)} %bitcast.54, bf16[16,2,176,1024]{3,2,1,0:T(8,128)(2,1)} %get-tuple-element.34.refs_0_, bf16[144,1024]{1,0:T(8,128)(2,1)S(1)} %collective-permute-done.7.refs_1_.a_ref), custom_call_target="tpu_custom_call", output_to_operand_aliasing={{0}: (1, {})} | custom-call | flops 8800000000 | tf_op jit(solution)/shard_map/sort/pallas_call | solution.py:260
  29.4 1.8 %collective-permute-done.3.refs_1_ = bf16[144,1024]{1,0:T(8,128)(2,1)S(1)} collective-permute-done((bf16[144,1024]{1,0:T(8,128)(2,1)S(1)}, bf16[144,1024]{1,0:T(8,128)(2,1)S(1)}, u32[]{:S(2)}, u32[]{:S(2)}) %collective-permute-start.3) | collective-permute-done | bytes 294944 | tf_op jit(solution)/shard_map/ppermute | solution.py:478
  31.9 3.3 %sort.5 = (bf16[16,2,176,1024]{3,2,1,0:T(8,128)(2,1)}, f32[8,128]{1,0:T(8,128)S(1)}) custom-call(bf16[16,2816,128]{2,1,0:T(8,128)(2,1)} %bitcast.55, bf16[16,2,176,1024]{3,2,1,0:T(8,128)(2,1)} %get-tuple-element.35.refs_0_, bf16[144,1024]{1,0:T(8,128)(2,1)S(1)} %collective-permute-done.3.refs_1_), custom_call_target="tpu_custom_call", output_to_operand_aliasing={{0}: (1, {})} | custom-call | flops 8800000000 | tf_op jit(solution)/shard_map/sort/pallas_call | solution.py:260
  35.2 1.9 %collective-permute-done.8.b_ref = bf16[144,1024]{1,0:T(8,128)(2,1)S(1)} collective-permute-done((bf16[144,1024]{1,0:T(8,128)(2,1)S(1)}, bf16[144,1024]{1,0:T(8,128)(2,1)S(1)}, u32[]{:S(2)}, u32[]{:S(2)}) %collective-permute-start.8) | collective-permute-done | bytes 294944 | tf_op jit(solution)/shard_map/ppermute | solution.py:478
  37.8 1.5 %collective-permute-done.11 = bf16[144,1024]{1,0:T(8,128)(2,1)S(1)} collective-permute-done((bf16[144,1024]{1,0:T(8,128)(2,1)S(1)}, bf16[144,1024]{1,0:T(8,128)(2,1)S(1)}, u32[]{:S(2)}, u32[]{:S(2)}) %collective-permute-start.11) | collective-permute-done | bytes 294944 | tf_op jit(solution)/shard_map/ppermute | solution.py:481
  39.5 1.6 %dispatch.5 = (bf16[16,64,1024]{2,1,0:T(8,128)(2,1)S(1)}, f32[16,64,128]{2,1,0:T(8,128)S(1)}, bf16[4,256,128]{2,1,0:T(8,128)(2,1)S(1)}, f32[8,128]{1,0:T(8,128)S(1)}) custom-call(s32[1]{0:T(128)} %bitcast.13.base_ref, bf16[64,1024]{1,0:T(8,128)(2,1)S(1)} %fusion.rw_ref, bf16[288,1024]{1,0:T(8,128)(2,1)S(1)} %pad_maximum_fusion.refs_0_.refs_1_, ...), custom_call_target="tpu_custom_call" | custom-call | flops 3300000000 | tf_op jit(solution)/shard_map/dispatch/pallas_call | solution.py:153
  41.1 1.5 %dispatch.6 = (bf16[16,64,1024]{2,1,0:T(8,128)(2,1)S(1)}, f32[16,64,128]{2,1,0:T(8,128)S(1)}, bf16[4,256,128]{2,1,0:T(8,128)(2,1)S(1)}) custom-call(s32[1]{0:T(128)} %bitcast.13.base_ref, bf16[64,1024]{1,0:T(8,128)(2,1)S(1)} %fusion.rw_ref, bf16[288,1024]{1,0:T(8,128)(2,1)S(1)} %stack.21.refs_0_.refs_1_, bf16[288,1024]{1,0:T(8,128)(2,1)S(1)} %stack.21.refs_0_.refs_1_, ...), custom_call_target="tpu_custom_call" | custom-call | flops 3300000000 | tf_op jit(solution)/shard_map/dispatch/pallas_call | solution.py:153
  42.6 1.5 %dispatch.4 = (bf16[16,64,1024]{2,1,0:T(8,128)(2,1)S(1)}, f32[16,64,128]{2,1,0:T(8,128)S(1)}, bf16[4,256,128]{2,1,0:T(8,128)(2,1)S(1)}) custom-call(s32[1]{0:T(128)} %bitcast.13.base_ref, bf16[64,1024]{1,0:T(8,128)(2,1)S(1)} %fusion.rw_ref, bf16[288,1024]{1,0:T(8,128)(2,1)S(1)} %constant_dynamic-update-slice_fusion.refs_0_.refs_1_, ...), custom_call_target="tpu_custom_call" | custom-call | flops 3300000000 | tf_op jit(solution)/shard_map/dispatch/pallas_call | solution.py:153
  44.1 1.5 %dispatch.7 = (bf16[16,64,1024]{2,1,0:T(8,128)(2,1)S(1)}, f32[16,64,128]{2,1,0:T(8,128)S(1)}, bf16[4,256,128]{2,1,0:T(8,128)(2,1)S(1)}) custom-call(s32[1]{0:T(128)} %bitcast.13.base_ref, bf16[64,1024]{1,0:T(8,128)(2,1)S(1)} %fusion.rw_ref, bf16[288,1024]{1,0:T(8,128)(2,1)S(1)} %constant_dynamic-update-slice_fusion.2.refs_0_.refs_1_, ...), custom_call_target="tpu_custom_call" | custom-call | flops 3300000000 | tf_op jit(solution)/shard_map/dispatch/pallas_call | solution.py:153
  45.7 12.2 %experts.1 = (bf16[16,64,1024]{2,1,0:T(8,128)(2,1)S(1)}, bf16[16,64,1024]{2,1,0:T(8,128)(2,1)S(1)}, bf16[16,64,1024]{2,1,0:T(8,128)(2,1)S(1)}, bf16[16,64,1024]{2,1,0:T(8,128)(2,1)S(1)}) custom-call(bf16[16,64,1024]{2,1,0:T(8,128)(2,1)S(1)} %get-tuple-element.33.refs_0_, bf16[16,64,1024]{2,1,0:T(8,128)(2,1)S(1)} %get-tuple-element.37.refs_1_, ...), custom_call_target="tpu_custom_call" | custom-call | flops 6600000000 | tf_op jit(solution)/shard_map/experts/pallas_call | solution.py:343
  60.8 1.6 %collective-permute-start.16 = (bf16[1,128,1024]{2,1,0:T(8,128)(2,1)S(1)}, bf16[1,128,1024]{2,1,0:T(8,128)(2,1)S(1)}, u32[]{:S(2)}, u32[]{:S(2)}) collective-permute-start(bf16[1,128,1024]{2,1,0:T(8,128)(2,1)S(1)} %add_convert_fusion.5), channel_id=1, source_target_pairs={{0,8},{4,12},{8,0},{12,4},{1,9},{5,13},{9,1},{13,5},{2,10},{6,14},... | collective-permute-start | bytes 786440 | tf_op jit(solution)/shard_map/ppermute | solution.py:478
  63.8 6.2 %collective-permute-done.16 = bf16[1,128,1024]{2,1,0:T(8,128)(2,1)S(1)} collective-permute-done((bf16[1,128,1024]{2,1,0:T(8,128)(2,1)S(1)}, bf16[1,128,1024]{2,1,0:T(8,128)(2,1)S(1)}, u32[]{:S(2)}, u32[]{:S(2)}) %collective-permute-start.16) | collective-permute-done | bytes 262176 | tf_op jit(solution)/shard_map/ppermute | solution.py:478
  70.9 1.6 %collective-permute-start.20 = (bf16[1,128,1024]{2,1,0:T(8,128)(2,1)S(1)}, bf16[1,128,1024]{2,1,0:T(8,128)(2,1)S(1)}, u32[]{:S(2)}, u32[]{:S(2)}) collective-permute-start(bf16[1,128,1024]{2,1,0:T(8,128)(2,1)S(1)} %add_convert_fusion.2), channel_id=1, source_target_pairs={{0,8},{4,12},{8,0},{12,4},{1,9},{5,13},{9,1},{13,5},{2,10},{6,14},... | collective-permute-start | bytes 786440 | tf_op jit(solution)/shard_map/ppermute | solution.py:478
  73.1 2.4 %collective-permute-done.14 = bf16[1,128,1024]{2,1,0:T(8,128)(2,1)S(1)} collective-permute-done((bf16[1,128,1024]{2,1,0:T(8,128)(2,1)S(1)}, bf16[1,128,1024]{2,1,0:T(8,128)(2,1)S(1)}, u32[]{:S(2)}, u32[]{:S(2)}) %collective-permute-start.14) | collective-permute-done | bytes 262176 | tf_op jit(solution)/shard_map/ppermute | solution.py:478
  75.5 2.1 %collective-permute-done.17 = bf16[1,128,1024]{2,1,0:T(8,128)(2,1)S(1)} collective-permute-done((bf16[1,128,1024]{2,1,0:T(8,128)(2,1)S(1)}, bf16[1,128,1024]{2,1,0:T(8,128)(2,1)S(1)}, u32[]{:S(2)}, u32[]{:S(2)}) %collective-permute-start.17) | collective-permute-done | bytes 262176 | tf_op jit(solution)/shard_map/ppermute | solution.py:481
  77.8 1.4 %collective-permute-start.18 = (bf16[1,128,1024]{2,1,0:T(8,128)(2,1)S(1)}, bf16[1,128,1024]{2,1,0:T(8,128)(2,1)S(1)}, u32[]{:S(2)}, u32[]{:S(2)}) collective-permute-start(bf16[1,128,1024]{2,1,0:T(8,128)(2,1)S(1)} %add_convert_fusion.3.refs_0_), channel_id=1, source_target_pairs={{0,3},{1,2},{2,1},{3,0},{4,7},{5,6},{6,5},{7,4},{8,11},{9,10},{10,... | collective-permute-start | bytes 786440 | tf_op jit(solution)/shard_map/ppermute | solution.py:481
  79.2 1.9 %collective-permute-done.20.c_ref = bf16[1,128,1024]{2,1,0:T(8,128)(2,1)S(1)} collective-permute-done((bf16[1,128,1024]{2,1,0:T(8,128)(2,1)S(1)}, bf16[1,128,1024]{2,1,0:T(8,128)(2,1)S(1)}, u32[]{:S(2)}, u32[]{:S(2)}) %collective-permute-start.20) | collective-permute-done | bytes 262176 | tf_op jit(solution)/shard_map/ppermute | solution.py:478
  82.0 6.2 %attention.1 = bf16[128,4096]{1,0:T(8,128)(2,1)} custom-call(s32[128,1]{1,0:T(8,128)S(1)} %copy.22.first_ref, s32[128,1]{1,0:T(8,128)S(1)} %copy.23.last_ref, s32[1,512]{1,0:T(1,128)S(1)} %bitcast.39, bf16[128,4608]{1,0:T(8,128)(2,1)S(1)} %bitcast.41, bf16[256,576]{1,0:T(8,128)(2,1)S(1)} %pad_maximum_fusion.1.refs_0_.refs_1_, ...), custom_call_target="tpu_custom_call" | custom-call | flops 6600000000 | tf_op jit(solution)/shard_map/attention/pallas_call | solution.py:447
  88.8 3.2 %collective-permute-done.21 = bf16[1,128,1024]{2,1,0:T(8,128)(2,1)S(1)} collective-permute-done((bf16[1,128,1024]{2,1,0:T(8,128)(2,1)S(1)}, bf16[1,128,1024]{2,1,0:T(8,128)(2,1)S(1)}, u32[]{:S(2)}, u32[]{:S(2)}) %collective-permute-start.21) | collective-permute-done | bytes 262176 | tf_op jit(solution)/shard_map/ppermute | solution.py:481
  (83 shorter events, 15.6 us)
Async XLA Ops:
  2.3 21.2 %collective-permute-start.7 = (bf16[144,1024]{1,0:T(8,128)(2,1)S(1)}, bf16[144,1024]{1,0:T(8,128)(2,1)S(1)}, u32[]{:S(2)}, u32[]{:S(2)}) collective-permute-start(bf16[144,1024]{1,0:T(8,128)(2,1)S(1)} %pad_maximum_fusion.2), channel_id=1, source_target_pairs={{0,1},{1,0},{2,3},{3,2},{4,5},{5,4},{6,7},{7,6},{8,9},{9,8},{10,11... | collective-permute-start | bytes 884744 | tf_op jit(solution)/shard_map/ppermute | solution.py:481
  5.4 15.9 %collective-permute-start.2 = (bf16[144,1024]{1,0:T(8,128)(2,1)S(1)}, bf16[144,1024]{1,0:T(8,128)(2,1)S(1)}, u32[]{:S(2)}, u32[]{:S(2)}) collective-permute-start(bf16[144,1024]{1,0:T(8,128)(2,1)S(1)} %pad_maximum_fusion.2), channel_id=1, source_target_pairs={{0,3},{1,2},{2,1},{3,0},{4,7},{5,6},{6,5},{7,4},{8,11},{9,10},{10,... | collective-permute-start | bytes 884744 | tf_op jit(solution)/shard_map/ppermute | solution.py:481
  7.9 13.3 %collective-permute-start.5 = (bf16[144,1024]{1,0:T(8,128)(2,1)S(1)}, bf16[144,1024]{1,0:T(8,128)(2,1)S(1)}, u32[]{:S(2)}, u32[]{:S(2)}) collective-permute-start(bf16[144,1024]{1,0:T(8,128)(2,1)S(1)} %pad_maximum_fusion.2), channel_id=1, source_target_pairs={{0,8},{4,12},{8,0},{12,4},{1,9},{5,13},{9,1},{13,5},{2,10},{6,14},... | collective-permute-start | bytes 884744 | tf_op jit(solution)/shard_map/ppermute | solution.py:478
  10.4 48.5 %collective-permute-start = (bf16[128,576]{1,0:T(8,128)(2,1)S(1)}, bf16[128,576]{1,0:T(8,128)(2,1)S(1)}, u32[]{:S(2)}, u32[]{:S(2)}) collective-permute-start(bf16[128,576]{1,0:T(8,128)(2,1)S(1)} %bitcast.44), channel_id=1, source_target_pairs={{0,8},{4,12},{8,0},{12,4},{1,9},{5,13},{9,1},{13,5},{2,10},{6,14},... | collective-permute-start | bytes 442376 | tf_op jit(solution)/shard_map/ppermute | solution.py:478
  21.2 18.2 %collective-permute-start.6 = (bf16[288,1024]{1,0:T(8,128)(2,1)S(1)}, bf16[288,1024]{1,0:T(8,128)(2,1)S(1)}, u32[]{:S(2)}, u32[]{:S(2)}) collective-permute-start(bf16[288,1024]{1,0:T(8,128)(2,1)S(1)} %pad_maximum_fusion.refs_0_.refs_1_), channel_id=1, source_target_pairs={{0,4},{4,0},{8,12},{12,8},{1,5},{5,1},{9,13},{13,9},{2,6},{6,2},{1... | collective-permute-start | bytes 1769480 | tf_op jit(solution)/shard_map/ppermute | solution.py:478
  21.3 9.9 %collective-permute-start.3 = (bf16[144,1024]{1,0:T(8,128)(2,1)S(1)}, bf16[144,1024]{1,0:T(8,128)(2,1)S(1)}, u32[]{:S(2)}, u32[]{:S(2)}) collective-permute-start(bf16[144,1024]{1,0:T(8,128)(2,1)S(1)} %collective-permute-done.2), channel_id=1, source_target_pairs={{0,8},{4,12},{8,0},{12,4},{1,9},{5,13},{9,1},{13,5},{2,10},{6,14},... | collective-permute-start | bytes 884744 | tf_op jit(solution)/shard_map/ppermute | solution.py:478
  22.9 14.3 %collective-permute-start.10 = (bf16[144,1024]{1,0:T(8,128)(2,1)S(1)}, bf16[144,1024]{1,0:T(8,128)(2,1)S(1)}, u32[]{:S(2)}, u32[]{:S(2)}) collective-permute-start(bf16[144,1024]{1,0:T(8,128)(2,1)S(1)} %collective-permute-done.2), channel_id=1, source_target_pairs={{0,1},{1,0},{2,3},{3,2},{4,5},{5,4},{6,7},{7,6},{8,9},{9,8},{10,11... | collective-permute-start | bytes 884744 | tf_op jit(solution)/shard_map/ppermute | solution.py:481
  23.6 13.5 %collective-permute-start.8 = (bf16[144,1024]{1,0:T(8,128)(2,1)S(1)}, bf16[144,1024]{1,0:T(8,128)(2,1)S(1)}, u32[]{:S(2)}, u32[]{:S(2)}) collective-permute-start(bf16[144,1024]{1,0:T(8,128)(2,1)S(1)} %collective-permute-done.7.refs_1_.a_ref), channel_id=1, source_target_pairs={{0,8},{4,12},{8,0},{12,4},{1,9},{5,13},{9,1},{13,5},{2,10},{6,14},... | collective-permute-start | bytes 884744 | tf_op jit(solution)/shard_map/ppermute | solution.py:478
  31.2 8.1 %collective-permute-start.11 = (bf16[144,1024]{1,0:T(8,128)(2,1)S(1)}, bf16[144,1024]{1,0:T(8,128)(2,1)S(1)}, u32[]{:S(2)}, u32[]{:S(2)}) collective-permute-start(bf16[144,1024]{1,0:T(8,128)(2,1)S(1)} %collective-permute-done.3.refs_1_), channel_id=1, source_target_pairs={{0,1},{1,0},{2,3},{3,2},{4,5},{5,4},{6,7},{7,6},{8,9},{9,8},{10,11... | collective-permute-start | bytes 884744 | tf_op jit(solution)/shard_map/ppermute | solution.py:481
  37.1 3.9 %collective-permute-start.9 = (bf16[288,1024]{1,0:T(8,128)(2,1)S(1)}, bf16[288,1024]{1,0:T(8,128)(2,1)S(1)}, u32[]{:S(2)}, u32[]{:S(2)}) collective-permute-start(bf16[288,1024]{1,0:T(8,128)(2,1)S(1)} %stack.21.refs_0_.refs_1_), channel_id=1, source_target_pairs={{0,4},{4,0},{8,12},{12,8},{1,5},{5,1},{9,13},{13,9},{2,6},{6,2},{1... | collective-permute-start | bytes 1769480 | tf_op jit(solution)/shard_map/ppermute | solution.py:478
  37.2 5.3 %collective-permute-start.4 = (bf16[288,1024]{1,0:T(8,128)(2,1)S(1)}, bf16[288,1024]{1,0:T(8,128)(2,1)S(1)}, u32[]{:S(2)}, u32[]{:S(2)}) collective-permute-start(bf16[288,1024]{1,0:T(8,128)(2,1)S(1)} %constant_dynamic-update-slice_fusion.refs_0_.refs_1_), channel_id=1, source_target_pairs={{0,4},{4,0},{8,12},{12,8},{1,5},{5,1},{9,13},{13,9},{2,6},{6,2},{1... | collective-permute-start | bytes 1769480 | tf_op jit(solution)/shard_map/ppermute | solution.py:478
  39.3 4.8 %collective-permute-start.12 = (bf16[288,1024]{1,0:T(8,128)(2,1)S(1)}, bf16[288,1024]{1,0:T(8,128)(2,1)S(1)}, u32[]{:S(2)}, u32[]{:S(2)}) collective-permute-start(bf16[288,1024]{1,0:T(8,128)(2,1)S(1)} %constant_dynamic-update-slice_fusion.2.refs_0_.refs_1_), channel_id=1, source_target_pairs={{0,4},{4,0},{8,12},{12,8},{1,5},{5,1},{9,13},{13,9},{2,6},{6,2},{1... | collective-permute-start | bytes 1769480 | tf_op jit(solution)/shard_map/ppermute | solution.py:478
  58.4 2.3 %collective-permute-start.15 = (bf16[1,256,1024]{2,1,0:T(8,128)(2,1)S(1)}, bf16[1,256,1024]{2,1,0:T(8,128)(2,1)S(1)}, u32[]{:S(2)}, u32[]{:S(2)}) collective-permute-start(bf16[1,256,1024]{2,1,0:T(8,128)(2,1)S(1)} %get-tuple-element.51), channel_id=1, source_target_pairs={{0,4},{4,0},{8,12},{12,8},{1,5},{5,1},{9,13},{13,9},{2,6},{6,2},{1... | collective-permute-start | bytes 1572872 | tf_op jit(solution)/shard_map/ppermute | solution.py:478
  59.0 23.0 %collective-permute-start.1 = (bf16[256,576]{1,0:T(8,128)(2,1)S(1)}, bf16[256,576]{1,0:T(8,128)(2,1)S(1)}, u32[]{:S(2)}, u32[]{:S(2)}) collective-permute-start(bf16[256,576]{1,0:T(8,128)(2,1)S(1)} %pad_maximum_fusion.1.refs_0_.refs_1_), channel_id=1, source_target_pairs={{0,4},{4,0},{8,12},{12,8},{1,5},{5,1},{9,13},{13,9},{2,6},{6,2},{1... | collective-permute-start | bytes 884744 | tf_op jit(solution)/shard_map/ppermute | solution.py:478
  59.6 3.5 %collective-permute-start.13 = (bf16[1,256,1024]{2,1,0:T(8,128)(2,1)S(1)}, bf16[1,256,1024]{2,1,0:T(8,128)(2,1)S(1)}, u32[]{:S(2)}, u32[]{:S(2)}) collective-permute-start(bf16[1,256,1024]{2,1,0:T(8,128)(2,1)S(1)} %get-tuple-element.47), channel_id=1, source_target_pairs={{0,4},{4,0},{8,12},{12,8},{1,5},{5,1},{9,13},{13,9},{2,6},{6,2},{1... | collective-permute-start | bytes 1572872 | tf_op jit(solution)/shard_map/ppermute | solution.py:478
  60.6 10.2 %collective-permute-start.19 = (bf16[1,256,1024]{2,1,0:T(8,128)(2,1)S(1)}, bf16[1,256,1024]{2,1,0:T(8,128)(2,1)S(1)}, u32[]{:S(2)}, u32[]{:S(2)}) collective-permute-start(bf16[1,256,1024]{2,1,0:T(8,128)(2,1)S(1)} %get-tuple-element.55), channel_id=1, source_target_pairs={{0,4},{4,0},{8,12},{12,8},{1,5},{5,1},{9,13},{13,9},{2,6},{6,2},{1... | collective-permute-start | bytes 1572872 | tf_op jit(solution)/shard_map/ppermute | solution.py:478
  60.8 9.2 %collective-permute-start.16 = (bf16[1,128,1024]{2,1,0:T(8,128)(2,1)S(1)}, bf16[1,128,1024]{2,1,0:T(8,128)(2,1)S(1)}, u32[]{:S(2)}, u32[]{:S(2)}) collective-permute-start(bf16[1,128,1024]{2,1,0:T(8,128)(2,1)S(1)} %add_convert_fusion.5), channel_id=1, source_target_pairs={{0,8},{4,12},{8,0},{12,4},{1,9},{5,13},{9,1},{13,5},{2,10},{6,14},... | collective-permute-start | bytes 786440 | tf_op jit(solution)/shard_map/ppermute | solution.py:478
  62.8 9.6 %collective-permute-start.22 = (bf16[1,256,1024]{2,1,0:T(8,128)(2,1)S(1)}, bf16[1,256,1024]{2,1,0:T(8,128)(2,1)S(1)}, u32[]{:S(2)}, u32[]{:S(2)}) collective-permute-start(bf16[1,256,1024]{2,1,0:T(8,128)(2,1)S(1)} %get-tuple-element.59), channel_id=1, source_target_pairs={{0,4},{4,0},{8,12},{12,8},{1,5},{5,1},{9,13},{13,9},{2,6},{6,2},{1... | collective-permute-start | bytes 1572872 | tf_op jit(solution)/shard_map/ppermute | solution.py:478
  63.2 12.4 %collective-permute-start.14 = (bf16[1,128,1024]{2,1,0:T(8,128)(2,1)S(1)}, bf16[1,128,1024]{2,1,0:T(8,128)(2,1)S(1)}, u32[]{:S(2)}, u32[]{:S(2)}) collective-permute-start(bf16[1,128,1024]{2,1,0:T(8,128)(2,1)S(1)} %add_convert_fusion.6), channel_id=1, source_target_pairs={{0,8},{4,12},{8,0},{12,4},{1,9},{5,13},{9,1},{13,5},{2,10},{6,14},... | collective-permute-start | bytes 786440 | tf_op jit(solution)/shard_map/ppermute | solution.py:478
  70.1 7.6 %collective-permute-start.17 = (bf16[1,128,1024]{2,1,0:T(8,128)(2,1)S(1)}, bf16[1,128,1024]{2,1,0:T(8,128)(2,1)S(1)}, u32[]{:S(2)}, u32[]{:S(2)}) collective-permute-start(bf16[1,128,1024]{2,1,0:T(8,128)(2,1)S(1)} %add_convert_fusion.4), channel_id=1, source_target_pairs={{0,1},{1,0},{2,3},{3,2},{4,5},{5,4},{6,7},{7,6},{8,9},{9,8},{10,11... | collective-permute-start | bytes 786440 | tf_op jit(solution)/shard_map/ppermute | solution.py:481
  70.9 10.3 %collective-permute-start.20 = (bf16[1,128,1024]{2,1,0:T(8,128)(2,1)S(1)}, bf16[1,128,1024]{2,1,0:T(8,128)(2,1)S(1)}, u32[]{:S(2)}, u32[]{:S(2)}) collective-permute-start(bf16[1,128,1024]{2,1,0:T(8,128)(2,1)S(1)} %add_convert_fusion.2), channel_id=1, source_target_pairs={{0,8},{4,12},{8,0},{12,4},{1,9},{5,13},{9,1},{13,5},{2,10},{6,14},... | collective-permute-start | bytes 786440 | tf_op jit(solution)/shard_map/ppermute | solution.py:478
  72.5 16.3 %collective-permute-start.23 = (bf16[1,128,1024]{2,1,0:T(8,128)(2,1)S(1)}, bf16[1,128,1024]{2,1,0:T(8,128)(2,1)S(1)}, u32[]{:S(2)}, u32[]{:S(2)}) collective-permute-start(bf16[1,128,1024]{2,1,0:T(8,128)(2,1)S(1)} %add_convert_fusion.1), channel_id=1, source_target_pairs={{0,8},{4,12},{8,0},{12,4},{1,9},{5,13},{9,1},{13,5},{2,10},{6,14},... | collective-permute-start | bytes 786440 | tf_op jit(solution)/shard_map/ppermute | solution.py:478
  77.8 14.2 %collective-permute-start.18 = (bf16[1,128,1024]{2,1,0:T(8,128)(2,1)S(1)}, bf16[1,128,1024]{2,1,0:T(8,128)(2,1)S(1)}, u32[]{:S(2)}, u32[]{:S(2)}) collective-permute-start(bf16[1,128,1024]{2,1,0:T(8,128)(2,1)S(1)} %add_convert_fusion.3.refs_0_), channel_id=1, source_target_pairs={{0,3},{1,2},{2,1},{3,0},{4,7},{5,6},{6,5},{7,4},{8,11},{9,10},{10,... | collective-permute-start | bytes 786440 | tf_op jit(solution)/shard_map/ppermute | solution.py:481
  81.3 10.7 %collective-permute-start.21 = (bf16[1,128,1024]{2,1,0:T(8,128)(2,1)S(1)}, bf16[1,128,1024]{2,1,0:T(8,128)(2,1)S(1)}, u32[]{:S(2)}, u32[]{:S(2)}) collective-permute-start(bf16[1,128,1024]{2,1,0:T(8,128)(2,1)S(1)} %join.1), channel_id=1, source_target_pairs={{0,1},{1,0},{2,3},{3,2},{4,5},{5,4},{6,7},{7,6},{8,9},{9,8},{10,11... | collective-permute-start | bytes 786440 | tf_op jit(solution)/shard_map/ppermute | solution.py:481
  (6 other events, 38.4 us)

commit v17 on v15

--- a/solution.py
+++ b/solution.py
@@ -20,7 +20,7 @@
 VMEM_EXPERTS = 24 * 2**20
 VMEM_SORT = 52 * 2**20
 PIECES = (0.5, 0.75, 1.0)
-DEPTH = 3
+DEPTH = 4
 PEAK = 1.1e9
 
 qk_scale = 192.0 ** (-0.5)

time: 91.6 us -> 91.6 us (level)
  no operation moved by 1% of the time
where the time goes in v17:
time: 91.6 us; the launch traced here: 91.3 us
  Pallas kernels  44.5 us (49%)
  starting transfers between devices  21.1 us (23%)
  waiting for transfers between devices  18.8 us (21%)
  other arithmetic  3.8 us (4%)
  local copies, waits for them, and re-layouts  2.17 us (2%)
  between operations  0.97 us (1%)
    pallas_call x3, Pallas kernels, sort_rows(): call(functools.partial(sort_kernel, start), 8, ((end - start) // group,),...  18 us
    pallas_call x1, Pallas kernels, experts(): call(functools.partial(expert_kernel, n), 6, (local // group, slots // si...  12.2 us
    ppermute x17, waiting for transfers between devices, flip(): return lax.ppermute(a, 'ctx', [(i, i ^ bit) for i in range(n_ctx)])  11.9 us
    ppermute x17, starting transfers between devices, flip(): return lax.ppermute(a, 'ctx', [(i, i ^ bit) for i in range(n_ctx)])  10.8 us
    ppermute x7, starting transfers between devices, shift(): return lax.ppermute(a, 'exp', [(i, i ^ d) for i in range(n_exp)])  10.3 us
    ppermute x7, waiting for transfers between devices, shift(): return lax.ppermute(a, 'exp', [(i, i ^ d) for i in range(n_exp)])  6.94 us
    pallas_call x1, Pallas kernels, attend(): call(functools.partial(attend_kernel, [at for _, at in parts], kdim), 6,...  6.17 us
    pallas_call x4, Pallas kernels, dispatch(): call(functools.partial(dispatch_kernel, starts, n_parts if row is not Non...  6.04 us
  transfers between devices with their start and end apart: 24, of which 8 were waited for; matrix products, arithmetic and copies ran while one was open for 4% of the time, Pallas kernels for 49%

profile of v17, /device:TPU:0, one launch (start us, length us, event | category | flops | bytes accessed | tf_op | source)
XLA Modules:
  0.0 91.3 jit_solution(15954397139137168517)
XLA Ops:
  2.3 3.1 %collective-permute-start.7 = (bf16[144,1024]{1,0:T(8,128)(2,1)S(1)}, bf16[144,1024]{1,0:T(8,128)(2,1)S(1)}, u32[]{:S(2)}, u32[]{:S(2)}) collective-permute-start(bf16[144,1024]{1,0:T(8,128)(2,1)S(1)} %pad_maximum_fusion.2), channel_id=1, source_target_pairs={{0,1},{1,0},{2,3},{3,2},{4,5},{5,4},{6,7},{7,6},{8,9},{9,8},{10,11... | collective-permute-start | bytes 884744 | tf_op jit(solution)/shard_map/ppermute | solution.py:481
  5.4 2.5 %collective-permute-start.2 = (bf16[144,1024]{1,0:T(8,128)(2,1)S(1)}, bf16[144,1024]{1,0:T(8,128)(2,1)S(1)}, u32[]{:S(2)}, u32[]{:S(2)}) collective-permute-start(bf16[144,1024]{1,0:T(8,128)(2,1)S(1)} %pad_maximum_fusion.2), channel_id=1, source_target_pairs={{0,3},{1,2},{2,1},{3,0},{4,7},{5,6},{6,5},{7,4},{8,11},{9,10},{10,... | collective-permute-start | bytes 884744 | tf_op jit(solution)/shard_map/ppermute | solution.py:481
  7.9 1.5 %collective-permute-start.5 = (bf16[144,1024]{1,0:T(8,128)(2,1)S(1)}, bf16[144,1024]{1,0:T(8,128)(2,1)S(1)}, u32[]{:S(2)}, u32[]{:S(2)}) collective-permute-start(bf16[144,1024]{1,0:T(8,128)(2,1)S(1)} %pad_maximum_fusion.2), channel_id=1, source_target_pairs={{0,8},{4,12},{8,0},{12,4},{1,9},{5,13},{9,1},{13,5},{2,10},{6,14},... | collective-permute-start | bytes 884744 | tf_op jit(solution)/shard_map/ppermute | solution.py:478
  9.4 1.1 %copy.21 = bf16[1,128,576]{2,1,0:T(8,128)(2,1)S(1)} copy(bf16[1,128,576]{1,2,0:T(8,128)(2,1)} %param.9) | data formatting | bytes 294912 | tf_op args[1]
  11.0 8.0 %sort.3 = (bf16[16,2,176,1024]{3,2,1,0:T(8,128)(2,1)}, f32[8,128]{1,0:T(8,128)}) custom-call(bf16[16,2816,128]{2,1,0:T(8,128)(2,1)} %bitcast.53), custom_call_target="tpu_custom_call" | custom-call | flops 8800000000 | tf_op jit(solution)/shard_map/sort/pallas_call | solution.py:260
  20.0 1.0 %collective-permute-done.2 = bf16[144,1024]{1,0:T(8,128)(2,1)S(1)} collective-permute-done((bf16[144,1024]{1,0:T(8,128)(2,1)S(1)}, bf16[144,1024]{1,0:T(8,128)(2,1)S(1)}, u32[]{:S(2)}, u32[]{:S(2)}) %collective-permute-start.2) | collective-permute-done | bytes 294944 | tf_op jit(solution)/shard_map/ppermute | solution.py:481
  21.0 1.5 %collective-permute-start.3 = (bf16[144,1024]{1,0:T(8,128)(2,1)S(1)}, bf16[144,1024]{1,0:T(8,128)(2,1)S(1)}, u32[]{:S(2)}, u32[]{:S(2)}) collective-permute-start(bf16[144,1024]{1,0:T(8,128)(2,1)S(1)} %collective-permute-done.2), channel_id=1, source_target_pairs={{0,8},{4,12},{8,0},{12,4},{1,9},{5,13},{9,1},{13,5},{2,10},{6,14},... | collective-permute-start | bytes 884744 | tf_op jit(solution)/shard_map/ppermute | solution.py:478
  23.6 5.3 %sort.4 = (bf16[16,2,176,1024]{3,2,1,0:T(8,128)(2,1)}, f32[8,128]{1,0:T(8,128)}) custom-call(bf16[16,2816,128]{2,1,0:T(8,128)(2,1)} %bitcast.54, bf16[16,2,176,1024]{3,2,1,0:T(8,128)(2,1)} %get-tuple-element.34.refs_0_, bf16[144,1024]{1,0:T(8,128)(2,1)S(1)} %collective-permute-done.7.refs_1_.a_ref), custom_call_target="tpu_custom_call", output_to_operand_aliasing={{0}: (1, {})} | custom-call | flops 8800000000 | tf_op jit(solution)/shard_map/sort/pallas_call | solution.py:260
  29.0 2.0 %collective-permute-done.3.refs_1_ = bf16[144,1024]{1,0:T(8,128)(2,1)S(1)} collective-permute-done((bf16[144,1024]{1,0:T(8,128)(2,1)S(1)}, bf16[144,1024]{1,0:T(8,128)(2,1)S(1)}, u32[]{:S(2)}, u32[]{:S(2)}) %collective-permute-start.3) | collective-permute-done | bytes 294944 | tf_op jit(solution)/shard_map/ppermute | solution.py:478
  31.5 4.7 %sort.5 = (bf16[16,2,176,1024]{3,2,1,0:T(8,128)(2,1)}, f32[8,128]{1,0:T(8,128)S(1)}) custom-call(bf16[16,2816,128]{2,1,0:T(8,128)(2,1)} %bitcast.55, bf16[16,2,176,1024]{3,2,1,0:T(8,128)(2,1)} %get-tuple-element.35.refs_0_, bf16[144,1024]{1,0:T(8,128)(2,1)S(1)} %collective-permute-done.3.refs_1_), custom_call_target="tpu_custom_call", output_to_operand_aliasing={{0}: (1, {})} | custom-call | flops 8800000000 | tf_op jit(solution)/shard_map/sort/pallas_call | solution.py:260
  37.9 1.6 %dispatch.5 = (bf16[16,64,1024]{2,1,0:T(8,128)(2,1)S(1)}, f32[16,64,128]{2,1,0:T(8,128)S(1)}, bf16[4,256,128]{2,1,0:T(8,128)(2,1)S(1)}, f32[8,128]{1,0:T(8,128)S(1)}) custom-call(s32[1]{0:T(128)} %bitcast.13.base_ref, bf16[64,1024]{1,0:T(8,128)(2,1)S(1)} %fusion.rw_ref, bf16[288,1024]{1,0:T(8,128)(2,1)S(1)} %pad_maximum_fusion.refs_0_.refs_1_, ...), custom_call_target="tpu_custom_call" | custom-call | flops 3300000000 | tf_op jit(solution)/shard_map/dispatch/pallas_call | solution.py:153
  39.5 1.5 %dispatch.6 = (bf16[16,64,1024]{2,1,0:T(8,128)(2,1)S(1)}, f32[16,64,128]{2,1,0:T(8,128)S(1)}, bf16[4,256,128]{2,1,0:T(8,128)(2,1)S(1)}) custom-call(s32[1]{0:T(128)} %bitcast.13.base_ref, bf16[64,1024]{1,0:T(8,128)(2,1)S(1)} %fusion.rw_ref, bf16[288,1024]{1,0:T(8,128)(2,1)S(1)} %stack.21.refs_0_.refs_1_, bf16[288,1024]{1,0:T(8,128)(2,1)S(1)} %stack.21.refs_0_.refs_1_, ...), custom_call_target="tpu_custom_call" | custom-call | flops 3300000000 | tf_op jit(solution)/shard_map/dispatch/pallas_call | solution.py:153
  41.0 1.5 %dispatch.4 = (bf16[16,64,1024]{2,1,0:T(8,128)(2,1)S(1)}, f32[16,64,128]{2,1,0:T(8,128)S(1)}, bf16[4,256,128]{2,1,0:T(8,128)(2,1)S(1)}) custom-call(s32[1]{0:T(128)} %bitcast.13.base_ref, bf16[64,1024]{1,0:T(8,128)(2,1)S(1)} %fusion.rw_ref, bf16[288,1024]{1,0:T(8,128)(2,1)S(1)} %constant_dynamic-update-slice_fusion.refs_0_.refs_1_, ...), custom_call_target="tpu_custom_call" | custom-call | flops 3300000000 | tf_op jit(solution)/shard_map/dispatch/pallas_call | solution.py:153
  42.5 1.5 %dispatch.7 = (bf16[16,64,1024]{2,1,0:T(8,128)(2,1)S(1)}, f32[16,64,128]{2,1,0:T(8,128)S(1)}, bf16[4,256,128]{2,1,0:T(8,128)(2,1)S(1)}) custom-call(s32[1]{0:T(128)} %bitcast.13.base_ref, bf16[64,1024]{1,0:T(8,128)(2,1)S(1)} %fusion.rw_ref, bf16[288,1024]{1,0:T(8,128)(2,1)S(1)} %constant_dynamic-update-slice_fusion.2.refs_0_.refs_1_, ...), custom_call_target="tpu_custom_call" | custom-call | flops 3300000000 | tf_op jit(solution)/shard_map/dispatch/pallas_call | solution.py:153
  44.1 12.2 %experts.1 = (bf16[16,64,1024]{2,1,0:T(8,128)(2,1)S(1)}, bf16[16,64,1024]{2,1,0:T(8,128)(2,1)S(1)}, bf16[16,64,1024]{2,1,0:T(8,128)(2,1)S(1)}, bf16[16,64,1024]{2,1,0:T(8,128)(2,1)S(1)}) custom-call(bf16[16,64,1024]{2,1,0:T(8,128)(2,1)S(1)} %get-tuple-element.33.refs_0_, bf16[16,64,1024]{2,1,0:T(8,128)(2,1)S(1)} %get-tuple-element.37.refs_1_, ...), custom_call_target="tpu_custom_call" | custom-call | flops 6600000000 | tf_op jit(solution)/shard_map/experts/pallas_call | solution.py:343
  59.2 1.6 %collective-permute-start.16 = (bf16[1,128,1024]{2,1,0:T(8,128)(2,1)S(1)}, bf16[1,128,1024]{2,1,0:T(8,128)(2,1)S(1)}, u32[]{:S(2)}, u32[]{:S(2)}) collective-permute-start(bf16[1,128,1024]{2,1,0:T(8,128)(2,1)S(1)} %add_convert_fusion.5), channel_id=1, source_target_pairs={{0,8},{4,12},{8,0},{12,4},{1,9},{5,13},{9,1},{13,5},{2,10},{6,14},... | collective-permute-start | bytes 786440 | tf_op jit(solution)/shard_map/ppermute | solution.py:478
  62.2 6.2 %collective-permute-done.16 = bf16[1,128,1024]{2,1,0:T(8,128)(2,1)S(1)} collective-permute-done((bf16[1,128,1024]{2,1,0:T(8,128)(2,1)S(1)}, bf16[1,128,1024]{2,1,0:T(8,128)(2,1)S(1)}, u32[]{:S(2)}, u32[]{:S(2)}) %collective-permute-start.16) | collective-permute-done | bytes 262176 | tf_op jit(solution)/shard_map/ppermute | solution.py:478
  69.3 1.6 %collective-permute-start.20 = (bf16[1,128,1024]{2,1,0:T(8,128)(2,1)S(1)}, bf16[1,128,1024]{2,1,0:T(8,128)(2,1)S(1)}, u32[]{:S(2)}, u32[]{:S(2)}) collective-permute-start(bf16[1,128,1024]{2,1,0:T(8,128)(2,1)S(1)} %add_convert_fusion.2), channel_id=1, source_target_pairs={{0,8},{4,12},{8,0},{12,4},{1,9},{5,13},{9,1},{13,5},{2,10},{6,14},... | collective-permute-start | bytes 786440 | tf_op jit(solution)/shard_map/ppermute | solution.py:478
  71.6 2.4 %collective-permute-done.14 = bf16[1,128,1024]{2,1,0:T(8,128)(2,1)S(1)} collective-permute-done((bf16[1,128,1024]{2,1,0:T(8,128)(2,1)S(1)}, bf16[1,128,1024]{2,1,0:T(8,128)(2,1)S(1)}, u32[]{:S(2)}, u32[]{:S(2)}) %collective-permute-start.14) | collective-permute-done | bytes 262176 | tf_op jit(solution)/shard_map/ppermute | solution.py:478
  73.9 2.1 %collective-permute-done.17 = bf16[1,128,1024]{2,1,0:T(8,128)(2,1)S(1)} collective-permute-done((bf16[1,128,1024]{2,1,0:T(8,128)(2,1)S(1)}, bf16[1,128,1024]{2,1,0:T(8,128)(2,1)S(1)}, u32[]{:S(2)}, u32[]{:S(2)}) %collective-permute-start.17) | collective-permute-done | bytes 262176 | tf_op jit(solution)/shard_map/ppermute | solution.py:481
  76.2 2.0 %collective-permute-start.18 = (bf16[1,128,1024]{2,1,0:T(8,128)(2,1)S(1)}, bf16[1,128,1024]{2,1,0:T(8,128)(2,1)S(1)}, u32[]{:S(2)}, u32[]{:S(2)}) collective-permute-start(bf16[1,128,1024]{2,1,0:T(8,128)(2,1)S(1)} %add_convert_fusion.3.refs_0_), channel_id=1, source_target_pairs={{0,3},{1,2},{2,1},{3,0},{4,7},{5,6},{6,5},{7,4},{8,11},{9,10},{10,... | collective-permute-start | bytes 786440 | tf_op jit(solution)/shard_map/ppermute | solution.py:481
  78.2 1.3 %collective-permute-done.20.c_ref = bf16[1,128,1024]{2,1,0:T(8,128)(2,1)S(1)} collective-permute-done((bf16[1,128,1024]{2,1,0:T(8,128)(2,1)S(1)}, bf16[1,128,1024]{2,1,0:T(8,128)(2,1)S(1)}, u32[]{:S(2)}, u32[]{:S(2)}) %collective-permute-start.20) | collective-permute-done | bytes 262176 | tf_op jit(solution)/shard_map/ppermute | solution.py:478
  80.5 6.2 %attention.1 = bf16[128,4096]{1,0:T(8,128)(2,1)} custom-call(s32[128,1]{1,0:T(8,128)S(1)} %copy.22.first_ref, s32[128,1]{1,0:T(8,128)S(1)} %copy.23.last_ref, s32[1,512]{1,0:T(1,128)S(1)} %bitcast.39, bf16[128,4608]{1,0:T(8,128)(2,1)S(1)} %bitcast.41, bf16[256,576]{1,0:T(8,128)(2,1)S(1)} %pad_maximum_fusion.1.refs_0_.refs_1_, ...), custom_call_target="tpu_custom_call" | custom-call | flops 6600000000 | tf_op jit(solution)/shard_map/attention/pallas_call | solution.py:447
  87.3 3.1 %collective-permute-done.21 = bf16[1,128,1024]{2,1,0:T(8,128)(2,1)S(1)} collective-permute-done((bf16[1,128,1024]{2,1,0:T(8,128)(2,1)S(1)}, bf16[1,128,1024]{2,1,0:T(8,128)(2,1)S(1)}, u32[]{:S(2)}, u32[]{:S(2)}) %collective-permute-start.21) | collective-permute-done | bytes 262176 | tf_op jit(solution)/shard_map/ppermute | solution.py:481
  (83 shorter events, 15.2 us)
Async XLA Ops:
  2.3 20.8 %collective-permute-start.7 = (bf16[144,1024]{1,0:T(8,128)(2,1)S(1)}, bf16[144,1024]{1,0:T(8,128)(2,1)S(1)}, u32[]{:S(2)}, u32[]{:S(2)}) collective-permute-start(bf16[144,1024]{1,0:T(8,128)(2,1)S(1)} %pad_maximum_fusion.2), channel_id=1, source_target_pairs={{0,1},{1,0},{2,3},{3,2},{4,5},{5,4},{6,7},{7,6},{8,9},{9,8},{10,11... | collective-permute-start | bytes 884744 | tf_op jit(solution)/shard_map/ppermute | solution.py:481
  5.4 15.6 %collective-permute-start.2 = (bf16[144,1024]{1,0:T(8,128)(2,1)S(1)}, bf16[144,1024]{1,0:T(8,128)(2,1)S(1)}, u32[]{:S(2)}, u32[]{:S(2)}) collective-permute-start(bf16[144,1024]{1,0:T(8,128)(2,1)S(1)} %pad_maximum_fusion.2), channel_id=1, source_target_pairs={{0,3},{1,2},{2,1},{3,0},{4,7},{5,6},{6,5},{7,4},{8,11},{9,10},{10,... | collective-permute-start | bytes 884744 | tf_op jit(solution)/shard_map/ppermute | solution.py:481
  7.9 12.0 %collective-permute-start.5 = (bf16[144,1024]{1,0:T(8,128)(2,1)S(1)}, bf16[144,1024]{1,0:T(8,128)(2,1)S(1)}, u32[]{:S(2)}, u32[]{:S(2)}) collective-permute-start(bf16[144,1024]{1,0:T(8,128)(2,1)S(1)} %pad_maximum_fusion.2), channel_id=1, source_target_pairs={{0,8},{4,12},{8,0},{12,4},{1,9},{5,13},{9,1},{13,5},{2,10},{6,14},... | collective-permute-start | bytes 884744 | tf_op jit(solution)/shard_map/ppermute | solution.py:478
  10.4 46.9 %collective-permute-start = (bf16[128,576]{1,0:T(8,128)(2,1)S(1)}, bf16[128,576]{1,0:T(8,128)(2,1)S(1)}, u32[]{:S(2)}, u32[]{:S(2)}) collective-permute-start(bf16[128,576]{1,0:T(8,128)(2,1)S(1)} %bitcast.44), channel_id=1, source_target_pairs={{0,8},{4,12},{8,0},{12,4},{1,9},{5,13},{9,1},{13,5},{2,10},{6,14},... | collective-permute-start | bytes 442376 | tf_op jit(solution)/shard_map/ppermute | solution.py:478
  20.0 17.8 %collective-permute-start.6 = (bf16[288,1024]{1,0:T(8,128)(2,1)S(1)}, bf16[288,1024]{1,0:T(8,128)(2,1)S(1)}, u32[]{:S(2)}, u32[]{:S(2)}) collective-permute-start(bf16[288,1024]{1,0:T(8,128)(2,1)S(1)} %pad_maximum_fusion.refs_0_.refs_1_), channel_id=1, source_target_pairs={{0,4},{4,0},{8,12},{12,8},{1,5},{5,1},{9,13},{13,9},{2,6},{6,2},{1... | collective-permute-start | bytes 1769480 | tf_op jit(solution)/shard_map/ppermute | solution.py:478
  21.0 9.9 %collective-permute-start.3 = (bf16[144,1024]{1,0:T(8,128)(2,1)S(1)}, bf16[144,1024]{1,0:T(8,128)(2,1)S(1)}, u32[]{:S(2)}, u32[]{:S(2)}) collective-permute-start(bf16[144,1024]{1,0:T(8,128)(2,1)S(1)} %collective-permute-done.2), channel_id=1, source_target_pairs={{0,8},{4,12},{8,0},{12,4},{1,9},{5,13},{9,1},{13,5},{2,10},{6,14},... | collective-permute-start | bytes 884744 | tf_op jit(solution)/shard_map/ppermute | solution.py:478
  22.5 13.8 %collective-permute-start.10 = (bf16[144,1024]{1,0:T(8,128)(2,1)S(1)}, bf16[144,1024]{1,0:T(8,128)(2,1)S(1)}, u32[]{:S(2)}, u32[]{:S(2)}) collective-permute-start(bf16[144,1024]{1,0:T(8,128)(2,1)S(1)} %collective-permute-done.2), channel_id=1, source_target_pairs={{0,1},{1,0},{2,3},{3,2},{4,5},{5,4},{6,7},{7,6},{8,9},{9,8},{10,11... | collective-permute-start | bytes 884744 | tf_op jit(solution)/shard_map/ppermute | solution.py:481
  23.1 13.1 %collective-permute-start.8 = (bf16[144,1024]{1,0:T(8,128)(2,1)S(1)}, bf16[144,1024]{1,0:T(8,128)(2,1)S(1)}, u32[]{:S(2)}, u32[]{:S(2)}) collective-permute-start(bf16[144,1024]{1,0:T(8,128)(2,1)S(1)} %collective-permute-done.7.refs_1_.a_ref), channel_id=1, source_target_pairs={{0,8},{4,12},{8,0},{12,4},{1,9},{5,13},{9,1},{13,5},{2,10},{6,14},... | collective-permute-start | bytes 884744 | tf_op jit(solution)/shard_map/ppermute | solution.py:478
  31.0 6.7 %collective-permute-start.11 = (bf16[144,1024]{1,0:T(8,128)(2,1)S(1)}, bf16[144,1024]{1,0:T(8,128)(2,1)S(1)}, u32[]{:S(2)}, u32[]{:S(2)}) collective-permute-start(bf16[144,1024]{1,0:T(8,128)(2,1)S(1)} %collective-permute-done.3.refs_1_), channel_id=1, source_target_pairs={{0,1},{1,0},{2,3},{3,2},{4,5},{5,4},{6,7},{7,6},{8,9},{9,8},{10,11... | collective-permute-start | bytes 884744 | tf_op jit(solution)/shard_map/ppermute | solution.py:481
  36.3 3.2 %collective-permute-start.9 = (bf16[288,1024]{1,0:T(8,128)(2,1)S(1)}, bf16[288,1024]{1,0:T(8,128)(2,1)S(1)}, u32[]{:S(2)}, u32[]{:S(2)}) collective-permute-start(bf16[288,1024]{1,0:T(8,128)(2,1)S(1)} %stack.21.refs_0_.refs_1_), channel_id=1, source_target_pairs={{0,4},{4,0},{8,12},{12,8},{1,5},{5,1},{9,13},{13,9},{2,6},{6,2},{1... | collective-permute-start | bytes 1769480 | tf_op jit(solution)/shard_map/ppermute | solution.py:478
  36.4 4.6 %collective-permute-start.4 = (bf16[288,1024]{1,0:T(8,128)(2,1)S(1)}, bf16[288,1024]{1,0:T(8,128)(2,1)S(1)}, u32[]{:S(2)}, u32[]{:S(2)}) collective-permute-start(bf16[288,1024]{1,0:T(8,128)(2,1)S(1)} %constant_dynamic-update-slice_fusion.refs_0_.refs_1_), channel_id=1, source_target_pairs={{0,4},{4,0},{8,12},{12,8},{1,5},{5,1},{9,13},{13,9},{2,6},{6,2},{1... | collective-permute-start | bytes 1769480 | tf_op jit(solution)/shard_map/ppermute | solution.py:478
  37.7 4.8 %collective-permute-start.12 = (bf16[288,1024]{1,0:T(8,128)(2,1)S(1)}, bf16[288,1024]{1,0:T(8,128)(2,1)S(1)}, u32[]{:S(2)}, u32[]{:S(2)}) collective-permute-start(bf16[288,1024]{1,0:T(8,128)(2,1)S(1)} %constant_dynamic-update-slice_fusion.2.refs_0_.refs_1_), channel_id=1, source_target_pairs={{0,4},{4,0},{8,12},{12,8},{1,5},{5,1},{9,13},{13,9},{2,6},{6,2},{1... | collective-permute-start | bytes 1769480 | tf_op jit(solution)/shard_map/ppermute | solution.py:478
  56.8 2.3 %collective-permute-start.15 = (bf16[1,256,1024]{2,1,0:T(8,128)(2,1)S(1)}, bf16[1,256,1024]{2,1,0:T(8,128)(2,1)S(1)}, u32[]{:S(2)}, u32[]{:S(2)}) collective-permute-start(bf16[1,256,1024]{2,1,0:T(8,128)(2,1)S(1)} %get-tuple-element.51), channel_id=1, source_target_pairs={{0,4},{4,0},{8,12},{12,8},{1,5},{5,1},{9,13},{13,9},{2,6},{6,2},{1... | collective-permute-start | bytes 1572872 | tf_op jit(solution)/shard_map/ppermute | solution.py:478
  57.4 23.1 %collective-permute-start.1 = (bf16[256,576]{1,0:T(8,128)(2,1)S(1)}, bf16[256,576]{1,0:T(8,128)(2,1)S(1)}, u32[]{:S(2)}, u32[]{:S(2)}) collective-permute-start(bf16[256,576]{1,0:T(8,128)(2,1)S(1)} %pad_maximum_fusion.1.refs_0_.refs_1_), channel_id=1, source_target_pairs={{0,4},{4,0},{8,12},{12,8},{1,5},{5,1},{9,13},{13,9},{2,6},{6,2},{1... | collective-permute-start | bytes 884744 | tf_op jit(solution)/shard_map/ppermute | solution.py:478
  58.0 3.5 %collective-permute-start.13 = (bf16[1,256,1024]{2,1,0:T(8,128)(2,1)S(1)}, bf16[1,256,1024]{2,1,0:T(8,128)(2,1)S(1)}, u32[]{:S(2)}, u32[]{:S(2)}) collective-permute-start(bf16[1,256,1024]{2,1,0:T(8,128)(2,1)S(1)} %get-tuple-element.47), channel_id=1, source_target_pairs={{0,4},{4,0},{8,12},{12,8},{1,5},{5,1},{9,13},{13,9},{2,6},{6,2},{1... | collective-permute-start | bytes 1572872 | tf_op jit(solution)/shard_map/ppermute | solution.py:478
  59.0 10.3 %collective-permute-start.19 = (bf16[1,256,1024]{2,1,0:T(8,128)(2,1)S(1)}, bf16[1,256,1024]{2,1,0:T(8,128)(2,1)S(1)}, u32[]{:S(2)}, u32[]{:S(2)}) collective-permute-start(bf16[1,256,1024]{2,1,0:T(8,128)(2,1)S(1)} %get-tuple-element.55), channel_id=1, source_target_pairs={{0,4},{4,0},{8,12},{12,8},{1,5},{5,1},{9,13},{13,9},{2,6},{6,2},{1... | collective-permute-start | bytes 1572872 | tf_op jit(solution)/shard_map/ppermute | solution.py:478
  59.2 9.2 %collective-permute-start.16 = (bf16[1,128,1024]{2,1,0:T(8,128)(2,1)S(1)}, bf16[1,128,1024]{2,1,0:T(8,128)(2,1)S(1)}, u32[]{:S(2)}, u32[]{:S(2)}) collective-permute-start(bf16[1,128,1024]{2,1,0:T(8,128)(2,1)S(1)} %add_convert_fusion.5), channel_id=1, source_target_pairs={{0,8},{4,12},{8,0},{12,4},{1,9},{5,13},{9,1},{13,5},{2,10},{6,14},... | collective-permute-start | bytes 786440 | tf_op jit(solution)/shard_map/ppermute | solution.py:478
  61.2 9.7 %collective-permute-start.22 = (bf16[1,256,1024]{2,1,0:T(8,128)(2,1)S(1)}, bf16[1,256,1024]{2,1,0:T(8,128)(2,1)S(1)}, u32[]{:S(2)}, u32[]{:S(2)}) collective-permute-start(bf16[1,256,1024]{2,1,0:T(8,128)(2,1)S(1)} %get-tuple-element.59), channel_id=1, source_target_pairs={{0,4},{4,0},{8,12},{12,8},{1,5},{5,1},{9,13},{13,9},{2,6},{6,2},{1... | collective-permute-start | bytes 1572872 | tf_op jit(solution)/shard_map/ppermute | solution.py:478
  61.6 12.4 %collective-permute-start.14 = (bf16[1,128,1024]{2,1,0:T(8,128)(2,1)S(1)}, bf16[1,128,1024]{2,1,0:T(8,128)(2,1)S(1)}, u32[]{:S(2)}, u32[]{:S(2)}) collective-permute-start(bf16[1,128,1024]{2,1,0:T(8,128)(2,1)S(1)} %add_convert_fusion.6), channel_id=1, source_target_pairs={{0,8},{4,12},{8,0},{12,4},{1,9},{5,13},{9,1},{13,5},{2,10},{6,14},... | collective-permute-start | bytes 786440 | tf_op jit(solution)/shard_map/ppermute | solution.py:478
  68.5 7.6 %collective-permute-start.17 = (bf16[1,128,1024]{2,1,0:T(8,128)(2,1)S(1)}, bf16[1,128,1024]{2,1,0:T(8,128)(2,1)S(1)}, u32[]{:S(2)}, u32[]{:S(2)}) collective-permute-start(bf16[1,128,1024]{2,1,0:T(8,128)(2,1)S(1)} %add_convert_fusion.4), channel_id=1, source_target_pairs={{0,1},{1,0},{2,3},{3,2},{4,5},{5,4},{6,7},{7,6},{8,9},{9,8},{10,11... | collective-permute-start | bytes 786440 | tf_op jit(solution)/shard_map/ppermute | solution.py:481
  69.3 10.2 %collective-permute-start.20 = (bf16[1,128,1024]{2,1,0:T(8,128)(2,1)S(1)}, bf16[1,128,1024]{2,1,0:T(8,128)(2,1)S(1)}, u32[]{:S(2)}, u32[]{:S(2)}) collective-permute-start(bf16[1,128,1024]{2,1,0:T(8,128)(2,1)S(1)} %add_convert_fusion.2), channel_id=1, source_target_pairs={{0,8},{4,12},{8,0},{12,4},{1,9},{5,13},{9,1},{13,5},{2,10},{6,14},... | collective-permute-start | bytes 786440 | tf_op jit(solution)/shard_map/ppermute | solution.py:478
  71.0 16.3 %collective-permute-start.23 = (bf16[1,128,1024]{2,1,0:T(8,128)(2,1)S(1)}, bf16[1,128,1024]{2,1,0:T(8,128)(2,1)S(1)}, u32[]{:S(2)}, u32[]{:S(2)}) collective-permute-start(bf16[1,128,1024]{2,1,0:T(8,128)(2,1)S(1)} %add_convert_fusion.1), channel_id=1, source_target_pairs={{0,8},{4,12},{8,0},{12,4},{1,9},{5,13},{9,1},{13,5},{2,10},{6,14},... | collective-permute-start | bytes 786440 | tf_op jit(solution)/shard_map/ppermute | solution.py:478
  76.2 14.2 %collective-permute-start.18 = (bf16[1,128,1024]{2,1,0:T(8,128)(2,1)S(1)}, bf16[1,128,1024]{2,1,0:T(8,128)(2,1)S(1)}, u32[]{:S(2)}, u32[]{:S(2)}) collective-permute-start(bf16[1,128,1024]{2,1,0:T(8,128)(2,1)S(1)} %add_convert_fusion.3.refs_0_), channel_id=1, source_target_pairs={{0,3},{1,2},{2,1},{3,0},{4,7},{5,6},{6,5},{7,4},{8,11},{9,10},{10,... | collective-permute-start | bytes 786440 | tf_op jit(solution)/shard_map/ppermute | solution.py:481
  79.7 10.7 %collective-permute-start.21 = (bf16[1,128,1024]{2,1,0:T(8,128)(2,1)S(1)}, bf16[1,128,1024]{2,1,0:T(8,128)(2,1)S(1)}, u32[]{:S(2)}, u32[]{:S(2)}) collective-permute-start(bf16[1,128,1024]{2,1,0:T(8,128)(2,1)S(1)} %join.1), channel_id=1, source_target_pairs={{0,1},{1,0},{2,3},{3,2},{4,5},{5,4},{6,7},{7,6},{8,9},{9,8},{10,11... | collective-permute-start | bytes 786440 | tf_op jit(solution)/shard_map/ppermute | solution.py:481
  (6 other events, 34.7 us)
